TPU v7x, 32 devices: a whole 2x2x4 slice. The times are simulated.
32 devices in a mesh: groups: 2 (over y), wide: 4 (over z), narrow: 4 (over x, core).
Axes of the slice: x: 2, y: 2, z: 4, core: 2. Of those that a mesh axis runs over, the one named last changes fastest.
Arguments:
- homolog_embedding: bfloat16 [256, 192, 256], P(('groups', 'narrow'), 'wide'), parts along dimension 0, may hold values from -6 to 6
- normalize_scale: float32 [256], replicated, may hold values from 0.1 to 1.9
- normalize_shift: float32 [256], replicated, may hold values from -3 to 3
- lhs_factor_matrix: bfloat16 [256, 32], replicated, may hold values from -0.375 to 0.375
- lhs_factor_shift: float32 [32], replicated, may hold values from -1 to 1
- rhs_factor_matrix: bfloat16 [256, 32], replicated, may hold values from -0.375 to 0.375
- rhs_factor_shift: float32 [32], replicated, may hold values from -1 to 1
- pair_update_matrix: bfloat16 [1024, 128], replicated, may hold values from -1.796875 to 1.796875
- pair_update_shift: float32 [128], replicated, may hold values from -3 to 3
Outputs:
- pair_update: bfloat16 [384, 192, 128], P(('groups', 'wide', 'narrow')), parts along dimension 0
There are 2 independent parts, one for each index of `groups`. A program takes and returns all parts, laid end to end along the dimension named above; an argument that names none is the same for every part. Nothing has to cross between parts.
All inputs are finite; a program needn't handle non-finite values.
Results may differ from a plain program's by a relative error of at most 0.0053.
Values may be sent and summed in bfloat16 or wider, within the bound.
No kernel may reach another device: no remote copies, remote signals or barrier semaphores. Data moves between devices by JAX's collectives and lax.ppermute only.
A program may use at most 64 MiB of HBM per device.

v0:
```python
import jax
import jax.numpy as jnp
from jax import lax
from jax.sharding import PartitionSpec as P

HOMOLOG_TOTAL = 128
HIDDEN_DEPTH = 32
CZ = 128
ROWS_DEV = 12


def map_through_matrix(
    homolog_embedding, normalize_scale, normalize_shift, mapping_matrix, additive_shift
):
    source_tensor = homolog_embedding.astype(jnp.float32)
    center = jnp.mean(source_tensor, axis=-1, keepdims=True)
    spread = jnp.mean((source_tensor - center) ** 2, axis=-1, keepdims=True)
    normed = (
        (source_tensor - center) / jnp.sqrt(spread + 1e-05) * normalize_scale + normalize_shift
    ).astype(jnp.bfloat16)
    flat = normed.reshape(-1, normed.shape[-1])
    return (
        jnp.dot(flat, mapping_matrix, preferred_element_type=jnp.float32) + additive_shift
    ).astype(jnp.bfloat16)


def pair_block(left_rows, right_cols, pair_update_matrix, pair_update_shift):
    count_rows = left_rows.shape[1] // HIDDEN_DEPTH
    count_cols = right_cols.shape[1] // HIDDEN_DEPTH
    outer = (
        lax.dot_general(
            left_rows, right_cols, (((0,), (0,)), ((), ())), preferred_element_type=jnp.float32
        )
        / HOMOLOG_TOTAL
    )
    outer = outer.astype(jnp.bfloat16).reshape(count_rows, HIDDEN_DEPTH, count_cols, HIDDEN_DEPTH)
    weights = pair_update_matrix.reshape(HIDDEN_DEPTH, HIDDEN_DEPTH, CZ)
    result = (
        lax.dot_general(
            outer, weights, (((1, 3), (0, 1)), ((), ())), preferred_element_type=jnp.float32
        )
        + pair_update_shift
    )
    return result.astype(jnp.bfloat16)


def on_device(
    homolog_embedding,
    normalize_scale,
    normalize_shift,
    lhs_factor_matrix,
    lhs_factor_shift,
    rhs_factor_matrix,
    rhs_factor_shift,
    pair_update_matrix,
    pair_update_shift,
):
    partition_down_axis = homolog_embedding.shape[0]
    partition_across_axis = homolog_embedding.shape[1]
    lhs_factor_tensor = map_through_matrix(
        homolog_embedding, normalize_scale, normalize_shift, lhs_factor_matrix, lhs_factor_shift
    )
    rhs_factor_tensor = map_through_matrix(
        homolog_embedding, normalize_scale, normalize_shift, rhs_factor_matrix, rhs_factor_shift
    )
    left_blocks = lhs_factor_tensor.reshape(
        partition_down_axis, partition_across_axis // ROWS_DEV, ROWS_DEV * HIDDEN_DEPTH
    )
    owned = lax.all_to_all(left_blocks, "narrow", split_axis=1, concat_axis=0, tiled=True)
    right_cols = lax.all_gather(
        rhs_factor_tensor.reshape(partition_down_axis, partition_across_axis * HIDDEN_DEPTH),
        "narrow",
        axis=0,
        tiled=True,
    )
    blocks = jnp.moveaxis(lax.all_gather(owned, "wide", axis=1, tiled=True), 1, 0)
    result = lax.map(
        lambda rows: pair_block(rows, right_cols, pair_update_matrix, pair_update_shift), blocks
    )
    grid_block = result.reshape(-1, partition_across_axis, CZ)
    return lax.all_to_all(grid_block, "wide", split_axis=0, concat_axis=1, tiled=True)


def solution(mesh):
    in_specs = (P(("groups", "narrow"), "wide", None), P(), P(), P(), P(), P(), P(), P(), P())
    out_specs = P(("groups", "wide", "narrow"), None, None)
    return jax.shard_map(
        on_device, mesh=mesh, in_specs=in_specs, out_specs=out_specs, check_vma=False
    )
```

profile of v0, /device:TPU:0, one launch (start us, length us, event | category | flops | bytes accessed | tf_op | source)
XLA Modules:
  0.0 85.3 jit_solution(11058291963337949803)
XLA Ops:
  0.0 0.0 copy-start
  0.0 0.0 copy-start.1
  0.0 0.0 copy-start.4
  0.0 0.0 copy-start.3
  0.0 0.0 copy-start.5
  0.0 1.5 %convert_reduce_fusion = f32[32,48]{1,0:T(8,128)S(1)} fusion(bf16[32,48,256]{2,1,0:T(8,128)(2,1)} %param.11), kind=kLoop, calls=%fused_computation.15 | loop fusion | flops 784896 | bytes 792576 | tf_op jit(solution)/shard_map/reduce_sum | solution.py:16
  1.5 1.6 %fusion.12 = f32[32,48]{1,0:T(8,128)S(1)} fusion(bf16[32,48,256]{2,1,0:T(8,128)(2,1)} %param.11, f32[32,48]{1,0:T(8,128)S(1)} %broadcast_multiply_fusion), kind=kLoop, calls=%fused_computation.18 | loop fusion | flops 1571328 | bytes 798720 | tf_op jit(solution)/shard_map/reduce_sum | solution.py:17
  3.2 0.0 copy-done.1
  3.2 0.0 copy-done.4
  3.2 0.0 copy-done.3
  3.2 0.0 copy-start.2
  3.2 0.0 copy-start.6
  3.2 0.5 fusion.15
  3.7 0.0 copy-done
  3.7 0.0 copy-done.5
  3.7 0.3 fusion.8
  4.1 0.2 copy.20
  4.3 0.3 reshape.37
  4.6 0.7 copy.21
  5.2 0.0 copy-start.7
  5.2 0.0 copy-start.8
  5.2 4.3 %all-to-all-start = ((bf16[32,4,384]{2,0,1:T(8,128)(2,1)}), bf16[32,4,384]{2,0,1:T(8,128)(2,1)S(1)}, u32[]{:S(2)}, u32[]{:S(2)}) async-start(bf16[32,4,384]{2,0,1:T(8,128)(2,1)} %copy.21), calls=%async_computation | async-start | bytes 196608 | tf_op jit(solution)/shard_map/all_to_all | solution.py:69
  9.6 0.0 copy-done.2
  9.6 0.0 copy-done.6
  9.6 0.3 fusion.9
  9.9 0.2 copy.22
  10.2 0.3 reshape.38
  10.5 7.0 %all_gather.7 = bf16[128,1536]{1,0:T(8,128)(2,1)S(1)} all-gather(bf16[32,1536]{1,0:T(8,128)(2,1)S(1)} %reshape.38), channel_id=1, replica_groups=mesh['groups'=2,'wide'=4,'narrow'=4] {'narrow'}, dimensions={0}, use_global_device_ids=true | all-gather | bytes 491520 | tf_op jit(solution)/shard_map/all_gather | solution.py:70
  17.5 0.0 all-to-all-done
  17.5 15.4 %all_gather.6 = bf16[128,4,384]{2,0,1:T(8,128)(2,1)S(1)} all-gather(bf16[128,1,384]{2,0,1:T(8,128)(2,1)S(1)} %bitcast.59), channel_id=1, replica_groups=mesh['groups'=2,'wide'=4,'narrow'=4] {'wide'}, dimensions={1}, use_global_device_ids=true | all-gather | bytes 491520 | tf_op jit(solution)/shard_map/all_gather | solution.py:76
  32.9 0.0 copy-done.7
  32.9 0.0 copy-done.8
  32.9 33.1 %while.10 = (s32[]{:T(128)}, bf16[4,12,48,128]{3,2,1,0:T(8,128)(2,1)S(1)}, bf16[4,128,384]{2,1,0:T(8,128)(2,1)S(1)}, bf16[128,1536]{1,0:T(8,128)(2,1)S(1)}, bf16...) while((s32[]{:T(128)}, bf16[4,12,48,128]{3,2,1,0:T(8,128)(2,1)S(1)}, ...), condition=%wide.region_3.0_spmd, body=%wide.region_2.0_spmd.sunk | while | flops 303316992 | bytes 5620309 | solution.py:77
  32.9 0.5 fusion.33
  33.4 4.4 %reshape.43 = bf16[12,32,48,32]{3,2,1,0:T(8,128)(2,1)} reshape(bf16[384,1536]{1,0:T(8,128)(2,1)S(1)} %fusion.33) | data formatting | bytes 2359296 | tf_op jit(solution)/shard_map/while/body/eval_jaxpr/reshape | solution.py:36
  37.8 3.4 %fusion.34 = bf16[4,12,48,128]{3,2,1,0:T(8,128)(2,1)S(1)} fusion(bf16[4,12,48,128]{3,2,1,0:T(8,128)(2,1)S(1)} %get-tuple-element.95, s32[]{:T(128)} %get-tuple-element.94, bf16[12,32,48,32]{3,2,1,0:T(8,128)(2,1)} %reshape.43, bf16[32,32,128,1]{2,1,0,3:T(8,128)(2,1)S(1)} %bitcast.60, f32[128]{0:T(128)S(1)} %get-tuple-element.106), kind=kOutput, calls=%fused_computation.6.clone.1 | convolution fusion | flops 151142400 | bytes 1589764 | tf_op jit(solution)/shard_map/while/body/eval_jaxpr/dot_general | solution.py:39
  41.2 0.5 fusion.33
  41.7 4.4 %reshape.43 = bf16[12,32,48,32]{3,2,1,0:T(8,128)(2,1)} reshape(bf16[384,1536]{1,0:T(8,128)(2,1)S(1)} %fusion.33) | data formatting | bytes 2359296 | tf_op jit(solution)/shard_map/while/body/eval_jaxpr/reshape | solution.py:36
  46.1 3.4 %fusion.34 = bf16[4,12,48,128]{3,2,1,0:T(8,128)(2,1)S(1)} fusion(bf16[4,12,48,128]{3,2,1,0:T(8,128)(2,1)S(1)} %get-tuple-element.95, s32[]{:T(128)} %get-tuple-element.94, bf16[12,32,48,32]{3,2,1,0:T(8,128)(2,1)} %reshape.43, bf16[32,32,128,1]{2,1,0,3:T(8,128)(2,1)S(1)} %bitcast.60, f32[128]{0:T(128)S(1)} %get-tuple-element.106), kind=kOutput, calls=%fused_computation.6.clone.1 | convolution fusion | flops 151142400 | bytes 1589764 | tf_op jit(solution)/shard_map/while/body/eval_jaxpr/dot_general | solution.py:39
  49.5 0.5 fusion.33
  50.0 4.4 %reshape.43 = bf16[12,32,48,32]{3,2,1,0:T(8,128)(2,1)} reshape(bf16[384,1536]{1,0:T(8,128)(2,1)S(1)} %fusion.33) | data formatting | bytes 2359296 | tf_op jit(solution)/shard_map/while/body/eval_jaxpr/reshape | solution.py:36
  54.3 3.4 %fusion.34 = bf16[4,12,48,128]{3,2,1,0:T(8,128)(2,1)S(1)} fusion(bf16[4,12,48,128]{3,2,1,0:T(8,128)(2,1)S(1)} %get-tuple-element.95, s32[]{:T(128)} %get-tuple-element.94, bf16[12,32,48,32]{3,2,1,0:T(8,128)(2,1)} %reshape.43, bf16[32,32,128,1]{2,1,0,3:T(8,128)(2,1)S(1)} %bitcast.60, f32[128]{0:T(128)S(1)} %get-tuple-element.106), kind=kOutput, calls=%fused_computation.6.clone.1 | convolution fusion | flops 151142400 | bytes 1589764 | tf_op jit(solution)/shard_map/while/body/eval_jaxpr/dot_general | solution.py:39
  57.7 0.5 fusion.33
  58.2 4.4 %reshape.43 = bf16[12,32,48,32]{3,2,1,0:T(8,128)(2,1)} reshape(bf16[384,1536]{1,0:T(8,128)(2,1)S(1)} %fusion.33) | data formatting | bytes 2359296 | tf_op jit(solution)/shard_map/while/body/eval_jaxpr/reshape | solution.py:36
  62.6 3.4 %fusion.34 = bf16[4,12,48,128]{3,2,1,0:T(8,128)(2,1)S(1)} fusion(bf16[4,12,48,128]{3,2,1,0:T(8,128)(2,1)S(1)} %get-tuple-element.95, s32[]{:T(128)} %get-tuple-element.94, bf16[12,32,48,32]{3,2,1,0:T(8,128)(2,1)} %reshape.43, bf16[32,32,128,1]{2,1,0,3:T(8,128)(2,1)S(1)} %bitcast.60, f32[128]{0:T(128)S(1)} %get-tuple-element.106), kind=kOutput, calls=%fused_computation.6.clone.1 | convolution fusion | flops 151142400 | bytes 1589764 | tf_op jit(solution)/shard_map/while/body/eval_jaxpr/dot_general | solution.py:39
  66.0 18.5 %all_to_all.36 = bf16[48,48,128]{2,1,0:T(8,128)(2,1)S(1)} all-to-all(bf16[48,48,128]{2,1,0:T(8,128)(2,1)S(1)} %bitcast.58), channel_id=1, replica_groups=mesh['groups'=2,'wide'=4,'narrow'=4] {'wide'}, dimensions={0} | all-to-all | bytes 1179648 | tf_op jit(solution)/shard_map/all_to_all | solution.py:81
  84.5 0.9 %copy.23 = bf16[12,4,48,128]{3,2,1,0:T(8,128)(2,1)} copy(bf16[12,4,48,128]{3,2,0,1:T(8,128)(2,1)S(1)} %bitcast.56) | data formatting | bytes 1179648 | tf_op jit(solution)/shard_map/all_to_all | solution.py:81
  (3 shorter events, 0.0 us)
Async XLA Ops:
  0.0 3.7 %copy-start = (bf16[256,32]{0,1:T(8,128)(2,1)S(1)}, bf16[256,32]{0,1:T(8,128)(2,1)}, u32[]{:S(2)}) copy-start(bf16[256,32]{0,1:T(8,128)(2,1)} %param.14) | copy-start | bytes 49156
  0.0 3.2 %copy-start.1 = (bf16[32,48,256]{2,1,0:T(8,128)(2,1)S(1)}, bf16[32,48,256]{2,1,0:T(8,128)(2,1)}, u32[]{:S(2)}) copy-start(bf16[32,48,256]{2,1,0:T(8,128)(2,1)} %param.11) | copy-start | bytes 2359300
  0.0 3.2 %copy-start.4 = (f32[256]{0:T(256)S(1)}, f32[256]{0:T(256)}, u32[]{:S(2)}) copy-start(f32[256]{0:T(256)} %param.12) | copy-start | bytes 3076
  0.0 3.2 %copy-start.3 = (f32[256]{0:T(256)S(1)}, f32[256]{0:T(256)}, u32[]{:S(2)}) copy-start(f32[256]{0:T(256)} %param.13) | copy-start | bytes 3076
  0.0 3.7 %copy-start.5 = (f32[32]{0:T(128)S(1)}, f32[32]{0:T(128)}, u32[]{:S(2)}) copy-start(f32[32]{0:T(128)} %param.15) | copy-start | bytes 388
  3.2 6.4 %copy-start.2 = (bf16[256,32]{0,1:T(8,128)(2,1)S(1)}, bf16[256,32]{0,1:T(8,128)(2,1)}, u32[]{:S(2)}) copy-start(bf16[256,32]{0,1:T(8,128)(2,1)} %param.16) | copy-start | bytes 49156
  3.2 6.4 %copy-start.6 = (f32[32]{0:T(128)S(1)}, f32[32]{0:T(128)}, u32[]{:S(2)}) copy-start(f32[32]{0:T(128)} %param.17) | copy-start | bytes 388
  5.2 27.7 %copy-start.7 = (bf16[1024,128]{1,0:T(8,128)(2,1)S(1)}, bf16[1024,128]{1,0:T(8,128)(2,1)}, u32[]{:S(2)}) copy-start(bf16[1024,128]{1,0:T(8,128)(2,1)} %param.18) | copy-start | bytes 786436
  5.2 27.7 %copy-start.8 = (f32[128]{0:T(128)S(1)}, f32[128]{0:T(128)}, u32[]{:S(2)}) copy-start(f32[128]{0:T(128)} %param.19) | copy-start | bytes 1540
  5.2 12.3 %all-to-all-start = ((bf16[32,4,384]{2,0,1:T(8,128)(2,1)}), bf16[32,4,384]{2,0,1:T(8,128)(2,1)S(1)}, u32[]{:S(2)}, u32[]{:S(2)}) async-start(bf16[32,4,384]{2,0,1:T(8,128)(2,1)} %copy.21), calls=%async_computation | async-start | bytes 196608 | tf_op jit(solution)/shard_map/all_to_all | solution.py:69
where the time goes:
time: 85.8 us; the launch traced here: 85.3 us
  blocking collectives  40.9 us (48%)
  local copies, waits for them, and re-layouts  20.1 us (23%)
  matrix products  16.2 us (19%)
  starting transfers between devices  4.35 us (5%)
  other arithmetic  3.62 us (4%)
    all_to_all x1, blocking collectives, on_device(): lax.all_to_all(grid_block, 'wide', split_axis=0, concat_axis=1, tiled=True)  18.5 us
    reshape x4, local copies, waits for them, and re-layouts, pair_block(): outer.astype(jnp.bfloat16)  17.5 us
    all_gather x1, blocking collectives, on_device(): lax.all_gather(owned, 'wide', axis=1, tiled=True)  15.4 us
    dot_general x4, matrix products, pair_block(): lax.dot_general(outer, weights, (((1, 3), (0, 1)), ((), ())), preferred_e...  13.6 us
    all_gather x1, blocking collectives, on_device(): lax.all_gather(rhs_factor_tensor.reshape(partition_down_axis, partition_a...  7.02 us
    all_to_all x1, starting transfers between devices, on_device(): lax.all_to_all(left_blocks, 'narrow', split_axis=1, concat_axis=0, tiled=...  4.35 us
    dot_general x4, matrix products, pair_block(): lax.dot_general(left_rows, right_cols, (((0,), (0,)), ((), ())), preferre...  1.98 us
  transfers between devices with their start and end apart: 1, of which 0 were waited for; matrix products, arithmetic and copies ran while one was open for 1% of the time, Pallas kernels for 0%

commit v1 on v0

v1 whole, which is shorter than its diff:
```python
import functools

import jax
import jax.numpy as jnp
from jax import lax
from jax.experimental import pallas as pl
from jax.experimental.pallas import tpu as pltpu
from jax.sharding import PartitionSpec as P

LANES = 128
VMEM_LIMIT = 50 * 1024 * 1024


def iota(shape, dim):
    return lax.broadcasted_iota(jnp.int32, shape, dim)


def features_kernel(
    x_ref, gain_ref, bias_ref, lm_ref, lb_ref, rm_ref, rb_ref,
    left_ref, right_ref,
    lo_ref, hi_ref, turned_ref, rows_ref,
):
    seqs, residues, depth = x_ref.shape
    hidden = lm_ref.shape[1]
    per = LANES // hidden
    slots = LANES // seqs
    minor = hidden // slots
    groups = residues // per
    own = lax.axis_index("narrow")

    gain = gain_ref[...].reshape(1, depth)
    bias = bias_ref[...].reshape(1, depth)
    step = 4
    for s in range(0, seqs, step):
        x = x_ref[s : s + step].reshape(step * residues, depth).astype(jnp.float32)
        x = x - jnp.mean(x, axis=-1, keepdims=True)
        spread = jnp.mean(x * x, axis=-1, keepdims=True)
        x = x * lax.rsqrt(spread + 1e-05) * gain + bias
        rows = pl.ds(s * residues, step * residues)
        lo_ref[rows, :] = x[:, :LANES]
        hi_ref[rows, :] = x[:, LANES:]

    spread_l = (iota((hidden, LANES), 1) % hidden == iota((hidden, LANES), 0))
    spread_r = iota((hidden, LANES), 1) % hidden == (iota((hidden, LANES), 0) + own * minor) % hidden
    spread_l = spread_l.astype(jnp.float32)
    spread_r = spread_r.astype(jnp.float32)

    def widen(m, pick):
        return jnp.dot(m, pick.astype(jnp.bfloat16), preferred_element_type=jnp.float32)

    def widen_bias(b, pick):
        b = jnp.broadcast_to(b.reshape(1, hidden), (8, hidden))
        return jnp.dot(
            b, pick, precision=lax.Precision.HIGHEST, preferred_element_type=jnp.float32
        )[:1]

    weights = jnp.concatenate(
        [widen(lm_ref[...], spread_l), widen(rm_ref[...], spread_r)], axis=1
    )
    shift = jnp.concatenate(
        [widen_bias(lb_ref[...], spread_l), widen_bias(rb_ref[...], spread_r)], axis=1
    )
    place = iota((depth, 2 * LANES), 1) % LANES // hidden
    total = None
    for k in range(per):
        part = jnp.concatenate(
            [
                jnp.concatenate(
                    [half[pl.ds(g * per + k, seqs, stride=residues), :] for half in (lo_ref, hi_ref)],
                    axis=1,
                )
                for g in range(groups)
            ],
            axis=0,
        ).astype(jnp.bfloat16)
        placed = jnp.where(place == k, weights, 0.0).astype(jnp.bfloat16)
        term = jnp.dot(part, placed, preferred_element_type=jnp.float32)
        total = term if total is None else total + term
    total = total + shift
    left_ref[...] = total[:, :LANES].astype(left_ref.dtype).reshape(groups, seqs, LANES)

    slot = iota((minor, LANES), 1) // seqs
    for block in range(groups // slots):
        turned_ref[...] = total[block * LANES : (block + 1) * LANES, LANES:].T
        for k in range(per):
            pieces = [turned_ref[pl.ds(k * hidden + q * minor, minor), :] for q in range(slots)]
            for g in range(slots):
                out = None
                for q in range(slots):
                    piece = pieces[q]
                    if q != g:
                        piece = pltpu.roll(piece, (q - g) % slots * seqs, axis=1)
                    out = piece if out is None else jnp.where(slot == q, piece, out)
                j = (block * slots + g) * per + k
                rows_ref[pl.ds(j, minor, stride=residues), :] = out
    right_ref[...] = rows_ref[...].astype(right_ref.dtype).reshape(minor, residues, LANES)


def pair_kernel(left_ref, right_ref, w_ref, shift_ref, out_ref, wf_ref, wide_ref, outer_ref, *, seqs_total):
    parts, groups, seqs, _ = left_ref.shape
    wides, _, minor, residues, _ = right_ref.shape
    cz = w_ref.shape[1]
    hidden = minor * parts
    per = LANES // hidden
    cols = wides * residues

    @pl.when(pl.program_id(0) == 0)
    def _():
        wf_ref[...] = w_ref[...].astype(jnp.float32)
        wide_ref[...] = jnp.zeros_like(wide_ref)
        for e in range(hidden):
            rows = wf_ref[pl.ds(e, hidden, stride=hidden), :].astype(jnp.bfloat16)
            for k in range(per):
                wide_ref[pl.ds(e * LANES + k * hidden, hidden), k * cz : (k + 1) * cz] = rows

    slot = iota((minor * residues, LANES), 1) // seqs
    for q in range(parts):
        left = jnp.concatenate(
            [
                jnp.concatenate([left_ref[(k - q) % parts, g] for k in range(parts)], axis=0)
                for g in range(groups)
            ],
            axis=1,
        )
        for w in range(wides):
            right = None
            for k in range(parts):
                chunk = right_ref[w, (k - q) % parts].reshape(minor * residues, LANES)
                right = chunk if right is None else jnp.where(slot == k, chunk, right)
            outer = jnp.dot(right, left, preferred_element_type=jnp.float32).astype(jnp.bfloat16)
            for e in range(minor):
                for g in range(groups):
                    outer_ref[
                        pl.ds(g * cols + w * residues, residues),
                        (q * minor + e) * LANES : (q * minor + e + 1) * LANES,
                    ] = outer[e * residues : (e + 1) * residues, g * LANES : (g + 1) * LANES]

    shift = shift_ref[...].reshape(1, cz)
    for g in range(groups):
        pair = jnp.dot(
            outer_ref[pl.ds(g * cols, cols), :], wide_ref[...], preferred_element_type=jnp.float32
        )
        for k in range(per):
            out_ref[g * per + k] = (
                pair[:, k * cz : (k + 1) * cz] * (1.0 / seqs_total) + shift
            ).astype(out_ref.dtype)


def vmem(count):
    return [pl.BlockSpec(memory_space=pltpu.VMEM)] * count


def on_device(wide, narrow, x, gain, bias, lm, lb, rm, rb, w, shift):
    seqs, residues, depth = x.shape
    hidden = lm.shape[1]
    cz = w.shape[1]
    per = LANES // hidden
    slots = LANES // seqs
    minor = hidden // slots
    own_rows = residues // narrow
    groups = own_rows // per
    left, right = pl.pallas_call(
        features_kernel,
        out_shape=(
            jax.ShapeDtypeStruct((residues // per, seqs, LANES), jnp.bfloat16),
            jax.ShapeDtypeStruct((minor, residues, LANES), jnp.bfloat16),
        ),
        in_specs=vmem(7),
        out_specs=tuple(vmem(2)),
        scratch_shapes=[
            pltpu.VMEM((seqs * residues, LANES), jnp.float32),
            pltpu.VMEM((seqs * residues, LANES), jnp.float32),
            pltpu.VMEM((LANES, LANES), jnp.float32),
            pltpu.VMEM((minor * residues, LANES), jnp.float32),
        ],
        compiler_params=pltpu.CompilerParams(vmem_limit_bytes=VMEM_LIMIT),
        name="features",
    )(x, gain, bias, lm, lb, rm, rb)
    right = lax.all_gather(right, ("wide", "narrow"), axis=0, tiled=False)
    right = right.reshape(wide, narrow, minor, residues, LANES)
    left = left.reshape(narrow, groups, seqs, LANES)
    left = lax.all_to_all(left, "narrow", split_axis=0, concat_axis=0, tiled=True)
    block = wide
    while block % 2 == 0 and block * residues > 192:
        block //= 2
    cols = block * residues
    return pl.pallas_call(
        functools.partial(pair_kernel, seqs_total=seqs * narrow),
        grid=(wide // block,),
        out_shape=jax.ShapeDtypeStruct((own_rows, wide * residues, cz), jnp.bfloat16),
        in_specs=[
            pl.BlockSpec((narrow, groups, seqs, LANES), lambda b: (0, 0, 0, 0)),
            pl.BlockSpec((block, narrow, minor, residues, LANES), lambda b: (b, 0, 0, 0, 0)),
            pl.BlockSpec(w.shape, lambda b: (0, 0)),
            pl.BlockSpec(shift.shape, lambda b: (0,)),
        ],
        out_specs=pl.BlockSpec((own_rows, cols, cz), lambda b: (0, b, 0)),
        scratch_shapes=[
            pltpu.VMEM(w.shape, jnp.float32),
            pltpu.VMEM((hidden * LANES, per * cz), jnp.bfloat16),
            pltpu.VMEM((groups * cols, hidden * LANES), jnp.bfloat16),
        ],
        compiler_params=pltpu.CompilerParams(vmem_limit_bytes=VMEM_LIMIT),
        name="pairs",
    )(left, right, w, shift)


def solution(mesh):
    in_specs = (P(("groups", "narrow"), "wide", None), P(), P(), P(), P(), P(), P(), P(), P())
    out_specs = P(("groups", "wide", "narrow"), None, None)
    return jax.shard_map(
        functools.partial(on_device, mesh.shape["wide"], mesh.shape["narrow"]),
        mesh=mesh,
        in_specs=in_specs,
        out_specs=out_specs,
        check_vma=False,
    )
```

time: 85.8 us -> 71.8 us (0.84)
  waiting for transfers between devices: 0.01 us -> 34.2 us
  blocking collectives: 40.9 us -> 8.3 us
  matrix products: 16.2 us -> 0 us
  between operations: 0.17 us -> 13.4 us
  local copies, waits for them, and re-layouts: 20.1 us -> 8.48 us
  Pallas kernels: 0 us -> 7 us
  starting transfers between devices: 4.35 us -> 0.01 us
  other arithmetic: 3.62 us -> 0 us
    all_gather x0 -> x1, waiting for transfers between devices: none -> 34.2 us  [on_device(): right = lax.all_gather(right, ('wide', 'narrow'), axis=0, tiled=False)]
    all_gather x2 -> x0, blocking collectives: 22.4 us -> none  [the longest x1 15.4 us: on_device(): lax.all_gather(owned, 'wide', axis=1, tiled=True)]
    reshape x7 -> x0, local copies, waits for them, and re-layouts: 18.7 us -> none  [the longest x4 17.5 us: pair_block(): outer.astype(jnp.bfloat16)]
    dot_general x10 -> x0, matrix products: 16.2 us -> none  [the longest x4 13.6 us: pair_block(): lax.dot_general(outer, weights, (((1, 3), (0, 1)), ((), ())), preferred_e...]
    all_to_all x1, blocking collectives: 18.5 us -> 8.3 us  [on_device(): lax.all_to_all(left, 'narrow', split_axis=0, concat_axis=0, tiled=True)]
    unnamed x18, local copies, waits for them, and re-layouts: 0.04 us -> 8.48 us
    pallas_call x0 -> x2, Pallas kernels: none -> 7 us  [the longest x1 4.88 us: on_device(): pl.pallas_call(functools.partial(pair_kernel, seqs_total=seqs * narrow),...]
    all_to_all x1 -> x0, starting transfers between devices: 4.35 us -> none  [on_device(): lax.all_to_all(left_blocks, 'narrow', split_axis=1, concat_axis=0, tiled=...]
  transfers between devices with their start and end apart: 1 -> 1, of which waited for: 0 -> 1; matrix products, arithmetic and copies ran while one was open for 1% -> 0% of each run, Pallas kernels for 0% -> 0%
where the time goes in v1:
time: 71.8 us; the launch traced here: 71.4 us
  waiting for transfers between devices  34.2 us (48%)
  between operations  13.4 us (19%)
  local copies, waits for them, and re-layouts  8.48 us (12%)
  blocking collectives  8.3 us (12%)
  Pallas kernels  7 us (10%)
    all_gather x1, waiting for transfers between devices, on_device(): right = lax.all_gather(right, ('wide', 'narrow'), axis=0, tiled=False)  34.2 us
    unnamed x18, local copies, waits for them, and re-layouts  8.48 us
    all_to_all x1, blocking collectives, on_device(): lax.all_to_all(left, 'narrow', split_axis=0, concat_axis=0, tiled=True)  8.3 us
    pallas_call x1, Pallas kernels, on_device(): pl.pallas_call(functools.partial(pair_kernel, seqs_total=seqs * narrow),...  4.88 us
    pallas_call x1, Pallas kernels, on_device(): pl.pallas_call(features_kernel, out_shape=(jax.ShapeDtypeStruct((residues...  2.12 us
  transfers between devices with their start and end apart: 1, of which 1 were waited for; matrix products, arithmetic and copies ran while one was open for 0% of the time, Pallas kernels for 0%

profile of v1, /device:TPU:0, one launch (start us, length us, event | category | flops | bytes accessed | tf_op | source)
XLA Modules:
  0.0 71.4 jit_solution(14218175657871253701)
XLA Ops:
  6.5 0.0 all-gather.3.cloned.1.call-start
  6.5 0.8 %copy.12.lm_ref = bf16[256,32]{1,0:T(8,128)(2,1)S(1)} copy(bf16[256,32]{0,1:T(8,128)(2,1)} %param.12) | data formatting | bytes 32768 | tf_op args[3]
  7.4 0.8 %copy.13.rm_ref = bf16[256,32]{1,0:T(8,128)(2,1)S(1)} copy(bf16[256,32]{0,1:T(8,128)(2,1)} %param.14) | data formatting | bytes 32768 | tf_op args[5]
  8.2 0.0 copy-start.1
  8.2 1.1 %copy-done.1 = bf16[32,48,256]{2,1,0:T(8,128)(2,1)S(1)} copy-done((bf16[32,48,256]{2,1,0:T(8,128)(2,1)S(1)}, bf16[32,48,256]{2,1,0:T(8,128)(2,1)}, u32[]{:S(2)}) %copy-start.1) | copy-done | bytes 786456
  9.3 0.0 copy-start.3
  9.4 0.7 copy-done.3
  10.0 0.0 copy-start.4
  10.0 0.7 copy-done.4
  10.7 0.0 copy-start.5
  10.7 0.7 copy-done.5
  11.4 0.0 copy-start.6
  11.4 0.7 copy-done.6
  12.0 2.1 %features.1 = (bf16[12,32,128]{2,1,0:T(8,128)(2,1)S(1)}, bf16[8,48,128]{2,1,0:T(8,128)(2,1)}) custom-call(bf16[32,48,256]{2,1,0:T(8,128)(2,1)S(1)} %copy-done.1, f32[256]{0:T(256)S(1)} %copy-done.3, f32[256]{0:T(256)S(1)} %copy-done.4, bf16[256,32]{1,0:T(8,128)(2,1)S(1)} %copy.12.lm_ref, f32[32]{0:T(128)S(1)} %copy-done.5, bf16[256,32]{1,0:T(8,128)(2,1)S(1)} %copy.13.rm_ref, ...), custom_call_target="tpu_custom_call" | custom-call | tf_op jit(solution)/shard_map/features/pallas_call | solution.py:162
  14.1 0.0 all-gather.3.cloned.1.call-update
  14.2 8.3 %all_to_all.5.left_ref = bf16[4,3,32,128]{3,2,1,0:T(8,128)(2,1)S(1)} all-to-all(bf16[4,3,32,128]{3,2,1,0:T(8,128)(2,1)S(1)} %bitcast.3), channel_id=1, replica_groups=mesh['groups'=2,'wide'=4,'narrow'=4] {'narrow'}, dimensions={0} | all-to-all | bytes 196608 | tf_op jit(solution)/shard_map/all_to_all | solution.py:182
  22.5 34.2 %all-gather.3.cloned.1.call-done = bf16[128,48,128]{2,1,0:T(8,128)(2,1)} async-done(((bf16[8,48,128]{2,1,0:T(8,128)(2,1)}), bf16[128,48,128]{2,1,0:T(8,128)(2,1)}) %all-gather.3.cloned.1.call-update) | async-done | bytes 1572880 | tf_op jit(solution)/shard_map/all_gather | solution.py:179
  56.7 0.0 copy-start
  56.7 1.4 %copy-done = bf16[128,48,128]{2,1,0:T(8,128)(2,1)S(1)} copy-done((bf16[128,48,128]{2,1,0:T(8,128)(2,1)S(1)}, bf16[128,48,128]{2,1,0:T(8,128)(2,1)}, u32[]{:S(2)}) %copy-start) | copy-done | bytes 1572888
  58.1 0.0 copy-start.2
  58.1 0.9 %copy-done.2 = bf16[1024,128]{1,0:T(8,128)(2,1)S(1)} copy-done((bf16[1024,128]{1,0:T(8,128)(2,1)S(1)}, bf16[1024,128]{1,0:T(8,128)(2,1)}, u32[]{:S(2)}) %copy-start.2) | copy-done | bytes 262168
  59.0 0.0 copy-start.7
  59.0 0.7 copy-done.7
  59.7 4.9 %pairs.1 = bf16[12,192,128]{2,1,0:T(8,128)(2,1)} custom-call(bf16[4,3,32,128]{3,2,1,0:T(8,128)(2,1)S(1)} %all_to_all.5.left_ref, bf16[4,4,8,48,128]{4,3,2,1,0:T(8,128)(2,1)S(1)} %bitcast.2, bf16[1024,128]{1,0:T(8,128)(2,1)S(1)} %copy-done.2, f32[128]{0:T(128)S(1)} %copy-done.7), custom_call_target="tpu_custom_call" | custom-call | tf_op jit(solution)/shard_map/pairs/pallas_call | solution.py:187
Async XLA Ops:
  6.5 50.1 %all-gather.3.cloned.1.call-start = ((), (), s32[]{:S(2)}) async-start(), calls=%async_computation.1 | async-start | bytes 1671168 | tf_op jit(solution)/shard_map/all_gather | solution.py:179
  8.2 1.1 %copy-start.1 = (bf16[32,48,256]{2,1,0:T(8,128)(2,1)S(1)}, bf16[32,48,256]{2,1,0:T(8,128)(2,1)}, u32[]{:S(2)}) copy-start(bf16[32,48,256]{2,1,0:T(8,128)(2,1)} %x_ref.1) | copy-start | bytes 2359300
  9.3 0.7 copy-start.3
  10.0 0.7 copy-start.4
  10.7 0.7 copy-start.5
  11.4 0.7 copy-start.6
  56.7 1.4 %copy-start = (bf16[128,48,128]{2,1,0:T(8,128)(2,1)S(1)}, bf16[128,48,128]{2,1,0:T(8,128)(2,1)}, u32[]{:S(2)}) copy-start(bf16[128,48,128]{2,1,0:T(8,128)(2,1)} %all-gather.3.cloned.1.call-done) | copy-start | bytes 4718596
  58.1 0.9 %copy-start.2 = (bf16[1024,128]{1,0:T(8,128)(2,1)S(1)}, bf16[1024,128]{1,0:T(8,128)(2,1)}, u32[]{:S(2)}) copy-start(bf16[1024,128]{1,0:T(8,128)(2,1)} %w_ref.1) | copy-start | bytes 786436
  59.0 0.7 copy-start.7
Sparse Core Ops, SparseCore 0:
  14.3 42.3 all-gather.2

commit v2 on v1

v2 whole, which is shorter than its diff:
```python
import functools

import jax
import jax.numpy as jnp
from jax import lax
from jax.experimental import pallas as pl
from jax.experimental.pallas import tpu as pltpu
from jax.sharding import PartitionSpec as P

LANES = 128
VMEM_LIMIT = 40 * 1024 * 1024
VMEM_ALL = 62 * 1024 * 1024


def iota(shape, dim):
    return lax.broadcasted_iota(jnp.int32, shape, dim)


def features_kernel(
    x_hbm, gain_hbm, bias_hbm, lm_hbm, lb_hbm, rm_hbm, rb_hbm,
    *refs, parts, pieces,
):
    left_refs, right_ref = refs[:parts], refs[parts]
    (x_ref, gain_ref, bias_ref, lm_ref, lb_ref, rm_ref, rb_ref,
     lo_ref, hi_ref, left_all, turned_ref, rows_ref, sems) = refs[parts + 1 :]
    seqs, residues, depth = x_ref.shape
    hidden = lm_ref.shape[0]
    per = LANES // hidden
    slots = LANES // seqs
    minor = hidden // slots
    groups = residues // per
    own = lax.axis_index("narrow")

    piece = seqs // pieces
    copies = [
        pltpu.make_async_copy(
            x_hbm.at[pl.ds(p * piece, piece)], x_ref.at[pl.ds(p * piece, piece)], sems.at[p]
        )
        for p in range(pieces)
    ]
    small = ((gain_hbm, gain_ref), (bias_hbm, bias_ref), (lm_hbm, lm_ref),
             (lb_hbm, lb_ref), (rm_hbm, rm_ref), (rb_hbm, rb_ref))
    rest = [pltpu.make_async_copy(a, b, sems.at[pieces + i]) for i, (a, b) in enumerate(small)]
    copies[0].start()
    for copy in rest:
        copy.start()
    for copy in copies[1:]:
        copy.start()
    for copy in rest:
        copy.wait()

    column, row = iota((hidden, LANES), 1) % hidden, iota((hidden, LANES), 0)
    spread_l = (column == row).astype(jnp.float32)
    spread_r = (column == (row ^ (own * minor))).astype(jnp.float32)

    def widen(m, pick):
        return lax.dot_general(
            m, pick.astype(jnp.bfloat16), (((0,), (0,)), ((), ())),
            preferred_element_type=jnp.float32,
        )

    def widen_bias(b, pick):
        b = jnp.broadcast_to(b.reshape(1, hidden), (8, hidden))
        return jnp.dot(
            b, pick, precision=lax.Precision.HIGHEST, preferred_element_type=jnp.float32
        )[:1]

    weights = jnp.concatenate(
        [widen(lm_ref[...], spread_l), widen(rm_ref[...], spread_r)], axis=1
    )
    shift = jnp.concatenate(
        [widen_bias(lb_ref[...], spread_l), widen_bias(rb_ref[...], spread_r)], axis=1
    )
    place = iota((depth, 2 * LANES), 1) % LANES // hidden

    gain = gain_ref[...].reshape(1, depth)
    bias = bias_ref[...].reshape(1, depth)
    step = 4
    for s in range(0, seqs, step):
        if s % piece == 0:
            copies[s // piece].wait()
        x = x_ref[s : s + step].reshape(step * residues, depth).astype(jnp.float32)
        x = x - jnp.mean(x, axis=-1, keepdims=True)
        spread = jnp.mean(x * x, axis=-1, keepdims=True)
        x = x * lax.rsqrt(spread + 1e-05) * gain + bias
        rows = pl.ds(s * residues, step * residues)
        lo_ref[rows, :] = x[:, :LANES]
        hi_ref[rows, :] = x[:, LANES:]

    total = None
    for k in range(per):
        part = jnp.concatenate(
            [
                jnp.concatenate(
                    [half[pl.ds(g * per + k, seqs, stride=residues), :] for half in (lo_ref, hi_ref)],
                    axis=1,
                )
                for g in range(groups)
            ],
            axis=0,
        ).astype(jnp.bfloat16)
        placed = jnp.where(place == k, weights, 0.0).astype(jnp.bfloat16)
        term = jnp.dot(part, placed, preferred_element_type=jnp.float32)
        total = term if total is None else total + term
    total = total + shift
    left_all[...] = total[:, :LANES].astype(left_all.dtype).reshape(groups, seqs, LANES)
    mine = groups // parts
    for m in range(parts):
        left_refs[m][...] = left_all[pl.ds((own ^ m) * mine, mine)]

    slot = iota((minor, LANES), 1) // seqs
    for block in range(groups // slots):
        turned_ref[...] = total[block * LANES : (block + 1) * LANES, LANES:].T
        for k in range(per):
            parts_of = [turned_ref[pl.ds(k * hidden + q * minor, minor), :] for q in range(slots)]
            for g in range(slots):
                out = None
                for q in range(slots):
                    moved = parts_of[q]
                    if q != g:
                        moved = pltpu.roll(moved, (q - g) % slots * seqs, axis=1)
                    out = moved if out is None else jnp.where(slot == q, moved, out)
                j = (block * slots + g) * per + k
                rows_ref[pl.ds(j, minor, stride=residues), :] = out
    right_ref[...] = rows_ref[...].astype(right_ref.dtype).reshape(minor, residues, LANES)


def weights_kernel(w_hbm, wide_ref, w_ref, wf_ref, sem, *, parts, hidden):
    copy = pltpu.make_async_copy(w_hbm, w_ref, sem)
    copy.start()
    cz = w_ref.shape[1]
    per = LANES // hidden
    minor = hidden // parts
    own = lax.axis_index("narrow")
    wide_ref[...] = jnp.zeros_like(wide_ref)
    copy.wait()
    wf_ref[...] = w_ref[...].astype(jnp.float32)
    for e in range(hidden):
        rows = wf_ref[pl.ds(e ^ (own * minor), hidden, stride=hidden), :].astype(jnp.bfloat16)
        for k in range(per):
            wide_ref[pl.ds(e * LANES + k * hidden, hidden), k * cz : (k + 1) * cz] = rows


def pair_kernel(*refs, wides, parts, relative, seqs_total):
    left_refs = refs[:parts]
    wide_ref, shift_ref, out_ref, outer_ref = refs[-4:]
    chunks = refs[parts:-4]
    groups, seqs, _ = left_refs[0].shape
    if relative:
        chunk_of = lambda d, m: chunks[d * parts + m][...]
    else:
        chunk_of = lambda d, m: chunks[0][d, m]
    minor, residues, _ = chunk_of(0, 0).shape
    cz = shift_ref.shape[0]
    per = LANES // (minor * parts)
    cols = wides * residues

    slot = iota((minor * residues, LANES), 1) // seqs
    for q in range(parts):
        left = jnp.concatenate(
            [
                jnp.concatenate([left_refs[q ^ k][g] for k in range(parts)], axis=0)
                for g in range(groups)
            ],
            axis=1,
        )
        for d in range(wides):
            if relative:
                at = lax.rem(lax.axis_index("wide") + (wides - d), wides)
            else:
                at = d
            right = None
            for k in range(parts):
                chunk = chunk_of(d, q ^ k).reshape(minor * residues, LANES)
                right = chunk if right is None else jnp.where(slot == k, chunk, right)
            outer = jnp.dot(right, left, preferred_element_type=jnp.float32).astype(jnp.bfloat16)
            for e in range(minor):
                for g in range(groups):
                    outer_ref[
                        pl.ds(pl.multiple_of(g * cols + at * residues, 16), residues),
                        (q * minor + e) * LANES : (q * minor + e + 1) * LANES,
                    ] = outer[e * residues : (e + 1) * residues, g * LANES : (g + 1) * LANES]

    shift = shift_ref[...].reshape(1, cz)
    for g in range(groups):
        pair = jnp.dot(
            outer_ref[pl.ds(g * cols, cols), :], wide_ref[...], preferred_element_type=jnp.float32
        )
        for k in range(per):
            out_ref[g * per + k] = (
                pair[:, k * cz : (k + 1) * cz] * (1.0 / seqs_total) + shift
            ).astype(out_ref.dtype)


def on_device(wide, narrow, x, gain, bias, lm, lb, rm, rb, w, shift):
    seqs, residues, depth = x.shape
    hidden = lm.shape[1]
    cz = w.shape[1]
    per = LANES // hidden
    slots = LANES // seqs
    minor = hidden // slots
    own_rows = residues // narrow
    groups = own_rows // per
    pieces = 4
    hbm = pl.BlockSpec(memory_space=pltpu.HBM)
    vmem = pl.BlockSpec(memory_space=pltpu.VMEM)
    params = pltpu.CompilerParams(vmem_limit_bytes=VMEM_LIMIT)
    left_shape = jax.ShapeDtypeStruct((groups, seqs, LANES), jnp.bfloat16)
    right_shape = jax.ShapeDtypeStruct((minor, residues, LANES), jnp.bfloat16)
    args = (x, gain, bias, lm.T, lb, rm.T, rb)
    *lefts, right = pl.pallas_call(
        functools.partial(features_kernel, parts=narrow, pieces=pieces),
        out_shape=(left_shape,) * narrow + (right_shape,),
        in_specs=[hbm] * len(args),
        out_specs=(vmem,) * (narrow + 1),
        scratch_shapes=[pltpu.VMEM(a.shape, a.dtype) for a in args]
        + [
            pltpu.VMEM((seqs * residues, LANES), jnp.float32),
            pltpu.VMEM((seqs * residues, LANES), jnp.float32),
            pltpu.VMEM((residues // per, seqs, LANES), jnp.bfloat16),
            pltpu.VMEM((LANES, LANES), jnp.float32),
            pltpu.VMEM((minor * residues, LANES), jnp.float32),
            pltpu.SemaphoreType.DMA((pieces + len(args) - 1,)),
        ],
        compiler_params=pltpu.CompilerParams(vmem_limit_bytes=VMEM_ALL),
        name="features",
    )(*args)

    def across(a, m):
        return lax.ppermute(a, "narrow", [(i, i ^ m) for i in range(narrow)])

    def along(a, d):
        return lax.ppermute(a, "wide", [(i, (i + d) % wide) for i in range(wide)])

    relative = wide * narrow <= 16
    lefts = [lefts[0]] + [across(lefts[m], m) for m in range(1, narrow)]
    if relative:
        rows = [right] + [along(right, d) for d in range(1, wide)]
        rights = [[chunk] for chunk in rows]
        bit, order = narrow // 2, [0]
        while bit:
            rights = [row + [across(chunk, bit) for chunk in row] for row in rights]
            order = order + [m ^ bit for m in order]
            bit //= 2
        rights = [row[order.index(m)] for row in rights for m in range(narrow)]
    else:
        every = lax.all_gather(right, ("wide", "narrow"), axis=0, tiled=False)
        every = every.reshape(wide, narrow, minor, residues, LANES)
        rights = [jnp.take(every, lax.axis_index("narrow") ^ jnp.arange(narrow), axis=1)]

    block_weights = pl.pallas_call(
        functools.partial(weights_kernel, parts=narrow, hidden=hidden),
        out_shape=jax.ShapeDtypeStruct((hidden * LANES, per * cz), jnp.bfloat16),
        in_specs=[hbm],
        out_specs=vmem,
        scratch_shapes=[
            pltpu.VMEM(w.shape, w.dtype),
            pltpu.VMEM(w.shape, jnp.float32),
            pltpu.SemaphoreType.DMA,
        ],
        compiler_params=params,
        name="block_weights",
    )(w)

    block = wide
    if not relative:
        while block % 2 == 0 and block * residues > 192:
            block //= 2
    cols = block * residues
    out_shape = jax.ShapeDtypeStruct((own_rows, wide * residues, cz), jnp.bfloat16)
    scratch = [pltpu.VMEM((groups * cols, hidden * LANES), jnp.bfloat16)]
    body = functools.partial(
        pair_kernel, wides=block, parts=narrow, relative=relative, seqs_total=seqs * narrow
    )
    if relative:
        specs = dict(in_specs=[vmem] * (narrow + len(rights) + 2), out_specs=vmem)
    else:
        specs = dict(
            grid=(wide // block,),
            in_specs=[pl.BlockSpec((groups, seqs, LANES), lambda b: (0, 0, 0))] * narrow
            + [
                pl.BlockSpec((block, narrow, minor, residues, LANES), lambda b: (b, 0, 0, 0, 0)),
                pl.BlockSpec((hidden * LANES, per * cz), lambda b: (0, 0)),
                pl.BlockSpec((cz,), lambda b: (0,)),
            ],
            out_specs=pl.BlockSpec((own_rows, cols, cz), lambda b: (0, b, 0)),
        )
    return pl.pallas_call(
        body,
        out_shape=out_shape,
        scratch_shapes=scratch,
        compiler_params=params,
        name="pairs",
        **specs,
    )(*lefts, *rights, block_weights, shift)


def solution(mesh):
    in_specs = (P(("groups", "narrow"), "wide", None), P(), P(), P(), P(), P(), P(), P(), P())
    out_specs = P(("groups", "wide", "narrow"), None, None)
    return jax.shard_map(
        functools.partial(on_device, mesh.shape["wide"], mesh.shape["narrow"]),
        mesh=mesh,
        in_specs=in_specs,
        out_specs=out_specs,
        check_vma=False,
    )
```

time: 71.8 us -> 34.7 us (0.48)
  waiting for transfers between devices: 34.2 us -> 9.8 us
  starting transfers between devices: 0.01 us -> 14.3 us
  between operations: 13.4 us -> 0.1 us
  blocking collectives: 8.3 us -> 0 us
  local copies, waits for them, and re-layouts: 8.48 us -> 0.96 us
  Pallas kernels: 7 us -> 9.37 us
    all_gather x1 -> x0, waiting for transfers between devices: 34.2 us -> none  [on_device(): right = lax.all_gather(right, ('wide', 'narrow'), axis=0, tiled=False)]
    ppermute x0 -> x18, starting transfers between devices: none -> 14.3 us  [the longest x15 9.42 us: across(): return lax.ppermute(a, 'narrow', [(i, i ^ m) for i in range(narrow)])]
    ppermute x0 -> x18, waiting for transfers between devices: none -> 9.8 us  [the longest x3 5.75 us: along(): return lax.ppermute(a, 'wide', [(i, (i + d) % wide) for i in range(wide)])]
    all_to_all x1 -> x0, blocking collectives: 8.3 us -> none  [on_device(): lax.all_to_all(left, 'narrow', split_axis=0, concat_axis=0, tiled=True)]
    unnamed x18 -> x8, local copies, waits for them, and re-layouts: 8.48 us -> 0.96 us
    pallas_call x2 -> x3, Pallas kernels: 7 us -> 9.37 us  [the longest x1 4.93 us: on_device(): pl.pallas_call(body, out_shape=out_shape, scratch_shapes=scratch, compile...]
  transfers between devices with their start and end apart: 1 -> 18, of which waited for: 1 -> 4; matrix products, arithmetic and copies ran while one was open for 0% -> 0% of each run, Pallas kernels for 0% -> 3%
where the time goes in v2:
time: 34.7 us; the launch traced here: 34.5 us
  starting transfers between devices  14.3 us (41%)
  waiting for transfers between devices  9.8 us (28%)
  Pallas kernels  9.37 us (27%)
  local copies, waits for them, and re-layouts  0.96 us (3%)
    ppermute x15, starting transfers between devices, across(): return lax.ppermute(a, 'narrow', [(i, i ^ m) for i in range(narrow)])  9.42 us
    ppermute x3, waiting for transfers between devices, along(): return lax.ppermute(a, 'wide', [(i, (i + d) % wide) for i in range(wide)])  5.75 us
    pallas_call x1, Pallas kernels, on_device(): pl.pallas_call(body, out_shape=out_shape, scratch_shapes=scratch, compile...  4.93 us
    ppermute x3, starting transfers between devices, along(): return lax.ppermute(a, 'wide', [(i, (i + d) % wide) for i in range(wide)])  4.85 us
    ppermute x15, waiting for transfers between devices, across(): return lax.ppermute(a, 'narrow', [(i, i ^ m) for i in range(narrow)])  4.05 us
    pallas_call x1, Pallas kernels, on_device(): pl.pallas_call(functools.partial(features_kernel, parts=narrow, pieces=pi...  3.56 us
    unnamed x8, local copies, waits for them, and re-layouts  0.96 us
    pallas_call x1, Pallas kernels, on_device(): pl.pallas_call(functools.partial(weights_kernel, parts=narrow, hidden=hid...  0.88 us
  transfers between devices with their start and end apart: 18, of which 4 were waited for; matrix products, arithmetic and copies ran while one was open for 0% of the time, Pallas kernels for 3%

profile of v2, /device:TPU:0, one launch (start us, length us, event | category | flops | bytes accessed | tf_op | source)
XLA Modules:
  0.0 34.5 jit_solution(17245462554060773484)
XLA Ops:
  0.0 0.0 copy-start.3
  0.0 3.6 %features.1 = (bf16[3,32,128]{2,1,0:T(8,128)(2,1)}, bf16[3,32,128]{2,1,0:T(8,128)(2,1)}, bf16[3,32,128]{2,1,0:T(8,128)(2,1)}, bf16[3,32,128]{2,1,0:T(8,128)(2,1)}, bf16[8,48,128]{2,1,0:T(8,128)(2,1)}) custom-call(bf16[32,48,256]{2,1,0:T(8,128)(2,1)} %x_hbm.1, f32[256]{0:T(256)} %gain_hbm.1, f32[256]{0:T(256)} %bias_hbm.1, bf16[32,256]{1,0:T(8,128)(2,1)} %bitcast.2, ...), custom_call_target="tpu_custom_call" | custom-call | tf_op jit(solution)/shard_map/features/pallas_call | solution.py:211
  3.6 0.5 %collective-permute-start = (bf16[3,32,128]{2,1,0:T(8,128)(2,1)}, bf16[3,32,128]{2,1,0:T(8,128)(2,1)S(1)}, u32[]{:S(2)}, u32[]{:S(2)}) collective-permute-start(bf16[3,32,128]{2,1,0:T(8,128)(2,1)} %get-tuple-element.11), channel_id=1, source_target_pairs={{0,1},{1,0},{2,3},{3,2},{4,5},{5,4},{6,7},{7,6},{8,9},{9,8},{10,11... | collective-permute-start | bytes 73736 | tf_op jit(solution)/shard_map/ppermute | solution.py:230
  4.1 2.6 %collective-permute-start.1 = (bf16[3,32,128]{2,1,0:T(8,128)(2,1)}, bf16[3,32,128]{2,1,0:T(8,128)(2,1)S(1)}, u32[]{:S(2)}, u32[]{:S(2)}) collective-permute-start(bf16[3,32,128]{2,1,0:T(8,128)(2,1)} %get-tuple-element.12), channel_id=1, source_target_pairs={{0,2},{1,3},{2,0},{3,1},{4,6},{5,7},{6,4},{7,5},{8,10},{9,11},{10,... | collective-permute-start | bytes 73736 | tf_op jit(solution)/shard_map/ppermute | solution.py:230
  6.7 0.1 collective-permute-start.2
  6.7 3.8 %collective-permute-start.14 = (bf16[8,48,128]{2,1,0:T(8,128)(2,1)}, bf16[8,48,128]{2,1,0:T(8,128)(2,1)S(1)}, u32[]{:S(2)}, u32[]{:S(2)}) collective-permute-start(bf16[8,48,128]{2,1,0:T(8,128)(2,1)} %get-tuple-element.14.refs_4_), channel_id=1, source_target_pairs={{0,12},{4,0},{8,4},{12,8},{1,13},{5,1},{9,5},{13,9},{2,14},{6,2},{... | collective-permute-start | bytes 294920 | tf_op jit(solution)/shard_map/ppermute | solution.py:233
  10.6 0.0 collective-permute-start.10
  10.6 0.0 collective-permute-done.refs_1_
  10.6 1.0 %collective-permute-start.6 = (bf16[8,48,128]{2,1,0:T(8,128)(2,1)}, bf16[8,48,128]{2,1,0:T(8,128)(2,1)S(1)}, u32[]{:S(2)}, u32[]{:S(2)}) collective-permute-start(bf16[8,48,128]{2,1,0:T(8,128)(2,1)} %get-tuple-element.14.refs_4_), channel_id=1, source_target_pairs={{0,4},{4,8},{8,12},{12,0},{1,5},{5,9},{9,13},{13,1},{2,6},{6,10},{... | collective-permute-start | bytes 294920 | tf_op jit(solution)/shard_map/ppermute | solution.py:233
  11.6 0.0 collective-permute-done.1.refs_2_
  11.6 1.5 %collective-permute-start.4 = (bf16[8,48,128]{2,1,0:T(8,128)(2,1)}, bf16[8,48,128]{2,1,0:T(8,128)(2,1)S(1)}, u32[]{:S(2)}, u32[]{:S(2)}) collective-permute-start(bf16[8,48,128]{2,1,0:T(8,128)(2,1)} %get-tuple-element.14.refs_4_), channel_id=1, source_target_pairs={{0,2},{1,3},{2,0},{3,1},{4,6},{5,7},{6,4},{7,5},{8,10},{9,11},{10,... | collective-permute-start | bytes 294920 | tf_op jit(solution)/shard_map/ppermute | solution.py:230
  13.1 0.0 collective-permute-done.2.refs_3_
  13.1 0.0 collective-permute-start.3
  13.1 1.0 %collective-permute-done.14.refs_16_ = bf16[8,48,128]{2,1,0:T(8,128)(2,1)S(1)} collective-permute-done((bf16[8,48,128]{2,1,0:T(8,128)(2,1)}, bf16[8,48,128]{2,1,0:T(8,128)(2,1)S(1)}, u32[]{:S(2)}, u32[]{:S(2)}) %collective-permute-start.14) | collective-permute-done | bytes 98336 | tf_op jit(solution)/shard_map/ppermute | solution.py:233
  14.1 1.5 %collective-permute-start.16 = (bf16[8,48,128]{2,1,0:T(8,128)(2,1)S(1)}, bf16[8,48,128]{2,1,0:T(8,128)(2,1)S(1)}, u32[]{:S(2)}, u32[]{:S(2)}) collective-permute-start(bf16[8,48,128]{2,1,0:T(8,128)(2,1)S(1)} %collective-permute-done.14.refs_16_), channel_id=1, source_target_pairs={{0,2},{1,3},{2,0},{3,1},{4,6},{5,7},{6,4},{7,5},{8,10},{9,11},{10,... | collective-permute-start | bytes 294920 | tf_op jit(solution)/shard_map/ppermute | solution.py:230
  15.6 4.8 %collective-permute-done.10.refs_12_ = bf16[8,48,128]{2,1,0:T(8,128)(2,1)S(1)} collective-permute-done((bf16[8,48,128]{2,1,0:T(8,128)(2,1)}, bf16[8,48,128]{2,1,0:T(8,128)(2,1)S(1)}, u32[]{:S(2)}, u32[]{:S(2)}) %collective-permute-start.10) | collective-permute-done | bytes 98336 | tf_op jit(solution)/shard_map/ppermute | solution.py:233
  20.3 0.0 collective-permute-start.15
  20.3 0.0 collective-permute-done.6.refs_8_
  20.3 1.5 %collective-permute-start.12 = (bf16[8,48,128]{2,1,0:T(8,128)(2,1)S(1)}, bf16[8,48,128]{2,1,0:T(8,128)(2,1)S(1)}, u32[]{:S(2)}, u32[]{:S(2)}) collective-permute-start(bf16[8,48,128]{2,1,0:T(8,128)(2,1)S(1)} %collective-permute-done.10.refs_12_), channel_id=1, source_target_pairs={{0,2},{1,3},{2,0},{3,1},{4,6},{5,7},{6,4},{7,5},{8,10},{9,11},{10,... | collective-permute-start | bytes 294920 | tf_op jit(solution)/shard_map/ppermute | solution.py:230
  21.8 0.0 collective-permute-done.4.refs_6_
  21.8 0.2 collective-permute-start.11
  22.1 0.0 collective-permute-done.3.refs_5_
  22.1 0.5 %collective-permute-start.8 = (bf16[8,48,128]{2,1,0:T(8,128)(2,1)S(1)}, bf16[8,48,128]{2,1,0:T(8,128)(2,1)S(1)}, u32[]{:S(2)}, u32[]{:S(2)}) collective-permute-start(bf16[8,48,128]{2,1,0:T(8,128)(2,1)S(1)} %collective-permute-done.6.refs_8_), channel_id=1, source_target_pairs={{0,2},{1,3},{2,0},{3,1},{4,6},{5,7},{6,4},{7,5},{8,10},{9,11},{10,... | collective-permute-start | bytes 294920 | tf_op jit(solution)/shard_map/ppermute | solution.py:230
  22.6 0.0 collective-permute-done.16.refs_18_
  22.6 0.0 collective-permute-start.7
  22.6 0.0 collective-permute-done.15.refs_17_
  22.6 0.5 %collective-permute-start.5 = (bf16[8,48,128]{2,1,0:T(8,128)(2,1)S(1)}, bf16[8,48,128]{2,1,0:T(8,128)(2,1)S(1)}, u32[]{:S(2)}, u32[]{:S(2)}) collective-permute-start(bf16[8,48,128]{2,1,0:T(8,128)(2,1)S(1)} %collective-permute-done.4.refs_6_), channel_id=1, source_target_pairs={{0,1},{1,0},{2,3},{3,2},{4,5},{5,4},{6,7},{7,6},{8,9},{9,8},{10,11... | collective-permute-start | bytes 294920 | tf_op jit(solution)/shard_map/ppermute | solution.py:230
  23.1 2.8 %collective-permute-done.12.refs_14_ = bf16[8,48,128]{2,1,0:T(8,128)(2,1)S(1)} collective-permute-done((bf16[8,48,128]{2,1,0:T(8,128)(2,1)S(1)}, bf16[8,48,128]{2,1,0:T(8,128)(2,1)S(1)}, u32[]{:S(2)}, u32[]{:S(2)}) %collective-permute-start.12) | collective-permute-done | bytes 98336 | tf_op jit(solution)/shard_map/ppermute | solution.py:230
  25.9 0.0 collective-permute-start.17
  25.9 0.0 collective-permute-done.11.refs_13_
  25.9 0.5 %collective-permute-start.13 = (bf16[8,48,128]{2,1,0:T(8,128)(2,1)S(1)}, bf16[8,48,128]{2,1,0:T(8,128)(2,1)S(1)}, u32[]{:S(2)}, u32[]{:S(2)}) collective-permute-start(bf16[8,48,128]{2,1,0:T(8,128)(2,1)S(1)} %collective-permute-done.12.refs_14_), channel_id=1, source_target_pairs={{0,1},{1,0},{2,3},{3,2},{4,5},{5,4},{6,7},{7,6},{8,9},{9,8},{10,11... | collective-permute-start | bytes 294920 | tf_op jit(solution)/shard_map/ppermute | solution.py:230
  26.4 1.2 %collective-permute-done.8.refs_10_ = bf16[8,48,128]{2,1,0:T(8,128)(2,1)S(1)} collective-permute-done((bf16[8,48,128]{2,1,0:T(8,128)(2,1)S(1)}, bf16[8,48,128]{2,1,0:T(8,128)(2,1)S(1)}, u32[]{:S(2)}, u32[]{:S(2)}) %collective-permute-start.8) | collective-permute-done | bytes 98336 | tf_op jit(solution)/shard_map/ppermute | solution.py:230
  27.6 0.0 collective-permute-start.9
  27.6 0.0 copy-start
  27.6 0.9 %copy-done = bf16[1024,128]{1,0:T(8,128)(2,1)S(1)} copy-done((bf16[1024,128]{1,0:T(8,128)(2,1)S(1)}, bf16[1024,128]{1,0:T(8,128)(2,1)}, u32[]{:S(2)}) %copy-start) | copy-done | bytes 262168
  28.6 0.0 copy-start.1
  28.6 0.0 copy-start.2
  28.6 0.9 %block_weights.1.refs_20_ = bf16[4096,512]{1,0:T(8,128)(2,1)S(1)} custom-call(bf16[1024,128]{1,0:T(8,128)(2,1)S(1)} %copy-done), custom_call_target="tpu_custom_call" | custom-call | tf_op jit(solution)/shard_map/block_weights/pallas_call | solution.py:251
  29.5 0.0 collective-permute-done.7.refs_9_
  29.5 0.0 collective-permute-done.5.refs_7_
  29.5 0.0 collective-permute-done.17.refs_19_
  29.5 0.0 collective-permute-done.13.refs_15_
  29.5 0.0 collective-permute-done.9.refs_11_
  29.5 0.0 copy-done.3
  29.6 0.0 copy-done.1
  29.6 0.0 copy-done.2
  29.6 4.9 %pairs.1 = bf16[12,192,128]{2,1,0:T(8,128)(2,1)} custom-call(bf16[3,32,128]{2,1,0:T(8,128)(2,1)S(1)} %copy-done.2, bf16[3,32,128]{2,1,0:T(8,128)(2,1)S(1)} %collective-permute-done.refs_1_, bf16[3,32,128]{2,1,0:T(8,128)(2,1)S(1)} %collective-permute-done.1.refs_2_, bf16[3,32,128]{2,1,0:T(8,128)(2,1)S(1)} %collective-permute-done.2.refs_3_, ...), custom_call_target="tpu_custom_call" | custom-call | tf_op jit(solution)/shard_map/pairs/pallas_call | solution.py:288
Async XLA Ops:
  0.0 29.5 %copy-start.3 = (f32[128]{0:T(128)S(1)}, f32[128]{0:T(128)}, u32[]{:S(2)}) copy-start(f32[128]{0:T(128)} %refs_21_.1) | copy-start | bytes 1540
  3.6 7.0 %collective-permute-start = (bf16[3,32,128]{2,1,0:T(8,128)(2,1)}, bf16[3,32,128]{2,1,0:T(8,128)(2,1)S(1)}, u32[]{:S(2)}, u32[]{:S(2)}) collective-permute-start(bf16[3,32,128]{2,1,0:T(8,128)(2,1)} %get-tuple-element.11), channel_id=1, source_target_pairs={{0,1},{1,0},{2,3},{3,2},{4,5},{5,4},{6,7},{7,6},{8,9},{9,8},{10,11... | collective-permute-start | bytes 73736 | tf_op jit(solution)/shard_map/ppermute | solution.py:230
  4.1 7.5 %collective-permute-start.1 = (bf16[3,32,128]{2,1,0:T(8,128)(2,1)}, bf16[3,32,128]{2,1,0:T(8,128)(2,1)S(1)}, u32[]{:S(2)}, u32[]{:S(2)}) collective-permute-start(bf16[3,32,128]{2,1,0:T(8,128)(2,1)} %get-tuple-element.12), channel_id=1, source_target_pairs={{0,2},{1,3},{2,0},{3,1},{4,6},{5,7},{6,4},{7,5},{8,10},{9,11},{10,... | collective-permute-start | bytes 73736 | tf_op jit(solution)/shard_map/ppermute | solution.py:230
  6.7 6.4 %collective-permute-start.2 = (bf16[3,32,128]{2,1,0:T(8,128)(2,1)}, bf16[3,32,128]{2,1,0:T(8,128)(2,1)S(1)}, u32[]{:S(2)}, u32[]{:S(2)}) collective-permute-start(bf16[3,32,128]{2,1,0:T(8,128)(2,1)} %get-tuple-element.13), channel_id=1, source_target_pairs={{0,3},{1,2},{2,1},{3,0},{4,7},{5,6},{6,5},{7,4},{8,11},{9,10},{10,... | collective-permute-start | bytes 73736 | tf_op jit(solution)/shard_map/ppermute | solution.py:230
  6.7 7.3 %collective-permute-start.14 = (bf16[8,48,128]{2,1,0:T(8,128)(2,1)}, bf16[8,48,128]{2,1,0:T(8,128)(2,1)S(1)}, u32[]{:S(2)}, u32[]{:S(2)}) collective-permute-start(bf16[8,48,128]{2,1,0:T(8,128)(2,1)} %get-tuple-element.14.refs_4_), channel_id=1, source_target_pairs={{0,12},{4,0},{8,4},{12,8},{1,13},{5,1},{9,5},{13,9},{2,14},{6,2},{... | collective-permute-start | bytes 294920 | tf_op jit(solution)/shard_map/ppermute | solution.py:233
  10.6 9.8 %collective-permute-start.10 = (bf16[8,48,128]{2,1,0:T(8,128)(2,1)}, bf16[8,48,128]{2,1,0:T(8,128)(2,1)S(1)}, u32[]{:S(2)}, u32[]{:S(2)}) collective-permute-start(bf16[8,48,128]{2,1,0:T(8,128)(2,1)} %get-tuple-element.14.refs_4_), channel_id=1, source_target_pairs={{0,8},{4,12},{8,0},{12,4},{1,9},{5,13},{9,1},{13,5},{2,10},{6,14},... | collective-permute-start | bytes 294920 | tf_op jit(solution)/shard_map/ppermute | solution.py:233
  10.6 9.8 %collective-permute-start.6 = (bf16[8,48,128]{2,1,0:T(8,128)(2,1)}, bf16[8,48,128]{2,1,0:T(8,128)(2,1)S(1)}, u32[]{:S(2)}, u32[]{:S(2)}) collective-permute-start(bf16[8,48,128]{2,1,0:T(8,128)(2,1)} %get-tuple-element.14.refs_4_), channel_id=1, source_target_pairs={{0,4},{4,8},{8,12},{12,0},{1,5},{5,9},{9,13},{13,1},{2,6},{6,10},{... | collective-permute-start | bytes 294920 | tf_op jit(solution)/shard_map/ppermute | solution.py:233
  11.6 10.2 %collective-permute-start.4 = (bf16[8,48,128]{2,1,0:T(8,128)(2,1)}, bf16[8,48,128]{2,1,0:T(8,128)(2,1)S(1)}, u32[]{:S(2)}, u32[]{:S(2)}) collective-permute-start(bf16[8,48,128]{2,1,0:T(8,128)(2,1)} %get-tuple-element.14.refs_4_), channel_id=1, source_target_pairs={{0,2},{1,3},{2,0},{3,1},{4,6},{5,7},{6,4},{7,5},{8,10},{9,11},{10,... | collective-permute-start | bytes 294920 | tf_op jit(solution)/shard_map/ppermute | solution.py:230
  13.1 9.0 %collective-permute-start.3 = (bf16[8,48,128]{2,1,0:T(8,128)(2,1)}, bf16[8,48,128]{2,1,0:T(8,128)(2,1)S(1)}, u32[]{:S(2)}, u32[]{:S(2)}) collective-permute-start(bf16[8,48,128]{2,1,0:T(8,128)(2,1)} %get-tuple-element.14.refs_4_), channel_id=1, source_target_pairs={{0,1},{1,0},{2,3},{3,2},{4,5},{5,4},{6,7},{7,6},{8,9},{9,8},{10,11... | collective-permute-start | bytes 294920 | tf_op jit(solution)/shard_map/ppermute | solution.py:230
  14.1 8.5 %collective-permute-start.16 = (bf16[8,48,128]{2,1,0:T(8,128)(2,1)S(1)}, bf16[8,48,128]{2,1,0:T(8,128)(2,1)S(1)}, u32[]{:S(2)}, u32[]{:S(2)}) collective-permute-start(bf16[8,48,128]{2,1,0:T(8,128)(2,1)S(1)} %collective-permute-done.14.refs_16_), channel_id=1, source_target_pairs={{0,2},{1,3},{2,0},{3,1},{4,6},{5,7},{6,4},{7,5},{8,10},{9,11},{10,... | collective-permute-start | bytes 294920 | tf_op jit(solution)/shard_map/ppermute | solution.py:230
  20.3 2.3 %collective-permute-start.15 = (bf16[8,48,128]{2,1,0:T(8,128)(2,1)S(1)}, bf16[8,48,128]{2,1,0:T(8,128)(2,1)S(1)}, u32[]{:S(2)}, u32[]{:S(2)}) collective-permute-start(bf16[8,48,128]{2,1,0:T(8,128)(2,1)S(1)} %collective-permute-done.14.refs_16_), channel_id=1, source_target_pairs={{0,1},{1,0},{2,3},{3,2},{4,5},{5,4},{6,7},{7,6},{8,9},{9,8},{10,11... | collective-permute-start | bytes 294920 | tf_op jit(solution)/shard_map/ppermute | solution.py:230
  20.3 5.6 %collective-permute-start.12 = (bf16[8,48,128]{2,1,0:T(8,128)(2,1)S(1)}, bf16[8,48,128]{2,1,0:T(8,128)(2,1)S(1)}, u32[]{:S(2)}, u32[]{:S(2)}) collective-permute-start(bf16[8,48,128]{2,1,0:T(8,128)(2,1)S(1)} %collective-permute-done.10.refs_12_), channel_id=1, source_target_pairs={{0,2},{1,3},{2,0},{3,1},{4,6},{5,7},{6,4},{7,5},{8,10},{9,11},{10,... | collective-permute-start | bytes 294920 | tf_op jit(solution)/shard_map/ppermute | solution.py:230
  21.8 4.1 %collective-permute-start.11 = (bf16[8,48,128]{2,1,0:T(8,128)(2,1)S(1)}, bf16[8,48,128]{2,1,0:T(8,128)(2,1)S(1)}, u32[]{:S(2)}, u32[]{:S(2)}) collective-permute-start(bf16[8,48,128]{2,1,0:T(8,128)(2,1)S(1)} %collective-permute-done.10.refs_12_), channel_id=1, source_target_pairs={{0,1},{1,0},{2,3},{3,2},{4,5},{5,4},{6,7},{7,6},{8,9},{9,8},{10,11... | collective-permute-start | bytes 294920 | tf_op jit(solution)/shard_map/ppermute | solution.py:230
  22.1 5.6 %collective-permute-start.8 = (bf16[8,48,128]{2,1,0:T(8,128)(2,1)S(1)}, bf16[8,48,128]{2,1,0:T(8,128)(2,1)S(1)}, u32[]{:S(2)}, u32[]{:S(2)}) collective-permute-start(bf16[8,48,128]{2,1,0:T(8,128)(2,1)S(1)} %collective-permute-done.6.refs_8_), channel_id=1, source_target_pairs={{0,2},{1,3},{2,0},{3,1},{4,6},{5,7},{6,4},{7,5},{8,10},{9,11},{10,... | collective-permute-start | bytes 294920 | tf_op jit(solution)/shard_map/ppermute | solution.py:230
  22.6 6.9 %collective-permute-start.7 = (bf16[8,48,128]{2,1,0:T(8,128)(2,1)S(1)}, bf16[8,48,128]{2,1,0:T(8,128)(2,1)S(1)}, u32[]{:S(2)}, u32[]{:S(2)}) collective-permute-start(bf16[8,48,128]{2,1,0:T(8,128)(2,1)S(1)} %collective-permute-done.6.refs_8_), channel_id=1, source_target_pairs={{0,1},{1,0},{2,3},{3,2},{4,5},{5,4},{6,7},{7,6},{8,9},{9,8},{10,11... | collective-permute-start | bytes 294920 | tf_op jit(solution)/shard_map/ppermute | solution.py:230
  22.6 6.9 %collective-permute-start.5 = (bf16[8,48,128]{2,1,0:T(8,128)(2,1)S(1)}, bf16[8,48,128]{2,1,0:T(8,128)(2,1)S(1)}, u32[]{:S(2)}, u32[]{:S(2)}) collective-permute-start(bf16[8,48,128]{2,1,0:T(8,128)(2,1)S(1)} %collective-permute-done.4.refs_6_), channel_id=1, source_target_pairs={{0,1},{1,0},{2,3},{3,2},{4,5},{5,4},{6,7},{7,6},{8,9},{9,8},{10,11... | collective-permute-start | bytes 294920 | tf_op jit(solution)/shard_map/ppermute | solution.py:230
  25.9 3.6 %collective-permute-start.17 = (bf16[8,48,128]{2,1,0:T(8,128)(2,1)S(1)}, bf16[8,48,128]{2,1,0:T(8,128)(2,1)S(1)}, u32[]{:S(2)}, u32[]{:S(2)}) collective-permute-start(bf16[8,48,128]{2,1,0:T(8,128)(2,1)S(1)} %collective-permute-done.16.refs_18_), channel_id=1, source_target_pairs={{0,1},{1,0},{2,3},{3,2},{4,5},{5,4},{6,7},{7,6},{8,9},{9,8},{10,11... | collective-permute-start | bytes 294920 | tf_op jit(solution)/shard_map/ppermute | solution.py:230
  25.9 3.6 %collective-permute-start.13 = (bf16[8,48,128]{2,1,0:T(8,128)(2,1)S(1)}, bf16[8,48,128]{2,1,0:T(8,128)(2,1)S(1)}, u32[]{:S(2)}, u32[]{:S(2)}) collective-permute-start(bf16[8,48,128]{2,1,0:T(8,128)(2,1)S(1)} %collective-permute-done.12.refs_14_), channel_id=1, source_target_pairs={{0,1},{1,0},{2,3},{3,2},{4,5},{5,4},{6,7},{7,6},{8,9},{9,8},{10,11... | collective-permute-start | bytes 294920 | tf_op jit(solution)/shard_map/ppermute | solution.py:230
  27.6 1.9 %collective-permute-start.9 = (bf16[8,48,128]{2,1,0:T(8,128)(2,1)S(1)}, bf16[8,48,128]{2,1,0:T(8,128)(2,1)S(1)}, u32[]{:S(2)}, u32[]{:S(2)}) collective-permute-start(bf16[8,48,128]{2,1,0:T(8,128)(2,1)S(1)} %collective-permute-done.8.refs_10_), channel_id=1, source_target_pairs={{0,1},{1,0},{2,3},{3,2},{4,5},{5,4},{6,7},{7,6},{8,9},{9,8},{10,11... | collective-permute-start | bytes 294920 | tf_op jit(solution)/shard_map/ppermute | solution.py:230
  27.6 1.0 %copy-start = (bf16[1024,128]{1,0:T(8,128)(2,1)S(1)}, bf16[1024,128]{1,0:T(8,128)(2,1)}, u32[]{:S(2)}) copy-start(bf16[1024,128]{1,0:T(8,128)(2,1)} %w_hbm.1) | copy-start | bytes 786436
  28.6 1.0 %copy-start.1 = (bf16[8,48,128]{2,1,0:T(8,128)(2,1)S(1)}, bf16[8,48,128]{2,1,0:T(8,128)(2,1)}, u32[]{:S(2)}) copy-start(bf16[8,48,128]{2,1,0:T(8,128)(2,1)} %get-tuple-element.14.refs_4_) | copy-start | bytes 294916
  28.6 1.0 %copy-start.2 = (bf16[3,32,128]{2,1,0:T(8,128)(2,1)S(1)}, bf16[3,32,128]{2,1,0:T(8,128)(2,1)}, u32[]{:S(2)}) copy-start(bf16[3,32,128]{2,1,0:T(8,128)(2,1)} %get-tuple-element.10.refs_0_) | copy-start | bytes 73732

commit v3 on v2

--- a/solution.py
+++ b/solution.py
@@ -8,6 +8,7 @@
 from jax.sharding import PartitionSpec as P
 
 LANES = 128
+RIGHT = -1
 VMEM_LIMIT = 40 * 1024 * 1024
 VMEM_ALL = 62 * 1024 * 1024
 
@@ -18,11 +19,11 @@
 
 def features_kernel(
     x_hbm, gain_hbm, bias_hbm, lm_hbm, lb_hbm, rm_hbm, rb_hbm,
-    *refs, parts, pieces,
+    *refs, packs, parts, pieces,
 ):
-    left_refs, right_ref = refs[:parts], refs[parts]
+    outs = refs[: len(packs)]
     (x_ref, gain_ref, bias_ref, lm_ref, lb_ref, rm_ref, rb_ref,
-     lo_ref, hi_ref, left_all, turned_ref, rows_ref, sems) = refs[parts + 1 :]
+     lo_ref, hi_ref, left_all, turned_ref, rows_ref, sems) = refs[len(packs) :]
     seqs, residues, depth = x_ref.shape
     hidden = lm_ref.shape[0]
     per = LANES // hidden
@@ -105,8 +106,6 @@
     total = total + shift
     left_all[...] = total[:, :LANES].astype(left_all.dtype).reshape(groups, seqs, LANES)
     mine = groups // parts
-    for m in range(parts):
-        left_refs[m][...] = left_all[pl.ds((own ^ m) * mine, mine)]
 
     slot = iota((minor, LANES), 1) // seqs
     for block in range(groups // slots):
@@ -122,7 +121,16 @@
                     out = moved if out is None else jnp.where(slot == q, moved, out)
                 j = (block * slots + g) * per + k
                 rows_ref[pl.ds(j, minor, stride=residues), :] = out
-    right_ref[...] = rows_ref[...].astype(right_ref.dtype).reshape(minor, residues, LANES)
+    right = rows_ref[...].astype(jnp.bfloat16)
+    for out, pack in zip(outs, packs):
+        at = 0
+        for item in pack:
+            if item == RIGHT:
+                rows = right
+            else:
+                rows = left_all[pl.ds((own ^ item) * mine, mine)].reshape(mine * seqs, LANES)
+            out[at : at + rows.shape[0], :] = rows
+            at += rows.shape[0]
 
 
 def weights_kernel(w_hbm, wide_ref, w_ref, wf_ref, sem, *, parts, hidden):
@@ -141,55 +149,79 @@
             wide_ref[pl.ds(e * LANES + k * hidden, hidden), k * cz : (k + 1) * cz] = rows
 
 
-def pair_kernel(*refs, wides, parts, relative, seqs_total):
-    left_refs = refs[:parts]
-    wide_ref, shift_ref, out_ref, outer_ref = refs[-4:]
-    chunks = refs[parts:-4]
-    groups, seqs, _ = left_refs[0].shape
-    if relative:
-        chunk_of = lambda d, m: chunks[d * parts + m][...]
-    else:
-        chunk_of = lambda d, m: chunks[0][d, m]
-    minor, residues, _ = chunk_of(0, 0).shape
+def pair_rows(left_of, right_of, wide_ref, shift_ref, outer_ref, store, *, wides, parts, minor, seqs_total):
     cz = shift_ref.shape[0]
     per = LANES // (minor * parts)
+    seqs = LANES // parts
+    groups = left_of(0).shape[0] // seqs
+    residues = right_of(0, 0).shape[0] // minor
     cols = wides * residues
-
+    lefts = [left_of(m) for m in range(parts)]
     slot = iota((minor * residues, LANES), 1) // seqs
     for q in range(parts):
         left = jnp.concatenate(
             [
-                jnp.concatenate([left_refs[q ^ k][g] for k in range(parts)], axis=0)
+                jnp.concatenate([lefts[q ^ k][g * seqs : (g + 1) * seqs] for k in range(parts)], axis=0)
                 for g in range(groups)
             ],
             axis=1,
         )
         for d in range(wides):
-            if relative:
-                at = lax.rem(lax.axis_index("wide") + (wides - d), wides)
-            else:
-                at = d
             right = None
             for k in range(parts):
-                chunk = chunk_of(d, q ^ k).reshape(minor * residues, LANES)
+                chunk = right_of(d, q ^ k)
                 right = chunk if right is None else jnp.where(slot == k, chunk, right)
             outer = jnp.dot(right, left, preferred_element_type=jnp.float32).astype(jnp.bfloat16)
             for e in range(minor):
                 for g in range(groups):
                     outer_ref[
-                        pl.ds(pl.multiple_of(g * cols + at * residues, 16), residues),
+                        pl.ds(g * cols + d * residues, residues),
                         (q * minor + e) * LANES : (q * minor + e + 1) * LANES,
                     ] = outer[e * residues : (e + 1) * residues, g * LANES : (g + 1) * LANES]
 
     shift = shift_ref[...].reshape(1, cz)
+    pairs = jnp.dot(outer_ref[...], wide_ref[...], preferred_element_type=jnp.float32)
     for g in range(groups):
-        pair = jnp.dot(
-            outer_ref[pl.ds(g * cols, cols), :], wide_ref[...], preferred_element_type=jnp.float32
-        )
         for k in range(per):
-            out_ref[g * per + k] = (
-                pair[:, k * cz : (k + 1) * cz] * (1.0 / seqs_total) + shift
-            ).astype(out_ref.dtype)
+            pair = pairs[g * cols : (g + 1) * cols, k * cz : (k + 1) * cz]
+            store(g * per + k, pair * (1.0 / seqs_total) + shift)
+
+
+def pair_kernel(*refs, places, block, **sizes):
+    wide_ref, shift_ref = refs[-7:-5] if block else refs[-6:-4]
+    out_hbm, outer_ref, done_ref, sem = refs[-4:]
+    parts, minor = sizes["parts"], sizes["minor"]
+    residues = done_ref.shape[1]
+    count = done_ref.shape[0] * minor * parts // LANES * (LANES // parts)
+
+    def left_of(m):
+        ref, at = places[m][:2]
+        return refs[ref][at : at + count, :]
+
+    def right_of(d, m):
+        ref, at = places[m][2:]
+        return refs[ref][at : at + minor * residues, :]
+
+    def store(row, pair):
+        done_ref[row] = pair.astype(done_ref.dtype)
+
+    pair_rows(left_of, right_of, wide_ref, shift_ref, outer_ref, store, wides=1, **sizes)
+    at = pl.multiple_of((lax.axis_index("wide") ^ block) * residues, 16)
+    copy = pltpu.make_async_copy(done_ref, out_hbm.at[:, pl.ds(at, residues), :], sem)
+    copy.start()
+    copy.wait()
+
+
+def pair_blocks_kernel(*refs, wides, parts, minor, **sizes):
+    left_refs, (right_ref, wide_ref, shift_ref, out_ref, outer_ref) = refs[:parts], refs[parts:]
+
+    def store(row, pair):
+        out_ref[row] = pair.astype(out_ref.dtype)
+
+    pair_rows(
+        lambda m: left_refs[m][...], lambda d, m: right_ref[d, m], wide_ref, shift_ref, outer_ref, store,
+        wides=wides, parts=parts, minor=minor, **sizes,
+    )
 
 
 def on_device(wide, narrow, x, gain, bias, lm, lb, rm, rb, w, shift):
@@ -205,14 +237,23 @@
     hbm = pl.BlockSpec(memory_space=pltpu.HBM)
     vmem = pl.BlockSpec(memory_space=pltpu.VMEM)
     params = pltpu.CompilerParams(vmem_limit_bytes=VMEM_LIMIT)
-    left_shape = jax.ShapeDtypeStruct((groups, seqs, LANES), jnp.bfloat16)
-    right_shape = jax.ShapeDtypeStruct((minor, residues, LANES), jnp.bfloat16)
+    direct = wide == 4 and narrow == 4
+    if direct:
+        packs = ((0,), (RIGHT,), (1, RIGHT), (2, 3, RIGHT))
+    else:
+        packs = tuple((m,) for m in range(narrow)) + ((RIGHT,),)
+    left_count, right_count = groups * seqs, minor * residues
     args = (x, gain, bias, lm.T, lb, rm.T, rb)
-    *lefts, right = pl.pallas_call(
-        functools.partial(features_kernel, parts=narrow, pieces=pieces),
-        out_shape=(left_shape,) * narrow + (right_shape,),
+    made = pl.pallas_call(
+        functools.partial(features_kernel, packs=packs, parts=narrow, pieces=pieces),
+        out_shape=tuple(
+            jax.ShapeDtypeStruct(
+                (sum(right_count if i == RIGHT else left_count for i in pack), LANES), jnp.bfloat16
+            )
+            for pack in packs
+        ),
         in_specs=[hbm] * len(args),
-        out_specs=(vmem,) * (narrow + 1),
+        out_specs=(vmem,) * len(packs),
         scratch_shapes=[pltpu.VMEM(a.shape, a.dtype) for a in args]
         + [
             pltpu.VMEM((seqs * residues, LANES), jnp.float32),
@@ -225,28 +266,6 @@
         compiler_params=pltpu.CompilerParams(vmem_limit_bytes=VMEM_ALL),
         name="features",
     )(*args)
-
-    def across(a, m):
-        return lax.ppermute(a, "narrow", [(i, i ^ m) for i in range(narrow)])
-
-    def along(a, d):
-        return lax.ppermute(a, "wide", [(i, (i + d) % wide) for i in range(wide)])
-
-    relative = wide * narrow <= 16
-    lefts = [lefts[0]] + [across(lefts[m], m) for m in range(1, narrow)]
-    if relative:
-        rows = [right] + [along(right, d) for d in range(1, wide)]
-        rights = [[chunk] for chunk in rows]
-        bit, order = narrow // 2, [0]
-        while bit:
-            rights = [row + [across(chunk, bit) for chunk in row] for row in rights]
-            order = order + [m ^ bit for m in order]
-            bit //= 2
-        rights = [row[order.index(m)] for row in rights for m in range(narrow)]
-    else:
-        every = lax.all_gather(right, ("wide", "narrow"), axis=0, tiled=False)
-        every = every.reshape(wide, narrow, minor, residues, LANES)
-        rights = [jnp.take(every, lax.axis_index("narrow") ^ jnp.arange(narrow), axis=1)]
 
     block_weights = pl.pallas_call(
         functools.partial(weights_kernel, parts=narrow, hidden=hidden),
@@ -262,37 +281,90 @@
         name="block_weights",
     )(w)
 
+    def across(a, m):
+        return lax.ppermute(a, "narrow", [(i, i ^ m) for i in range(narrow)])
+
+    def along(a, d):
+        return lax.ppermute(a, "wide", [(i, i ^ d) for i in range(wide)])
+
+    sizes = dict(parts=narrow, minor=minor, seqs_total=seqs * narrow)
+    out_shape = jax.ShapeDtypeStruct((own_rows, wide * residues, cz), jnp.bfloat16)
+    if direct:
+        return pairs_by_block(made, across, along, block_weights, shift, out_shape, residues, sizes, params)
+
+    lefts = [made[0]] + [across(made[m], m) for m in range(1, narrow)]
+    every = lax.all_gather(made[narrow], ("wide", "narrow"), axis=0, tiled=False)
+    every = every.reshape(wide, narrow, right_count, LANES)
+    every = jnp.take(every, lax.axis_index("narrow") ^ jnp.arange(narrow), axis=1)
     block = wide
-    if not relative:
-        while block % 2 == 0 and block * residues > 192:
-            block //= 2
+    while block % 2 == 0 and block * residues > 192:
+        block //= 2
     cols = block * residues
-    out_shape = jax.ShapeDtypeStruct((own_rows, wide * residues, cz), jnp.bfloat16)
-    scratch = [pltpu.VMEM((groups * cols, hidden * LANES), jnp.bfloat16)]
-    body = functools.partial(
-        pair_kernel, wides=block, parts=narrow, relative=relative, seqs_total=seqs * narrow
-    )
-    if relative:
-        specs = dict(in_specs=[vmem] * (narrow + len(rights) + 2), out_specs=vmem)
-    else:
-        specs = dict(
-            grid=(wide // block,),
-            in_specs=[pl.BlockSpec((groups, seqs, LANES), lambda b: (0, 0, 0))] * narrow
-            + [
-                pl.BlockSpec((block, narrow, minor, residues, LANES), lambda b: (b, 0, 0, 0, 0)),
-                pl.BlockSpec((hidden * LANES, per * cz), lambda b: (0, 0)),
-                pl.BlockSpec((cz,), lambda b: (0,)),
-            ],
-            out_specs=pl.BlockSpec((own_rows, cols, cz), lambda b: (0, b, 0)),
-        )
     return pl.pallas_call(
-        body,
+        functools.partial(pair_blocks_kernel, wides=block, **sizes),
+        grid=(wide // block,),
+        in_specs=[pl.BlockSpec((left_count, LANES), lambda b: (0, 0))] * narrow
+        + [
+            pl.BlockSpec((block, narrow, right_count, LANES), lambda b: (b, 0, 0, 0)),
+            pl.BlockSpec((hidden * LANES, per * cz), lambda b: (0, 0)),
+            pl.BlockSpec((cz,), lambda b: (0,)),
+        ],
+        out_specs=pl.BlockSpec((own_rows, cols, cz), lambda b: (0, b, 0)),
         out_shape=out_shape,
-        scratch_shapes=scratch,
+        scratch_shapes=[pltpu.VMEM((groups * cols, hidden * LANES), jnp.bfloat16)],
         compiler_params=params,
         name="pairs",
-        **specs,
-    )(*lefts, *rights, block_weights, shift)
+    )(*lefts, every, block_weights, shift)
+
+
+def pairs_by_block(made, across, along, block_weights, shift, out_shape, residues, sizes, params):
+    left_own, right, to_core, to_chip = made
+    far = {d: along(right, d) for d in (2, 3, 1)}
+    left_count, right_count = left_own.shape[0], right.shape[0]
+    chip = across(to_chip, 2)
+    core = across(to_core, 1)
+    both = across(chip, 1)
+
+    hbm = pl.BlockSpec(memory_space=pltpu.HBM)
+    vmem = pl.BlockSpec(memory_space=pltpu.VMEM)
+    own_rows, cols, cz = out_shape.shape
+    hidden = sizes["parts"] * sizes["minor"]
+    out = None
+    for d in range(cols // residues):
+        operands = [left_own, core, chip, both]
+        if d == 0:
+            operands.append(right)
+            rights = ((4, 0), (1, left_count), (2, 2 * left_count), (3, 2 * left_count))
+        else:
+            other = across(far[d], 2)
+            operands += [far[d], across(far[d], 1), other, across(other, 1)]
+            rights = tuple((4 + m, 0) for m in range(4))
+        places = tuple(
+            (m, left_count if m == 3 else 0) + rights[m] for m in range(4)
+        )
+        operands += [block_weights, shift]
+        specs = [vmem] * len(operands)
+        aliases = {}
+        if out is not None:
+            aliases = {len(operands): 0}
+            operands.append(out)
+            specs.append(hbm)
+        out = pl.pallas_call(
+            functools.partial(pair_kernel, places=places, block=d, **sizes),
+            out_shape=out_shape,
+            in_specs=specs,
+            out_specs=hbm,
+            input_output_aliases=aliases,
+            scratch_shapes=[
+                pltpu.VMEM((own_rows * hidden // LANES * residues, hidden * LANES), jnp.bfloat16),
+                pltpu.VMEM((own_rows, residues, cz), jnp.bfloat16),
+                pltpu.SemaphoreType.DMA,
+            ],
+            compiler_params=params,
+            cost_estimate=pl.CostEstimate(flops=1_500_000_000, bytes_accessed=5_000_000, transcendentals=0),
+            name=f"pairs_{d}",
+        )(*operands)
+    return out
 
 
 def solution(mesh):

time: 34.7 us -> 35.4 us (1.020)
  Pallas kernels: 9.37 us -> 11.9 us
  waiting for transfers between devices: 9.8 us -> 8.49 us
  starting transfers between devices: 14.3 us -> 13.7 us
    pallas_call x2 -> x5, Pallas kernels: 8.5 us -> 11 us  [the longest x4 7.35 us: pairs_by_block(): pl.pallas_call(functools.partial(pair_kernel, places=places, block=d, **s...]
    ppermute x3, waiting for transfers between devices: 5.75 us -> 3.44 us  [along(): return lax.ppermute(a, 'wide', [(i, i ^ d) for i in range(wide)])]
    ppermute x15 -> x12, starting transfers between devices: 9.42 us -> 7.92 us  [across(): return lax.ppermute(a, 'narrow', [(i, i ^ m) for i in range(narrow)])]
    ppermute x15 -> x12, waiting for transfers between devices: 4.05 us -> 5.06 us  [across(): return lax.ppermute(a, 'narrow', [(i, i ^ m) for i in range(narrow)])]
    ppermute x3, starting transfers between devices: 4.85 us -> 5.76 us  [along(): return lax.ppermute(a, 'wide', [(i, i ^ d) for i in range(wide)])]
  transfers between devices with their start and end apart: 18 -> 15, of which waited for: 4 -> 4; matrix products, arithmetic and copies ran while one was open for 0% -> 0% of each run, Pallas kernels for 3% -> 18%
where the time goes in v3:
time: 35.4 us; the launch traced here: 35.1 us
  starting transfers between devices  13.7 us (39%)
  Pallas kernels  11.9 us (34%)
  waiting for transfers between devices  8.49 us (24%)
  local copies, waits for them, and re-layouts  0.96 us (3%)
    ppermute x12, starting transfers between devices, across(): return lax.ppermute(a, 'narrow', [(i, i ^ m) for i in range(narrow)])  7.92 us
    pallas_call x4, Pallas kernels, pairs_by_block(): pl.pallas_call(functools.partial(pair_kernel, places=places, block=d, **s...  7.35 us
    ppermute x3, starting transfers between devices, along(): return lax.ppermute(a, 'wide', [(i, i ^ d) for i in range(wide)])  5.76 us
    ppermute x12, waiting for transfers between devices, across(): return lax.ppermute(a, 'narrow', [(i, i ^ m) for i in range(narrow)])  5.06 us
    pallas_call x1, Pallas kernels, on_device(): pl.pallas_call(functools.partial(features_kernel, packs=packs, parts=narr...  3.66 us
    ppermute x3, waiting for transfers between devices, along(): return lax.ppermute(a, 'wide', [(i, i ^ d) for i in range(wide)])  3.44 us
    unnamed x8, local copies, waits for them, and re-layouts  0.96 us
    pallas_call x1, Pallas kernels, on_device(): pl.pallas_call(functools.partial(weights_kernel, parts=narrow, hidden=hid...  0.88 us
  transfers between devices with their start and end apart: 15, of which 4 were waited for; matrix products, arithmetic and copies ran while one was open for 0% of the time, Pallas kernels for 18%

profile of v3, /device:TPU:0, one launch (start us, length us, event | category | flops | bytes accessed | tf_op | source)
XLA Modules:
  0.0 35.1 jit_solution(5280974403752364198)
XLA Ops:
  0.0 0.0 copy-start.2
  0.0 3.7 %features.1 = (bf16[96,128]{1,0:T(8,128)(2,1)}, bf16[384,128]{1,0:T(8,128)(2,1)}, bf16[480,128]{1,0:T(8,128)(2,1)}, bf16[576,128]{1,0:T(8,128)(2,1)}) custom-call(bf16[32,48,256]{2,1,0:T(8,128)(2,1)} %x_hbm.1, f32[256]{0:T(256)} %gain_hbm.1, f32[256]{0:T(256)} %bias_hbm.1, bf16[32,256]{1,0:T(8,128)(2,1)} %bitcast.2, f32[32]{0:T(128)} %lb_hbm.1, ...), custom_call_target="tpu_custom_call" | custom-call | tf_op jit(solution)/shard_map/features/pallas_call | solution.py:247
  3.7 3.0 %collective-permute-start.1 = (bf16[576,128]{1,0:T(8,128)(2,1)}, bf16[576,128]{1,0:T(8,128)(2,1)S(1)}, u32[]{:S(2)}, u32[]{:S(2)}) collective-permute-start(bf16[576,128]{1,0:T(8,128)(2,1)} %get-tuple-element.11), channel_id=1, source_target_pairs={{0,2},{1,3},{2,0},{3,1},{4,6},{5,7},{6,4},{7,5},{8,10},{9,11},{10,... | collective-permute-start | bytes 442376 | tf_op jit(solution)/shard_map/ppermute | solution.py:285
  6.7 1.6 %collective-permute-start.11 = (bf16[384,128]{1,0:T(8,128)(2,1)}, bf16[384,128]{1,0:T(8,128)(2,1)S(1)}, u32[]{:S(2)}, u32[]{:S(2)}) collective-permute-start(bf16[384,128]{1,0:T(8,128)(2,1)} %get-tuple-element.12.refs_4_), channel_id=1, source_target_pairs={{0,4},{4,0},{8,12},{12,8},{1,5},{5,1},{9,13},{13,9},{2,6},{6,2},{1... | collective-permute-start | bytes 294920 | tf_op jit(solution)/shard_map/ppermute | solution.py:288
  8.3 2.5 %collective-permute-done.1.refs_2_ = bf16[576,128]{1,0:T(8,128)(2,1)S(1)} collective-permute-done((bf16[576,128]{1,0:T(8,128)(2,1)}, bf16[576,128]{1,0:T(8,128)(2,1)S(1)}, u32[]{:S(2)}, u32[]{:S(2)}) %collective-permute-start.1) | collective-permute-done | bytes 147488 | tf_op jit(solution)/shard_map/ppermute | solution.py:285
  10.7 0.0 collective-permute-start.2
  10.7 0.5 %collective-permute-start = (bf16[480,128]{1,0:T(8,128)(2,1)}, bf16[480,128]{1,0:T(8,128)(2,1)S(1)}, u32[]{:S(2)}, u32[]{:S(2)}) collective-permute-start(bf16[480,128]{1,0:T(8,128)(2,1)} %get-tuple-element.10), channel_id=1, source_target_pairs={{0,1},{1,0},{2,3},{3,2},{4,5},{5,4},{6,7},{7,6},{8,9},{9,8},{10,11... | collective-permute-start | bytes 368648 | tf_op jit(solution)/shard_map/ppermute | solution.py:285
  11.2 2.8 %collective-permute-start.7 = (bf16[384,128]{1,0:T(8,128)(2,1)}, bf16[384,128]{1,0:T(8,128)(2,1)S(1)}, u32[]{:S(2)}, u32[]{:S(2)}) collective-permute-start(bf16[384,128]{1,0:T(8,128)(2,1)} %get-tuple-element.12.refs_4_), channel_id=1, source_target_pairs={{0,8},{4,12},{8,0},{12,4},{1,9},{5,13},{9,1},{13,5},{2,10},{6,14},... | collective-permute-start | bytes 294920 | tf_op jit(solution)/shard_map/ppermute | solution.py:288
  14.1 1.3 %collective-permute-start.3 = (bf16[384,128]{1,0:T(8,128)(2,1)}, bf16[384,128]{1,0:T(8,128)(2,1)S(1)}, u32[]{:S(2)}, u32[]{:S(2)}) collective-permute-start(bf16[384,128]{1,0:T(8,128)(2,1)} %get-tuple-element.12.refs_4_), channel_id=1, source_target_pairs={{0,12},{4,8},{8,4},{12,0},{1,13},{5,9},{9,5},{13,1},{2,14},{6,10},... | collective-permute-start | bytes 294920 | tf_op jit(solution)/shard_map/ppermute | solution.py:288
  15.4 0.0 collective-permute-done.11.refs_4_
  15.4 1.5 %collective-permute-start.13 = (bf16[384,128]{1,0:T(8,128)(2,1)S(1)}, bf16[384,128]{1,0:T(8,128)(2,1)S(1)}, u32[]{:S(2)}, u32[]{:S(2)}) collective-permute-start(bf16[384,128]{1,0:T(8,128)(2,1)S(1)} %collective-permute-done.11.refs_4_), channel_id=1, source_target_pairs={{0,2},{1,3},{2,0},{3,1},{4,6},{5,7},{6,4},{7,5},{8,10},{9,11},{10,... | collective-permute-start | bytes 294920 | tf_op jit(solution)/shard_map/ppermute | solution.py:285
  16.9 0.0 copy-start
  16.9 0.9 %copy-done = bf16[1024,128]{1,0:T(8,128)(2,1)S(1)} copy-done((bf16[1024,128]{1,0:T(8,128)(2,1)S(1)}, bf16[1024,128]{1,0:T(8,128)(2,1)}, u32[]{:S(2)}) %copy-start) | copy-done | bytes 262168
  17.9 0.0 copy-start.1
  17.9 0.0 copy-start.3
  17.9 0.9 %block_weights.1.refs_5_.refs_8_ = bf16[4096,512]{1,0:T(8,128)(2,1)S(1)} custom-call(bf16[1024,128]{1,0:T(8,128)(2,1)S(1)} %copy-done), custom_call_target="tpu_custom_call" | custom-call | tf_op jit(solution)/shard_map/block_weights/pallas_call | solution.py:270
  18.8 3.4 %collective-permute-done.7.refs_4_ = bf16[384,128]{1,0:T(8,128)(2,1)S(1)} collective-permute-done((bf16[384,128]{1,0:T(8,128)(2,1)}, bf16[384,128]{1,0:T(8,128)(2,1)S(1)}, u32[]{:S(2)}, u32[]{:S(2)}) %collective-permute-start.7) | collective-permute-done | bytes 98336 | tf_op jit(solution)/shard_map/ppermute | solution.py:288
  22.2 0.0 collective-permute-start.12
  22.2 0.0 collective-permute-done.3.refs_4_
  22.2 1.8 %collective-permute-start.9 = (bf16[384,128]{1,0:T(8,128)(2,1)S(1)}, bf16[384,128]{1,0:T(8,128)(2,1)S(1)}, u32[]{:S(2)}, u32[]{:S(2)}) collective-permute-start(bf16[384,128]{1,0:T(8,128)(2,1)S(1)} %collective-permute-done.7.refs_4_), channel_id=1, source_target_pairs={{0,2},{1,3},{2,0},{3,1},{4,6},{5,7},{6,4},{7,5},{8,10},{9,11},{10,... | collective-permute-start | bytes 294920 | tf_op jit(solution)/shard_map/ppermute | solution.py:285
  24.0 0.0 collective-permute-done.refs_1_
  24.0 0.2 collective-permute-start.8
  24.2 0.0 collective-permute-done.13.refs_6_
  24.2 0.3 collective-permute-start.5
  24.6 0.0 collective-permute-done.2.refs_3_
  24.6 0.0 collective-permute-start.14
  24.6 0.0 copy-done.2
  24.6 0.0 copy-done.1
  24.6 0.0 copy-done.3
  24.6 1.8 %pairs_0.1.refs_10_ = bf16[12,192,128]{2,1,0:T(8,128)(2,1)} custom-call(bf16[96,128]{1,0:T(8,128)(2,1)S(1)} %copy-done.1, bf16[480,128]{1,0:T(8,128)(2,1)S(1)} %collective-permute-done.refs_1_, bf16[576,128]{1,0:T(8,128)(2,1)S(1)} %collective-permute-done.1.refs_2_, bf16[576,128]{1,0:T(8,128)(2,1)S(1)} %collective-permute-done.2.refs_3_, ...), custom_call_target="tpu_custom_call" | custom-call | flops 1500000000 | bytes 5000000 | tf_op jit(solution)/shard_map/pairs_0/pallas_call | solution.py:352
  26.4 0.0 collective-permute-done.12.refs_5_
  26.4 0.6 %collective-permute-start.4 = (bf16[384,128]{1,0:T(8,128)(2,1)S(1)}, bf16[384,128]{1,0:T(8,128)(2,1)S(1)}, u32[]{:S(2)}, u32[]{:S(2)}) collective-permute-start(bf16[384,128]{1,0:T(8,128)(2,1)S(1)} %collective-permute-done.3.refs_4_), channel_id=1, source_target_pairs={{0,1},{1,0},{2,3},{3,2},{4,5},{5,4},{6,7},{7,6},{8,9},{9,8},{10,11... | collective-permute-start | bytes 294920 | tf_op jit(solution)/shard_map/ppermute | solution.py:285
  27.0 0.8 %collective-permute-done.9.refs_6_ = bf16[384,128]{1,0:T(8,128)(2,1)S(1)} collective-permute-done((bf16[384,128]{1,0:T(8,128)(2,1)S(1)}, bf16[384,128]{1,0:T(8,128)(2,1)S(1)}, u32[]{:S(2)}, u32[]{:S(2)}) %collective-permute-start.9) | collective-permute-done | bytes 98336 | tf_op jit(solution)/shard_map/ppermute | solution.py:285
  27.8 0.0 collective-permute-start.10
  27.8 1.8 %collective-permute-done.5.refs_6_ = bf16[384,128]{1,0:T(8,128)(2,1)S(1)} collective-permute-done((bf16[384,128]{1,0:T(8,128)(2,1)S(1)}, bf16[384,128]{1,0:T(8,128)(2,1)S(1)}, u32[]{:S(2)}, u32[]{:S(2)}) %collective-permute-start.5) | collective-permute-done | bytes 98336 | tf_op jit(solution)/shard_map/ppermute | solution.py:285
  29.6 0.0 collective-permute-start.6
  29.6 0.0 collective-permute-done.14.refs_7_
  29.6 1.8 %pairs_1.1.refs_10_ = bf16[12,192,128]{2,1,0:T(8,128)(2,1)} custom-call(bf16[96,128]{1,0:T(8,128)(2,1)S(1)} %copy-done.1, bf16[480,128]{1,0:T(8,128)(2,1)S(1)} %collective-permute-done.refs_1_, bf16[576,128]{1,0:T(8,128)(2,1)S(1)} %collective-permute-done.1.refs_2_, ...), custom_call_target="tpu_custom_call", output_to_operand_aliasing={{}: (10, {})} | custom-call | flops 1500000000 | bytes 5000000 | tf_op jit(solution)/shard_map/pairs_1/pallas_call | solution.py:352
  31.4 0.0 collective-permute-done.8.refs_5_
  31.4 0.0 collective-permute-done.10.refs_7_
  31.4 1.8 %pairs_2.1.refs_10_ = bf16[12,192,128]{2,1,0:T(8,128)(2,1)} custom-call(bf16[96,128]{1,0:T(8,128)(2,1)S(1)} %copy-done.1, bf16[480,128]{1,0:T(8,128)(2,1)S(1)} %collective-permute-done.refs_1_, bf16[576,128]{1,0:T(8,128)(2,1)S(1)} %collective-permute-done.1.refs_2_, ...), custom_call_target="tpu_custom_call", output_to_operand_aliasing={{}: (10, {})} | custom-call | flops 1500000000 | bytes 5000000 | tf_op jit(solution)/shard_map/pairs_2/pallas_call | solution.py:352
  33.3 0.0 collective-permute-done.4.refs_5_
  33.3 0.0 collective-permute-done.6.refs_7_
  33.3 1.9 %pairs_3.1 = bf16[12,192,128]{2,1,0:T(8,128)(2,1)} custom-call(bf16[96,128]{1,0:T(8,128)(2,1)S(1)} %copy-done.1, bf16[480,128]{1,0:T(8,128)(2,1)S(1)} %collective-permute-done.refs_1_, bf16[576,128]{1,0:T(8,128)(2,1)S(1)} %collective-permute-done.1.refs_2_, bf16[576,128]{1,0:T(8,128)(2,1)S(1)} %collective-permute-done.2.refs_3_, ...), custom_call_target="tpu_custom_call", output_to_operand_aliasing={{}: (10, {})} | custom-call | flops 1500000000 | bytes 5000000 | tf_op jit(solution)/shard_map/pairs_3/pallas_call | solution.py:352
Async XLA Ops:
  0.0 24.6 %copy-start.2 = (f32[128]{0:T(128)S(1)}, f32[128]{0:T(128)}, u32[]{:S(2)}) copy-start(f32[128]{0:T(128)} %refs_9_.5) | copy-start | bytes 1540
  3.7 7.1 %collective-permute-start.1 = (bf16[576,128]{1,0:T(8,128)(2,1)}, bf16[576,128]{1,0:T(8,128)(2,1)S(1)}, u32[]{:S(2)}, u32[]{:S(2)}) collective-permute-start(bf16[576,128]{1,0:T(8,128)(2,1)} %get-tuple-element.11), channel_id=1, source_target_pairs={{0,2},{1,3},{2,0},{3,1},{4,6},{5,7},{6,4},{7,5},{8,10},{9,11},{10,... | collective-permute-start | bytes 442376 | tf_op jit(solution)/shard_map/ppermute | solution.py:285
  6.7 8.8 %collective-permute-start.11 = (bf16[384,128]{1,0:T(8,128)(2,1)}, bf16[384,128]{1,0:T(8,128)(2,1)S(1)}, u32[]{:S(2)}, u32[]{:S(2)}) collective-permute-start(bf16[384,128]{1,0:T(8,128)(2,1)} %get-tuple-element.12.refs_4_), channel_id=1, source_target_pairs={{0,4},{4,0},{8,12},{12,8},{1,5},{5,1},{9,13},{13,9},{2,6},{6,2},{1... | collective-permute-start | bytes 294920 | tf_op jit(solution)/shard_map/ppermute | solution.py:288
  10.7 13.8 %collective-permute-start.2 = (bf16[576,128]{1,0:T(8,128)(2,1)S(1)}, bf16[576,128]{1,0:T(8,128)(2,1)S(1)}, u32[]{:S(2)}, u32[]{:S(2)}) collective-permute-start(bf16[576,128]{1,0:T(8,128)(2,1)S(1)} %collective-permute-done.1.refs_2_), channel_id=1, source_target_pairs={{0,1},{1,0},{2,3},{3,2},{4,5},{5,4},{6,7},{7,6},{8,9},{9,8},{10,11... | collective-permute-start | bytes 442376 | tf_op jit(solution)/shard_map/ppermute | solution.py:285
  10.7 13.2 %collective-permute-start = (bf16[480,128]{1,0:T(8,128)(2,1)}, bf16[480,128]{1,0:T(8,128)(2,1)S(1)}, u32[]{:S(2)}, u32[]{:S(2)}) collective-permute-start(bf16[480,128]{1,0:T(8,128)(2,1)} %get-tuple-element.10), channel_id=1, source_target_pairs={{0,1},{1,0},{2,3},{3,2},{4,5},{5,4},{6,7},{7,6},{8,9},{9,8},{10,11... | collective-permute-start | bytes 368648 | tf_op jit(solution)/shard_map/ppermute | solution.py:285
  11.2 11.0 %collective-permute-start.7 = (bf16[384,128]{1,0:T(8,128)(2,1)}, bf16[384,128]{1,0:T(8,128)(2,1)S(1)}, u32[]{:S(2)}, u32[]{:S(2)}) collective-permute-start(bf16[384,128]{1,0:T(8,128)(2,1)} %get-tuple-element.12.refs_4_), channel_id=1, source_target_pairs={{0,8},{4,12},{8,0},{12,4},{1,9},{5,13},{9,1},{13,5},{2,10},{6,14},... | collective-permute-start | bytes 294920 | tf_op jit(solution)/shard_map/ppermute | solution.py:288
  14.1 8.1 %collective-permute-start.3 = (bf16[384,128]{1,0:T(8,128)(2,1)}, bf16[384,128]{1,0:T(8,128)(2,1)S(1)}, u32[]{:S(2)}, u32[]{:S(2)}) collective-permute-start(bf16[384,128]{1,0:T(8,128)(2,1)} %get-tuple-element.12.refs_4_), channel_id=1, source_target_pairs={{0,12},{4,8},{8,4},{12,0},{1,13},{5,9},{9,5},{13,1},{2,14},{6,10},... | collective-permute-start | bytes 294920 | tf_op jit(solution)/shard_map/ppermute | solution.py:288
  15.4 8.8 %collective-permute-start.13 = (bf16[384,128]{1,0:T(8,128)(2,1)S(1)}, bf16[384,128]{1,0:T(8,128)(2,1)S(1)}, u32[]{:S(2)}, u32[]{:S(2)}) collective-permute-start(bf16[384,128]{1,0:T(8,128)(2,1)S(1)} %collective-permute-done.11.refs_4_), channel_id=1, source_target_pairs={{0,2},{1,3},{2,0},{3,1},{4,6},{5,7},{6,4},{7,5},{8,10},{9,11},{10,... | collective-permute-start | bytes 294920 | tf_op jit(solution)/shard_map/ppermute | solution.py:285
  16.9 0.9 %copy-start = (bf16[1024,128]{1,0:T(8,128)(2,1)S(1)}, bf16[1024,128]{1,0:T(8,128)(2,1)}, u32[]{:S(2)}) copy-start(bf16[1024,128]{1,0:T(8,128)(2,1)} %w_hbm.1) | copy-start | bytes 786436
  17.9 6.7 %copy-start.1 = (bf16[96,128]{1,0:T(8,128)(2,1)S(1)}, bf16[96,128]{1,0:T(8,128)(2,1)}, u32[]{:S(2)}) copy-start(bf16[96,128]{1,0:T(8,128)(2,1)} %get-tuple-element.9.refs_0_) | copy-start | bytes 73732
  17.9 6.7 %copy-start.3 = (bf16[384,128]{1,0:T(8,128)(2,1)S(1)}, bf16[384,128]{1,0:T(8,128)(2,1)}, u32[]{:S(2)}) copy-start(bf16[384,128]{1,0:T(8,128)(2,1)} %get-tuple-element.12.refs_4_) | copy-start | bytes 294916
  22.2 4.2 %collective-permute-start.12 = (bf16[384,128]{1,0:T(8,128)(2,1)S(1)}, bf16[384,128]{1,0:T(8,128)(2,1)S(1)}, u32[]{:S(2)}, u32[]{:S(2)}) collective-permute-start(bf16[384,128]{1,0:T(8,128)(2,1)S(1)} %collective-permute-done.11.refs_4_), channel_id=1, source_target_pairs={{0,1},{1,0},{2,3},{3,2},{4,5},{5,4},{6,7},{7,6},{8,9},{9,8},{10,11... | collective-permute-start | bytes 294920 | tf_op jit(solution)/shard_map/ppermute | solution.py:285
  22.2 5.5 %collective-permute-start.9 = (bf16[384,128]{1,0:T(8,128)(2,1)S(1)}, bf16[384,128]{1,0:T(8,128)(2,1)S(1)}, u32[]{:S(2)}, u32[]{:S(2)}) collective-permute-start(bf16[384,128]{1,0:T(8,128)(2,1)S(1)} %collective-permute-done.7.refs_4_), channel_id=1, source_target_pairs={{0,2},{1,3},{2,0},{3,1},{4,6},{5,7},{6,4},{7,5},{8,10},{9,11},{10,... | collective-permute-start | bytes 294920 | tf_op jit(solution)/shard_map/ppermute | solution.py:285
  24.0 7.4 %collective-permute-start.8 = (bf16[384,128]{1,0:T(8,128)(2,1)S(1)}, bf16[384,128]{1,0:T(8,128)(2,1)S(1)}, u32[]{:S(2)}, u32[]{:S(2)}) collective-permute-start(bf16[384,128]{1,0:T(8,128)(2,1)S(1)} %collective-permute-done.7.refs_4_), channel_id=1, source_target_pairs={{0,1},{1,0},{2,3},{3,2},{4,5},{5,4},{6,7},{7,6},{8,9},{9,8},{10,11... | collective-permute-start | bytes 294920 | tf_op jit(solution)/shard_map/ppermute | solution.py:285
  24.2 5.3 %collective-permute-start.5 = (bf16[384,128]{1,0:T(8,128)(2,1)S(1)}, bf16[384,128]{1,0:T(8,128)(2,1)S(1)}, u32[]{:S(2)}, u32[]{:S(2)}) collective-permute-start(bf16[384,128]{1,0:T(8,128)(2,1)S(1)} %collective-permute-done.3.refs_4_), channel_id=1, source_target_pairs={{0,2},{1,3},{2,0},{3,1},{4,6},{5,7},{6,4},{7,5},{8,10},{9,11},{10,... | collective-permute-start | bytes 294920 | tf_op jit(solution)/shard_map/ppermute | solution.py:285
  24.6 5.0 %collective-permute-start.14 = (bf16[384,128]{1,0:T(8,128)(2,1)S(1)}, bf16[384,128]{1,0:T(8,128)(2,1)S(1)}, u32[]{:S(2)}, u32[]{:S(2)}) collective-permute-start(bf16[384,128]{1,0:T(8,128)(2,1)S(1)} %collective-permute-done.13.refs_6_), channel_id=1, source_target_pairs={{0,1},{1,0},{2,3},{3,2},{4,5},{5,4},{6,7},{7,6},{8,9},{9,8},{10,11... | collective-permute-start | bytes 294920 | tf_op jit(solution)/shard_map/ppermute | solution.py:285
  26.4 6.8 %collective-permute-start.4 = (bf16[384,128]{1,0:T(8,128)(2,1)S(1)}, bf16[384,128]{1,0:T(8,128)(2,1)S(1)}, u32[]{:S(2)}, u32[]{:S(2)}) collective-permute-start(bf16[384,128]{1,0:T(8,128)(2,1)S(1)} %collective-permute-done.3.refs_4_), channel_id=1, source_target_pairs={{0,1},{1,0},{2,3},{3,2},{4,5},{5,4},{6,7},{7,6},{8,9},{9,8},{10,11... | collective-permute-start | bytes 294920 | tf_op jit(solution)/shard_map/ppermute | solution.py:285
  27.8 3.7 %collective-permute-start.10 = (bf16[384,128]{1,0:T(8,128)(2,1)S(1)}, bf16[384,128]{1,0:T(8,128)(2,1)S(1)}, u32[]{:S(2)}, u32[]{:S(2)}) collective-permute-start(bf16[384,128]{1,0:T(8,128)(2,1)S(1)} %collective-permute-done.9.refs_6_), channel_id=1, source_target_pairs={{0,1},{1,0},{2,3},{3,2},{4,5},{5,4},{6,7},{7,6},{8,9},{9,8},{10,11... | collective-permute-start | bytes 294920 | tf_op jit(solution)/shard_map/ppermute | solution.py:285
  29.6 3.7 %collective-permute-start.6 = (bf16[384,128]{1,0:T(8,128)(2,1)S(1)}, bf16[384,128]{1,0:T(8,128)(2,1)S(1)}, u32[]{:S(2)}, u32[]{:S(2)}) collective-permute-start(bf16[384,128]{1,0:T(8,128)(2,1)S(1)} %collective-permute-done.5.refs_6_), channel_id=1, source_target_pairs={{0,1},{1,0},{2,3},{3,2},{4,5},{5,4},{6,7},{7,6},{8,9},{9,8},{10,11... | collective-permute-start | bytes 294920 | tf_op jit(solution)/shard_map/ppermute | solution.py:285

commit v4 on v2

v4 whole, which is shorter than its diff:
```python
import functools

import jax
import jax.numpy as jnp
from jax import lax
from jax.experimental import pallas as pl
from jax.experimental.pallas import tpu as pltpu
from jax.sharding import PartitionSpec as P

LANES = 128
VMEM_LIMIT = 40 * 1024 * 1024
VMEM_ALL = 62 * 1024 * 1024


def iota(shape, dim):
    return lax.broadcasted_iota(jnp.int32, shape, dim)


def features_kernel(
    x_hbm, gain_hbm, bias_hbm, lm_hbm, lb_hbm, rm_hbm, rb_hbm,
    *refs, halves, pieces,
):
    left_ref, right_refs = refs[0], refs[1 : 1 + halves]
    (x_ref, gain_ref, bias_ref, lm_ref, lb_ref, rm_ref, rb_ref,
     lo_ref, hi_ref, turned_ref, rows_ref, sems) = refs[1 + halves :]
    seqs, residues, depth = x_ref.shape
    hidden = lm_ref.shape[0]
    per = LANES // hidden
    slots = LANES // seqs
    minor = hidden // slots
    groups = residues // per
    own = lax.axis_index("narrow")

    piece = seqs // pieces
    copies = [
        pltpu.make_async_copy(
            x_hbm.at[pl.ds(p * piece, piece)], x_ref.at[pl.ds(p * piece, piece)], sems.at[p]
        )
        for p in range(pieces)
    ]
    small = ((gain_hbm, gain_ref), (bias_hbm, bias_ref), (lm_hbm, lm_ref),
             (lb_hbm, lb_ref), (rm_hbm, rm_ref), (rb_hbm, rb_ref))
    rest = [pltpu.make_async_copy(a, b, sems.at[pieces + i]) for i, (a, b) in enumerate(small)]
    copies[0].start()
    for copy in rest:
        copy.start()
    for copy in copies[1:]:
        copy.start()
    for copy in rest:
        copy.wait()

    column, row = iota((hidden, LANES), 1) % hidden, iota((hidden, LANES), 0)
    spread_l = (column == row).astype(jnp.float32)
    spread_r = (column == (row ^ (own * minor))).astype(jnp.float32)

    def widen(m, pick):
        return lax.dot_general(
            m, pick.astype(jnp.bfloat16), (((0,), (0,)), ((), ())),
            preferred_element_type=jnp.float32,
        )

    def widen_bias(b, pick):
        b = jnp.broadcast_to(b.reshape(1, hidden), (8, hidden))
        return jnp.dot(
            b, pick, precision=lax.Precision.HIGHEST, preferred_element_type=jnp.float32
        )[:1]

    weights = jnp.concatenate(
        [widen(lm_ref[...], spread_l), widen(rm_ref[...], spread_r)], axis=1
    )
    shift = jnp.concatenate(
        [widen_bias(lb_ref[...], spread_l), widen_bias(rb_ref[...], spread_r)], axis=1
    )
    place = iota((depth, 2 * LANES), 1) % LANES // hidden

    gain = gain_ref[...].reshape(1, depth)
    bias = bias_ref[...].reshape(1, depth)
    step = 4
    for s in range(0, seqs, step):
        if s % piece == 0:
            copies[s // piece].wait()
        x = x_ref[s : s + step].reshape(step * residues, depth).astype(jnp.float32)
        x = x - jnp.mean(x, axis=-1, keepdims=True)
        spread = jnp.mean(x * x, axis=-1, keepdims=True)
        x = x * lax.rsqrt(spread + 1e-05) * gain + bias
        rows = pl.ds(s * residues, step * residues)
        lo_ref[rows, :] = x[:, :LANES]
        hi_ref[rows, :] = x[:, LANES:]

    total = None
    for k in range(per):
        part = jnp.concatenate(
            [
                jnp.concatenate(
                    [half[pl.ds(g * per + k, seqs, stride=residues), :] for half in (lo_ref, hi_ref)],
                    axis=1,
                )
                for g in range(groups)
            ],
            axis=0,
        ).astype(jnp.bfloat16)
        placed = jnp.where(place == k, weights, 0.0).astype(jnp.bfloat16)
        term = jnp.dot(part, placed, preferred_element_type=jnp.float32)
        total = term if total is None else total + term
    total = total + shift
    left_ref[...] = total[:, :LANES].astype(left_ref.dtype).reshape(left_ref.shape)

    slot = iota((minor, LANES), 1) // seqs
    for block in range(groups // slots):
        turned_ref[...] = total[block * LANES : (block + 1) * LANES, LANES:].T
        for k in range(per):
            parts_of = [turned_ref[pl.ds(k * hidden + q * minor, minor), :] for q in range(slots)]
            for g in range(slots):
                out = None
                for q in range(slots):
                    moved = parts_of[q]
                    if q != g:
                        moved = pltpu.roll(moved, (q - g) % slots * seqs, axis=1)
                    out = moved if out is None else jnp.where(slot == q, moved, out)
                j = (block * slots + g) * per + k
                rows_ref[pl.ds(j, minor, stride=residues), :] = out
    right = rows_ref[...].astype(jnp.bfloat16)
    count = minor * residues // halves
    for h, right_ref in enumerate(right_refs):
        for copy in range(right_ref.shape[0]):
            right_ref[copy] = right[h * count : (h + 1) * count]


def weights_kernel(w_hbm, wide_ref, w_ref, wf_ref, sem, *, parts, hidden, halves):
    copy = pltpu.make_async_copy(w_hbm, w_ref, sem)
    copy.start()
    cz = w_ref.shape[1]
    per = LANES // hidden
    minor = hidden // parts
    count = minor // halves
    own = lax.axis_index("narrow")
    wide_ref[...] = jnp.zeros_like(wide_ref)
    copy.wait()
    wf_ref[...] = w_ref[...].astype(jnp.float32)
    for e in range(hidden):
        q, h, i = e // minor, e % minor // count, e % count
        rows = wf_ref[pl.ds(e ^ (own * minor), hidden, stride=hidden), :].astype(jnp.bfloat16)
        for k in range(per):
            at = ((h * parts + q) * count + i) * LANES + k * hidden
            wide_ref[at : at + hidden, k * cz : (k + 1) * cz] = rows


def outer_rows(left_ref, right_of, outer_ref, *, wides, parts, minor):
    seqs = LANES // parts
    own = lax.axis_index("narrow")
    lefts = [left_ref[own ^ m] for m in range(parts)]
    groups = lefts[0].shape[0] // seqs
    residues = right_of(0, 0).shape[0] // minor
    cols = wides * residues
    slot = iota((minor * residues, LANES), 1) // seqs
    for q in range(parts):
        left = jnp.concatenate(
            [
                jnp.concatenate([lefts[q ^ k][g * seqs : (g + 1) * seqs] for k in range(parts)], axis=0)
                for g in range(groups)
            ],
            axis=1,
        )
        for d in range(wides):
            right = None
            for k in range(parts):
                chunk = right_of(d, q ^ k)
                right = chunk if right is None else jnp.where(slot == k, chunk, right)
            outer = jnp.dot(right, left, preferred_element_type=jnp.float32).astype(jnp.bfloat16)
            for e in range(minor):
                for g in range(groups):
                    outer_ref[
                        pl.ds(g * cols + d * residues, residues),
                        (q * minor + e) * LANES : (q * minor + e + 1) * LANES,
                    ] = outer[e * residues : (e + 1) * residues, g * LANES : (g + 1) * LANES]


def sums_kernel(left_ref, *refs, part, **sizes):
    rights, (wide_ref, sums_ref, outer_ref) = refs[: sizes["parts"]], refs[sizes["parts"] :]
    outer_rows(left_ref, lambda d, m: rights[m][d], outer_ref, **sizes)
    depth = outer_ref.shape[1]
    sums_ref[...] = jnp.dot(
        outer_ref[...], wide_ref[part * depth : (part + 1) * depth], preferred_element_type=jnp.float32
    )


def pairs_kernel(left_ref, *refs, part, seqs_total, **sizes):
    rights, refs = refs[: sizes["parts"]], refs[sizes["parts"] :]
    wide_ref, sums_ref, shift_ref, out_hbm, outer_ref, done_ref, sems = refs
    outer_rows(left_ref, lambda d, m: rights[m][d], outer_ref, **sizes)
    depth = outer_ref.shape[1]
    own_rows, cols, cz = done_ref.shape
    per = wide_ref.shape[1] // cz
    shift = shift_ref[...].reshape(1, cz)
    copies = []
    for g in range(own_rows // per):
        rows = slice(g * cols, (g + 1) * cols)
        pairs = sums_ref[rows] + jnp.dot(
            outer_ref[rows], wide_ref[part * depth : (part + 1) * depth], preferred_element_type=jnp.float32
        )
        for k in range(per):
            pair = pairs[:, k * cz : (k + 1) * cz] * (1.0 / seqs_total) + shift
            done_ref[g * per + k] = pair.astype(done_ref.dtype)
        copies.append(
            pltpu.make_async_copy(
                done_ref.at[pl.ds(g * per, per)], out_hbm.at[pl.ds(g * per, per)], sems.at[g]
            )
        )
        copies[-1].start()
    for copy in copies:
        copy.wait()


def pair_blocks_kernel(left_ref, right_ref, wide_ref, shift_ref, out_ref, outer_ref, *, seqs_total, **sizes):
    outer_rows(left_ref, lambda d, m: right_ref[d, m], outer_ref, **sizes)
    own_rows, cols, cz = out_ref.shape
    per = wide_ref.shape[1] // cz
    shift = shift_ref[...].reshape(1, cz)
    for g in range(own_rows // per):
        pairs = jnp.dot(
            outer_ref[pl.ds(g * cols, cols), :], wide_ref[...], preferred_element_type=jnp.float32
        )
        for k in range(per):
            pair = pairs[:, k * cz : (k + 1) * cz] * (1.0 / seqs_total) + shift
            out_ref[g * per + k] = pair.astype(out_ref.dtype)


def on_device(wide, narrow, x, gain, bias, lm, lb, rm, rb, w, shift):
    seqs, residues, depth = x.shape
    hidden = lm.shape[1]
    cz = w.shape[1]
    per = LANES // hidden
    slots = LANES // seqs
    minor = hidden // slots
    own_rows = residues // narrow
    groups = own_rows // per
    pieces = 4
    hbm = pl.BlockSpec(memory_space=pltpu.HBM)
    vmem = pl.BlockSpec(memory_space=pltpu.VMEM)
    params = pltpu.CompilerParams(vmem_limit_bytes=VMEM_LIMIT)
    direct = wide * narrow <= 16
    halves, copies = (2, wide) if direct else (1, 1)
    count = minor // halves
    args = (x, gain, bias, lm.T, lb, rm.T, rb)
    left, *rights = pl.pallas_call(
        functools.partial(features_kernel, halves=halves, pieces=pieces),
        out_shape=(jax.ShapeDtypeStruct((narrow, groups * seqs, LANES), jnp.bfloat16),)
        + (jax.ShapeDtypeStruct((copies, count * residues, LANES), jnp.bfloat16),) * halves,
        in_specs=[hbm] * len(args),
        out_specs=(vmem,) * (1 + halves),
        scratch_shapes=[pltpu.VMEM(a.shape, a.dtype) for a in args]
        + [
            pltpu.VMEM((seqs * residues, LANES), jnp.float32),
            pltpu.VMEM((seqs * residues, LANES), jnp.float32),
            pltpu.VMEM((LANES, LANES), jnp.float32),
            pltpu.VMEM((minor * residues, LANES), jnp.float32),
            pltpu.SemaphoreType.DMA((pieces + len(args) - 1,)),
        ],
        compiler_params=pltpu.CompilerParams(vmem_limit_bytes=VMEM_ALL),
        name="features",
    )(*args)

    block_weights = pl.pallas_call(
        functools.partial(weights_kernel, parts=narrow, hidden=hidden, halves=halves),
        out_shape=jax.ShapeDtypeStruct((hidden * LANES, per * cz), jnp.bfloat16),
        in_specs=[hbm],
        out_specs=vmem,
        scratch_shapes=[
            pltpu.VMEM(w.shape, w.dtype),
            pltpu.VMEM(w.shape, jnp.float32),
            pltpu.SemaphoreType.DMA,
        ],
        compiler_params=params,
        name="block_weights",
    )(w)

    out_shape = jax.ShapeDtypeStruct((own_rows, wide * residues, cz), jnp.bfloat16)
    if direct:
        held = []
        for right in rights:
            chunks = [lax.all_to_all(right, "wide", split_axis=0, concat_axis=0, tiled=True)]
            bit, order = narrow // 2, [0]
            while bit:
                chunks += [lax.ppermute(c, "narrow", [(i, i ^ bit) for i in range(narrow)]) for c in chunks]
                order += [m ^ bit for m in order]
                bit //= 2
            held.append([chunks[order.index(m)] for m in range(narrow)])
        left = lax.all_to_all(left, "narrow", split_axis=0, concat_axis=0, tiled=True)
        sizes = dict(wides=wide, parts=narrow, minor=count)
        cols = wide * residues
        cost = pl.CostEstimate(flops=2_000_000_000, bytes_accessed=5_000_000, transcendentals=0)
        outer = pltpu.VMEM((groups * cols, narrow * count * LANES), jnp.bfloat16)
        sums = pl.pallas_call(
            functools.partial(sums_kernel, part=0, **sizes),
            out_shape=jax.ShapeDtypeStruct((groups * cols, per * cz), jnp.float32),
            in_specs=[vmem] * (2 + narrow),
            out_specs=vmem,
            scratch_shapes=[outer],
            compiler_params=params,
            cost_estimate=cost,
            name="sums",
        )(left, *held[0], block_weights)
        return pl.pallas_call(
            functools.partial(pairs_kernel, part=1, seqs_total=seqs * narrow, **sizes),
            out_shape=out_shape,
            in_specs=[vmem] * (4 + narrow),
            out_specs=hbm,
            scratch_shapes=[
                outer, pltpu.VMEM(out_shape.shape, out_shape.dtype), pltpu.SemaphoreType.DMA((groups,))
            ],
            compiler_params=params,
            cost_estimate=cost,
            name="pairs",
        )(left, *held[1], block_weights, sums, shift)

    left = lax.all_to_all(left, "narrow", split_axis=0, concat_axis=0, tiled=True)
    every = lax.all_gather(rights[0][0], ("wide", "narrow"), axis=0, tiled=False)
    every = every.reshape(wide, narrow, minor * residues, LANES)
    every = jnp.take(every, lax.axis_index("narrow") ^ jnp.arange(narrow), axis=1)
    block = wide
    while block % 2 == 0 and block * residues > 192:
        block //= 2
    cols = block * residues
    return pl.pallas_call(
        functools.partial(
            pair_blocks_kernel, wides=block, parts=narrow, minor=minor, seqs_total=seqs * narrow
        ),
        grid=(wide // block,),
        in_specs=[
            pl.BlockSpec(left.shape, lambda b: (0, 0, 0)),
            pl.BlockSpec((block, narrow, minor * residues, LANES), lambda b: (b, 0, 0, 0)),
            pl.BlockSpec((hidden * LANES, per * cz), lambda b: (0, 0)),
            pl.BlockSpec((cz,), lambda b: (0,)),
        ],
        out_specs=pl.BlockSpec((own_rows, cols, cz), lambda b: (0, b, 0)),
        out_shape=out_shape,
        scratch_shapes=[pltpu.VMEM((groups * cols, hidden * LANES), jnp.bfloat16)],
        compiler_params=params,
        name="pairs",
    )(left, every, block_weights, shift)


def solution(mesh):
    in_specs = (P(("groups", "narrow"), "wide", None), P(), P(), P(), P(), P(), P(), P(), P())
    out_specs = P(("groups", "wide", "narrow"), None, None)
    return jax.shard_map(
        functools.partial(on_device, mesh.shape["wide"], mesh.shape["narrow"]),
        mesh=mesh,
        in_specs=in_specs,
        out_specs=out_specs,
        check_vma=False,
    )
```

time: 34.7 us -> 44.4 us (1.28)
  blocking collectives: 0 us -> 13.8 us
  waiting for transfers between devices: 9.8 us -> 4.83 us
  local copies, waits for them, and re-layouts: 0.96 us -> 5.07 us
  starting transfers between devices: 14.3 us -> 10.8 us
    all_to_all x0 -> x1, blocking collectives: none -> 13.8 us  [on_device(): lax.all_to_all(right, 'wide', split_axis=0, concat_axis=0, tiled=True)]
    ppermute x18 -> x6, starting transfers between devices: 14.3 us -> 4.14 us  [on_device(): lax.ppermute(c, 'narrow', [(i, i ^ bit) for i in range(narrow)])]
    ppermute x18 -> x6, waiting for transfers between devices: 9.8 us -> 0.02 us  [on_device(): lax.ppermute(c, 'narrow', [(i, i ^ bit) for i in range(narrow)])]
    all_to_all x0 -> x2, starting transfers between devices: none -> 6.67 us  [the longest x1 3.36 us: on_device(): lax.all_to_all(right, 'wide', split_axis=0, concat_axis=0, tiled=True)]
    all_to_all x0 -> x2, waiting for transfers between devices: none -> 4.81 us  [the longest x1 4.81 us: on_device(): lax.all_to_all(right, 'wide', split_axis=0, concat_axis=0, tiled=True)]
    unnamed x8, local copies, waits for them, and re-layouts: 0.96 us -> 5.07 us
    pallas_call x2 -> x3, Pallas kernels: 8.5 us -> 8.41 us  [the longest x1 3.66 us: on_device(): pl.pallas_call(functools.partial(features_kernel, halves=halves, pieces=p...]
  transfers between devices with their start and end apart: 18 -> 8, of which waited for: 4 -> 1; matrix products, arithmetic and copies ran while one was open for 0% -> 0% of each run, Pallas kernels for 3% -> 7%
where the time goes in v4:
time: 44.4 us; the launch traced here: 43.9 us
  blocking collectives  13.8 us (31%)
  starting transfers between devices  10.8 us (24%)
  Pallas kernels  9.29 us (21%)
  local copies, waits for them, and re-layouts  5.07 us (11%)
  waiting for transfers between devices  4.83 us (11%)
    all_to_all x1, blocking collectives, on_device(): lax.all_to_all(right, 'wide', split_axis=0, concat_axis=0, tiled=True)  13.8 us
    unnamed x8, local copies, waits for them, and re-layouts  5.07 us
    all_to_all x1, waiting for transfers between devices, on_device(): lax.all_to_all(right, 'wide', split_axis=0, concat_axis=0, tiled=True)  4.81 us
    ppermute x6, starting transfers between devices, on_device(): lax.ppermute(c, 'narrow', [(i, i ^ bit) for i in range(narrow)])  4.14 us
    pallas_call x1, Pallas kernels, on_device(): pl.pallas_call(functools.partial(features_kernel, halves=halves, pieces=p...  3.66 us
    all_to_all x1, starting transfers between devices, on_device(): lax.all_to_all(right, 'wide', split_axis=0, concat_axis=0, tiled=True)  3.36 us
    all_to_all x1, starting transfers between devices, on_device(): lax.all_to_all(left, 'narrow', split_axis=0, concat_axis=0, tiled=True)  3.3 us
    pallas_call x1, Pallas kernels, on_device(): pl.pallas_call(functools.partial(pairs_kernel, part=1, seqs_total=seqs *...  2.74 us
  transfers between devices with their start and end apart: 8, of which 1 were waited for; matrix products, arithmetic and copies ran while one was open for 0% of the time, Pallas kernels for 7%

profile of v4, /device:TPU:0, one launch (start us, length us, event | category | flops | bytes accessed | tf_op | source)
XLA Modules:
  0.0 43.9 jit_solution(11131396282551467567)
XLA Ops:
  0.0 3.7 %features.1 = (bf16[4,96,128]{2,1,0:T(8,128)(2,1)}, bf16[4,192,128]{2,1,0:T(8,128)(2,1)}, bf16[4,192,128]{2,1,0:T(8,128)(2,1)}) custom-call(bf16[32,48,256]{2,1,0:T(8,128)(2,1)} %x_hbm.1, f32[256]{0:T(256)} %gain_hbm.1, f32[256]{0:T(256)} %bias_hbm.1, bf16[32,256]{1,0:T(8,128)(2,1)} %bitcast.2, f32[32]{0:T(128)} %lb_hbm.1, bf16[32,256]{1,0:T(8,128)(2,1)} %bitcast.3, ...), custom_call_target="tpu_custom_call" | custom-call | tf_op jit(solution)/shard_map/features/pallas_call | solution.py:245
  3.7 13.8 %all_to_all.15.refs_0_ = bf16[4,192,128]{2,1,0:T(8,128)(2,1)S(1)} all-to-all(bf16[4,192,128]{2,1,0:T(8,128)(2,1)} %get-tuple-element.10), channel_id=1, replica_groups=mesh['groups'=2,'wide'=4,'narrow'=4] {'wide'}, dimensions={0} | all-to-all | bytes 393216 | tf_op jit(solution)/shard_map/all_to_all | solution.py:281
  17.5 3.4 %all-to-all-start.1 = ((bf16[4,192,128]{2,1,0:T(8,128)(2,1)}), bf16[4,192,128]{2,1,0:T(8,128)(2,1)S(1)}, u32[]{:S(2)}, u32[]{:S(2)}) async-start(bf16[4,192,128]{2,1,0:T(8,128)(2,1)} %get-tuple-element.9), calls=%async_computation.1 | async-start | bytes 393216 | tf_op jit(solution)/shard_map/all_to_all | solution.py:281
  20.9 1.6 %collective-permute-start.4 = (bf16[4,192,128]{2,1,0:T(8,128)(2,1)S(1)}, bf16[4,192,128]{2,1,0:T(8,128)(2,1)S(1)}, u32[]{:S(2)}, u32[]{:S(2)}) collective-permute-start(bf16[4,192,128]{2,1,0:T(8,128)(2,1)S(1)} %all_to_all.15.refs_0_), channel_id=1, source_target_pairs={{0,2},{1,3},{2,0},{3,1},{4,6},{5,7},{6,4},{7,5},{8,10},{9,11},{10,... | collective-permute-start | bytes 589832 | tf_op jit(solution)/shard_map/ppermute | solution.py:284
  22.4 4.8 %all-to-all-done.1.refs_0_ = bf16[4,192,128]{2,1,0:T(8,128)(2,1)S(1)} async-done(((bf16[4,192,128]{2,1,0:T(8,128)(2,1)}), bf16[4,192,128]{2,1,0:T(8,128)(2,1)S(1)}, u32[]{:S(2)}, u32[]{:S(2)}) %all-to-all-start.1) | async-done | bytes 196640 | tf_op jit(solution)/shard_map/all_to_all | solution.py:281
  27.2 1.5 %collective-permute-start.1 = (bf16[4,192,128]{2,1,0:T(8,128)(2,1)S(1)}, bf16[4,192,128]{2,1,0:T(8,128)(2,1)S(1)}, u32[]{:S(2)}, u32[]{:S(2)}) collective-permute-start(bf16[4,192,128]{2,1,0:T(8,128)(2,1)S(1)} %all-to-all-done.1.refs_0_), channel_id=1, source_target_pairs={{0,2},{1,3},{2,0},{3,1},{4,6},{5,7},{6,4},{7,5},{8,10},{9,11},{10,... | collective-permute-start | bytes 589832 | tf_op jit(solution)/shard_map/ppermute | solution.py:284
  28.7 0.0 collective-permute-start.3
  28.7 0.0 collective-permute-done.4.refs_2_
  28.7 0.5 %collective-permute-start.5 = (bf16[4,192,128]{2,1,0:T(8,128)(2,1)S(1)}, bf16[4,192,128]{2,1,0:T(8,128)(2,1)S(1)}, u32[]{:S(2)}, u32[]{:S(2)}) collective-permute-start(bf16[4,192,128]{2,1,0:T(8,128)(2,1)S(1)} %collective-permute-done.4.refs_2_), channel_id=1, source_target_pairs={{0,1},{1,0},{2,3},{3,2},{4,5},{5,4},{6,7},{7,6},{8,9},{9,8},{10,11... | collective-permute-start | bytes 589832 | tf_op jit(solution)/shard_map/ppermute | solution.py:284
  29.2 3.3 %all-to-all-start = ((bf16[4,96,128]{2,1,0:T(8,128)(2,1)}), bf16[4,96,128]{2,1,0:T(8,128)(2,1)S(1)}, u32[]{:S(2)}, u32[]{:S(2)}) async-start(bf16[4,96,128]{2,1,0:T(8,128)(2,1)} %get-tuple-element.8), calls=%async_computation | async-start | bytes 196608 | tf_op jit(solution)/shard_map/all_to_all | solution.py:288
  32.5 0.5 %collective-permute-start = (bf16[4,192,128]{2,1,0:T(8,128)(2,1)S(1)}, bf16[4,192,128]{2,1,0:T(8,128)(2,1)S(1)}, u32[]{:S(2)}, u32[]{:S(2)}) collective-permute-start(bf16[4,192,128]{2,1,0:T(8,128)(2,1)S(1)} %all-to-all-done.1.refs_0_), channel_id=1, source_target_pairs={{0,1},{1,0},{2,3},{3,2},{4,5},{5,4},{6,7},{7,6},{8,9},{9,8},{10,11... | collective-permute-start | bytes 589832 | tf_op jit(solution)/shard_map/ppermute | solution.py:284
  33.0 0.0 collective-permute-done.1.refs_2_
  33.0 0.1 collective-permute-start.2
  33.1 0.0 copy-start.2
  33.1 0.9 %copy-done.2 = bf16[1024,128]{1,0:T(8,128)(2,1)S(1)} copy-done((bf16[1024,128]{1,0:T(8,128)(2,1)S(1)}, bf16[1024,128]{1,0:T(8,128)(2,1)}, u32[]{:S(2)}) %copy-start.2) | copy-done | bytes 262168
  34.1 0.0 copy-start.3
  34.1 0.9 %block_weights.1.refs_4_ = bf16[4096,512]{1,0:T(8,128)(2,1)S(1)} custom-call(bf16[1024,128]{1,0:T(8,128)(2,1)S(1)} %copy-done.2), custom_call_target="tpu_custom_call" | custom-call | tf_op jit(solution)/shard_map/block_weights/pallas_call | solution.py:263
  35.0 0.0 copy-start
  35.0 1.9 %copy-done = bf16[4096,512]{1,0:T(8,128)(2,1)} copy-done((bf16[4096,512]{1,0:T(8,128)(2,1)}, bf16[4096,512]{1,0:T(8,128)(2,1)S(1)}, u32[]{:S(2)}) %copy-start) | copy-done | bytes 4194328
  36.9 0.0 all-to-all-done.left_ref
  36.9 0.0 collective-permute-done.3.refs_1_
  36.9 0.0 collective-permute-done.5.refs_3_
  36.9 0.0 copy-start.1
  36.9 2.2 %copy-done.1 = bf16[4096,512]{1,0:T(8,128)(2,1)S(1)} copy-done((bf16[4096,512]{1,0:T(8,128)(2,1)S(1)}, bf16[4096,512]{1,0:T(8,128)(2,1)}, u32[]{:S(2)}) %copy-start.1) | copy-done | bytes 4194328
  39.1 2.0 %sums.1.refs_5_ = f32[576,512]{1,0:T(8,128)S(1)} custom-call(bf16[4,96,128]{2,1,0:T(8,128)(2,1)S(1)} %all-to-all-done.left_ref, bf16[4,192,128]{2,1,0:T(8,128)(2,1)S(1)} %all_to_all.15.refs_0_, bf16[4,192,128]{2,1,0:T(8,128)(2,1)S(1)} %collective-permute-done.3.refs_1_, bf16[4,192,128]{2,1,0:T(8,128)(2,1)S(1)} %collective-permute-done.4.refs_2_, ...), custom_call_target="tpu_custom_call" | custom-call | flops 2000000000 | bytes 5000000 | tf_op jit(solution)/shard_map/sums/pallas_call | solution.py:293
  41.1 0.0 collective-permute-done.refs_1_
  41.1 0.0 collective-permute-done.2.refs_3_
  41.1 0.0 copy-done.3
  41.2 2.7 %pairs.1 = bf16[12,192,128]{2,1,0:T(8,128)(2,1)} custom-call(bf16[4,96,128]{2,1,0:T(8,128)(2,1)S(1)} %all-to-all-done.left_ref, bf16[4,192,128]{2,1,0:T(8,128)(2,1)S(1)} %all-to-all-done.1.refs_0_, bf16[4,192,128]{2,1,0:T(8,128)(2,1)S(1)} %collective-permute-done.refs_1_, bf16[4,192,128]{2,1,0:T(8,128)(2,1)S(1)} %collective-permute-done.1.refs_2_, ...), custom_call_target="tpu_custom_call" | custom-call | flops 2000000000 | bytes 5000000 | tf_op jit(solution)/shard_map/pairs/pallas_call | solution.py:303
Async XLA Ops:
  17.5 9.7 %all-to-all-start.1 = ((bf16[4,192,128]{2,1,0:T(8,128)(2,1)}), bf16[4,192,128]{2,1,0:T(8,128)(2,1)S(1)}, u32[]{:S(2)}, u32[]{:S(2)}) async-start(bf16[4,192,128]{2,1,0:T(8,128)(2,1)} %get-tuple-element.9), calls=%async_computation.1 | async-start | bytes 393216 | tf_op jit(solution)/shard_map/all_to_all | solution.py:281
  20.9 7.9 %collective-permute-start.4 = (bf16[4,192,128]{2,1,0:T(8,128)(2,1)S(1)}, bf16[4,192,128]{2,1,0:T(8,128)(2,1)S(1)}, u32[]{:S(2)}, u32[]{:S(2)}) collective-permute-start(bf16[4,192,128]{2,1,0:T(8,128)(2,1)S(1)} %all_to_all.15.refs_0_), channel_id=1, source_target_pairs={{0,2},{1,3},{2,0},{3,1},{4,6},{5,7},{6,4},{7,5},{8,10},{9,11},{10,... | collective-permute-start | bytes 589832 | tf_op jit(solution)/shard_map/ppermute | solution.py:284
  27.2 5.8 %collective-permute-start.1 = (bf16[4,192,128]{2,1,0:T(8,128)(2,1)S(1)}, bf16[4,192,128]{2,1,0:T(8,128)(2,1)S(1)}, u32[]{:S(2)}, u32[]{:S(2)}) collective-permute-start(bf16[4,192,128]{2,1,0:T(8,128)(2,1)S(1)} %all-to-all-done.1.refs_0_), channel_id=1, source_target_pairs={{0,2},{1,3},{2,0},{3,1},{4,6},{5,7},{6,4},{7,5},{8,10},{9,11},{10,... | collective-permute-start | bytes 589832 | tf_op jit(solution)/shard_map/ppermute | solution.py:284
  28.7 8.2 %collective-permute-start.3 = (bf16[4,192,128]{2,1,0:T(8,128)(2,1)S(1)}, bf16[4,192,128]{2,1,0:T(8,128)(2,1)S(1)}, u32[]{:S(2)}, u32[]{:S(2)}) collective-permute-start(bf16[4,192,128]{2,1,0:T(8,128)(2,1)S(1)} %all_to_all.15.refs_0_), channel_id=1, source_target_pairs={{0,1},{1,0},{2,3},{3,2},{4,5},{5,4},{6,7},{7,6},{8,9},{9,8},{10,11... | collective-permute-start | bytes 589832 | tf_op jit(solution)/shard_map/ppermute | solution.py:284
  28.7 8.2 %collective-permute-start.5 = (bf16[4,192,128]{2,1,0:T(8,128)(2,1)S(1)}, bf16[4,192,128]{2,1,0:T(8,128)(2,1)S(1)}, u32[]{:S(2)}, u32[]{:S(2)}) collective-permute-start(bf16[4,192,128]{2,1,0:T(8,128)(2,1)S(1)} %collective-permute-done.4.refs_2_), channel_id=1, source_target_pairs={{0,1},{1,0},{2,3},{3,2},{4,5},{5,4},{6,7},{7,6},{8,9},{9,8},{10,11... | collective-permute-start | bytes 589832 | tf_op jit(solution)/shard_map/ppermute | solution.py:284
  29.2 7.7 %all-to-all-start = ((bf16[4,96,128]{2,1,0:T(8,128)(2,1)}), bf16[4,96,128]{2,1,0:T(8,128)(2,1)S(1)}, u32[]{:S(2)}, u32[]{:S(2)}) async-start(bf16[4,96,128]{2,1,0:T(8,128)(2,1)} %get-tuple-element.8), calls=%async_computation | async-start | bytes 196608 | tf_op jit(solution)/shard_map/all_to_all | solution.py:288
  32.5 8.6 %collective-permute-start = (bf16[4,192,128]{2,1,0:T(8,128)(2,1)S(1)}, bf16[4,192,128]{2,1,0:T(8,128)(2,1)S(1)}, u32[]{:S(2)}, u32[]{:S(2)}) collective-permute-start(bf16[4,192,128]{2,1,0:T(8,128)(2,1)S(1)} %all-to-all-done.1.refs_0_), channel_id=1, source_target_pairs={{0,1},{1,0},{2,3},{3,2},{4,5},{5,4},{6,7},{7,6},{8,9},{9,8},{10,11... | collective-permute-start | bytes 589832 | tf_op jit(solution)/shard_map/ppermute | solution.py:284
  33.0 8.1 %collective-permute-start.2 = (bf16[4,192,128]{2,1,0:T(8,128)(2,1)S(1)}, bf16[4,192,128]{2,1,0:T(8,128)(2,1)S(1)}, u32[]{:S(2)}, u32[]{:S(2)}) collective-permute-start(bf16[4,192,128]{2,1,0:T(8,128)(2,1)S(1)} %collective-permute-done.1.refs_2_), channel_id=1, source_target_pairs={{0,1},{1,0},{2,3},{3,2},{4,5},{5,4},{6,7},{7,6},{8,9},{9,8},{10,11... | collective-permute-start | bytes 589832 | tf_op jit(solution)/shard_map/ppermute | solution.py:284
  33.1 0.9 %copy-start.2 = (bf16[1024,128]{1,0:T(8,128)(2,1)S(1)}, bf16[1024,128]{1,0:T(8,128)(2,1)}, u32[]{:S(2)}) copy-start(bf16[1024,128]{1,0:T(8,128)(2,1)} %w_hbm.1) | copy-start | bytes 786436
  34.1 7.1 %copy-start.3 = (f32[128]{0:T(128)S(1)}, f32[128]{0:T(128)}, u32[]{:S(2)}) copy-start(f32[128]{0:T(128)} %refs_6_.1) | copy-start | bytes 1540
  35.0 1.9 %copy-start = (bf16[4096,512]{1,0:T(8,128)(2,1)}, bf16[4096,512]{1,0:T(8,128)(2,1)S(1)}, u32[]{:S(2)}) copy-start(bf16[4096,512]{1,0:T(8,128)(2,1)S(1)} %block_weights.1.refs_4_) | copy-start | bytes 12582916
  36.9 2.2 %copy-start.1 = (bf16[4096,512]{1,0:T(8,128)(2,1)S(1)}, bf16[4096,512]{1,0:T(8,128)(2,1)}, u32[]{:S(2)}) copy-start(bf16[4096,512]{1,0:T(8,128)(2,1)} %copy-done) | copy-start | bytes 12582916

commit v5 on v3

--- a/solution.py
+++ b/solution.py
@@ -133,7 +133,8 @@
             at += rows.shape[0]
 
 
-def weights_kernel(w_hbm, wide_ref, w_ref, wf_ref, sem, *, parts, hidden):
+def weights_kernel(w_hbm, after_ref, wide_ref, w_ref, wf_ref, sem, *, parts, hidden):
+    del after_ref
     copy = pltpu.make_async_copy(w_hbm, w_ref, sem)
     copy.start()
     cz = w_ref.shape[1]
@@ -147,6 +148,13 @@
         rows = wf_ref[pl.ds(e ^ (own * minor), hidden, stride=hidden), :].astype(jnp.bfloat16)
         for k in range(per):
             wide_ref[pl.ds(e * LANES + k * hidden, hidden), k * cz : (k + 1) * cz] = rows
+
+
+def pack_kernel(first_ref, second_ref, after_ref, out_ref):
+    del after_ref
+    count = first_ref.shape[0]
+    out_ref[:count] = first_ref[...]
+    out_ref[count:] = second_ref[...]
 
 
 def pair_rows(left_of, right_of, wide_ref, shift_ref, outer_ref, store, *, wides, parts, minor, seqs_total):
@@ -187,29 +195,40 @@
             store(g * per + k, pair * (1.0 / seqs_total) + shift)
 
 
-def pair_kernel(*refs, places, block, **sizes):
-    wide_ref, shift_ref = refs[-7:-5] if block else refs[-6:-4]
-    out_hbm, outer_ref, done_ref, sem = refs[-4:]
+def pair_kernel(*refs, places, blocks, **sizes):
+    out_hbm, outer_ref, done_ref, sems = refs[-4:]
+    wide_ref, shift_ref = refs[sizes.pop("operands") : ][:2]
     parts, minor = sizes["parts"], sizes["minor"]
-    residues = done_ref.shape[1]
-    count = done_ref.shape[0] * minor * parts // LANES * (LANES // parts)
+    own_rows, cols, _ = done_ref.shape
+    residues = cols // len(blocks)
+    left_count = own_rows * minor
+    right_count = minor * residues
 
     def left_of(m):
         ref, at = places[m][:2]
-        return refs[ref][at : at + count, :]
+        return refs[ref][at : at + left_count, :]
 
     def right_of(d, m):
         ref, at = places[m][2:]
-        return refs[ref][at : at + minor * residues, :]
+        return refs[ref][at + d * right_count : at + (d + 1) * right_count, :]
 
     def store(row, pair):
         done_ref[row] = pair.astype(done_ref.dtype)
 
-    pair_rows(left_of, right_of, wide_ref, shift_ref, outer_ref, store, wides=1, **sizes)
-    at = pl.multiple_of((lax.axis_index("wide") ^ block) * residues, 16)
-    copy = pltpu.make_async_copy(done_ref, out_hbm.at[:, pl.ds(at, residues), :], sem)
-    copy.start()
-    copy.wait()
+    pair_rows(left_of, right_of, wide_ref, shift_ref, outer_ref, store, wides=len(blocks), **sizes)
+    copies = []
+    for d, block in enumerate(blocks):
+        at = pl.multiple_of((lax.axis_index("wide") ^ block) * residues, 16)
+        copies.append(
+            pltpu.make_async_copy(
+                done_ref.at[:, pl.ds(d * residues, residues), :],
+                out_hbm.at[:, pl.ds(at, residues), :],
+                sems.at[d],
+            )
+        )
+        copies[-1].start()
+    for copy in copies:
+        copy.wait()
 
 
 def pair_blocks_kernel(*refs, wides, parts, minor, **sizes):
@@ -270,7 +289,7 @@
     block_weights = pl.pallas_call(
         functools.partial(weights_kernel, parts=narrow, hidden=hidden),
         out_shape=jax.ShapeDtypeStruct((hidden * LANES, per * cz), jnp.bfloat16),
-        in_specs=[hbm],
+        in_specs=[hbm, pl.BlockSpec(memory_space=pl.ANY)],
         out_specs=vmem,
         scratch_shapes=[
             pltpu.VMEM(w.shape, w.dtype),
@@ -279,7 +298,7 @@
         ],
         compiler_params=params,
         name="block_weights",
-    )(w)
+    )(w, made[0])
 
     def across(a, m):
         return lax.ppermute(a, "narrow", [(i, i ^ m) for i in range(narrow)])
@@ -319,29 +338,41 @@
 
 def pairs_by_block(made, across, along, block_weights, shift, out_shape, residues, sizes, params):
     left_own, right, to_core, to_chip = made
-    far = {d: along(right, d) for d in (2, 3, 1)}
     left_count, right_count = left_own.shape[0], right.shape[0]
+    hbm = pl.BlockSpec(memory_space=pltpu.HBM)
+    vmem = pl.BlockSpec(memory_space=pltpu.VMEM)
+    anywhere = pl.BlockSpec(memory_space=pl.ANY)
+
+    far = along(right, 2)
+    near = along(right, 1)
+    last = along(far, 1)
     chip = across(to_chip, 2)
     core = across(to_core, 1)
     both = across(chip, 1)
-
-    hbm = pl.BlockSpec(memory_space=pltpu.HBM)
-    vmem = pl.BlockSpec(memory_space=pltpu.VMEM)
-    own_rows, cols, cz = out_shape.shape
+    middle = pl.pallas_call(
+        pack_kernel,
+        out_shape=jax.ShapeDtypeStruct((2 * right_count, LANES), jnp.bfloat16),
+        in_specs=[vmem, vmem, anywhere],
+        out_specs=vmem,
+        compiler_params=params,
+        name="pack",
+    )(near, far, block_weights)
+
+    own_rows, _, cz = out_shape.shape
     hidden = sizes["parts"] * sizes["minor"]
+    groups = own_rows * hidden // LANES
     out = None
-    for d in range(cols // residues):
+    for blocks, chunk in (((0,), right), ((1, 2), middle), ((3,), last)):
         operands = [left_own, core, chip, both]
-        if d == 0:
+        if chunk is right:
             operands.append(right)
             rights = ((4, 0), (1, left_count), (2, 2 * left_count), (3, 2 * left_count))
         else:
-            other = across(far[d], 2)
-            operands += [far[d], across(far[d], 1), other, across(other, 1)]
+            other = across(chunk, 2)
+            operands += [chunk, across(chunk, 1), other, across(other, 1)]
             rights = tuple((4 + m, 0) for m in range(4))
-        places = tuple(
-            (m, left_count if m == 3 else 0) + rights[m] for m in range(4)
-        )
+        places = tuple((m, left_count if m == 3 else 0) + rights[m] for m in range(4))
+        count = len(operands)
         operands += [block_weights, shift]
         specs = [vmem] * len(operands)
         aliases = {}
@@ -349,20 +380,23 @@
             aliases = {len(operands): 0}
             operands.append(out)
             specs.append(hbm)
+        cols = len(blocks) * residues
         out = pl.pallas_call(
-            functools.partial(pair_kernel, places=places, block=d, **sizes),
+            functools.partial(pair_kernel, places=places, blocks=blocks, operands=count, **sizes),
             out_shape=out_shape,
             in_specs=specs,
             out_specs=hbm,
             input_output_aliases=aliases,
             scratch_shapes=[
-                pltpu.VMEM((own_rows * hidden // LANES * residues, hidden * LANES), jnp.bfloat16),
-                pltpu.VMEM((own_rows, residues, cz), jnp.bfloat16),
-                pltpu.SemaphoreType.DMA,
+                pltpu.VMEM((groups * cols, hidden * LANES), jnp.bfloat16),
+                pltpu.VMEM((own_rows, cols, cz), jnp.bfloat16),
+                pltpu.SemaphoreType.DMA((len(blocks),)),
             ],
             compiler_params=params,
-            cost_estimate=pl.CostEstimate(flops=1_500_000_000, bytes_accessed=5_000_000, transcendentals=0),
-            name=f"pairs_{d}",
+            cost_estimate=pl.CostEstimate(
+                flops=1_500_000_000 * len(blocks), bytes_accessed=5_000_000, transcendentals=0
+            ),
+            name=f"pairs_{blocks[0]}",
         )(*operands)
     return out
 

time: 35.4 us -> 30.9 us (0.87)
  waiting for transfers between devices: 8.49 us -> 5.99 us
  starting transfers between devices: 13.7 us -> 11.8 us
  Pallas kernels: 11.9 us -> 11 us
  local copies, waits for them, and re-layouts: 0.96 us -> 1.7 us
    ppermute x12 -> x9, starting transfers between devices: 7.92 us -> 4.67 us  [across(): return lax.ppermute(a, 'narrow', [(i, i ^ m) for i in range(narrow)])]
    ppermute x12 -> x9, waiting for transfers between devices: 5.06 us -> 3.33 us  [across(): return lax.ppermute(a, 'narrow', [(i, i ^ m) for i in range(narrow)])]
    ppermute x3, starting transfers between devices: 5.76 us -> 7.12 us  [along(): return lax.ppermute(a, 'wide', [(i, i ^ d) for i in range(wide)])]
    pallas_call x4, Pallas kernels: 7.35 us -> 6.52 us  [the longest x3 6.5 us: pairs_by_block(): pl.pallas_call(functools.partial(pair_kernel, places=places, blocks=block...]
    ppermute x3, waiting for transfers between devices: 3.44 us -> 2.66 us  [along(): return lax.ppermute(a, 'wide', [(i, i ^ d) for i in range(wide)])]
    unnamed x8 -> x10, local copies, waits for them, and re-layouts: 0.96 us -> 1.7 us
  transfers between devices with their start and end apart: 15 -> 12, of which waited for: 4 -> 2; matrix products, arithmetic and copies ran while one was open for 0% -> 0% of each run, Pallas kernels for 18% -> 18%
where the time goes in v5:
time: 30.9 us; the launch traced here: 30.6 us
  starting transfers between devices  11.8 us (38%)
  Pallas kernels  11 us (36%)
  waiting for transfers between devices  5.99 us (19%)
  local copies, waits for them, and re-layouts  1.7 us (6%)
    ppermute x3, starting transfers between devices, along(): return lax.ppermute(a, 'wide', [(i, i ^ d) for i in range(wide)])  7.12 us
    pallas_call x3, Pallas kernels, pairs_by_block(): pl.pallas_call(functools.partial(pair_kernel, places=places, blocks=block...  6.5 us
    ppermute x9, starting transfers between devices, across(): return lax.ppermute(a, 'narrow', [(i, i ^ m) for i in range(narrow)])  4.67 us
    pallas_call x1, Pallas kernels, on_device(): pl.pallas_call(functools.partial(features_kernel, packs=packs, parts=narr...  3.65 us
    ppermute x9, waiting for transfers between devices, across(): return lax.ppermute(a, 'narrow', [(i, i ^ m) for i in range(narrow)])  3.33 us
    ppermute x3, waiting for transfers between devices, along(): return lax.ppermute(a, 'wide', [(i, i ^ d) for i in range(wide)])  2.66 us
    unnamed x10, local copies, waits for them, and re-layouts  1.7 us
    pallas_call x1, Pallas kernels, on_device(): pl.pallas_call(functools.partial(weights_kernel, parts=narrow, hidden=hid...  0.88 us
  transfers between devices with their start and end apart: 12, of which 2 were waited for; matrix products, arithmetic and copies ran while one was open for 0% of the time, Pallas kernels for 18%

profile of v5, /device:TPU:0, one launch (start us, length us, event | category | flops | bytes accessed | tf_op | source)
XLA Modules:
  0.0 30.6 jit_solution(16284754431501379768)
XLA Ops:
  0.0 3.6 %features.1 = (bf16[96,128]{1,0:T(8,128)(2,1)}, bf16[384,128]{1,0:T(8,128)(2,1)}, bf16[480,128]{1,0:T(8,128)(2,1)}, bf16[576,128]{1,0:T(8,128)(2,1)}) custom-call(bf16[32,48,256]{2,1,0:T(8,128)(2,1)} %x_hbm.1, f32[256]{0:T(256)} %gain_hbm.1, f32[256]{0:T(256)} %bias_hbm.1, bf16[32,256]{1,0:T(8,128)(2,1)} %bitcast.2, f32[32]{0:T(128)} %lb_hbm.1, ...), custom_call_target="tpu_custom_call" | custom-call | tf_op jit(solution)/shard_map/features/pallas_call | solution.py:266
  3.7 4.1 %collective-permute-start.3 = (bf16[384,128]{1,0:T(8,128)(2,1)}, bf16[384,128]{1,0:T(8,128)(2,1)S(1)}, u32[]{:S(2)}, u32[]{:S(2)}) collective-permute-start(bf16[384,128]{1,0:T(8,128)(2,1)} %get-tuple-element.12.refs_4_), channel_id=1, source_target_pairs={{0,8},{4,12},{8,0},{12,4},{1,9},{5,13},{9,1},{13,5},{2,10},{6,14},... | collective-permute-start | bytes 294920 | tf_op jit(solution)/shard_map/ppermute | solution.py:307
  7.8 1.6 %collective-permute-start.8 = (bf16[384,128]{1,0:T(8,128)(2,1)}, bf16[384,128]{1,0:T(8,128)(2,1)S(1)}, u32[]{:S(2)}, u32[]{:S(2)}) collective-permute-start(bf16[384,128]{1,0:T(8,128)(2,1)} %get-tuple-element.12.refs_4_), channel_id=1, source_target_pairs={{0,4},{4,0},{8,12},{12,8},{1,5},{5,1},{9,13},{13,9},{2,6},{6,2},{1... | collective-permute-start | bytes 294920 | tf_op jit(solution)/shard_map/ppermute | solution.py:307
  9.3 1.5 %collective-permute-start.1 = (bf16[576,128]{1,0:T(8,128)(2,1)}, bf16[576,128]{1,0:T(8,128)(2,1)S(1)}, u32[]{:S(2)}, u32[]{:S(2)}) collective-permute-start(bf16[576,128]{1,0:T(8,128)(2,1)} %get-tuple-element.11), channel_id=1, source_target_pairs={{0,2},{1,3},{2,0},{3,1},{4,6},{5,7},{6,4},{7,5},{8,10},{9,11},{10,... | collective-permute-start | bytes 442376 | tf_op jit(solution)/shard_map/ppermute | solution.py:304
  10.8 0.0 copy-start
  10.8 0.9 %copy-done = bf16[1024,128]{1,0:T(8,128)(2,1)S(1)} copy-done((bf16[1024,128]{1,0:T(8,128)(2,1)S(1)}, bf16[1024,128]{1,0:T(8,128)(2,1)}, u32[]{:S(2)}) %copy-start) | copy-done | bytes 262168
  11.8 0.0 copy-start.1
  11.8 0.7 %copy-done.1 = bf16[96,128]{1,0:T(8,128)(2,1)S(1)} copy-done((bf16[96,128]{1,0:T(8,128)(2,1)S(1)}, bf16[96,128]{1,0:T(8,128)(2,1)}, u32[]{:S(2)}) %copy-start.1) | copy-done | bytes 24600
  12.5 0.0 copy-start.4
  12.5 0.0 copy-start.2
  12.5 0.0 copy-start.3
  12.5 0.9 %block_weights.1.after_ref.refs_5_.refs_8_ = bf16[4096,512]{1,0:T(8,128)(2,1)S(1)} custom-call(bf16[1024,128]{1,0:T(8,128)(2,1)S(1)} %copy-done, bf16[96,128]{1,0:T(8,128)(2,1)S(1)} %copy-done.1), custom_call_target="tpu_custom_call" | custom-call | tf_op jit(solution)/shard_map/block_weights/pallas_call | solution.py:289
  13.4 0.0 collective-permute-done.3.second_ref
  13.4 0.0 collective-permute-done.8.first_ref
  13.5 1.4 %collective-permute-start.10 = (bf16[768,128]{1,0:T(8,128)(2,1)S(1)}, bf16[768,128]{1,0:T(8,128)(2,1)S(1)}, u32[]{:S(2)}, u32[]{:S(2)}) collective-permute-start(bf16[768,128]{1,0:T(8,128)(2,1)S(1)} %pack.1.refs_4_), channel_id=1, source_target_pairs={{0,2},{1,3},{2,0},{3,1},{4,6},{5,7},{6,4},{7,5},{8,10},{9,11},{10,... | collective-permute-start | bytes 589832 | tf_op jit(solution)/shard_map/ppermute | solution.py:304
  14.8 1.4 %collective-permute-start.4 = (bf16[384,128]{1,0:T(8,128)(2,1)S(1)}, bf16[384,128]{1,0:T(8,128)(2,1)S(1)}, u32[]{:S(2)}, u32[]{:S(2)}) collective-permute-start(bf16[384,128]{1,0:T(8,128)(2,1)S(1)} %collective-permute-done.3.second_ref), channel_id=1, source_target_pairs={{0,4},{4,0},{8,12},{12,8},{1,5},{5,1},{9,13},{13,9},{2,6},{6,2},{1... | collective-permute-start | bytes 294920 | tf_op jit(solution)/shard_map/ppermute | solution.py:307
  16.3 0.0 collective-permute-done.1.refs_2_
  16.3 0.0 collective-permute-start.2
  16.3 0.0 copy-done.4
  16.3 0.5 %collective-permute-start = (bf16[480,128]{1,0:T(8,128)(2,1)S(1)}, bf16[480,128]{1,0:T(8,128)(2,1)S(1)}, u32[]{:S(2)}, u32[]{:S(2)}) collective-permute-start(bf16[480,128]{1,0:T(8,128)(2,1)S(1)} %copy-done.4), channel_id=1, source_target_pairs={{0,1},{1,0},{2,3},{3,2},{4,5},{5,4},{6,7},{7,6},{8,9},{9,8},{10,11... | collective-permute-start | bytes 368648 | tf_op jit(solution)/shard_map/ppermute | solution.py:304
  16.8 2.7 %collective-permute-done.4.refs_4_ = bf16[384,128]{1,0:T(8,128)(2,1)S(1)} collective-permute-done((bf16[384,128]{1,0:T(8,128)(2,1)S(1)}, bf16[384,128]{1,0:T(8,128)(2,1)S(1)}, u32[]{:S(2)}, u32[]{:S(2)}) %collective-permute-start.4) | collective-permute-done | bytes 98336 | tf_op jit(solution)/shard_map/ppermute | solution.py:307
  19.4 0.7 %collective-permute-start.6 = (bf16[384,128]{1,0:T(8,128)(2,1)S(1)}, bf16[384,128]{1,0:T(8,128)(2,1)S(1)}, u32[]{:S(2)}, u32[]{:S(2)}) collective-permute-start(bf16[384,128]{1,0:T(8,128)(2,1)S(1)} %collective-permute-done.4.refs_4_), channel_id=1, source_target_pairs={{0,2},{1,3},{2,0},{3,1},{4,6},{5,7},{6,4},{7,5},{8,10},{9,11},{10,... | collective-permute-start | bytes 294920 | tf_op jit(solution)/shard_map/ppermute | solution.py:304
  20.2 0.0 collective-permute-start.9
  20.2 0.0 collective-permute-done.10.refs_6_
  20.2 0.5 %collective-permute-start.11 = (bf16[768,128]{1,0:T(8,128)(2,1)S(1)}, bf16[768,128]{1,0:T(8,128)(2,1)S(1)}, u32[]{:S(2)}, u32[]{:S(2)}) collective-permute-start(bf16[768,128]{1,0:T(8,128)(2,1)S(1)} %collective-permute-done.10.refs_6_), channel_id=1, source_target_pairs={{0,1},{1,0},{2,3},{3,2},{4,5},{5,4},{6,7},{7,6},{8,9},{9,8},{10,11... | collective-permute-start | bytes 589832 | tf_op jit(solution)/shard_map/ppermute | solution.py:304
  20.7 0.0 collective-permute-done.refs_1_
  20.7 0.1 collective-permute-start.5
  20.8 3.3 %collective-permute-done.6.refs_6_ = bf16[384,128]{1,0:T(8,128)(2,1)S(1)} collective-permute-done((bf16[384,128]{1,0:T(8,128)(2,1)S(1)}, bf16[384,128]{1,0:T(8,128)(2,1)S(1)}, u32[]{:S(2)}, u32[]{:S(2)}) %collective-permute-start.6) | collective-permute-done | bytes 98336 | tf_op jit(solution)/shard_map/ppermute | solution.py:304
  24.1 0.0 collective-permute-start.7
  24.1 0.0 collective-permute-done.2.refs_3_
  24.1 0.0 copy-done.2
  24.1 0.0 copy-done.3
  24.1 1.8 %pairs_0.1.refs_10_ = bf16[12,192,128]{2,1,0:T(8,128)(2,1)} custom-call(bf16[96,128]{1,0:T(8,128)(2,1)S(1)} %copy-done.1, bf16[480,128]{1,0:T(8,128)(2,1)S(1)} %collective-permute-done.refs_1_, bf16[576,128]{1,0:T(8,128)(2,1)S(1)} %collective-permute-done.1.refs_2_, bf16[576,128]{1,0:T(8,128)(2,1)S(1)} %collective-permute-done.2.refs_3_, ...), custom_call_target="tpu_custom_call" | custom-call | flops 1500000000 | bytes 5000000 | tf_op jit(solution)/shard_map/pairs_0/pallas_call | solution.py:384
  25.9 0.0 collective-permute-done.9.refs_5_
  25.9 0.0 collective-permute-done.11.refs_7_
  25.9 2.8 %pairs_1.1.refs_10_ = bf16[12,192,128]{2,1,0:T(8,128)(2,1)} custom-call(bf16[96,128]{1,0:T(8,128)(2,1)S(1)} %copy-done.1, bf16[480,128]{1,0:T(8,128)(2,1)S(1)} %collective-permute-done.refs_1_, bf16[576,128]{1,0:T(8,128)(2,1)S(1)} %collective-permute-done.1.refs_2_, ...), custom_call_target="tpu_custom_call", output_to_operand_aliasing={{}: (10, {})} | custom-call | flops 3000000000 | bytes 5000000 | tf_op jit(solution)/shard_map/pairs_1/pallas_call | solution.py:384
  28.8 0.0 collective-permute-done.5.refs_5_
  28.8 0.0 collective-permute-done.7.refs_7_
  28.8 1.8 %pairs_3.1 = bf16[12,192,128]{2,1,0:T(8,128)(2,1)} custom-call(bf16[96,128]{1,0:T(8,128)(2,1)S(1)} %copy-done.1, bf16[480,128]{1,0:T(8,128)(2,1)S(1)} %collective-permute-done.refs_1_, bf16[576,128]{1,0:T(8,128)(2,1)S(1)} %collective-permute-done.1.refs_2_, bf16[576,128]{1,0:T(8,128)(2,1)S(1)} %collective-permute-done.2.refs_3_, ...), custom_call_target="tpu_custom_call", output_to_operand_aliasing={{}: (10, {})} | custom-call | flops 1500000000 | bytes 5000000 | tf_op jit(solution)/shard_map/pairs_3/pallas_call | solution.py:384
  (1 shorter events, 0.0 us)
Async XLA Ops:
  3.7 9.8 %collective-permute-start.3 = (bf16[384,128]{1,0:T(8,128)(2,1)}, bf16[384,128]{1,0:T(8,128)(2,1)S(1)}, u32[]{:S(2)}, u32[]{:S(2)}) collective-permute-start(bf16[384,128]{1,0:T(8,128)(2,1)} %get-tuple-element.12.refs_4_), channel_id=1, source_target_pairs={{0,8},{4,12},{8,0},{12,4},{1,9},{5,13},{9,1},{13,5},{2,10},{6,14},... | collective-permute-start | bytes 294920 | tf_op jit(solution)/shard_map/ppermute | solution.py:307
  7.8 5.7 %collective-permute-start.8 = (bf16[384,128]{1,0:T(8,128)(2,1)}, bf16[384,128]{1,0:T(8,128)(2,1)S(1)}, u32[]{:S(2)}, u32[]{:S(2)}) collective-permute-start(bf16[384,128]{1,0:T(8,128)(2,1)} %get-tuple-element.12.refs_4_), channel_id=1, source_target_pairs={{0,4},{4,0},{8,12},{12,8},{1,5},{5,1},{9,13},{13,9},{2,6},{6,2},{1... | collective-permute-start | bytes 294920 | tf_op jit(solution)/shard_map/ppermute | solution.py:307
  9.3 6.9 %collective-permute-start.1 = (bf16[576,128]{1,0:T(8,128)(2,1)}, bf16[576,128]{1,0:T(8,128)(2,1)S(1)}, u32[]{:S(2)}, u32[]{:S(2)}) collective-permute-start(bf16[576,128]{1,0:T(8,128)(2,1)} %get-tuple-element.11), channel_id=1, source_target_pairs={{0,2},{1,3},{2,0},{3,1},{4,6},{5,7},{6,4},{7,5},{8,10},{9,11},{10,... | collective-permute-start | bytes 442376 | tf_op jit(solution)/shard_map/ppermute | solution.py:304
  10.8 0.9 %copy-start = (bf16[1024,128]{1,0:T(8,128)(2,1)S(1)}, bf16[1024,128]{1,0:T(8,128)(2,1)}, u32[]{:S(2)}) copy-start(bf16[1024,128]{1,0:T(8,128)(2,1)} %w_hbm.1) | copy-start | bytes 786436
  11.8 0.7 %copy-start.1 = (bf16[96,128]{1,0:T(8,128)(2,1)S(1)}, bf16[96,128]{1,0:T(8,128)(2,1)}, u32[]{:S(2)}) copy-start(bf16[96,128]{1,0:T(8,128)(2,1)} %get-tuple-element.9.after_ref.refs_0_) | copy-start | bytes 73732
  12.5 3.8 %copy-start.4 = (bf16[480,128]{1,0:T(8,128)(2,1)S(1)}, bf16[480,128]{1,0:T(8,128)(2,1)}, u32[]{:S(2)}) copy-start(bf16[480,128]{1,0:T(8,128)(2,1)} %get-tuple-element.10) | copy-start | bytes 368644
  12.5 11.6 %copy-start.2 = (f32[128]{0:T(128)S(1)}, f32[128]{0:T(128)}, u32[]{:S(2)}) copy-start(f32[128]{0:T(128)} %refs_9_.3) | copy-start | bytes 1540
  12.5 11.6 %copy-start.3 = (bf16[384,128]{1,0:T(8,128)(2,1)S(1)}, bf16[384,128]{1,0:T(8,128)(2,1)}, u32[]{:S(2)}) copy-start(bf16[384,128]{1,0:T(8,128)(2,1)} %get-tuple-element.12.refs_4_) | copy-start | bytes 294916
  13.5 6.7 %collective-permute-start.10 = (bf16[768,128]{1,0:T(8,128)(2,1)S(1)}, bf16[768,128]{1,0:T(8,128)(2,1)S(1)}, u32[]{:S(2)}, u32[]{:S(2)}) collective-permute-start(bf16[768,128]{1,0:T(8,128)(2,1)S(1)} %pack.1.refs_4_), channel_id=1, source_target_pairs={{0,2},{1,3},{2,0},{3,1},{4,6},{5,7},{6,4},{7,5},{8,10},{9,11},{10,... | collective-permute-start | bytes 589832 | tf_op jit(solution)/shard_map/ppermute | solution.py:304
  14.8 4.6 %collective-permute-start.4 = (bf16[384,128]{1,0:T(8,128)(2,1)S(1)}, bf16[384,128]{1,0:T(8,128)(2,1)S(1)}, u32[]{:S(2)}, u32[]{:S(2)}) collective-permute-start(bf16[384,128]{1,0:T(8,128)(2,1)S(1)} %collective-permute-done.3.second_ref), channel_id=1, source_target_pairs={{0,4},{4,0},{8,12},{12,8},{1,5},{5,1},{9,13},{13,9},{2,6},{6,2},{1... | collective-permute-start | bytes 294920 | tf_op jit(solution)/shard_map/ppermute | solution.py:307
  16.3 7.8 %collective-permute-start.2 = (bf16[576,128]{1,0:T(8,128)(2,1)S(1)}, bf16[576,128]{1,0:T(8,128)(2,1)S(1)}, u32[]{:S(2)}, u32[]{:S(2)}) collective-permute-start(bf16[576,128]{1,0:T(8,128)(2,1)S(1)} %collective-permute-done.1.refs_2_), channel_id=1, source_target_pairs={{0,1},{1,0},{2,3},{3,2},{4,5},{5,4},{6,7},{7,6},{8,9},{9,8},{10,11... | collective-permute-start | bytes 442376 | tf_op jit(solution)/shard_map/ppermute | solution.py:304
  16.3 4.4 %collective-permute-start = (bf16[480,128]{1,0:T(8,128)(2,1)S(1)}, bf16[480,128]{1,0:T(8,128)(2,1)S(1)}, u32[]{:S(2)}, u32[]{:S(2)}) collective-permute-start(bf16[480,128]{1,0:T(8,128)(2,1)S(1)} %copy-done.4), channel_id=1, source_target_pairs={{0,1},{1,0},{2,3},{3,2},{4,5},{5,4},{6,7},{7,6},{8,9},{9,8},{10,11... | collective-permute-start | bytes 368648 | tf_op jit(solution)/shard_map/ppermute | solution.py:304
  19.4 4.6 %collective-permute-start.6 = (bf16[384,128]{1,0:T(8,128)(2,1)S(1)}, bf16[384,128]{1,0:T(8,128)(2,1)S(1)}, u32[]{:S(2)}, u32[]{:S(2)}) collective-permute-start(bf16[384,128]{1,0:T(8,128)(2,1)S(1)} %collective-permute-done.4.refs_4_), channel_id=1, source_target_pairs={{0,2},{1,3},{2,0},{3,1},{4,6},{5,7},{6,4},{7,5},{8,10},{9,11},{10,... | collective-permute-start | bytes 294920 | tf_op jit(solution)/shard_map/ppermute | solution.py:304
  20.2 5.8 %collective-permute-start.9 = (bf16[768,128]{1,0:T(8,128)(2,1)S(1)}, bf16[768,128]{1,0:T(8,128)(2,1)S(1)}, u32[]{:S(2)}, u32[]{:S(2)}) collective-permute-start(bf16[768,128]{1,0:T(8,128)(2,1)S(1)} %pack.1.refs_4_), channel_id=1, source_target_pairs={{0,1},{1,0},{2,3},{3,2},{4,5},{5,4},{6,7},{7,6},{8,9},{9,8},{10,11... | collective-permute-start | bytes 589832 | tf_op jit(solution)/shard_map/ppermute | solution.py:304
  20.2 5.8 %collective-permute-start.11 = (bf16[768,128]{1,0:T(8,128)(2,1)S(1)}, bf16[768,128]{1,0:T(8,128)(2,1)S(1)}, u32[]{:S(2)}, u32[]{:S(2)}) collective-permute-start(bf16[768,128]{1,0:T(8,128)(2,1)S(1)} %collective-permute-done.10.refs_6_), channel_id=1, source_target_pairs={{0,1},{1,0},{2,3},{3,2},{4,5},{5,4},{6,7},{7,6},{8,9},{9,8},{10,11... | collective-permute-start | bytes 589832 | tf_op jit(solution)/shard_map/ppermute | solution.py:304
  20.7 8.1 %collective-permute-start.5 = (bf16[384,128]{1,0:T(8,128)(2,1)S(1)}, bf16[384,128]{1,0:T(8,128)(2,1)S(1)}, u32[]{:S(2)}, u32[]{:S(2)}) collective-permute-start(bf16[384,128]{1,0:T(8,128)(2,1)S(1)} %collective-permute-done.4.refs_4_), channel_id=1, source_target_pairs={{0,1},{1,0},{2,3},{3,2},{4,5},{5,4},{6,7},{7,6},{8,9},{9,8},{10,11... | collective-permute-start | bytes 294920 | tf_op jit(solution)/shard_map/ppermute | solution.py:304
  24.1 4.7 %collective-permute-start.7 = (bf16[384,128]{1,0:T(8,128)(2,1)S(1)}, bf16[384,128]{1,0:T(8,128)(2,1)S(1)}, u32[]{:S(2)}, u32[]{:S(2)}) collective-permute-start(bf16[384,128]{1,0:T(8,128)(2,1)S(1)} %collective-permute-done.6.refs_6_), channel_id=1, source_target_pairs={{0,1},{1,0},{2,3},{3,2},{4,5},{5,4},{6,7},{7,6},{8,9},{9,8},{10,11... | collective-permute-start | bytes 294920 | tf_op jit(solution)/shard_map/ppermute | solution.py:304

commit v6 on v3

--- a/solution.py
+++ b/solution.py
@@ -18,12 +18,12 @@
 
 
 def features_kernel(
-    x_hbm, gain_hbm, bias_hbm, lm_hbm, lb_hbm, rm_hbm, rb_hbm,
+    x_hbm, gain_hbm, bias_hbm, lm_hbm, lb_hbm, rm_hbm, rb_hbm, w_hbm,
     *refs, packs, parts, pieces,
 ):
-    outs = refs[: len(packs)]
+    outs, w_ref = refs[: len(packs)], refs[len(packs)]
     (x_ref, gain_ref, bias_ref, lm_ref, lb_ref, rm_ref, rb_ref,
-     lo_ref, hi_ref, left_all, turned_ref, rows_ref, sems) = refs[len(packs) :]
+     lo_ref, hi_ref, left_all, turned_ref, rows_ref, sems) = refs[len(packs) + 1 :]
     seqs, residues, depth = x_ref.shape
     hidden = lm_ref.shape[0]
     per = LANES // hidden
@@ -47,6 +47,8 @@
         copy.start()
     for copy in copies[1:]:
         copy.start()
+    w_copy = pltpu.make_async_copy(w_hbm, w_ref, sems.at[pieces + len(small)])
+    w_copy.start()
     for copy in rest:
         copy.wait()
 
@@ -131,89 +133,126 @@
                 rows = left_all[pl.ds((own ^ item) * mine, mine)].reshape(mine * seqs, LANES)
             out[at : at + rows.shape[0], :] = rows
             at += rows.shape[0]
-
-
-def weights_kernel(w_hbm, wide_ref, w_ref, wf_ref, sem, *, parts, hidden):
-    copy = pltpu.make_async_copy(w_hbm, w_ref, sem)
-    copy.start()
+    w_copy.wait()
+
+
+def block_weights(w_ref, wide_ref, wf_ref, *, parts, minor):
     cz = w_ref.shape[1]
-    per = LANES // hidden
-    minor = hidden // parts
+    hidden = parts * minor
+    half = minor // 2
+    rows_each = wide_ref.shape[0] // hidden // hidden
     own = lax.axis_index("narrow")
     wide_ref[...] = jnp.zeros_like(wide_ref)
-    copy.wait()
     wf_ref[...] = w_ref[...].astype(jnp.float32)
     for e in range(hidden):
         rows = wf_ref[pl.ds(e ^ (own * minor), hidden, stride=hidden), :].astype(jnp.bfloat16)
-        for k in range(per):
-            wide_ref[pl.ds(e * LANES + k * hidden, hidden), k * cz : (k + 1) * cz] = rows
+        q, e2, t = e // minor, e % minor // half, e % half
+        for k in range(rows_each):
+            at = ((((q * half + t) * 2 + e2) * rows_each) + k) * hidden
+            wide_ref[at : at + hidden, k * cz : (k + 1) * cz] = rows
+
+
+def pack_kernel(*refs, count):
+    out_ref, at = refs[-1], 0
+    for ref in refs[:count]:
+        out_ref[at : at + ref.shape[0]] = ref[...]
+        at += ref.shape[0]
 
 
 def pair_rows(left_of, right_of, wide_ref, shift_ref, outer_ref, store, *, wides, parts, minor, seqs_total):
     cz = shift_ref.shape[0]
-    per = LANES // (minor * parts)
+    half = minor // 2
     seqs = LANES // parts
     groups = left_of(0).shape[0] // seqs
     residues = right_of(0, 0).shape[0] // minor
     cols = wides * residues
     lefts = [left_of(m) for m in range(parts)]
     slot = iota((minor * residues, LANES), 1) // seqs
+    low = iota((LANES, LANES), 1) < LANES // 2
+    zero = jnp.zeros((LANES, LANES), jnp.float32)
     for q in range(parts):
-        left = jnp.concatenate(
-            [
-                jnp.concatenate([lefts[q ^ k][g * seqs : (g + 1) * seqs] for k in range(parts)], axis=0)
-                for g in range(groups)
-            ],
-            axis=1,
-        )
+        blocks = []
+        for g in range(groups):
+            rows = jnp.concatenate([lefts[q ^ k][g * seqs : (g + 1) * seqs] for k in range(parts)], axis=0)
+            rows = rows.astype(jnp.float32)
+            turned = pltpu.roll(rows, LANES // 2, axis=1)
+            for first, second in ((rows, turned), (turned, rows)):
+                blocks.append(
+                    jnp.concatenate([jnp.where(low, first, zero), jnp.where(low, zero, second)], axis=0)
+                )
+        left = jnp.concatenate(blocks, axis=1).astype(jnp.bfloat16)
         for d in range(wides):
             right = None
             for k in range(parts):
                 chunk = right_of(d, q ^ k)
                 right = chunk if right is None else jnp.where(slot == k, chunk, right)
+            right = jnp.concatenate([right[: half * residues], right[half * residues :]], axis=1)
             outer = jnp.dot(right, left, preferred_element_type=jnp.float32).astype(jnp.bfloat16)
-            for e in range(minor):
-                for g in range(groups):
+            for t in range(half):
+                for g in range(2 * groups):
                     outer_ref[
                         pl.ds(g * cols + d * residues, residues),
-                        (q * minor + e) * LANES : (q * minor + e + 1) * LANES,
-                    ] = outer[e * residues : (e + 1) * residues, g * LANES : (g + 1) * LANES]
+                        (q * half + t) * LANES : (q * half + t + 1) * LANES,
+                    ] = outer[t * residues : (t + 1) * residues, g * LANES : (g + 1) * LANES]
 
     shift = shift_ref[...].reshape(1, cz)
     pairs = jnp.dot(outer_ref[...], wide_ref[...], preferred_element_type=jnp.float32)
-    for g in range(groups):
-        for k in range(per):
+    rows_each = wide_ref.shape[1] // cz
+    for g in range(2 * groups):
+        for k in range(rows_each):
             pair = pairs[g * cols : (g + 1) * cols, k * cz : (k + 1) * cz]
-            store(g * per + k, pair * (1.0 / seqs_total) + shift)
-
-
-def pair_kernel(*refs, places, block, **sizes):
-    wide_ref, shift_ref = refs[-7:-5] if block else refs[-6:-4]
-    out_hbm, outer_ref, done_ref, sem = refs[-4:]
+            store(g * rows_each + k, pair * (1.0 / seqs_total) + shift)
+
+
+def pair_kernel(*refs, places, blocks, first, **sizes):
+    operands = sizes.pop("operands")
+    shift_ref = refs[operands + 1]
+    if first:
+        out_hbm, wide_ref, outer_ref, done_ref, sems, wf_ref = refs[-6:]
+    else:
+        wide_ref = refs[operands]
+        out_hbm, outer_ref, done_ref, sems = refs[-4:]
     parts, minor = sizes["parts"], sizes["minor"]
-    residues = done_ref.shape[1]
-    count = done_ref.shape[0] * minor * parts // LANES * (LANES // parts)
+    own_rows, cols, _ = done_ref.shape
+    residues = cols // len(blocks)
+    left_count = own_rows * minor
+    right_count = minor * residues
 
     def left_of(m):
         ref, at = places[m][:2]
-        return refs[ref][at : at + count, :]
+        return refs[ref][at : at + left_count, :]
 
     def right_of(d, m):
         ref, at = places[m][2:]
-        return refs[ref][at : at + minor * residues, :]
+        return refs[ref][at + d * right_count : at + (d + 1) * right_count, :]
 
     def store(row, pair):
         done_ref[row] = pair.astype(done_ref.dtype)
 
-    pair_rows(left_of, right_of, wide_ref, shift_ref, outer_ref, store, wides=1, **sizes)
-    at = pl.multiple_of((lax.axis_index("wide") ^ block) * residues, 16)
-    copy = pltpu.make_async_copy(done_ref, out_hbm.at[:, pl.ds(at, residues), :], sem)
-    copy.start()
-    copy.wait()
+    if first:
+        block_weights(refs[operands], wide_ref, wf_ref, parts=parts, minor=minor)
+    pair_rows(left_of, right_of, wide_ref, shift_ref, outer_ref, store, wides=len(blocks), **sizes)
+    copies = []
+    for d, block in enumerate(blocks):
+        at = pl.multiple_of((lax.axis_index("wide") ^ block) * residues, 16)
+        copies.append(
+            pltpu.make_async_copy(
+                done_ref.at[:, pl.ds(d * residues, residues), :],
+                out_hbm.at[:, pl.ds(at, residues), :],
+                sems.at[d],
+            )
+        )
+        copies[-1].start()
+    for copy in copies:
+        copy.wait()
 
 
 def pair_blocks_kernel(*refs, wides, parts, minor, **sizes):
-    left_refs, (right_ref, wide_ref, shift_ref, out_ref, outer_ref) = refs[:parts], refs[parts:]
+    left_refs, (right_ref, w_ref, shift_ref, out_ref, wide_ref, wf_ref, outer_ref) = refs[:parts], refs[parts:]
+
+    @pl.when(pl.program_id(0) == 0)
+    def _():
+        block_weights(w_ref, wide_ref, wf_ref, parts=parts, minor=minor)
 
     def store(row, pair):
         out_ref[row] = pair.astype(out_ref.dtype)
@@ -239,21 +278,22 @@
     params = pltpu.CompilerParams(vmem_limit_bytes=VMEM_LIMIT)
     direct = wide == 4 and narrow == 4
     if direct:
-        packs = ((0,), (RIGHT,), (1, RIGHT), (2, 3, RIGHT))
+        packs = ((0,), (RIGHT,), (1, RIGHT), (2, 3))
     else:
         packs = tuple((m,) for m in range(narrow)) + ((RIGHT,),)
     left_count, right_count = groups * seqs, minor * residues
     args = (x, gain, bias, lm.T, lb, rm.T, rb)
-    made = pl.pallas_call(
+    *made, w = pl.pallas_call(
         functools.partial(features_kernel, packs=packs, parts=narrow, pieces=pieces),
         out_shape=tuple(
             jax.ShapeDtypeStruct(
                 (sum(right_count if i == RIGHT else left_count for i in pack), LANES), jnp.bfloat16
             )
             for pack in packs
-        ),
-        in_specs=[hbm] * len(args),
-        out_specs=(vmem,) * len(packs),
+        )
+        + (jax.ShapeDtypeStruct(w.shape, w.dtype),),
+        in_specs=[hbm] * (len(args) + 1),
+        out_specs=(vmem,) * (len(packs) + 1),
         scratch_shapes=[pltpu.VMEM(a.shape, a.dtype) for a in args]
         + [
             pltpu.VMEM((seqs * residues, LANES), jnp.float32),
@@ -261,25 +301,11 @@
             pltpu.VMEM((residues // per, seqs, LANES), jnp.bfloat16),
             pltpu.VMEM((LANES, LANES), jnp.float32),
             pltpu.VMEM((minor * residues, LANES), jnp.float32),
-            pltpu.SemaphoreType.DMA((pieces + len(args) - 1,)),
+            pltpu.SemaphoreType.DMA((pieces + len(args),)),
         ],
         compiler_params=pltpu.CompilerParams(vmem_limit_bytes=VMEM_ALL),
         name="features",
-    )(*args)
-
-    block_weights = pl.pallas_call(
-        functools.partial(weights_kernel, parts=narrow, hidden=hidden),
-        out_shape=jax.ShapeDtypeStruct((hidden * LANES, per * cz), jnp.bfloat16),
-        in_specs=[hbm],
-        out_specs=vmem,
-        scratch_shapes=[
-            pltpu.VMEM(w.shape, w.dtype),
-            pltpu.VMEM(w.shape, jnp.float32),
-            pltpu.SemaphoreType.DMA,
-        ],
-        compiler_params=params,
-        name="block_weights",
-    )(w)
+    )(*args, w)
 
     def across(a, m):
         return lax.ppermute(a, "narrow", [(i, i ^ m) for i in range(narrow)])
@@ -290,7 +316,7 @@
     sizes = dict(parts=narrow, minor=minor, seqs_total=seqs * narrow)
     out_shape = jax.ShapeDtypeStruct((own_rows, wide * residues, cz), jnp.bfloat16)
     if direct:
-        return pairs_by_block(made, across, along, block_weights, shift, out_shape, residues, sizes, params)
+        return pairs_by_block(made, across, along, w, shift, out_shape, residues, sizes, params)
 
     lefts = [made[0]] + [across(made[m], m) for m in range(1, narrow)]
     every = lax.all_gather(made[narrow], ("wide", "narrow"), axis=0, tiled=False)
@@ -306,64 +332,104 @@
         in_specs=[pl.BlockSpec((left_count, LANES), lambda b: (0, 0))] * narrow
         + [
             pl.BlockSpec((block, narrow, right_count, LANES), lambda b: (b, 0, 0, 0)),
-            pl.BlockSpec((hidden * LANES, per * cz), lambda b: (0, 0)),
+            pl.BlockSpec(w.shape, lambda b: (0, 0)),
             pl.BlockSpec((cz,), lambda b: (0,)),
         ],
         out_specs=pl.BlockSpec((own_rows, cols, cz), lambda b: (0, b, 0)),
         out_shape=out_shape,
-        scratch_shapes=[pltpu.VMEM((groups * cols, hidden * LANES), jnp.bfloat16)],
+        scratch_shapes=[
+            pltpu.VMEM((hidden * LANES // 2, 2 * cz), jnp.bfloat16),
+            pltpu.VMEM(w.shape, jnp.float32),
+            pltpu.VMEM((2 * groups * cols, hidden * LANES // 2), jnp.bfloat16),
+        ],
         compiler_params=params,
         name="pairs",
-    )(*lefts, every, block_weights, shift)
-
-
-def pairs_by_block(made, across, along, block_weights, shift, out_shape, residues, sizes, params):
+    )(*lefts, every, w, shift)
+
+
+COST = {0: 4_000_000_000, 1: 1_000_000_000, 3: 1_000_000_000}
+
+
+def pairs_by_block(made, across, along, w, shift, out_shape, residues, sizes, params):
     left_own, right, to_core, to_chip = made
-    far = {d: along(right, d) for d in (2, 3, 1)}
     left_count, right_count = left_own.shape[0], right.shape[0]
-    chip = across(to_chip, 2)
-    core = across(to_core, 1)
-    both = across(chip, 1)
-
     hbm = pl.BlockSpec(memory_space=pltpu.HBM)
     vmem = pl.BlockSpec(memory_space=pltpu.VMEM)
-    own_rows, cols, cz = out_shape.shape
+    own_rows, _, cz = out_shape.shape
     hidden = sizes["parts"] * sizes["minor"]
-    out = None
-    for d in range(cols // residues):
-        operands = [left_own, core, chip, both]
-        if d == 0:
-            operands.append(right)
-            rights = ((4, 0), (1, left_count), (2, 2 * left_count), (3, 2 * left_count))
+    groups = own_rows * hidden // LANES
+
+    def pack(*chunks, after):
+        return pl.pallas_call(
+            functools.partial(pack_kernel, count=len(chunks)),
+            out_shape=jax.ShapeDtypeStruct((sum(c.shape[0] for c in chunks), LANES), jnp.bfloat16),
+            in_specs=[vmem] * (len(chunks) + len(after)),
+            out_specs=vmem,
+            compiler_params=params,
+            name="pack",
+        )(*chunks, *after)
+
+    def pairs(lefts, rights, blocks, weights, out=None, after=()):
+        operands = []
+        places = []
+        for (a, at), (b, bt) in zip(lefts, rights):
+            places.append((len(operands), at, len(operands) + 1, bt))
+            operands += [a, b]
+        count = len(operands)
+        operands += [weights, shift, *after]
+        specs = [vmem] * len(operands)
+        aliases, shapes, outs = {}, [out_shape], [hbm]
+        cols = len(blocks) * residues
+        scratch = [
+            pltpu.VMEM((2 * groups * cols, hidden * LANES // 2), jnp.bfloat16),
+            pltpu.VMEM((own_rows, cols, cz), jnp.bfloat16),
+            pltpu.SemaphoreType.DMA((len(blocks),)),
+        ]
+        if out is None:
+            shapes.append(jax.ShapeDtypeStruct((hidden * LANES // 2, 2 * cz), jnp.bfloat16))
+            outs.append(vmem)
+            scratch.append(pltpu.VMEM(weights.shape, jnp.float32))
         else:
-            other = across(far[d], 2)
-            operands += [far[d], across(far[d], 1), other, across(other, 1)]
-            rights = tuple((4 + m, 0) for m in range(4))
-        places = tuple(
-            (m, left_count if m == 3 else 0) + rights[m] for m in range(4)
-        )
-        operands += [block_weights, shift]
-        specs = [vmem] * len(operands)
-        aliases = {}
-        if out is not None:
             aliases = {len(operands): 0}
             operands.append(out)
             specs.append(hbm)
-        out = pl.pallas_call(
-            functools.partial(pair_kernel, places=places, block=d, **sizes),
-            out_shape=out_shape,
+        return pl.pallas_call(
+            functools.partial(
+                pair_kernel, places=places, blocks=blocks, operands=count, first=out is None, **sizes
+            ),
+            out_shape=shapes,
             in_specs=specs,
-            out_specs=hbm,
+            out_specs=outs,
             input_output_aliases=aliases,
-            scratch_shapes=[
-                pltpu.VMEM((own_rows * hidden // LANES * residues, hidden * LANES), jnp.bfloat16),
-                pltpu.VMEM((own_rows, residues, cz), jnp.bfloat16),
-                pltpu.SemaphoreType.DMA,
-            ],
+            scratch_shapes=scratch,
             compiler_params=params,
-            cost_estimate=pl.CostEstimate(flops=1_500_000_000, bytes_accessed=5_000_000, transcendentals=0),
-            name=f"pairs_{d}",
+            cost_estimate=pl.CostEstimate(
+                flops=COST[blocks[0]], bytes_accessed=1000, transcendentals=0
+            ),
+            name=f"pairs_{blocks[0]}",
         )(*operands)
+
+    far = along(right, 2)
+    near = along(right, 1)
+    last = along(far, 1)
+    chip = across(right, 2)
+    chip_left = across(to_chip, 2)
+    core = across(pack(to_core, chip_left, chip, after=(far, near)), 1)
+    split = to_core.shape[0]
+    lefts = ((left_own, 0), (core, 0), (chip_left, 0), (core, split + left_count))
+    own = ((right, 0), (core, left_count), (chip, 0), (core, split + 2 * left_count))
+    out, weights = pairs(lefts, own, (0,), w, after=(last,))
+
+    middle = pack(near, far, after=(chip,))
+    beside = across(middle, 1)
+    other = across(middle, 2)
+    onward = across(pack(other, after=(weights,)), 1)
+    middle = ((middle, 0), (beside, 0), (other, 0), (onward, 0))
+    (out,) = pairs(lefts, middle, (1, 2), weights, out)
+
+    other = across(last, 2)
+    both = across(pack(last, other, after=()), 1)
+    (out,) = pairs(lefts, ((last, 0), (both, 0), (other, 0), (both, right_count)), (3,), weights, out)
     return out
 
 

time: 35.4 us -> 30.5 us (0.86)
  starting transfers between devices: 13.7 us -> 9.81 us
  Pallas kernels: 11.9 us -> 9.89 us
  local copies, waits for them, and re-layouts: 0.96 us -> 1.55 us
  waiting for transfers between devices: 8.49 us -> 8.94 us
    ppermute x12 -> x8, starting transfers between devices: 7.92 us -> 3.55 us  [across(): return lax.ppermute(a, 'narrow', [(i, i ^ m) for i in range(narrow)])]
    pallas_call x5 -> x7, Pallas kernels: 8.23 us -> 6.17 us  [the longest x3 6.11 us: pairs(): pl.pallas_call(functools.partial(pair_kernel, places=places, blocks=block...]
    unnamed x8 -> x10, local copies, waits for them, and re-layouts: 0.96 us -> 1.55 us
    ppermute x3, starting transfers between devices: 5.76 us -> 6.26 us  [along(): return lax.ppermute(a, 'wide', [(i, i ^ d) for i in range(wide)])]
    ppermute x3, waiting for transfers between devices: 3.44 us -> 3.84 us  [along(): return lax.ppermute(a, 'wide', [(i, i ^ d) for i in range(wide)])]
    ppermute x12 -> x8, waiting for transfers between devices: 5.06 us -> 5.1 us  [across(): return lax.ppermute(a, 'narrow', [(i, i ^ m) for i in range(narrow)])]
  transfers between devices with their start and end apart: 15 -> 11, of which waited for: 4 -> 4; matrix products, arithmetic and copies ran while one was open for 0% -> 0% of each run, Pallas kernels for 18% -> 15%
where the time goes in v6:
time: 30.5 us; the launch traced here: 30.3 us
  Pallas kernels  9.89 us (32%)
  starting transfers between devices  9.81 us (32%)
  waiting for transfers between devices  8.94 us (29%)
  local copies, waits for them, and re-layouts  1.55 us (5%)
    ppermute x3, starting transfers between devices, along(): return lax.ppermute(a, 'wide', [(i, i ^ d) for i in range(wide)])  6.26 us
    pallas_call x3, Pallas kernels, pairs(): pl.pallas_call(functools.partial(pair_kernel, places=places, blocks=block...  6.11 us
    ppermute x8, waiting for transfers between devices, across(): return lax.ppermute(a, 'narrow', [(i, i ^ m) for i in range(narrow)])  5.1 us
    ppermute x3, waiting for transfers between devices, along(): return lax.ppermute(a, 'wide', [(i, i ^ d) for i in range(wide)])  3.84 us
    pallas_call x1, Pallas kernels, on_device(): pl.pallas_call(functools.partial(features_kernel, packs=packs, parts=narr...  3.72 us
    ppermute x8, starting transfers between devices, across(): return lax.ppermute(a, 'narrow', [(i, i ^ m) for i in range(narrow)])  3.55 us
    unnamed x10, local copies, waits for them, and re-layouts  1.55 us
  transfers between devices with their start and end apart: 11, of which 4 were waited for; matrix products, arithmetic and copies ran while one was open for 0% of the time, Pallas kernels for 15%

profile of v6, /device:TPU:0, one launch (start us, length us, event | category | flops | bytes accessed | tf_op | source)
XLA Modules:
  0.0 30.3 jit_solution(16997295187429061356)
XLA Ops:
  0.0 3.7 %features.1 = (bf16[96,128]{1,0:T(8,128)(2,1)}, bf16[384,128]{1,0:T(8,128)(2,1)}, bf16[480,128]{1,0:T(8,128)(2,1)}, bf16[192,128]{1,0:T(8,128)(2,1)}, bf16[1024,128]{1,0:T(8,128)(2,1)}) custom-call(bf16[32,48,256]{2,1,0:T(8,128)(2,1)} %x_hbm.1, f32[256]{0:T(256)} %gain_hbm.1, f32[256]{0:T(256)} %bias_hbm.1, bf16[32,256]{1,0:T(8,128)(2,1)} %bitcast.2, ...), custom_call_target="tpu_custom_call" | custom-call | tf_op jit(solution)/shard_map/features/pallas_call | solution.py:286
  3.7 4.1 %collective-permute-start = (bf16[384,128]{1,0:T(8,128)(2,1)}, bf16[384,128]{1,0:T(8,128)(2,1)S(1)}, u32[]{:S(2)}, u32[]{:S(2)}) collective-permute-start(bf16[384,128]{1,0:T(8,128)(2,1)} %get-tuple-element.13.refs_1_), channel_id=1, source_target_pairs={{0,8},{4,12},{8,0},{12,4},{1,9},{5,13},{9,1},{13,5},{2,10},{6,14},... | collective-permute-start | bytes 294920 | tf_op jit(solution)/shard_map/ppermute | solution.py:314
  7.8 1.5 %collective-permute-start.3 = (bf16[384,128]{1,0:T(8,128)(2,1)}, bf16[384,128]{1,0:T(8,128)(2,1)S(1)}, u32[]{:S(2)}, u32[]{:S(2)}) collective-permute-start(bf16[384,128]{1,0:T(8,128)(2,1)} %get-tuple-element.13.refs_1_), channel_id=1, source_target_pairs={{0,2},{1,3},{2,0},{3,1},{4,6},{5,7},{6,4},{7,5},{8,10},{9,11},{10,... | collective-permute-start | bytes 294920 | tf_op jit(solution)/shard_map/ppermute | solution.py:311
  9.3 1.6 %collective-permute-start.4 = (bf16[384,128]{1,0:T(8,128)(2,1)}, bf16[384,128]{1,0:T(8,128)(2,1)S(1)}, u32[]{:S(2)}, u32[]{:S(2)}) collective-permute-start(bf16[384,128]{1,0:T(8,128)(2,1)} %get-tuple-element.13.refs_1_), channel_id=1, source_target_pairs={{0,4},{4,0},{8,12},{12,8},{1,5},{5,1},{9,13},{13,9},{2,6},{6,2},{1... | collective-permute-start | bytes 294920 | tf_op jit(solution)/shard_map/ppermute | solution.py:314
  10.9 0.5 %collective-permute-start.2 = (bf16[192,128]{1,0:T(8,128)(2,1)}, bf16[192,128]{1,0:T(8,128)(2,1)S(1)}, u32[]{:S(2)}, u32[]{:S(2)}) collective-permute-start(bf16[192,128]{1,0:T(8,128)(2,1)} %get-tuple-element.15), channel_id=1, source_target_pairs={{0,2},{1,3},{2,0},{3,1},{4,6},{5,7},{6,4},{7,5},{8,10},{9,11},{10,... | collective-permute-start | bytes 147464 | tf_op jit(solution)/shard_map/ppermute | solution.py:311
  11.4 3.8 %collective-permute-done.2.refs_1_.refs_4_ = bf16[192,128]{1,0:T(8,128)(2,1)S(1)} collective-permute-done((bf16[192,128]{1,0:T(8,128)(2,1)}, bf16[192,128]{1,0:T(8,128)(2,1)S(1)}, u32[]{:S(2)}, u32[]{:S(2)}) %collective-permute-start.2) | collective-permute-done | bytes 49184 | tf_op jit(solution)/shard_map/ppermute | solution.py:311
  15.2 0.0 collective-permute-done.refs_3_.refs_1_
  15.2 0.0 collective-permute-done.3.refs_2_.refs_5_
  15.2 0.0 collective-permute-done.4.refs_4_.refs_0_
  15.2 0.0 copy-start
  15.2 0.9 %copy-done = bf16[480,128]{1,0:T(8,128)(2,1)S(1)} copy-done((bf16[480,128]{1,0:T(8,128)(2,1)S(1)}, bf16[480,128]{1,0:T(8,128)(2,1)}, u32[]{:S(2)}) %copy-start) | copy-done | bytes 122904
  16.1 0.0 copy-start.1
  16.2 0.0 copy-start.2
  16.2 0.0 copy-start.3
  16.2 0.1 collective-permute-start.5
  16.3 0.6 %collective-permute-start.1 = (bf16[384,128]{1,0:T(8,128)(2,1)S(1)}, bf16[384,128]{1,0:T(8,128)(2,1)S(1)}, u32[]{:S(2)}, u32[]{:S(2)}) collective-permute-start(bf16[384,128]{1,0:T(8,128)(2,1)S(1)} %collective-permute-done.refs_3_.refs_1_), channel_id=1, source_target_pairs={{0,4},{4,0},{8,12},{12,8},{1,5},{5,1},{9,13},{13,9},{2,6},{6,2},{1... | collective-permute-start | bytes 294920 | tf_op jit(solution)/shard_map/ppermute | solution.py:314
  16.8 0.8 %collective-permute-start.9 = (bf16[768,128]{1,0:T(8,128)(2,1)S(1)}, bf16[768,128]{1,0:T(8,128)(2,1)S(1)}, u32[]{:S(2)}, u32[]{:S(2)}) collective-permute-start(bf16[768,128]{1,0:T(8,128)(2,1)S(1)} %pack.6.refs_1_), channel_id=1, source_target_pairs={{0,2},{1,3},{2,0},{3,1},{4,6},{5,7},{6,4},{7,5},{8,10},{9,11},{10,... | collective-permute-start | bytes 589832 | tf_op jit(solution)/shard_map/ppermute | solution.py:311
  17.6 0.0 collective-permute-start.8
  17.6 3.8 %collective-permute-done.1.refs_0_.refs_10_.refs_1_ = bf16[384,128]{1,0:T(8,128)(2,1)S(1)} collective-permute-done((bf16[384,128]{1,0:T(8,128)(2,1)S(1)}, bf16[384,128]{1,0:T(8,128)(2,1)S(1)}, u32[]{:S(2)}, u32[]{:S(2)}) %collective-permute-start.1) | collective-permute-done | bytes 98336 | tf_op jit(solution)/shard_map/ppermute | solution.py:314
  21.5 0.5 %collective-permute-start.6 = (bf16[384,128]{1,0:T(8,128)(2,1)S(1)}, bf16[384,128]{1,0:T(8,128)(2,1)S(1)}, u32[]{:S(2)}, u32[]{:S(2)}) collective-permute-start(bf16[384,128]{1,0:T(8,128)(2,1)S(1)} %collective-permute-done.1.refs_0_.refs_10_.refs_1_), channel_id=1, source_target_pairs={{0,2},{1,3},{2,0},{3,1},{4,6},{5,7},{6,4},{7,5},{8,10},{9,11},{10,... | collective-permute-start | bytes 294920 | tf_op jit(solution)/shard_map/ppermute | solution.py:311
  22.0 0.0 collective-permute-done.5.refs_2_.refs_3_.refs_6_.refs_7_
  22.0 0.0 copy-start.4
  22.0 0.0 copy-done.1
  22.0 0.0 copy-done.2
  22.0 0.0 copy-done.3
  22.0 0.6 %copy-done.4 = f32[128]{0:T(128)S(1)} copy-done((f32[128]{0:T(128)S(1)}, f32[128]{0:T(128)}, u32[]{:S(2)}) %copy-start.4) | copy-done | bytes 536
  22.7 2.2 %pairs_0.1 = (bf16[12,192,128]{2,1,0:T(8,128)(2,1)}, bf16[2048,256]{1,0:T(8,128)(2,1)S(1)}) custom-call(bf16[96,128]{1,0:T(8,128)(2,1)S(1)} %copy-done.3, bf16[384,128]{1,0:T(8,128)(2,1)S(1)} %copy-done.2, bf16[1056,128]{1,0:T(8,128)(2,1)S(1)} %collective-permute-done.5.refs_2_.refs_3_.refs_6_.refs_7_, ...), custom_call_target="tpu_custom_call" | custom-call | flops 4000000000 | bytes 1000 | tf_op jit(solution)/shard_map/pairs_0/pallas_call | solution.py:396
  24.9 0.0 collective-permute-done.9.refs_0_.refs_5_
  24.9 0.1 collective-permute-start.10
  25.0 1.1 %collective-permute-done.6.refs_1_.refs_5_ = bf16[384,128]{1,0:T(8,128)(2,1)S(1)} collective-permute-done((bf16[384,128]{1,0:T(8,128)(2,1)S(1)}, bf16[384,128]{1,0:T(8,128)(2,1)S(1)}, u32[]{:S(2)}, u32[]{:S(2)}) %collective-permute-start.6) | collective-permute-done | bytes 98336 | tf_op jit(solution)/shard_map/ppermute | solution.py:311
  26.1 0.1 collective-permute-start.7
  26.2 0.0 collective-permute-done.8.refs_3_
  26.2 0.2 collective-permute-done.10.refs_7_
  26.4 2.3 %pairs_1.1.refs_10_ = bf16[12,192,128]{2,1,0:T(8,128)(2,1)} custom-call(bf16[96,128]{1,0:T(8,128)(2,1)S(1)} %copy-done.3, bf16[768,128]{1,0:T(8,128)(2,1)S(1)} %pack.6.refs_1_, bf16[1056,128]{1,0:T(8,128)(2,1)S(1)} %collective-permute-done.5.refs_2_.refs_3_.refs_6_.refs_7_, ...), custom_call_target="tpu_custom_call", output_to_operand_aliasing={{}: (10, {})} | custom-call | flops 1000000000 | bytes 1000 | tf_op jit(solution)/shard_map/pairs_1/pallas_call | solution.py:396
  28.7 0.0 collective-permute-done.7.refs_3_.refs_7_
  28.7 1.6 %pairs_3.1 = bf16[12,192,128]{2,1,0:T(8,128)(2,1)} custom-call(bf16[96,128]{1,0:T(8,128)(2,1)S(1)} %copy-done.3, bf16[384,128]{1,0:T(8,128)(2,1)S(1)} %collective-permute-done.1.refs_0_.refs_10_.refs_1_, bf16[1056,128]{1,0:T(8,128)(2,1)S(1)} %collective-permute-done.5.refs_2_.refs_3_.refs_6_.refs_7_, ...), custom_call_target="tpu_custom_call", output_to_operand_aliasing={{}: (10, {})} | custom-call | flops 1000000000 | bytes 1000 | tf_op jit(solution)/shard_map/pairs_3/pallas_call | solution.py:396
  (4 shorter events, 0.1 us)
Async XLA Ops:
  3.7 11.5 %collective-permute-start = (bf16[384,128]{1,0:T(8,128)(2,1)}, bf16[384,128]{1,0:T(8,128)(2,1)S(1)}, u32[]{:S(2)}, u32[]{:S(2)}) collective-permute-start(bf16[384,128]{1,0:T(8,128)(2,1)} %get-tuple-element.13.refs_1_), channel_id=1, source_target_pairs={{0,8},{4,12},{8,0},{12,4},{1,9},{5,13},{9,1},{13,5},{2,10},{6,14},... | collective-permute-start | bytes 294920 | tf_op jit(solution)/shard_map/ppermute | solution.py:314
  7.8 7.4 %collective-permute-start.3 = (bf16[384,128]{1,0:T(8,128)(2,1)}, bf16[384,128]{1,0:T(8,128)(2,1)S(1)}, u32[]{:S(2)}, u32[]{:S(2)}) collective-permute-start(bf16[384,128]{1,0:T(8,128)(2,1)} %get-tuple-element.13.refs_1_), channel_id=1, source_target_pairs={{0,2},{1,3},{2,0},{3,1},{4,6},{5,7},{6,4},{7,5},{8,10},{9,11},{10,... | collective-permute-start | bytes 294920 | tf_op jit(solution)/shard_map/ppermute | solution.py:311
  9.3 5.9 %collective-permute-start.4 = (bf16[384,128]{1,0:T(8,128)(2,1)}, bf16[384,128]{1,0:T(8,128)(2,1)S(1)}, u32[]{:S(2)}, u32[]{:S(2)}) collective-permute-start(bf16[384,128]{1,0:T(8,128)(2,1)} %get-tuple-element.13.refs_1_), channel_id=1, source_target_pairs={{0,4},{4,0},{8,12},{12,8},{1,5},{5,1},{9,13},{13,9},{2,6},{6,2},{1... | collective-permute-start | bytes 294920 | tf_op jit(solution)/shard_map/ppermute | solution.py:314
  10.9 4.3 %collective-permute-start.2 = (bf16[192,128]{1,0:T(8,128)(2,1)}, bf16[192,128]{1,0:T(8,128)(2,1)S(1)}, u32[]{:S(2)}, u32[]{:S(2)}) collective-permute-start(bf16[192,128]{1,0:T(8,128)(2,1)} %get-tuple-element.15), channel_id=1, source_target_pairs={{0,2},{1,3},{2,0},{3,1},{4,6},{5,7},{6,4},{7,5},{8,10},{9,11},{10,... | collective-permute-start | bytes 147464 | tf_op jit(solution)/shard_map/ppermute | solution.py:311
  15.2 0.9 %copy-start = (bf16[480,128]{1,0:T(8,128)(2,1)S(1)}, bf16[480,128]{1,0:T(8,128)(2,1)}, u32[]{:S(2)}) copy-start(bf16[480,128]{1,0:T(8,128)(2,1)} %get-tuple-element.14.refs_0_) | copy-start | bytes 368644
  16.1 5.9 %copy-start.1 = (bf16[1024,128]{1,0:T(8,128)(2,1)S(1)}, bf16[1024,128]{1,0:T(8,128)(2,1)}, u32[]{:S(2)}) copy-start(bf16[1024,128]{1,0:T(8,128)(2,1)} %get-tuple-element.16.refs_8_) | copy-start | bytes 786436
  16.2 5.9 %copy-start.2 = (bf16[384,128]{1,0:T(8,128)(2,1)S(1)}, bf16[384,128]{1,0:T(8,128)(2,1)}, u32[]{:S(2)}) copy-start(bf16[384,128]{1,0:T(8,128)(2,1)} %get-tuple-element.13.refs_1_) | copy-start | bytes 294916
  16.2 5.9 %copy-start.3 = (bf16[96,128]{1,0:T(8,128)(2,1)S(1)}, bf16[96,128]{1,0:T(8,128)(2,1)}, u32[]{:S(2)}) copy-start(bf16[96,128]{1,0:T(8,128)(2,1)} %get-tuple-element.12.refs_0_) | copy-start | bytes 73732
  16.2 5.8 %collective-permute-start.5 = (bf16[1056,128]{1,0:T(8,128)(2,1)S(1)}, bf16[1056,128]{1,0:T(8,128)(2,1)S(1)}, u32[]{:S(2)}, u32[]{:S(2)}) collective-permute-start(bf16[1056,128]{1,0:T(8,128)(2,1)S(1)} %pack.4), channel_id=1, source_target_pairs={{0,1},{1,0},{2,3},{3,2},{4,5},{5,4},{6,7},{7,6},{8,9},{9,8},{10,11... | collective-permute-start | bytes 811016 | tf_op jit(solution)/shard_map/ppermute | solution.py:311
  16.3 5.2 %collective-permute-start.1 = (bf16[384,128]{1,0:T(8,128)(2,1)S(1)}, bf16[384,128]{1,0:T(8,128)(2,1)S(1)}, u32[]{:S(2)}, u32[]{:S(2)}) collective-permute-start(bf16[384,128]{1,0:T(8,128)(2,1)S(1)} %collective-permute-done.refs_3_.refs_1_), channel_id=1, source_target_pairs={{0,4},{4,0},{8,12},{12,8},{1,5},{5,1},{9,13},{13,9},{2,6},{6,2},{1... | collective-permute-start | bytes 294920 | tf_op jit(solution)/shard_map/ppermute | solution.py:314
  16.8 8.0 %collective-permute-start.9 = (bf16[768,128]{1,0:T(8,128)(2,1)S(1)}, bf16[768,128]{1,0:T(8,128)(2,1)S(1)}, u32[]{:S(2)}, u32[]{:S(2)}) collective-permute-start(bf16[768,128]{1,0:T(8,128)(2,1)S(1)} %pack.6.refs_1_), channel_id=1, source_target_pairs={{0,2},{1,3},{2,0},{3,1},{4,6},{5,7},{6,4},{7,5},{8,10},{9,11},{10,... | collective-permute-start | bytes 589832 | tf_op jit(solution)/shard_map/ppermute | solution.py:311
  17.6 8.6 %collective-permute-start.8 = (bf16[768,128]{1,0:T(8,128)(2,1)S(1)}, bf16[768,128]{1,0:T(8,128)(2,1)S(1)}, u32[]{:S(2)}, u32[]{:S(2)}) collective-permute-start(bf16[768,128]{1,0:T(8,128)(2,1)S(1)} %pack.6.refs_1_), channel_id=1, source_target_pairs={{0,1},{1,0},{2,3},{3,2},{4,5},{5,4},{6,7},{7,6},{8,9},{9,8},{10,11... | collective-permute-start | bytes 589832 | tf_op jit(solution)/shard_map/ppermute | solution.py:311
  21.5 4.6 %collective-permute-start.6 = (bf16[384,128]{1,0:T(8,128)(2,1)S(1)}, bf16[384,128]{1,0:T(8,128)(2,1)S(1)}, u32[]{:S(2)}, u32[]{:S(2)}) collective-permute-start(bf16[384,128]{1,0:T(8,128)(2,1)S(1)} %collective-permute-done.1.refs_0_.refs_10_.refs_1_), channel_id=1, source_target_pairs={{0,2},{1,3},{2,0},{3,1},{4,6},{5,7},{6,4},{7,5},{8,10},{9,11},{10,... | collective-permute-start | bytes 294920 | tf_op jit(solution)/shard_map/ppermute | solution.py:311
  22.0 0.7 %copy-start.4 = (f32[128]{0:T(128)S(1)}, f32[128]{0:T(128)}, u32[]{:S(2)}) copy-start(f32[128]{0:T(128)} %refs_9_.5) | copy-start | bytes 1540
  24.9 1.5 %collective-permute-start.10 = (bf16[768,128]{1,0:T(8,128)(2,1)S(1)}, bf16[768,128]{1,0:T(8,128)(2,1)S(1)}, u32[]{:S(2)}, u32[]{:S(2)}) collective-permute-start(bf16[768,128]{1,0:T(8,128)(2,1)S(1)} %pack.7), channel_id=1, source_target_pairs={{0,1},{1,0},{2,3},{3,2},{4,5},{5,4},{6,7},{7,6},{8,9},{9,8},{10,11... | collective-permute-start | bytes 589832 | tf_op jit(solution)/shard_map/ppermute | solution.py:311
  26.1 2.6 %collective-permute-start.7 = (bf16[768,128]{1,0:T(8,128)(2,1)S(1)}, bf16[768,128]{1,0:T(8,128)(2,1)S(1)}, u32[]{:S(2)}, u32[]{:S(2)}) collective-permute-start(bf16[768,128]{1,0:T(8,128)(2,1)S(1)} %pack.5), channel_id=1, source_target_pairs={{0,1},{1,0},{2,3},{3,2},{4,5},{5,4},{6,7},{7,6},{8,9},{9,8},{10,11... | collective-permute-start | bytes 589832 | tf_op jit(solution)/shard_map/ppermute | solution.py:311

commit v7 on v6

--- a/solution.py
+++ b/solution.py
@@ -18,11 +18,11 @@
 
 
 def features_kernel(
-    x_hbm, gain_hbm, bias_hbm, lm_hbm, lb_hbm, rm_hbm, rb_hbm, w_hbm,
+    x_hbm, gain_hbm, bias_hbm, lm_hbm, lb_hbm, rm_hbm, rb_hbm, w_hbm, shift_hbm,
     *refs, packs, parts, pieces,
 ):
-    outs, w_ref = refs[: len(packs)], refs[len(packs)]
-    (x_ref, gain_ref, bias_ref, lm_ref, lb_ref, rm_ref, rb_ref,
+    outs, wf_ref = refs[: len(packs)], refs[len(packs)]
+    (x_ref, gain_ref, bias_ref, lm_ref, lb_ref, rm_ref, rb_ref, w_ref, shift_ref,
      lo_ref, hi_ref, left_all, turned_ref, rows_ref, sems) = refs[len(packs) + 1 :]
     seqs, residues, depth = x_ref.shape
     hidden = lm_ref.shape[0]
@@ -47,8 +47,12 @@
         copy.start()
     for copy in copies[1:]:
         copy.start()
-    w_copy = pltpu.make_async_copy(w_hbm, w_ref, sems.at[pieces + len(small)])
-    w_copy.start()
+    late = [
+        pltpu.make_async_copy(a, b, sems.at[pieces + len(small) + i])
+        for i, (a, b) in enumerate(((w_hbm, w_ref), (shift_hbm, shift_ref)))
+    ]
+    for copy in late:
+        copy.start()
     for copy in rest:
         copy.wait()
 
@@ -133,17 +137,19 @@
                 rows = left_all[pl.ds((own ^ item) * mine, mine)].reshape(mine * seqs, LANES)
             out[at : at + rows.shape[0], :] = rows
             at += rows.shape[0]
-    w_copy.wait()
-
-
-def block_weights(w_ref, wide_ref, wf_ref, *, parts, minor):
-    cz = w_ref.shape[1]
+    for copy in late:
+        copy.wait()
+    wf_ref[: w_ref.shape[0]] = w_ref[...].astype(jnp.float32)
+    wf_ref[w_ref.shape[0] :] = jnp.broadcast_to(shift_ref[...].reshape(1, -1), (8, shift_ref.shape[0]))
+
+
+def block_weights(wf_ref, wide_ref, *, parts, minor):
+    cz = wf_ref.shape[1]
     hidden = parts * minor
     half = minor // 2
     rows_each = wide_ref.shape[0] // hidden // hidden
     own = lax.axis_index("narrow")
     wide_ref[...] = jnp.zeros_like(wide_ref)
-    wf_ref[...] = w_ref[...].astype(jnp.float32)
     for e in range(hidden):
         rows = wf_ref[pl.ds(e ^ (own * minor), hidden, stride=hidden), :].astype(jnp.bfloat16)
         q, e2, t = e // minor, e % minor // half, e % half
@@ -159,28 +165,30 @@
         at += ref.shape[0]
 
 
-def pair_rows(left_of, right_of, wide_ref, shift_ref, outer_ref, store, *, wides, parts, minor, seqs_total):
-    cz = shift_ref.shape[0]
+def pair_rows(left_of, right_of, wide_ref, shift, outer_ref, store, *, wides, parts, minor, seqs_total):
+    cz = shift.shape[1]
     half = minor // 2
     seqs = LANES // parts
     groups = left_of(0).shape[0] // seqs
     residues = right_of(0, 0).shape[0] // minor
     cols = wides * residues
-    lefts = [left_of(m) for m in range(parts)]
     slot = iota((minor * residues, LANES), 1) // seqs
-    low = iota((LANES, LANES), 1) < LANES // 2
-    zero = jnp.zeros((LANES, LANES), jnp.float32)
-    for q in range(parts):
-        blocks = []
+    low = iota((seqs, LANES), 1) < LANES // 2
+    zero = jnp.zeros((seqs, LANES), jnp.float32)
+
+    lefts = []
+    for m in range(parts):
+        halves = []
         for g in range(groups):
-            rows = jnp.concatenate([lefts[q ^ k][g * seqs : (g + 1) * seqs] for k in range(parts)], axis=0)
-            rows = rows.astype(jnp.float32)
+            rows = left_of(m)[g * seqs : (g + 1) * seqs].astype(jnp.float32)
             turned = pltpu.roll(rows, LANES // 2, axis=1)
             for first, second in ((rows, turned), (turned, rows)):
-                blocks.append(
-                    jnp.concatenate([jnp.where(low, first, zero), jnp.where(low, zero, second)], axis=0)
-                )
-        left = jnp.concatenate(blocks, axis=1).astype(jnp.bfloat16)
+                halves.append((jnp.where(low, first, zero), jnp.where(low, zero, second)))
+        lefts.append(
+            [jnp.concatenate([h[i] for h in halves], axis=1).astype(jnp.bfloat16) for i in range(2)]
+        )
+    for q in range(parts):
+        left = jnp.concatenate([lefts[q ^ k][i] for i in range(2) for k in range(parts)], axis=0)
         for d in range(wides):
             right = None
             for k in range(parts):
@@ -195,7 +203,6 @@
                         (q * half + t) * LANES : (q * half + t + 1) * LANES,
                     ] = outer[t * residues : (t + 1) * residues, g * LANES : (g + 1) * LANES]
 
-    shift = shift_ref[...].reshape(1, cz)
     pairs = jnp.dot(outer_ref[...], wide_ref[...], preferred_element_type=jnp.float32)
     rows_each = wide_ref.shape[1] // cz
     for g in range(2 * groups):
@@ -206,11 +213,10 @@
 
 def pair_kernel(*refs, places, blocks, first, **sizes):
     operands = sizes.pop("operands")
-    shift_ref = refs[operands + 1]
     if first:
-        out_hbm, wide_ref, outer_ref, done_ref, sems, wf_ref = refs[-6:]
+        out_hbm, wide_ref, shift_ref, outer_ref, done_ref, sems = refs[-6:]
     else:
-        wide_ref = refs[operands]
+        wide_ref, shift_ref = refs[operands : operands + 2]
         out_hbm, outer_ref, done_ref, sems = refs[-4:]
     parts, minor = sizes["parts"], sizes["minor"]
     own_rows, cols, _ = done_ref.shape
@@ -230,8 +236,10 @@
         done_ref[row] = pair.astype(done_ref.dtype)
 
     if first:
-        block_weights(refs[operands], wide_ref, wf_ref, parts=parts, minor=minor)
-    pair_rows(left_of, right_of, wide_ref, shift_ref, outer_ref, store, wides=len(blocks), **sizes)
+        wf_ref = refs[operands]
+        block_weights(wf_ref, wide_ref, parts=parts, minor=minor)
+        shift_ref[...] = wf_ref[wf_ref.shape[0] - 8 :]
+    pair_rows(left_of, right_of, wide_ref, shift_ref[:1], outer_ref, store, wides=len(blocks), **sizes)
     copies = []
     for d, block in enumerate(blocks):
         at = pl.multiple_of((lax.axis_index("wide") ^ block) * residues, 16)
@@ -248,17 +256,18 @@
 
 
 def pair_blocks_kernel(*refs, wides, parts, minor, **sizes):
-    left_refs, (right_ref, w_ref, shift_ref, out_ref, wide_ref, wf_ref, outer_ref) = refs[:parts], refs[parts:]
+    left_refs, (right_ref, wf_ref, out_ref, wide_ref, outer_ref) = refs[:parts], refs[parts:]
 
     @pl.when(pl.program_id(0) == 0)
     def _():
-        block_weights(w_ref, wide_ref, wf_ref, parts=parts, minor=minor)
+        block_weights(wf_ref, wide_ref, parts=parts, minor=minor)
 
     def store(row, pair):
         out_ref[row] = pair.astype(out_ref.dtype)
 
     pair_rows(
-        lambda m: left_refs[m][...], lambda d, m: right_ref[d, m], wide_ref, shift_ref, outer_ref, store,
+        lambda m: left_refs[m][...], lambda d, m: right_ref[d, m],
+        wide_ref, wf_ref[wf_ref.shape[0] - 8 :][:1], outer_ref, store,
         wides=wides, parts=parts, minor=minor, **sizes,
     )
 
@@ -282,7 +291,7 @@
     else:
         packs = tuple((m,) for m in range(narrow)) + ((RIGHT,),)
     left_count, right_count = groups * seqs, minor * residues
-    args = (x, gain, bias, lm.T, lb, rm.T, rb)
+    args = (x, gain, bias, lm.T, lb, rm.T, rb, w, shift)
     *made, w = pl.pallas_call(
         functools.partial(features_kernel, packs=packs, parts=narrow, pieces=pieces),
         out_shape=tuple(
@@ -291,8 +300,8 @@
             )
             for pack in packs
         )
-        + (jax.ShapeDtypeStruct(w.shape, w.dtype),),
-        in_specs=[hbm] * (len(args) + 1),
+        + (jax.ShapeDtypeStruct((w.shape[0] + 8, cz), jnp.float32),),
+        in_specs=[hbm] * len(args),
         out_specs=(vmem,) * (len(packs) + 1),
         scratch_shapes=[pltpu.VMEM(a.shape, a.dtype) for a in args]
         + [
@@ -301,11 +310,11 @@
             pltpu.VMEM((residues // per, seqs, LANES), jnp.bfloat16),
             pltpu.VMEM((LANES, LANES), jnp.float32),
             pltpu.VMEM((minor * residues, LANES), jnp.float32),
-            pltpu.SemaphoreType.DMA((pieces + len(args),)),
+            pltpu.SemaphoreType.DMA((pieces + len(args) - 1,)),
         ],
         compiler_params=pltpu.CompilerParams(vmem_limit_bytes=VMEM_ALL),
         name="features",
-    )(*args, w)
+    )(*args)
 
     def across(a, m):
         return lax.ppermute(a, "narrow", [(i, i ^ m) for i in range(narrow)])
@@ -316,7 +325,7 @@
     sizes = dict(parts=narrow, minor=minor, seqs_total=seqs * narrow)
     out_shape = jax.ShapeDtypeStruct((own_rows, wide * residues, cz), jnp.bfloat16)
     if direct:
-        return pairs_by_block(made, across, along, w, shift, out_shape, residues, sizes, params)
+        return pairs_by_block(made, across, along, w, out_shape, residues, sizes, params)
 
     lefts = [made[0]] + [across(made[m], m) for m in range(1, narrow)]
     every = lax.all_gather(made[narrow], ("wide", "narrow"), axis=0, tiled=False)
@@ -333,24 +342,19 @@
         + [
             pl.BlockSpec((block, narrow, right_count, LANES), lambda b: (b, 0, 0, 0)),
             pl.BlockSpec(w.shape, lambda b: (0, 0)),
-            pl.BlockSpec((cz,), lambda b: (0,)),
         ],
         out_specs=pl.BlockSpec((own_rows, cols, cz), lambda b: (0, b, 0)),
         out_shape=out_shape,
         scratch_shapes=[
             pltpu.VMEM((hidden * LANES // 2, 2 * cz), jnp.bfloat16),
-            pltpu.VMEM(w.shape, jnp.float32),
             pltpu.VMEM((2 * groups * cols, hidden * LANES // 2), jnp.bfloat16),
         ],
         compiler_params=params,
         name="pairs",
-    )(*lefts, every, w, shift)
-
-
-COST = {0: 4_000_000_000, 1: 1_000_000_000, 3: 1_000_000_000}
-
-
-def pairs_by_block(made, across, along, w, shift, out_shape, residues, sizes, params):
+    )(*lefts, every, w)
+
+
+def pairs_by_block(made, across, along, w, out_shape, residues, sizes, params):
     left_own, right, to_core, to_chip = made
     left_count, right_count = left_own.shape[0], right.shape[0]
     hbm = pl.BlockSpec(memory_space=pltpu.HBM)
@@ -369,14 +373,14 @@
             name="pack",
         )(*chunks, *after)
 
-    def pairs(lefts, rights, blocks, weights, out=None, after=()):
+    def pairs(lefts, rights, blocks, *weights, out=None, after=()):
         operands = []
         places = []
         for (a, at), (b, bt) in zip(lefts, rights):
             places.append((len(operands), at, len(operands) + 1, bt))
             operands += [a, b]
         count = len(operands)
-        operands += [weights, shift, *after]
+        operands += [*weights, *after]
         specs = [vmem] * len(operands)
         aliases, shapes, outs = {}, [out_shape], [hbm]
         cols = len(blocks) * residues
@@ -387,8 +391,8 @@
         ]
         if out is None:
             shapes.append(jax.ShapeDtypeStruct((hidden * LANES // 2, 2 * cz), jnp.bfloat16))
-            outs.append(vmem)
-            scratch.append(pltpu.VMEM(weights.shape, jnp.float32))
+            shapes.append(jax.ShapeDtypeStruct((8, cz), jnp.float32))
+            outs += [vmem, vmem]
         else:
             aliases = {len(operands): 0}
             operands.append(out)
@@ -404,7 +408,7 @@
             scratch_shapes=scratch,
             compiler_params=params,
             cost_estimate=pl.CostEstimate(
-                flops=COST[blocks[0]], bytes_accessed=1000, transcendentals=0
+                flops=1000, bytes_accessed=1000, transcendentals=0
             ),
             name=f"pairs_{blocks[0]}",
         )(*operands)
@@ -414,22 +418,22 @@
     last = along(far, 1)
     chip = across(right, 2)
     chip_left = across(to_chip, 2)
-    core = across(pack(to_core, chip_left, chip, after=(far, near)), 1)
-    split = to_core.shape[0]
-    lefts = ((left_own, 0), (core, 0), (chip_left, 0), (core, split + left_count))
-    own = ((right, 0), (core, left_count), (chip, 0), (core, split + 2 * left_count))
-    out, weights = pairs(lefts, own, (0,), w, after=(last,))
-
-    middle = pack(near, far, after=(chip,))
+    core = across(to_core, 1)
+    middle = pack(near, far, after=(chip, core))
     beside = across(middle, 1)
+    both = across(pack(chip_left, chip, after=(last,)), 1)
+    lefts = ((left_own, 0), (core, 0), (chip_left, 0), (both, left_count))
+    own = ((right, 0), (core, left_count), (chip, 0), (both, 2 * left_count))
+    out, *weights = pairs(lefts, own, (0,), w)
+
     other = across(middle, 2)
-    onward = across(pack(other, after=(weights,)), 1)
+    onward = across(pack(other, after=weights[:1]), 1)
     middle = ((middle, 0), (beside, 0), (other, 0), (onward, 0))
-    (out,) = pairs(lefts, middle, (1, 2), weights, out)
+    (out,) = pairs(lefts, middle, (1, 2), *weights, out=out)
 
     other = across(last, 2)
     both = across(pack(last, other, after=()), 1)
-    (out,) = pairs(lefts, ((last, 0), (both, 0), (other, 0), (both, right_count)), (3,), weights, out)
+    (out,) = pairs(lefts, ((last, 0), (both, 0), (other, 0), (both, right_count)), (3,), *weights, out=out)
     return out
 
 

time: 30.5 us -> 28.8 us (0.944)
  waiting for transfers between devices: 8.94 us -> 6.31 us
  starting transfers between devices: 9.81 us -> 12.3 us
  local copies, waits for them, and re-layouts: 1.55 us -> 0.01 us
    ppermute x8 -> x9, starting transfers between devices: 3.55 us -> 5.78 us  [across(): return lax.ppermute(a, 'narrow', [(i, i ^ m) for i in range(narrow)])]
    ppermute x3, waiting for transfers between devices: 3.84 us -> 2.1 us  [along(): return lax.ppermute(a, 'wide', [(i, i ^ d) for i in range(wide)])]
    unnamed x10 -> x6, local copies, waits for them, and re-layouts: 1.55 us -> 0.01 us
    ppermute x8 -> x9, waiting for transfers between devices: 5.1 us -> 4.21 us  [across(): return lax.ppermute(a, 'narrow', [(i, i ^ m) for i in range(narrow)])]
  transfers between devices with their start and end apart: 11 -> 12, of which waited for: 4 -> 4; matrix products, arithmetic and copies ran while one was open for 0% -> 0% of each run, Pallas kernels for 15% -> 16%
where the time goes in v7:
time: 28.8 us; the launch traced here: 28.6 us
  starting transfers between devices  12.3 us (43%)
  Pallas kernels  9.9 us (34%)
  waiting for transfers between devices  6.31 us (22%)
    ppermute x3, starting transfers between devices, along(): return lax.ppermute(a, 'wide', [(i, i ^ d) for i in range(wide)])  6.49 us
    pallas_call x3, Pallas kernels, pairs(): pl.pallas_call(functools.partial(pair_kernel, places=places, blocks=block...  6.01 us
    ppermute x9, starting transfers between devices, across(): return lax.ppermute(a, 'narrow', [(i, i ^ m) for i in range(narrow)])  5.78 us
    ppermute x9, waiting for transfers between devices, across(): return lax.ppermute(a, 'narrow', [(i, i ^ m) for i in range(narrow)])  4.21 us
    pallas_call x1, Pallas kernels, on_device(): pl.pallas_call(functools.partial(features_kernel, packs=packs, parts=narr...  3.83 us
    ppermute x3, waiting for transfers between devices, along(): return lax.ppermute(a, 'wide', [(i, i ^ d) for i in range(wide)])  2.1 us
  transfers between devices with their start and end apart: 12, of which 4 were waited for; matrix products, arithmetic and copies ran while one was open for 0% of the time, Pallas kernels for 16%

profile of v7, /device:TPU:0, one launch (start us, length us, event | category | flops | bytes accessed | tf_op | source)
XLA Modules:
  0.0 28.6 jit_solution(16688410607766197720)
XLA Ops:
  0.0 3.8 %features.1 = (bf16[96,128]{1,0:T(8,128)(2,1)}, bf16[384,128]{1,0:T(8,128)(2,1)}, bf16[480,128]{1,0:T(8,128)(2,1)}, bf16[192,128]{1,0:T(8,128)(2,1)}, f32[1032,128]{1,0:T(8,128)}) custom-call(bf16[32,48,256]{2,1,0:T(8,128)(2,1)} %x_hbm.1, f32[256]{0:T(256)} %gain_hbm.1, f32[256]{0:T(256)} %bias_hbm.1, bf16[32,256]{1,0:T(8,128)(2,1)} %bitcast.2, f32[32]{0:T(128)} %lb_hbm.1, ...), custom_call_target="tpu_custom_call" | custom-call | tf_op jit(solution)/shard_map/features/pallas_call | solution.py:295
  3.8 0.0 copy-start
  3.9 4.1 %collective-permute-start = (bf16[384,128]{1,0:T(8,128)(2,1)}, bf16[384,128]{1,0:T(8,128)(2,1)S(1)}, u32[]{:S(2)}, u32[]{:S(2)}) collective-permute-start(bf16[384,128]{1,0:T(8,128)(2,1)} %get-tuple-element.14.refs_1_), channel_id=1, source_target_pairs={{0,8},{4,12},{8,0},{12,4},{1,9},{5,13},{9,1},{13,5},{2,10},{6,14},... | collective-permute-start | bytes 294920 | tf_op jit(solution)/shard_map/ppermute | solution.py:323
  8.0 0.0 collective-permute-start.2
  8.0 1.5 %collective-permute-start.6 = (bf16[384,128]{1,0:T(8,128)(2,1)}, bf16[384,128]{1,0:T(8,128)(2,1)S(1)}, u32[]{:S(2)}, u32[]{:S(2)}) collective-permute-start(bf16[384,128]{1,0:T(8,128)(2,1)} %get-tuple-element.14.refs_1_), channel_id=1, source_target_pairs={{0,2},{1,3},{2,0},{3,1},{4,6},{5,7},{6,4},{7,5},{8,10},{9,11},{10,... | collective-permute-start | bytes 294920 | tf_op jit(solution)/shard_map/ppermute | solution.py:320
  9.4 1.6 %collective-permute-start.8 = (bf16[384,128]{1,0:T(8,128)(2,1)}, bf16[384,128]{1,0:T(8,128)(2,1)S(1)}, u32[]{:S(2)}, u32[]{:S(2)}) collective-permute-start(bf16[384,128]{1,0:T(8,128)(2,1)} %get-tuple-element.14.refs_1_), channel_id=1, source_target_pairs={{0,4},{4,0},{8,12},{12,8},{1,5},{5,1},{9,13},{13,9},{2,6},{6,2},{1... | collective-permute-start | bytes 294920 | tf_op jit(solution)/shard_map/ppermute | solution.py:323
  11.0 2.1 %collective-permute-done.refs_1_ = bf16[384,128]{1,0:T(8,128)(2,1)S(1)} collective-permute-done((bf16[384,128]{1,0:T(8,128)(2,1)}, bf16[384,128]{1,0:T(8,128)(2,1)S(1)}, u32[]{:S(2)}, u32[]{:S(2)}) %collective-permute-start) | collective-permute-done | bytes 98336 | tf_op jit(solution)/shard_map/ppermute | solution.py:323
  13.1 0.8 %collective-permute-start.1 = (bf16[384,128]{1,0:T(8,128)(2,1)S(1)}, bf16[384,128]{1,0:T(8,128)(2,1)S(1)}, u32[]{:S(2)}, u32[]{:S(2)}) collective-permute-start(bf16[384,128]{1,0:T(8,128)(2,1)S(1)} %collective-permute-done.refs_1_), channel_id=1, source_target_pairs={{0,4},{4,0},{8,12},{12,8},{1,5},{5,1},{9,13},{13,9},{2,6},{6,2},{1... | collective-permute-start | bytes 294920 | tf_op jit(solution)/shard_map/ppermute | solution.py:323
  13.9 1.5 %collective-permute-start.5 = (bf16[192,128]{1,0:T(8,128)(2,1)}, bf16[192,128]{1,0:T(8,128)(2,1)S(1)}, u32[]{:S(2)}, u32[]{:S(2)}) collective-permute-start(bf16[192,128]{1,0:T(8,128)(2,1)} %get-tuple-element.16), channel_id=1, source_target_pairs={{0,2},{1,3},{2,0},{3,1},{4,6},{5,7},{6,4},{7,5},{8,10},{9,11},{10,... | collective-permute-start | bytes 147464 | tf_op jit(solution)/shard_map/ppermute | solution.py:320
  15.4 0.0 collective-permute-done.6.refs_1_.refs_5_.refs_2_
  15.4 0.0 collective-permute-done.8.refs_0_
  15.4 0.0 collective-permute-done.2.refs_2_.refs_3_
  15.5 0.0 copy-start.1
  15.5 0.0 copy-start.2
  15.5 0.6 %collective-permute-start.10 = (bf16[768,128]{1,0:T(8,128)(2,1)S(1)}, bf16[768,128]{1,0:T(8,128)(2,1)S(1)}, u32[]{:S(2)}, u32[]{:S(2)}) collective-permute-start(bf16[768,128]{1,0:T(8,128)(2,1)S(1)} %pack.6.refs_1_), channel_id=1, source_target_pairs={{0,2},{1,3},{2,0},{3,1},{4,6},{5,7},{6,4},{7,5},{8,10},{9,11},{10,... | collective-permute-start | bytes 589832 | tf_op jit(solution)/shard_map/ppermute | solution.py:320
  16.1 2.6 %collective-permute-done.5.refs_0_.refs_4_ = bf16[192,128]{1,0:T(8,128)(2,1)S(1)} collective-permute-done((bf16[192,128]{1,0:T(8,128)(2,1)}, bf16[192,128]{1,0:T(8,128)(2,1)S(1)}, u32[]{:S(2)}, u32[]{:S(2)}) %collective-permute-start.5) | collective-permute-done | bytes 49184 | tf_op jit(solution)/shard_map/ppermute | solution.py:320
  18.7 0.0 collective-permute-done.1.refs_0_.refs_2_.refs_1_
  18.7 0.1 collective-permute-start.7
  18.8 1.7 %collective-permute-start.3 = (bf16[384,128]{1,0:T(8,128)(2,1)S(1)}, bf16[384,128]{1,0:T(8,128)(2,1)S(1)}, u32[]{:S(2)}, u32[]{:S(2)}) collective-permute-start(bf16[384,128]{1,0:T(8,128)(2,1)S(1)} %collective-permute-done.1.refs_0_.refs_2_.refs_1_), channel_id=1, source_target_pairs={{0,2},{1,3},{2,0},{3,1},{4,6},{5,7},{6,4},{7,5},{8,10},{9,11},{10,... | collective-permute-start | bytes 294920 | tf_op jit(solution)/shard_map/ppermute | solution.py:320
  20.5 0.2 collective-permute-start.9
  20.6 0.0 collective-permute-done.7.refs_6_.refs_7_
  20.6 0.0 copy-done
  20.6 0.0 copy-done.1
  20.6 0.0 copy-done.2
  20.6 2.1 %pairs_0.1 = (bf16[12,192,128]{2,1,0:T(8,128)(2,1)}, bf16[2048,256]{1,0:T(8,128)(2,1)S(1)}, f32[8,128]{1,0:T(8,128)S(1)}) custom-call(bf16[96,128]{1,0:T(8,128)(2,1)S(1)} %copy-done.1, bf16[384,128]{1,0:T(8,128)(2,1)S(1)} %copy-done.2, bf16[480,128]{1,0:T(8,128)(2,1)S(1)} %collective-permute-done.2.refs_2_.refs_3_, ...), custom_call_target="tpu_custom_call" | custom-call | flops 1000 | bytes 1000 | tf_op jit(solution)/shard_map/pairs_0/pallas_call | solution.py:400
  22.7 0.3 collective-permute-done.10.refs_0_.refs_5_
  23.0 0.2 collective-permute-start.11
  23.2 1.4 %collective-permute-done.3.refs_1_.refs_5_ = bf16[384,128]{1,0:T(8,128)(2,1)S(1)} collective-permute-done((bf16[384,128]{1,0:T(8,128)(2,1)S(1)}, bf16[384,128]{1,0:T(8,128)(2,1)S(1)}, u32[]{:S(2)}, u32[]{:S(2)}) %collective-permute-start.3) | collective-permute-done | bytes 98336 | tf_op jit(solution)/shard_map/ppermute | solution.py:320
  24.6 0.1 collective-permute-start.4
  24.7 0.0 collective-permute-done.9.refs_3_
  24.7 0.0 collective-permute-done.11.refs_7_
  24.7 2.3 %pairs_1.1.refs_10_ = bf16[12,192,128]{2,1,0:T(8,128)(2,1)} custom-call(bf16[96,128]{1,0:T(8,128)(2,1)S(1)} %copy-done.1, bf16[768,128]{1,0:T(8,128)(2,1)S(1)} %pack.6.refs_1_, bf16[480,128]{1,0:T(8,128)(2,1)S(1)} %collective-permute-done.2.refs_2_.refs_3_, bf16[768,128]{1,0:T(8,128)(2,1)S(1)} %collective-permute-done.9.refs_3_, ...), custom_call_target="tpu_custom_call", output_to_operand_aliasing={{}: (10, {})} | custom-call | flops 1000 | bytes 1000 | tf_op jit(solution)/shard_map/pairs_1/pallas_call | solution.py:400
  27.0 0.0 collective-permute-done.4.refs_3_.refs_7_
  27.0 1.6 %pairs_3.1 = bf16[12,192,128]{2,1,0:T(8,128)(2,1)} custom-call(bf16[96,128]{1,0:T(8,128)(2,1)S(1)} %copy-done.1, bf16[384,128]{1,0:T(8,128)(2,1)S(1)} %collective-permute-done.1.refs_0_.refs_2_.refs_1_, bf16[480,128]{1,0:T(8,128)(2,1)S(1)} %collective-permute-done.2.refs_2_.refs_3_, ...), custom_call_target="tpu_custom_call", output_to_operand_aliasing={{}: (10, {})} | custom-call | flops 1000 | bytes 1000 | tf_op jit(solution)/shard_map/pairs_3/pallas_call | solution.py:400
  (4 shorter events, 0.1 us)
Async XLA Ops:
  3.8 16.8 %copy-start = (f32[1032,128]{1,0:T(8,128)S(1)}, f32[1032,128]{1,0:T(8,128)}, u32[]{:S(2)}) copy-start(f32[1032,128]{1,0:T(8,128)} %get-tuple-element.17.refs_8_) | copy-start | bytes 1585156
  3.9 9.3 %collective-permute-start = (bf16[384,128]{1,0:T(8,128)(2,1)}, bf16[384,128]{1,0:T(8,128)(2,1)S(1)}, u32[]{:S(2)}, u32[]{:S(2)}) collective-permute-start(bf16[384,128]{1,0:T(8,128)(2,1)} %get-tuple-element.14.refs_1_), channel_id=1, source_target_pairs={{0,8},{4,12},{8,0},{12,4},{1,9},{5,13},{9,1},{13,5},{2,10},{6,14},... | collective-permute-start | bytes 294920 | tf_op jit(solution)/shard_map/ppermute | solution.py:323
  8.0 7.5 %collective-permute-start.2 = (bf16[480,128]{1,0:T(8,128)(2,1)}, bf16[480,128]{1,0:T(8,128)(2,1)S(1)}, u32[]{:S(2)}, u32[]{:S(2)}) collective-permute-start(bf16[480,128]{1,0:T(8,128)(2,1)} %get-tuple-element.15), channel_id=1, source_target_pairs={{0,1},{1,0},{2,3},{3,2},{4,5},{5,4},{6,7},{7,6},{8,9},{9,8},{10,11... | collective-permute-start | bytes 368648 | tf_op jit(solution)/shard_map/ppermute | solution.py:320
  8.0 7.5 %collective-permute-start.6 = (bf16[384,128]{1,0:T(8,128)(2,1)}, bf16[384,128]{1,0:T(8,128)(2,1)S(1)}, u32[]{:S(2)}, u32[]{:S(2)}) collective-permute-start(bf16[384,128]{1,0:T(8,128)(2,1)} %get-tuple-element.14.refs_1_), channel_id=1, source_target_pairs={{0,2},{1,3},{2,0},{3,1},{4,6},{5,7},{6,4},{7,5},{8,10},{9,11},{10,... | collective-permute-start | bytes 294920 | tf_op jit(solution)/shard_map/ppermute | solution.py:320
  9.4 6.0 %collective-permute-start.8 = (bf16[384,128]{1,0:T(8,128)(2,1)}, bf16[384,128]{1,0:T(8,128)(2,1)S(1)}, u32[]{:S(2)}, u32[]{:S(2)}) collective-permute-start(bf16[384,128]{1,0:T(8,128)(2,1)} %get-tuple-element.14.refs_1_), channel_id=1, source_target_pairs={{0,4},{4,0},{8,12},{12,8},{1,5},{5,1},{9,13},{13,9},{2,6},{6,2},{1... | collective-permute-start | bytes 294920 | tf_op jit(solution)/shard_map/ppermute | solution.py:323
  13.1 5.5 %collective-permute-start.1 = (bf16[384,128]{1,0:T(8,128)(2,1)S(1)}, bf16[384,128]{1,0:T(8,128)(2,1)S(1)}, u32[]{:S(2)}, u32[]{:S(2)}) collective-permute-start(bf16[384,128]{1,0:T(8,128)(2,1)S(1)} %collective-permute-done.refs_1_), channel_id=1, source_target_pairs={{0,4},{4,0},{8,12},{12,8},{1,5},{5,1},{9,13},{13,9},{2,6},{6,2},{1... | collective-permute-start | bytes 294920 | tf_op jit(solution)/shard_map/ppermute | solution.py:323
  13.9 4.7 %collective-permute-start.5 = (bf16[192,128]{1,0:T(8,128)(2,1)}, bf16[192,128]{1,0:T(8,128)(2,1)S(1)}, u32[]{:S(2)}, u32[]{:S(2)}) collective-permute-start(bf16[192,128]{1,0:T(8,128)(2,1)} %get-tuple-element.16), channel_id=1, source_target_pairs={{0,2},{1,3},{2,0},{3,1},{4,6},{5,7},{6,4},{7,5},{8,10},{9,11},{10,... | collective-permute-start | bytes 147464 | tf_op jit(solution)/shard_map/ppermute | solution.py:320
  15.5 5.2 %copy-start.1 = (bf16[96,128]{1,0:T(8,128)(2,1)S(1)}, bf16[96,128]{1,0:T(8,128)(2,1)}, u32[]{:S(2)}) copy-start(bf16[96,128]{1,0:T(8,128)(2,1)} %get-tuple-element.13.refs_0_) | copy-start | bytes 73732
  15.5 5.2 %copy-start.2 = (bf16[384,128]{1,0:T(8,128)(2,1)S(1)}, bf16[384,128]{1,0:T(8,128)(2,1)}, u32[]{:S(2)}) copy-start(bf16[384,128]{1,0:T(8,128)(2,1)} %get-tuple-element.14.refs_1_) | copy-start | bytes 294916
  15.5 7.5 %collective-permute-start.10 = (bf16[768,128]{1,0:T(8,128)(2,1)S(1)}, bf16[768,128]{1,0:T(8,128)(2,1)S(1)}, u32[]{:S(2)}, u32[]{:S(2)}) collective-permute-start(bf16[768,128]{1,0:T(8,128)(2,1)S(1)} %pack.6.refs_1_), channel_id=1, source_target_pairs={{0,2},{1,3},{2,0},{3,1},{4,6},{5,7},{6,4},{7,5},{8,10},{9,11},{10,... | collective-permute-start | bytes 589832 | tf_op jit(solution)/shard_map/ppermute | solution.py:320
  18.7 2.0 %collective-permute-start.7 = (bf16[576,128]{1,0:T(8,128)(2,1)S(1)}, bf16[576,128]{1,0:T(8,128)(2,1)S(1)}, u32[]{:S(2)}, u32[]{:S(2)}) collective-permute-start(bf16[576,128]{1,0:T(8,128)(2,1)S(1)} %pack.5), channel_id=1, source_target_pairs={{0,1},{1,0},{2,3},{3,2},{4,5},{5,4},{6,7},{7,6},{8,9},{9,8},{10,11... | collective-permute-start | bytes 442376 | tf_op jit(solution)/shard_map/ppermute | solution.py:320
  18.8 5.8 %collective-permute-start.3 = (bf16[384,128]{1,0:T(8,128)(2,1)S(1)}, bf16[384,128]{1,0:T(8,128)(2,1)S(1)}, u32[]{:S(2)}, u32[]{:S(2)}) collective-permute-start(bf16[384,128]{1,0:T(8,128)(2,1)S(1)} %collective-permute-done.1.refs_0_.refs_2_.refs_1_), channel_id=1, source_target_pairs={{0,2},{1,3},{2,0},{3,1},{4,6},{5,7},{6,4},{7,5},{8,10},{9,11},{10,... | collective-permute-start | bytes 294920 | tf_op jit(solution)/shard_map/ppermute | solution.py:320
  20.5 4.2 %collective-permute-start.9 = (bf16[768,128]{1,0:T(8,128)(2,1)S(1)}, bf16[768,128]{1,0:T(8,128)(2,1)S(1)}, u32[]{:S(2)}, u32[]{:S(2)}) collective-permute-start(bf16[768,128]{1,0:T(8,128)(2,1)S(1)} %pack.6.refs_1_), channel_id=1, source_target_pairs={{0,1},{1,0},{2,3},{3,2},{4,5},{5,4},{6,7},{7,6},{8,9},{9,8},{10,11... | collective-permute-start | bytes 589832 | tf_op jit(solution)/shard_map/ppermute | solution.py:320
  23.0 1.7 %collective-permute-start.11 = (bf16[768,128]{1,0:T(8,128)(2,1)S(1)}, bf16[768,128]{1,0:T(8,128)(2,1)S(1)}, u32[]{:S(2)}, u32[]{:S(2)}) collective-permute-start(bf16[768,128]{1,0:T(8,128)(2,1)S(1)} %pack.7), channel_id=1, source_target_pairs={{0,1},{1,0},{2,3},{3,2},{4,5},{5,4},{6,7},{7,6},{8,9},{9,8},{10,11... | collective-permute-start | bytes 589832 | tf_op jit(solution)/shard_map/ppermute | solution.py:320
  24.6 2.4 %collective-permute-start.4 = (bf16[768,128]{1,0:T(8,128)(2,1)S(1)}, bf16[768,128]{1,0:T(8,128)(2,1)S(1)}, u32[]{:S(2)}, u32[]{:S(2)}) collective-permute-start(bf16[768,128]{1,0:T(8,128)(2,1)S(1)} %pack.4), channel_id=1, source_target_pairs={{0,1},{1,0},{2,3},{3,2},{4,5},{5,4},{6,7},{7,6},{8,9},{9,8},{10,11... | collective-permute-start | bytes 589832 | tf_op jit(solution)/shard_map/ppermute | solution.py:320

commit v8 on v7

v8 whole, which is shorter than its diff:
```python
import functools

import jax
import jax.numpy as jnp
from jax import lax
from jax.experimental import pallas as pl
from jax.experimental.pallas import tpu as pltpu
from jax.sharding import PartitionSpec as P

LANES = 128
RIGHT = -1
VMEM_LIMIT = 40 * 1024 * 1024
VMEM_ALL = 62 * 1024 * 1024


def iota(shape, dim):
    return lax.broadcasted_iota(jnp.int32, shape, dim)


def features_kernel(*refs, packs, parts, pieces):
    args, refs = refs[:9], refs[9:]
    outs, wf_hbm, refs = refs[: len(packs)], refs[len(packs)], refs[len(packs) + 1 :]
    held, (lo_ref, hi_ref, left_ref, turned_ref, rows_ref, right_ref, wf_ref, sems) = refs[:9], refs[9:]
    x_ref, gain_ref, bias_ref, lm_ref, lb_ref, rm_ref, rb_ref, w_ref, shift_ref = held
    seqs, residues, depth = x_ref.shape
    hidden = lm_ref.shape[0]
    per = LANES // hidden
    slots = LANES // seqs
    minor = hidden // slots
    groups = residues // per
    own = lax.axis_index("narrow")

    piece = seqs // pieces
    copies = [
        pltpu.make_async_copy(
            args[0].at[pl.ds(p * piece, piece)], x_ref.at[pl.ds(p * piece, piece)], sems.at[p]
        )
        for p in range(pieces)
    ]
    rest = [
        pltpu.make_async_copy(a, b, sems.at[pieces + i]) for i, (a, b) in enumerate(zip(args[1:], held[1:]))
    ]
    for copy in copies[:1] + rest[:2] + copies[1:] + rest[2:]:
        copy.start()
    free = pieces + len(rest)

    def norm(p):
        gain = gain_ref[...].reshape(1, depth)
        bias = bias_ref[...].reshape(1, depth)
        step = min(4, piece)
        for s in range(p * piece, (p + 1) * piece, step):
            x = x_ref[s : s + step].reshape(step * residues, depth).astype(jnp.float32)
            x = x - jnp.mean(x, axis=-1, keepdims=True)
            spread = jnp.mean(x * x, axis=-1, keepdims=True)
            x = x * lax.rsqrt(spread + 1e-05) * gain + bias
            rows = pl.ds(s * residues, step * residues)
            lo_ref[rows, :] = x[:, :LANES]
            hi_ref[rows, :] = x[:, LANES:]

    for copy in rest[:2]:
        copy.wait()
    for p in range(pieces - 1):
        copies[p].wait()
        norm(p)
    for copy in copies[-1:] + rest[2:]:
        copy.wait()
    count = w_ref.shape[0]
    wf_ref[:count] = w_ref[...].astype(jnp.float32)
    wf_ref[count:] = jnp.broadcast_to(shift_ref[...].reshape(1, -1), (8, shift_ref.shape[0]))
    norm(pieces - 1)

    column, row = iota((hidden, LANES), 1) % hidden, iota((hidden, LANES), 0)
    spread_l = (column == row).astype(jnp.float32)
    spread_r = (column == (row ^ (own * minor))).astype(jnp.float32)

    def widen(m, pick):
        return lax.dot_general(
            m, pick.astype(jnp.bfloat16), (((0,), (0,)), ((), ())),
            preferred_element_type=jnp.float32,
        )

    def widen_bias(b, pick):
        b = jnp.broadcast_to(b.reshape(1, hidden), (8, hidden))
        return jnp.dot(
            b, pick, precision=lax.Precision.HIGHEST, preferred_element_type=jnp.float32
        )[:1]

    weights = jnp.concatenate(
        [widen(lm_ref[...], spread_l), widen(rm_ref[...], spread_r)], axis=1
    )
    shift = jnp.concatenate(
        [widen_bias(lb_ref[...], spread_l), widen_bias(rb_ref[...], spread_r)], axis=1
    )
    place = iota((depth, 2 * LANES), 1) % LANES // hidden
    sends = [pltpu.make_async_copy(wf_ref, wf_hbm, sems.at[free])]
    sends[0].start()

    total = None
    for k in range(per):
        part = jnp.concatenate(
            [
                jnp.concatenate(
                    [half[pl.ds(g * per + k, seqs, stride=residues), :] for half in (lo_ref, hi_ref)],
                    axis=1,
                )
                for g in range(groups)
            ],
            axis=0,
        ).astype(jnp.bfloat16)
        placed = jnp.where(place == k, weights, 0.0).astype(jnp.bfloat16)
        term = jnp.dot(part, placed, preferred_element_type=jnp.float32)
        total = term if total is None else total + term
    total = total + shift
    left_ref[...] = total[:, :LANES].astype(left_ref.dtype)

    slot = iota((minor, LANES), 1) // seqs
    for block in range(groups // slots):
        turned_ref[...] = total[block * LANES : (block + 1) * LANES, LANES:].T
        for k in range(per):
            parts_of = [turned_ref[pl.ds(k * hidden + q * minor, minor), :] for q in range(slots)]
            for g in range(slots):
                out = None
                for q in range(slots):
                    moved = parts_of[q]
                    if q != g:
                        moved = pltpu.roll(moved, (q - g) % slots * seqs, axis=1)
                    out = moved if out is None else jnp.where(slot == q, moved, out)
                j = (block * slots + g) * per + k
                rows_ref[pl.ds(j, minor, stride=residues), :] = out
    right_ref[...] = rows_ref[...].astype(right_ref.dtype)

    mine = left_ref.shape[0] // parts
    for out, pack in zip(outs, packs):
        at = 0
        for item in pack:
            if item == RIGHT:
                rows = right_ref
            else:
                rows = left_ref.at[pl.ds(pl.multiple_of((own ^ item) * mine, 16), mine)]
            free += 1
            sends.append(
                pltpu.make_async_copy(rows, out.at[pl.ds(at, rows.shape[0])], sems.at[free])
            )
            sends[-1].start()
            at += rows.shape[0]
    for copy in sends:
        copy.wait()


def block_weights(wf_ref, wide_ref, *, parts, minor):
    cz = wf_ref.shape[1]
    hidden = parts * minor
    half = minor // 2
    rows_each = wide_ref.shape[0] // hidden // hidden
    own = lax.axis_index("narrow")
    wide_ref[...] = jnp.zeros_like(wide_ref)
    for e in range(hidden):
        rows = wf_ref[pl.ds(e ^ (own * minor), hidden, stride=hidden), :].astype(jnp.bfloat16)
        q, e2, t = e // minor, e % minor // half, e % half
        for k in range(rows_each):
            at = ((((q * half + t) * 2 + e2) * rows_each) + k) * hidden
            wide_ref[at : at + hidden, k * cz : (k + 1) * cz] = rows


def pack_kernel(*refs, count):
    out_ref, at = refs[-1], 0
    for ref in refs[:count]:
        out_ref[at : at + ref.shape[0]] = ref[...]
        at += ref.shape[0]


def spread_left(left_of, spread_ref, *, parts):
    seqs = LANES // parts
    low = iota((seqs, LANES), 1) < LANES // 2
    zero = jnp.zeros((seqs, LANES), jnp.float32)
    for m in range(parts):
        left = left_of(m)
        for g in range(left.shape[0] // seqs):
            rows = left[g * seqs : (g + 1) * seqs].astype(jnp.float32)
            turned = pltpu.roll(rows, LANES // 2, axis=1)
            for half, (first, second) in enumerate(((rows, turned), (turned, rows))):
                lanes = pl.ds((2 * g + half) * LANES, LANES)
                spread_ref[m, 0, :, lanes] = jnp.where(low, first, zero).astype(spread_ref.dtype)
                spread_ref[m, 1, :, lanes] = jnp.where(low, zero, second).astype(spread_ref.dtype)


def pair_rows(spread_ref, right_of, wide_ref, shift, outer_ref, store, *, wides, parts, minor, seqs_total):
    cz = shift.shape[1]
    half = minor // 2
    seqs = LANES // parts
    halves = spread_ref.shape[3] // LANES
    residues = right_of(0, 0).shape[0] // minor
    cols = wides * residues
    slot = iota((minor * residues, LANES), 1) // seqs
    for q in range(parts):
        left = jnp.concatenate([spread_ref[q ^ k, i] for i in range(2) for k in range(parts)], axis=0)
        for d in range(wides):
            right = None
            for k in range(parts):
                chunk = right_of(d, q ^ k)
                right = chunk if right is None else jnp.where(slot == k, chunk, right)
            right = jnp.concatenate([right[: half * residues], right[half * residues :]], axis=1)
            outer = jnp.dot(right, left, preferred_element_type=jnp.float32).astype(jnp.bfloat16)
            for t in range(half):
                for g in range(halves):
                    outer_ref[
                        pl.ds(g * cols + d * residues, residues),
                        (q * half + t) * LANES : (q * half + t + 1) * LANES,
                    ] = outer[t * residues : (t + 1) * residues, g * LANES : (g + 1) * LANES]

    pairs = jnp.dot(outer_ref[...], wide_ref[...], preferred_element_type=jnp.float32)
    rows_each = wide_ref.shape[1] // cz
    for g in range(halves):
        for k in range(rows_each):
            pair = pairs[g * cols : (g + 1) * cols, k * cz : (k + 1) * cz]
            store(g * rows_each + k, pair * (1.0 / seqs_total) + shift)


def pair_kernel(*refs, operands, rights, blocks, earlier, lefts=None, **sizes):
    parts, minor = sizes["parts"], sizes["minor"]
    inputs, refs = refs[:operands], refs[operands:]
    if lefts is not None:
        wf_ref, done_ref, spread_ref, wide_ref, shift_ref, outer_ref = refs
        own_rows = done_ref.shape[0]
        block_weights(wf_ref, wide_ref, parts=parts, minor=minor)
        shift_ref[...] = wf_ref[wf_ref.shape[0] - 8 :]
        count = own_rows * minor
        spread_left(lambda m: inputs[lefts[m][0]][lefts[m][1] : lefts[m][1] + count, :], spread_ref, parts=parts)
    elif not earlier:
        spread_ref, wide_ref, shift_ref, done_ref, outer_ref = refs
    else:
        spread_ref, wide_ref, shift_ref = refs[:3]
        before, (out_hbm, outer_ref, done_ref, sems) = refs[3 : 3 + len(earlier)], refs[3 + len(earlier) :]
    residues = done_ref.shape[1] // len(blocks)
    copies = []

    def write(ref, places):
        for d, block in enumerate(places):
            at = pl.multiple_of((lax.axis_index("wide") ^ block) * residues, 16)
            copies.append(
                pltpu.make_async_copy(
                    ref.at[:, pl.ds(d * residues, residues), :],
                    out_hbm.at[:, pl.ds(at, residues), :],
                    sems.at[len(copies)],
                )
            )
            copies[-1].start()

    if earlier:
        for ref, places in zip(before, earlier):
            write(ref, places)

    def right_of(d, m):
        ref, at = rights[m]
        at += d * minor * residues
        return inputs[ref][at : at + minor * residues, :]

    def store(row, pair):
        done_ref[row] = pair.astype(done_ref.dtype)

    pair_rows(spread_ref, right_of, wide_ref, shift_ref[:1], outer_ref, store, wides=len(blocks), **sizes)
    if earlier:
        write(done_ref, blocks)
        for copy in copies:
            copy.wait()


def pair_blocks_kernel(*refs, wides, parts, minor, **sizes):
    left_refs, (right_ref, wf_ref, out_ref, spread_ref, wide_ref, outer_ref) = refs[:parts], refs[parts:]

    @pl.when(pl.program_id(0) == 0)
    def _():
        block_weights(wf_ref, wide_ref, parts=parts, minor=minor)
        spread_left(lambda m: left_refs[m][...], spread_ref, parts=parts)

    def store(row, pair):
        out_ref[row] = pair.astype(out_ref.dtype)

    pair_rows(
        spread_ref, lambda d, m: right_ref[d, m],
        wide_ref, wf_ref[wf_ref.shape[0] - 8 :][:1], outer_ref, store,
        wides=wides, parts=parts, minor=minor, **sizes,
    )


def on_device(wide, narrow, x, gain, bias, lm, lb, rm, rb, w, shift):
    seqs, residues, depth = x.shape
    hidden = lm.shape[1]
    cz = w.shape[1]
    per = LANES // hidden
    slots = LANES // seqs
    minor = hidden // slots
    own_rows = residues // narrow
    groups = own_rows // per
    pieces = 4
    hbm = pl.BlockSpec(memory_space=pltpu.HBM)
    vmem = pl.BlockSpec(memory_space=pltpu.VMEM)
    params = pltpu.CompilerParams(vmem_limit_bytes=VMEM_LIMIT)
    direct = wide == 4 and narrow == 4
    if direct:
        packs = ((0,), (RIGHT,), (1, RIGHT), (2, 3, RIGHT))
    else:
        packs = tuple((m,) for m in range(narrow)) + ((RIGHT,),)
    left_count, right_count = groups * seqs, minor * residues
    args = (x, gain, bias, lm.T, lb, rm.T, rb, w, shift)
    *made, w = pl.pallas_call(
        functools.partial(features_kernel, packs=packs, parts=narrow, pieces=pieces),
        out_shape=tuple(
            jax.ShapeDtypeStruct(
                (sum(right_count if i == RIGHT else left_count for i in pack), LANES), jnp.bfloat16
            )
            for pack in packs
        )
        + (jax.ShapeDtypeStruct((w.shape[0] + 8, cz), jnp.float32),),
        in_specs=[hbm] * len(args),
        out_specs=(hbm,) * (len(packs) + 1),
        scratch_shapes=[pltpu.VMEM(a.shape, a.dtype) for a in args]
        + [
            pltpu.VMEM((seqs * residues, LANES), jnp.float32),
            pltpu.VMEM((seqs * residues, LANES), jnp.float32),
            pltpu.VMEM((residues // per * seqs, LANES), jnp.bfloat16),
            pltpu.VMEM((LANES, LANES), jnp.float32),
            pltpu.VMEM((minor * residues, LANES), jnp.float32),
            pltpu.VMEM((minor * residues, LANES), jnp.bfloat16),
            pltpu.VMEM((w.shape[0] + 8, cz), jnp.float32),
            pltpu.SemaphoreType.DMA((pieces + len(args) + sum(len(pack) for pack in packs),)),
        ],
        compiler_params=pltpu.CompilerParams(vmem_limit_bytes=VMEM_ALL),
        name="features",
    )(*args)

    def across(a, m):
        return lax.ppermute(a, "narrow", [(i, i ^ m) for i in range(narrow)])

    def along(a, d):
        return lax.ppermute(a, "wide", [(i, i ^ d) for i in range(wide)])

    sizes = dict(parts=narrow, minor=minor, seqs_total=seqs * narrow)
    out_shape = jax.ShapeDtypeStruct((own_rows, wide * residues, cz), jnp.bfloat16)
    if direct:
        return pairs_by_block(made, across, along, w, out_shape, residues, sizes, params)

    lefts = [made[0]] + [across(made[m], m) for m in range(1, narrow)]
    every = lax.all_gather(made[narrow], ("wide", "narrow"), axis=0, tiled=False)
    every = every.reshape(wide, narrow, right_count, LANES)
    every = jnp.take(every, lax.axis_index("narrow") ^ jnp.arange(narrow), axis=1)
    block = wide
    while block % 2 == 0 and block * residues > 192:
        block //= 2
    cols = block * residues
    return pl.pallas_call(
        functools.partial(pair_blocks_kernel, wides=block, **sizes),
        grid=(wide // block,),
        in_specs=[pl.BlockSpec((left_count, LANES), lambda b: (0, 0))] * narrow
        + [
            pl.BlockSpec((block, narrow, right_count, LANES), lambda b: (b, 0, 0, 0)),
            pl.BlockSpec(w.shape, lambda b: (0, 0)),
        ],
        out_specs=pl.BlockSpec((own_rows, cols, cz), lambda b: (0, b, 0)),
        out_shape=out_shape,
        scratch_shapes=[
            pltpu.VMEM((narrow, 2, seqs, 2 * groups * LANES), jnp.bfloat16),
            pltpu.VMEM((hidden * LANES // 2, 2 * cz), jnp.bfloat16),
            pltpu.VMEM((2 * groups * cols, hidden * LANES // 2), jnp.bfloat16),
        ],
        compiler_params=params,
        name="pairs",
    )(*lefts, every, w)


def pairs_by_block(made, across, along, w, out_shape, residues, sizes, params):
    left_own, right, to_core, to_chip = made
    left_count, right_count = left_own.shape[0], right.shape[0]
    hbm = pl.BlockSpec(memory_space=pltpu.HBM)
    vmem = pl.BlockSpec(memory_space=pltpu.VMEM)
    own_rows, _, cz = out_shape.shape
    narrow = sizes["parts"]
    hidden = narrow * sizes["minor"]
    groups = own_rows * hidden // LANES

    def pack(*chunks, after):
        return pl.pallas_call(
            functools.partial(pack_kernel, count=len(chunks)),
            out_shape=jax.ShapeDtypeStruct((sum(c.shape[0] for c in chunks), LANES), jnp.bfloat16),
            in_specs=[vmem] * (len(chunks) + len(after)),
            out_specs=vmem,
            compiler_params=params,
            name="pack",
        )(*chunks, *after)

    def pairs(rights, blocks, *shared, lefts=None, earlier=()):
        operands, places = [], []
        for chunks in (rights, lefts or ()):
            places.append([])
            for chunk, at in chunks:
                places[-1].append((len(operands), at))
                operands.append(chunk)
        count = len(operands)
        operands += shared
        cols = len(blocks) * residues
        done = jax.ShapeDtypeStruct((own_rows, cols, cz), jnp.bfloat16)
        shapes, outs = [done], [vmem]
        scratch = [pltpu.VMEM((2 * groups * cols, hidden * LANES // 2), jnp.bfloat16)]
        if lefts is not None:
            shapes += [
                jax.ShapeDtypeStruct((narrow, 2, LANES // narrow, 2 * groups * LANES), jnp.bfloat16),
                jax.ShapeDtypeStruct((hidden * LANES // 2, 2 * cz), jnp.bfloat16),
                jax.ShapeDtypeStruct((8, cz), jnp.float32),
            ]
            outs += [vmem] * 3
        if earlier:
            operands += [ref for ref, _ in earlier]
            shapes, outs = [out_shape], [hbm]
            scratch += [
                pltpu.VMEM(done.shape, done.dtype),
                pltpu.SemaphoreType.DMA((len(blocks) + sum(len(b) for _, b in earlier),)),
            ]
        return pl.pallas_call(
            functools.partial(
                pair_kernel, operands=count, rights=places[0], blocks=blocks,
                earlier=[b for _, b in earlier], lefts=lefts and places[1], **sizes,
            ),
            out_shape=shapes,
            in_specs=[vmem] * len(operands),
            out_specs=outs,
            scratch_shapes=scratch,
            compiler_params=params,
            cost_estimate=pl.CostEstimate(flops=1000, bytes_accessed=1000, transcendentals=0),
            name=f"pairs_{blocks[0]}",
        )(*operands)

    far = along(right, 2)
    near = along(right, 1)
    last = along(far, 1)
    chip = across(to_chip, 2)
    core = across(to_core, 1)
    middle = pack(near, far, after=(chip, core))
    beside = across(middle, 1)
    both = across(pack(chip, after=(last,)), 1)
    lefts = ((left_own, 0), (core, 0), (chip, 0), (both, left_count))
    own = ((right, 0), (core, left_count), (chip, 2 * left_count), (both, 2 * left_count))
    first, *shared = pairs(own, (0,), w, lefts=lefts)

    other = across(middle, 2)
    onward = across(pack(other, after=shared[1:2]), 1)
    (second,) = pairs(((middle, 0), (beside, 0), (other, 0), (onward, 0)), (1, 2), *shared)

    other = across(last, 2)
    both = across(pack(last, other, after=()), 1)
    (out,) = pairs(
        ((last, 0), (both, 0), (other, 0), (both, right_count)), (3,), *shared,
        earlier=((first, (0,)), (second, (1, 2))),
    )
    return out


def solution(mesh):
    in_specs = (P(("groups", "narrow"), "wide", None), P(), P(), P(), P(), P(), P(), P(), P())
    out_specs = P(("groups", "wide", "narrow"), None, None)
    return jax.shard_map(
        functools.partial(on_device, mesh.shape["wide"], mesh.shape["narrow"]),
        mesh=mesh,
        in_specs=in_specs,
        out_specs=out_specs,
        check_vma=False,
    )
```

time: 28.8 us -> 27.9 us (0.969)
  waiting for transfers between devices: 6.31 us -> 8.17 us
  Pallas kernels: 9.9 us -> 8.52 us
  starting transfers between devices: 12.3 us -> 11 us
    ppermute x3, waiting for transfers between devices: 2.1 us -> 4.89 us  [along(): return lax.ppermute(a, 'wide', [(i, i ^ d) for i in range(wide)])]
    pallas_call x3, Pallas kernels: 6.01 us -> 4.67 us  [pairs(): pl.pallas_call(functools.partial(pair_kernel, operands=count, rights=plac...]
    ppermute x9 -> x8, starting transfers between devices: 5.78 us -> 4.46 us  [across(): return lax.ppermute(a, 'narrow', [(i, i ^ m) for i in range(narrow)])]
    ppermute x9 -> x8, waiting for transfers between devices: 4.21 us -> 3.28 us  [across(): return lax.ppermute(a, 'narrow', [(i, i ^ m) for i in range(narrow)])]
  transfers between devices with their start and end apart: 12 -> 11, of which waited for: 4 -> 6; matrix products, arithmetic and copies ran while one was open for 0% -> 0% of each run, Pallas kernels for 16% -> 11%
where the time goes in v8:
time: 27.9 us; the launch traced here: 27.8 us
  starting transfers between devices  11 us (39%)
  Pallas kernels  8.52 us (31%)
  waiting for transfers between devices  8.17 us (29%)
    ppermute x3, starting transfers between devices, along(): return lax.ppermute(a, 'wide', [(i, i ^ d) for i in range(wide)])  6.52 us
    ppermute x3, waiting for transfers between devices, along(): return lax.ppermute(a, 'wide', [(i, i ^ d) for i in range(wide)])  4.89 us
    pallas_call x3, Pallas kernels, pairs(): pl.pallas_call(functools.partial(pair_kernel, operands=count, rights=plac...  4.67 us
    ppermute x8, starting transfers between devices, across(): return lax.ppermute(a, 'narrow', [(i, i ^ m) for i in range(narrow)])  4.46 us
    pallas_call x1, Pallas kernels, on_device(): pl.pallas_call(functools.partial(features_kernel, packs=packs, parts=narr...  3.8 us
    ppermute x8, waiting for transfers between devices, across(): return lax.ppermute(a, 'narrow', [(i, i ^ m) for i in range(narrow)])  3.28 us
  transfers between devices with their start and end apart: 11, of which 6 were waited for; matrix products, arithmetic and copies ran while one was open for 0% of the time, Pallas kernels for 11%

profile of v8, /device:TPU:0, one launch (start us, length us, event | category | flops | bytes accessed | tf_op | source)
XLA Modules:
  0.0 27.8 jit_solution(13922639029406983978)
XLA Ops:
  0.0 3.8 %features.1 = (bf16[96,128]{1,0:T(8,128)(2,1)}, bf16[384,128]{1,0:T(8,128)(2,1)}, bf16[480,128]{1,0:T(8,128)(2,1)}, bf16[576,128]{1,0:T(8,128)(2,1)}, f32[1032,128]{1,0:T(8,128)}) custom-call(bf16[32,48,256]{2,1,0:T(8,128)(2,1)} %refs_0_.1, f32[256]{0:T(256)} %refs_1_.1, f32[256]{0:T(256)} %refs_2_.1, bf16[32,256]{1,0:T(8,128)(2,1)} %bitcast.2, f32[32]{0:T(128)} %refs_4_.1, ...), custom_call_target="tpu_custom_call" | custom-call | tf_op jit(solution)/shard_map/features/pallas_call | solution.py:306
  3.8 4.1 %collective-permute-start = (bf16[384,128]{1,0:T(8,128)(2,1)}, bf16[384,128]{1,0:T(8,128)(2,1)S(1)}, u32[]{:S(2)}, u32[]{:S(2)}) collective-permute-start(bf16[384,128]{1,0:T(8,128)(2,1)} %get-tuple-element.14.refs_0_), channel_id=1, source_target_pairs={{0,8},{4,12},{8,0},{12,4},{1,9},{5,13},{9,1},{13,5},{2,10},{6,14},... | collective-permute-start | bytes 294920 | tf_op jit(solution)/shard_map/ppermute | solution.py:336
  7.9 1.5 %collective-permute-start.5 = (bf16[576,128]{1,0:T(8,128)(2,1)}, bf16[576,128]{1,0:T(8,128)(2,1)S(1)}, u32[]{:S(2)}, u32[]{:S(2)}) collective-permute-start(bf16[576,128]{1,0:T(8,128)(2,1)} %get-tuple-element.16), channel_id=1, source_target_pairs={{0,2},{1,3},{2,0},{3,1},{4,6},{5,7},{6,4},{7,5},{8,10},{9,11},{10,... | collective-permute-start | bytes 442376 | tf_op jit(solution)/shard_map/ppermute | solution.py:333
  9.4 0.0 copy-start
  9.4 0.0 collective-permute-start.4
  9.4 1.6 %collective-permute-start.7 = (bf16[384,128]{1,0:T(8,128)(2,1)}, bf16[384,128]{1,0:T(8,128)(2,1)S(1)}, u32[]{:S(2)}, u32[]{:S(2)}) collective-permute-start(bf16[384,128]{1,0:T(8,128)(2,1)} %get-tuple-element.14.refs_0_), channel_id=1, source_target_pairs={{0,4},{4,0},{8,12},{12,8},{1,5},{5,1},{9,13},{13,9},{2,6},{6,2},{1... | collective-permute-start | bytes 294920 | tf_op jit(solution)/shard_map/ppermute | solution.py:336
  11.0 2.1 %collective-permute-done.refs_1_ = bf16[384,128]{1,0:T(8,128)(2,1)S(1)} collective-permute-done((bf16[384,128]{1,0:T(8,128)(2,1)}, bf16[384,128]{1,0:T(8,128)(2,1)S(1)}, u32[]{:S(2)}, u32[]{:S(2)}) %collective-permute-start) | collective-permute-done | bytes 98336 | tf_op jit(solution)/shard_map/ppermute | solution.py:336
  13.0 0.8 %collective-permute-start.1 = (bf16[384,128]{1,0:T(8,128)(2,1)S(1)}, bf16[384,128]{1,0:T(8,128)(2,1)S(1)}, u32[]{:S(2)}, u32[]{:S(2)}) collective-permute-start(bf16[384,128]{1,0:T(8,128)(2,1)S(1)} %collective-permute-done.refs_1_), channel_id=1, source_target_pairs={{0,4},{4,0},{8,12},{12,8},{1,5},{5,1},{9,13},{13,9},{2,6},{6,2},{1... | collective-permute-start | bytes 294920 | tf_op jit(solution)/shard_map/ppermute | solution.py:336
  13.9 1.4 %collective-permute-done.7.refs_0_ = bf16[384,128]{1,0:T(8,128)(2,1)S(1)} collective-permute-done((bf16[384,128]{1,0:T(8,128)(2,1)}, bf16[384,128]{1,0:T(8,128)(2,1)S(1)}, u32[]{:S(2)}, u32[]{:S(2)}) %collective-permute-start.7) | collective-permute-done | bytes 98336 | tf_op jit(solution)/shard_map/ppermute | solution.py:336
  15.3 0.0 collective-permute-done.4.refs_1_.refs_5_.refs_3_
  15.3 0.0 collective-permute-done.5.refs_0_.refs_2_.refs_6_
  15.3 0.0 copy-start.1
  15.3 0.0 copy-start.2
  15.3 0.9 %collective-permute-start.9 = (bf16[768,128]{1,0:T(8,128)(2,1)S(1)}, bf16[768,128]{1,0:T(8,128)(2,1)S(1)}, u32[]{:S(2)}, u32[]{:S(2)}) collective-permute-start(bf16[768,128]{1,0:T(8,128)(2,1)S(1)} %pack.6.refs_0_), channel_id=1, source_target_pairs={{0,2},{1,3},{2,0},{3,1},{4,6},{5,7},{6,4},{7,5},{8,10},{9,11},{10,... | collective-permute-start | bytes 589832 | tf_op jit(solution)/shard_map/ppermute | solution.py:333
  16.2 1.4 %collective-permute-done.1.refs_0_.refs_1_ = bf16[384,128]{1,0:T(8,128)(2,1)S(1)} collective-permute-done((bf16[384,128]{1,0:T(8,128)(2,1)S(1)}, bf16[384,128]{1,0:T(8,128)(2,1)S(1)}, u32[]{:S(2)}, u32[]{:S(2)}) %collective-permute-start.1) | collective-permute-done | bytes 98336 | tf_op jit(solution)/shard_map/ppermute | solution.py:336
  17.7 0.1 collective-permute-start.6
  17.8 1.7 %collective-permute-start.2 = (bf16[384,128]{1,0:T(8,128)(2,1)S(1)}, bf16[384,128]{1,0:T(8,128)(2,1)S(1)}, u32[]{:S(2)}, u32[]{:S(2)}) collective-permute-start(bf16[384,128]{1,0:T(8,128)(2,1)S(1)} %collective-permute-done.1.refs_0_.refs_1_), channel_id=1, source_target_pairs={{0,2},{1,3},{2,0},{3,1},{4,6},{5,7},{6,4},{7,5},{8,10},{9,11},{10,... | collective-permute-start | bytes 294920 | tf_op jit(solution)/shard_map/ppermute | solution.py:333
  19.4 0.2 collective-permute-start.8
  19.6 0.0 collective-permute-done.6.refs_3_.refs_7_
  19.6 0.0 copy-done
  19.6 0.0 copy-done.1
  19.6 0.0 copy-done.2
  19.6 1.5 %pairs_0.1 = (bf16[12,48,128]{2,1,0:T(8,128)(2,1)S(1)}, bf16[4,2,32,768]{3,2,1,0:T(8,128)(2,1)S(1)}, bf16[2048,256]{1,0:T(8,128)(2,1)S(1)}, f32[8,128]{1,0:T(8,128)S(1)}) custom-call(bf16[384,128]{1,0:T(8,128)(2,1)S(1)} %copy-done.1, bf16[480,128]{1,0:T(8,128)(2,1)S(1)} %collective-permute-done.4.refs_1_.refs_5_.refs_3_, ...), custom_call_target="tpu_custom_call" | custom-call | flops 1000 | bytes 1000 | tf_op jit(solution)/shard_map/pairs_0/pallas_call | solution.py:418
  21.1 1.9 %collective-permute-done.9.refs_0_.refs_2_ = bf16[768,128]{1,0:T(8,128)(2,1)S(1)} collective-permute-done((bf16[768,128]{1,0:T(8,128)(2,1)S(1)}, bf16[768,128]{1,0:T(8,128)(2,1)S(1)}, u32[]{:S(2)}, u32[]{:S(2)}) %collective-permute-start.9) | collective-permute-done | bytes 196640 | tf_op jit(solution)/shard_map/ppermute | solution.py:333
  23.1 0.1 collective-permute-start.10
  23.1 1.0 %collective-permute-done.2.refs_1_.refs_2_ = bf16[384,128]{1,0:T(8,128)(2,1)S(1)} collective-permute-done((bf16[384,128]{1,0:T(8,128)(2,1)S(1)}, bf16[384,128]{1,0:T(8,128)(2,1)S(1)}, u32[]{:S(2)}, u32[]{:S(2)}) %collective-permute-start.2) | collective-permute-done | bytes 98336 | tf_op jit(solution)/shard_map/ppermute | solution.py:333
  24.1 0.1 collective-permute-start.3
  24.2 0.0 collective-permute-done.8.refs_1_
  24.2 0.4 %collective-permute-done.10.refs_3_ = bf16[768,128]{1,0:T(8,128)(2,1)S(1)} collective-permute-done((bf16[768,128]{1,0:T(8,128)(2,1)S(1)}, bf16[768,128]{1,0:T(8,128)(2,1)S(1)}, u32[]{:S(2)}, u32[]{:S(2)}) %collective-permute-start.10) | collective-permute-done | bytes 196640 | tf_op jit(solution)/shard_map/ppermute | solution.py:333
  24.6 1.6 %pairs_1.1.refs_8_ = bf16[12,96,128]{2,1,0:T(8,128)(2,1)S(1)} custom-call(bf16[768,128]{1,0:T(8,128)(2,1)S(1)} %pack.6.refs_0_, bf16[768,128]{1,0:T(8,128)(2,1)S(1)} %collective-permute-done.8.refs_1_, bf16[768,128]{1,0:T(8,128)(2,1)S(1)} %collective-permute-done.9.refs_0_.refs_2_, bf16[768,128]{1,0:T(8,128)(2,1)S(1)} %collective-permute-done.10.refs_3_, ...), custom_call_target="tpu_custom_call" | custom-call | flops 1000 | bytes 1000 | tf_op jit(solution)/shard_map/pairs_1/pallas_call | solution.py:418
  26.2 0.0 collective-permute-done.3.refs_1_.refs_3_
  26.2 1.6 %pairs_3.1 = bf16[12,192,128]{2,1,0:T(8,128)(2,1)} custom-call(bf16[384,128]{1,0:T(8,128)(2,1)S(1)} %collective-permute-done.1.refs_0_.refs_1_, bf16[768,128]{1,0:T(8,128)(2,1)S(1)} %collective-permute-done.3.refs_1_.refs_3_, bf16[384,128]{1,0:T(8,128)(2,1)S(1)} %collective-permute-done.2.refs_1_.refs_2_, ...), custom_call_target="tpu_custom_call" | custom-call | flops 1000 | bytes 1000 | tf_op jit(solution)/shard_map/pairs_3/pallas_call | solution.py:418
  (4 shorter events, 0.1 us)
Async XLA Ops:
  3.8 9.2 %collective-permute-start = (bf16[384,128]{1,0:T(8,128)(2,1)}, bf16[384,128]{1,0:T(8,128)(2,1)S(1)}, u32[]{:S(2)}, u32[]{:S(2)}) collective-permute-start(bf16[384,128]{1,0:T(8,128)(2,1)} %get-tuple-element.14.refs_0_), channel_id=1, source_target_pairs={{0,8},{4,12},{8,0},{12,4},{1,9},{5,13},{9,1},{13,5},{2,10},{6,14},... | collective-permute-start | bytes 294920 | tf_op jit(solution)/shard_map/ppermute | solution.py:336
  7.9 7.4 %collective-permute-start.5 = (bf16[576,128]{1,0:T(8,128)(2,1)}, bf16[576,128]{1,0:T(8,128)(2,1)S(1)}, u32[]{:S(2)}, u32[]{:S(2)}) collective-permute-start(bf16[576,128]{1,0:T(8,128)(2,1)} %get-tuple-element.16), channel_id=1, source_target_pairs={{0,2},{1,3},{2,0},{3,1},{4,6},{5,7},{6,4},{7,5},{8,10},{9,11},{10,... | collective-permute-start | bytes 442376 | tf_op jit(solution)/shard_map/ppermute | solution.py:333
  9.4 10.2 %copy-start = (f32[1032,128]{1,0:T(8,128)S(1)}, f32[1032,128]{1,0:T(8,128)}, u32[]{:S(2)}) copy-start(f32[1032,128]{1,0:T(8,128)} %get-tuple-element.18.refs_8_) | copy-start | bytes 1585156
  9.4 5.9 %collective-permute-start.4 = (bf16[480,128]{1,0:T(8,128)(2,1)}, bf16[480,128]{1,0:T(8,128)(2,1)S(1)}, u32[]{:S(2)}, u32[]{:S(2)}) collective-permute-start(bf16[480,128]{1,0:T(8,128)(2,1)} %get-tuple-element.15), channel_id=1, source_target_pairs={{0,1},{1,0},{2,3},{3,2},{4,5},{5,4},{6,7},{7,6},{8,9},{9,8},{10,11... | collective-permute-start | bytes 368648 | tf_op jit(solution)/shard_map/ppermute | solution.py:333
  9.4 5.9 %collective-permute-start.7 = (bf16[384,128]{1,0:T(8,128)(2,1)}, bf16[384,128]{1,0:T(8,128)(2,1)S(1)}, u32[]{:S(2)}, u32[]{:S(2)}) collective-permute-start(bf16[384,128]{1,0:T(8,128)(2,1)} %get-tuple-element.14.refs_0_), channel_id=1, source_target_pairs={{0,4},{4,0},{8,12},{12,8},{1,5},{5,1},{9,13},{13,9},{2,6},{6,2},{1... | collective-permute-start | bytes 294920 | tf_op jit(solution)/shard_map/ppermute | solution.py:336
  13.0 4.6 %collective-permute-start.1 = (bf16[384,128]{1,0:T(8,128)(2,1)S(1)}, bf16[384,128]{1,0:T(8,128)(2,1)S(1)}, u32[]{:S(2)}, u32[]{:S(2)}) collective-permute-start(bf16[384,128]{1,0:T(8,128)(2,1)S(1)} %collective-permute-done.refs_1_), channel_id=1, source_target_pairs={{0,4},{4,0},{8,12},{12,8},{1,5},{5,1},{9,13},{13,9},{2,6},{6,2},{1... | collective-permute-start | bytes 294920 | tf_op jit(solution)/shard_map/ppermute | solution.py:336
  15.3 4.3 %copy-start.1 = (bf16[384,128]{1,0:T(8,128)(2,1)S(1)}, bf16[384,128]{1,0:T(8,128)(2,1)}, u32[]{:S(2)}) copy-start(bf16[384,128]{1,0:T(8,128)(2,1)} %get-tuple-element.14.refs_0_) | copy-start | bytes 294916
  15.3 4.3 %copy-start.2 = (bf16[96,128]{1,0:T(8,128)(2,1)S(1)}, bf16[96,128]{1,0:T(8,128)(2,1)}, u32[]{:S(2)}) copy-start(bf16[96,128]{1,0:T(8,128)(2,1)} %get-tuple-element.17.refs_4_) | copy-start | bytes 73732
  15.3 7.7 %collective-permute-start.9 = (bf16[768,128]{1,0:T(8,128)(2,1)S(1)}, bf16[768,128]{1,0:T(8,128)(2,1)S(1)}, u32[]{:S(2)}, u32[]{:S(2)}) collective-permute-start(bf16[768,128]{1,0:T(8,128)(2,1)S(1)} %pack.6.refs_0_), channel_id=1, source_target_pairs={{0,2},{1,3},{2,0},{3,1},{4,6},{5,7},{6,4},{7,5},{8,10},{9,11},{10,... | collective-permute-start | bytes 589832 | tf_op jit(solution)/shard_map/ppermute | solution.py:333
  17.7 1.9 %collective-permute-start.6 = (bf16[576,128]{1,0:T(8,128)(2,1)S(1)}, bf16[576,128]{1,0:T(8,128)(2,1)S(1)}, u32[]{:S(2)}, u32[]{:S(2)}) collective-permute-start(bf16[576,128]{1,0:T(8,128)(2,1)S(1)} %pack.5), channel_id=1, source_target_pairs={{0,1},{1,0},{2,3},{3,2},{4,5},{5,4},{6,7},{7,6},{8,9},{9,8},{10,11... | collective-permute-start | bytes 442376 | tf_op jit(solution)/shard_map/ppermute | solution.py:333
  17.8 6.3 %collective-permute-start.2 = (bf16[384,128]{1,0:T(8,128)(2,1)S(1)}, bf16[384,128]{1,0:T(8,128)(2,1)S(1)}, u32[]{:S(2)}, u32[]{:S(2)}) collective-permute-start(bf16[384,128]{1,0:T(8,128)(2,1)S(1)} %collective-permute-done.1.refs_0_.refs_1_), channel_id=1, source_target_pairs={{0,2},{1,3},{2,0},{3,1},{4,6},{5,7},{6,4},{7,5},{8,10},{9,11},{10,... | collective-permute-start | bytes 294920 | tf_op jit(solution)/shard_map/ppermute | solution.py:333
  19.4 4.8 %collective-permute-start.8 = (bf16[768,128]{1,0:T(8,128)(2,1)S(1)}, bf16[768,128]{1,0:T(8,128)(2,1)S(1)}, u32[]{:S(2)}, u32[]{:S(2)}) collective-permute-start(bf16[768,128]{1,0:T(8,128)(2,1)S(1)} %pack.6.refs_0_), channel_id=1, source_target_pairs={{0,1},{1,0},{2,3},{3,2},{4,5},{5,4},{6,7},{7,6},{8,9},{9,8},{10,11... | collective-permute-start | bytes 589832 | tf_op jit(solution)/shard_map/ppermute | solution.py:333
  23.1 1.5 %collective-permute-start.10 = (bf16[768,128]{1,0:T(8,128)(2,1)S(1)}, bf16[768,128]{1,0:T(8,128)(2,1)S(1)}, u32[]{:S(2)}, u32[]{:S(2)}) collective-permute-start(bf16[768,128]{1,0:T(8,128)(2,1)S(1)} %pack.7), channel_id=1, source_target_pairs={{0,1},{1,0},{2,3},{3,2},{4,5},{5,4},{6,7},{7,6},{8,9},{9,8},{10,11... | collective-permute-start | bytes 589832 | tf_op jit(solution)/shard_map/ppermute | solution.py:333
  24.1 2.1 %collective-permute-start.3 = (bf16[768,128]{1,0:T(8,128)(2,1)S(1)}, bf16[768,128]{1,0:T(8,128)(2,1)S(1)}, u32[]{:S(2)}, u32[]{:S(2)}) collective-permute-start(bf16[768,128]{1,0:T(8,128)(2,1)S(1)} %pack.4), channel_id=1, source_target_pairs={{0,1},{1,0},{2,3},{3,2},{4,5},{5,4},{6,7},{7,6},{8,9},{9,8},{10,11... | collective-permute-start | bytes 589832 | tf_op jit(solution)/shard_map/ppermute | solution.py:333

commit v9 on v8

--- a/solution.py
+++ b/solution.py
@@ -429,12 +429,12 @@
             name=f"pairs_{blocks[0]}",
         )(*operands)
 
-    far = along(right, 2)
     near = along(right, 1)
+    core = across(to_core, 1)
+    far = pack(along(right, 2), after=(near,))
     last = along(far, 1)
     chip = across(to_chip, 2)
-    core = across(to_core, 1)
-    middle = pack(near, far, after=(chip, core))
+    middle = pack(near, far, after=(core,))
     beside = across(middle, 1)
     both = across(pack(chip, after=(last,)), 1)
     lefts = ((left_own, 0), (core, 0), (chip, 0), (both, left_count))
@@ -442,7 +442,7 @@
     first, *shared = pairs(own, (0,), w, lefts=lefts)
 
     other = across(middle, 2)
-    onward = across(pack(other, after=shared[1:2]), 1)
+    onward = across(pack(other, after=(shared[1],)), 1)
     (second,) = pairs(((middle, 0), (beside, 0), (other, 0), (onward, 0)), (1, 2), *shared)
 
     other = across(last, 2)

time: 27.9 us -> 28 us (level)
  waiting for transfers between devices: 8.17 us -> 7.67 us
  starting transfers between devices: 11 us -> 11.4 us
    ppermute x8, waiting for transfers between devices: 3.28 us -> 1.56 us  [across(): return lax.ppermute(a, 'narrow', [(i, i ^ m) for i in range(narrow)])]
    ppermute x3, waiting for transfers between devices: 4.89 us -> 6.11 us  [along(): return lax.ppermute(a, 'wide', [(i, i ^ d) for i in range(wide)])]
    ppermute x8, starting transfers between devices: 4.46 us -> 5.33 us  [across(): return lax.ppermute(a, 'narrow', [(i, i ^ m) for i in range(narrow)])]
    ppermute x3, starting transfers between devices: 6.52 us -> 6.09 us  [along(): return lax.ppermute(a, 'wide', [(i, i ^ d) for i in range(wide)])]
  transfers between devices with their start and end apart: 11 -> 11, of which waited for: 6 -> 3; matrix products, arithmetic and copies ran while one was open for 0% -> 0% of each run, Pallas kernels for 11% -> 11%
where the time goes in v9:
time: 28 us; the launch traced here: 27.8 us
  starting transfers between devices  11.4 us (41%)
  Pallas kernels  8.58 us (31%)
  waiting for transfers between devices  7.67 us (27%)
    ppermute x3, waiting for transfers between devices, along(): return lax.ppermute(a, 'wide', [(i, i ^ d) for i in range(wide)])  6.11 us
    ppermute x3, starting transfers between devices, along(): return lax.ppermute(a, 'wide', [(i, i ^ d) for i in range(wide)])  6.09 us
    ppermute x8, starting transfers between devices, across(): return lax.ppermute(a, 'narrow', [(i, i ^ m) for i in range(narrow)])  5.33 us
    pallas_call x3, Pallas kernels, pairs(): pl.pallas_call(functools.partial(pair_kernel, operands=count, rights=plac...  4.73 us
    pallas_call x1, Pallas kernels, on_device(): pl.pallas_call(functools.partial(features_kernel, packs=packs, parts=narr...  3.8 us
    ppermute x8, waiting for transfers between devices, across(): return lax.ppermute(a, 'narrow', [(i, i ^ m) for i in range(narrow)])  1.56 us
  transfers between devices with their start and end apart: 11, of which 3 were waited for; matrix products, arithmetic and copies ran while one was open for 0% of the time, Pallas kernels for 11%

profile of v9, /device:TPU:0, one launch (start us, length us, event | category | flops | bytes accessed | tf_op | source)
XLA Modules:
  0.0 27.8 jit_solution(4936074883254713725)
XLA Ops:
  0.0 3.8 %features.1 = (bf16[96,128]{1,0:T(8,128)(2,1)}, bf16[384,128]{1,0:T(8,128)(2,1)}, bf16[480,128]{1,0:T(8,128)(2,1)}, bf16[576,128]{1,0:T(8,128)(2,1)}, f32[1032,128]{1,0:T(8,128)}) custom-call(bf16[32,48,256]{2,1,0:T(8,128)(2,1)} %refs_0_.1, f32[256]{0:T(256)} %refs_1_.1, f32[256]{0:T(256)} %refs_2_.1, bf16[32,256]{1,0:T(8,128)(2,1)} %bitcast.2, f32[32]{0:T(128)} %refs_4_.1, ...), custom_call_target="tpu_custom_call" | custom-call | tf_op jit(solution)/shard_map/features/pallas_call | solution.py:306
  3.8 3.1 %collective-permute-start.1 = (bf16[384,128]{1,0:T(8,128)(2,1)}, bf16[384,128]{1,0:T(8,128)(2,1)S(1)}, u32[]{:S(2)}, u32[]{:S(2)}) collective-permute-start(bf16[384,128]{1,0:T(8,128)(2,1)} %get-tuple-element.14.refs_0_), channel_id=1, source_target_pairs={{0,4},{4,0},{8,12},{12,8},{1,5},{5,1},{9,13},{13,9},{2,6},{6,2},{1... | collective-permute-start | bytes 294920 | tf_op jit(solution)/shard_map/ppermute | solution.py:336
  6.9 2.6 %collective-permute-start = (bf16[384,128]{1,0:T(8,128)(2,1)}, bf16[384,128]{1,0:T(8,128)(2,1)S(1)}, u32[]{:S(2)}, u32[]{:S(2)}) collective-permute-start(bf16[384,128]{1,0:T(8,128)(2,1)} %get-tuple-element.14.refs_0_), channel_id=1, source_target_pairs={{0,8},{4,12},{8,0},{12,4},{1,9},{5,13},{9,1},{13,5},{2,10},{6,14},... | collective-permute-start | bytes 294920 | tf_op jit(solution)/shard_map/ppermute | solution.py:336
  9.5 0.0 collective-permute-start.5
  9.5 1.5 %collective-permute-start.6 = (bf16[576,128]{1,0:T(8,128)(2,1)}, bf16[576,128]{1,0:T(8,128)(2,1)S(1)}, u32[]{:S(2)}, u32[]{:S(2)}) collective-permute-start(bf16[576,128]{1,0:T(8,128)(2,1)} %get-tuple-element.16), channel_id=1, source_target_pairs={{0,2},{1,3},{2,0},{3,1},{4,6},{5,7},{6,4},{7,5},{8,10},{9,11},{10,... | collective-permute-start | bytes 442376 | tf_op jit(solution)/shard_map/ppermute | solution.py:333
  11.0 0.0 collective-permute-done.1.refs_1_.refs_0_
  11.0 3.4 %collective-permute-done.refs_0_ = bf16[384,128]{1,0:T(8,128)(2,1)S(1)} collective-permute-done((bf16[384,128]{1,0:T(8,128)(2,1)}, bf16[384,128]{1,0:T(8,128)(2,1)S(1)}, u32[]{:S(2)}, u32[]{:S(2)}) %collective-permute-start) | collective-permute-done | bytes 98336 | tf_op jit(solution)/shard_map/ppermute | solution.py:336
  14.4 0.0 copy-start
  14.4 0.4 %collective-permute-start.2 = (bf16[384,128]{1,0:T(8,128)(2,1)S(1)}, bf16[384,128]{1,0:T(8,128)(2,1)S(1)}, u32[]{:S(2)}, u32[]{:S(2)}) collective-permute-start(bf16[384,128]{1,0:T(8,128)(2,1)S(1)} %pack.5.refs_1_), channel_id=1, source_target_pairs={{0,4},{4,0},{8,12},{12,8},{1,5},{5,1},{9,13},{13,9},{2,6},{6,2},{1... | collective-permute-start | bytes 294920 | tf_op jit(solution)/shard_map/ppermute | solution.py:336
  14.8 0.0 collective-permute-done.5.refs_1_.refs_5_.refs_2_
  14.9 0.0 copy-start.1
  14.9 0.0 copy-start.2
  14.9 1.6 %collective-permute-start.9 = (bf16[768,128]{1,0:T(8,128)(2,1)S(1)}, bf16[768,128]{1,0:T(8,128)(2,1)S(1)}, u32[]{:S(2)}, u32[]{:S(2)}) collective-permute-start(bf16[768,128]{1,0:T(8,128)(2,1)S(1)} %pack.8.refs_0_), channel_id=1, source_target_pairs={{0,2},{1,3},{2,0},{3,1},{4,6},{5,7},{6,4},{7,5},{8,10},{9,11},{10,... | collective-permute-start | bytes 589832 | tf_op jit(solution)/shard_map/ppermute | solution.py:333
  16.4 0.0 collective-permute-done.6.refs_0_.refs_2_.refs_6_
  16.4 2.7 %collective-permute-done.2.refs_0_.refs_1_ = bf16[384,128]{1,0:T(8,128)(2,1)S(1)} collective-permute-done((bf16[384,128]{1,0:T(8,128)(2,1)S(1)}, bf16[384,128]{1,0:T(8,128)(2,1)S(1)}, u32[]{:S(2)}, u32[]{:S(2)}) %collective-permute-start.2) | collective-permute-done | bytes 98336 | tf_op jit(solution)/shard_map/ppermute | solution.py:336
  19.1 0.1 collective-permute-start.7
  19.2 1.6 %collective-permute-start.3 = (bf16[384,128]{1,0:T(8,128)(2,1)S(1)}, bf16[384,128]{1,0:T(8,128)(2,1)S(1)}, u32[]{:S(2)}, u32[]{:S(2)}) collective-permute-start(bf16[384,128]{1,0:T(8,128)(2,1)S(1)} %collective-permute-done.2.refs_0_.refs_1_), channel_id=1, source_target_pairs={{0,2},{1,3},{2,0},{3,1},{4,6},{5,7},{6,4},{7,5},{8,10},{9,11},{10,... | collective-permute-start | bytes 294920 | tf_op jit(solution)/shard_map/ppermute | solution.py:333
  20.8 0.2 collective-permute-start.8
  20.9 0.0 collective-permute-done.7.refs_3_.refs_7_
  20.9 0.0 copy-done
  20.9 0.0 copy-done.1
  20.9 0.0 copy-done.2
  21.0 1.5 %pairs_0.1 = (bf16[12,48,128]{2,1,0:T(8,128)(2,1)S(1)}, bf16[4,2,32,768]{3,2,1,0:T(8,128)(2,1)S(1)}, bf16[2048,256]{1,0:T(8,128)(2,1)S(1)}, f32[8,128]{1,0:T(8,128)S(1)}) custom-call(bf16[384,128]{1,0:T(8,128)(2,1)S(1)} %copy-done.1, bf16[480,128]{1,0:T(8,128)(2,1)S(1)} %collective-permute-done.5.refs_1_.refs_5_.refs_2_, ...), custom_call_target="tpu_custom_call" | custom-call | flops 1000 | bytes 1000 | tf_op jit(solution)/shard_map/pairs_0/pallas_call | solution.py:418
  22.4 0.0 collective-permute-done.9.refs_0_.refs_2_
  22.5 0.4 %collective-permute-start.10 = (bf16[768,128]{1,0:T(8,128)(2,1)S(1)}, bf16[768,128]{1,0:T(8,128)(2,1)S(1)}, u32[]{:S(2)}, u32[]{:S(2)}) collective-permute-start(bf16[768,128]{1,0:T(8,128)(2,1)S(1)} %pack.9), channel_id=1, source_target_pairs={{0,1},{1,0},{2,3},{3,2},{4,5},{5,4},{6,7},{7,6},{8,9},{9,8},{10,11... | collective-permute-start | bytes 589832 | tf_op jit(solution)/shard_map/ppermute | solution.py:333
  22.9 1.5 %collective-permute-done.3.refs_1_.refs_2_ = bf16[384,128]{1,0:T(8,128)(2,1)S(1)} collective-permute-done((bf16[384,128]{1,0:T(8,128)(2,1)S(1)}, bf16[384,128]{1,0:T(8,128)(2,1)S(1)}, u32[]{:S(2)}, u32[]{:S(2)}) %collective-permute-start.3) | collective-permute-done | bytes 98336 | tf_op jit(solution)/shard_map/ppermute | solution.py:333
  24.4 0.1 collective-permute-start.4
  24.5 0.0 collective-permute-done.8.refs_1_
  24.5 0.0 collective-permute-done.10.refs_3_
  24.5 1.6 %pairs_1.1.refs_8_ = bf16[12,96,128]{2,1,0:T(8,128)(2,1)S(1)} custom-call(bf16[768,128]{1,0:T(8,128)(2,1)S(1)} %pack.8.refs_0_, bf16[768,128]{1,0:T(8,128)(2,1)S(1)} %collective-permute-done.8.refs_1_, bf16[768,128]{1,0:T(8,128)(2,1)S(1)} %collective-permute-done.9.refs_0_.refs_2_, bf16[768,128]{1,0:T(8,128)(2,1)S(1)} %collective-permute-done.10.refs_3_, ...), custom_call_target="tpu_custom_call" | custom-call | flops 1000 | bytes 1000 | tf_op jit(solution)/shard_map/pairs_1/pallas_call | solution.py:418
  26.2 0.0 collective-permute-done.4.refs_1_.refs_3_
  26.2 1.6 %pairs_3.1 = bf16[12,192,128]{2,1,0:T(8,128)(2,1)} custom-call(bf16[384,128]{1,0:T(8,128)(2,1)S(1)} %collective-permute-done.2.refs_0_.refs_1_, bf16[768,128]{1,0:T(8,128)(2,1)S(1)} %collective-permute-done.4.refs_1_.refs_3_, bf16[384,128]{1,0:T(8,128)(2,1)S(1)} %collective-permute-done.3.refs_1_.refs_2_, ...), custom_call_target="tpu_custom_call" | custom-call | flops 1000 | bytes 1000 | tf_op jit(solution)/shard_map/pairs_3/pallas_call | solution.py:418
  (5 shorter events, 0.1 us)
Async XLA Ops:
  3.8 7.2 %collective-permute-start.1 = (bf16[384,128]{1,0:T(8,128)(2,1)}, bf16[384,128]{1,0:T(8,128)(2,1)S(1)}, u32[]{:S(2)}, u32[]{:S(2)}) collective-permute-start(bf16[384,128]{1,0:T(8,128)(2,1)} %get-tuple-element.14.refs_0_), channel_id=1, source_target_pairs={{0,4},{4,0},{8,12},{12,8},{1,5},{5,1},{9,13},{13,9},{2,6},{6,2},{1... | collective-permute-start | bytes 294920 | tf_op jit(solution)/shard_map/ppermute | solution.py:336
  6.9 7.5 %collective-permute-start = (bf16[384,128]{1,0:T(8,128)(2,1)}, bf16[384,128]{1,0:T(8,128)(2,1)S(1)}, u32[]{:S(2)}, u32[]{:S(2)}) collective-permute-start(bf16[384,128]{1,0:T(8,128)(2,1)} %get-tuple-element.14.refs_0_), channel_id=1, source_target_pairs={{0,8},{4,12},{8,0},{12,4},{1,9},{5,13},{9,1},{13,5},{2,10},{6,14},... | collective-permute-start | bytes 294920 | tf_op jit(solution)/shard_map/ppermute | solution.py:336
  9.5 5.4 %collective-permute-start.5 = (bf16[480,128]{1,0:T(8,128)(2,1)}, bf16[480,128]{1,0:T(8,128)(2,1)S(1)}, u32[]{:S(2)}, u32[]{:S(2)}) collective-permute-start(bf16[480,128]{1,0:T(8,128)(2,1)} %get-tuple-element.15), channel_id=1, source_target_pairs={{0,1},{1,0},{2,3},{3,2},{4,5},{5,4},{6,7},{7,6},{8,9},{9,8},{10,11... | collective-permute-start | bytes 368648 | tf_op jit(solution)/shard_map/ppermute | solution.py:333
  9.5 7.0 %collective-permute-start.6 = (bf16[576,128]{1,0:T(8,128)(2,1)}, bf16[576,128]{1,0:T(8,128)(2,1)S(1)}, u32[]{:S(2)}, u32[]{:S(2)}) collective-permute-start(bf16[576,128]{1,0:T(8,128)(2,1)} %get-tuple-element.16), channel_id=1, source_target_pairs={{0,2},{1,3},{2,0},{3,1},{4,6},{5,7},{6,4},{7,5},{8,10},{9,11},{10,... | collective-permute-start | bytes 442376 | tf_op jit(solution)/shard_map/ppermute | solution.py:333
  14.4 6.5 %copy-start = (f32[1032,128]{1,0:T(8,128)S(1)}, f32[1032,128]{1,0:T(8,128)}, u32[]{:S(2)}) copy-start(f32[1032,128]{1,0:T(8,128)} %get-tuple-element.18.refs_8_) | copy-start | bytes 1585156
  14.4 4.7 %collective-permute-start.2 = (bf16[384,128]{1,0:T(8,128)(2,1)S(1)}, bf16[384,128]{1,0:T(8,128)(2,1)S(1)}, u32[]{:S(2)}, u32[]{:S(2)}) collective-permute-start(bf16[384,128]{1,0:T(8,128)(2,1)S(1)} %pack.5.refs_1_), channel_id=1, source_target_pairs={{0,4},{4,0},{8,12},{12,8},{1,5},{5,1},{9,13},{13,9},{2,6},{6,2},{1... | collective-permute-start | bytes 294920 | tf_op jit(solution)/shard_map/ppermute | solution.py:336
  14.9 6.1 %copy-start.1 = (bf16[384,128]{1,0:T(8,128)(2,1)S(1)}, bf16[384,128]{1,0:T(8,128)(2,1)}, u32[]{:S(2)}) copy-start(bf16[384,128]{1,0:T(8,128)(2,1)} %get-tuple-element.14.refs_0_) | copy-start | bytes 294916
  14.9 6.1 %copy-start.2 = (bf16[96,128]{1,0:T(8,128)(2,1)S(1)}, bf16[96,128]{1,0:T(8,128)(2,1)}, u32[]{:S(2)}) copy-start(bf16[96,128]{1,0:T(8,128)(2,1)} %get-tuple-element.17.refs_4_) | copy-start | bytes 73732
  14.9 7.5 %collective-permute-start.9 = (bf16[768,128]{1,0:T(8,128)(2,1)S(1)}, bf16[768,128]{1,0:T(8,128)(2,1)S(1)}, u32[]{:S(2)}, u32[]{:S(2)}) collective-permute-start(bf16[768,128]{1,0:T(8,128)(2,1)S(1)} %pack.8.refs_0_), channel_id=1, source_target_pairs={{0,2},{1,3},{2,0},{3,1},{4,6},{5,7},{6,4},{7,5},{8,10},{9,11},{10,... | collective-permute-start | bytes 589832 | tf_op jit(solution)/shard_map/ppermute | solution.py:333
  19.1 1.8 %collective-permute-start.7 = (bf16[576,128]{1,0:T(8,128)(2,1)S(1)}, bf16[576,128]{1,0:T(8,128)(2,1)S(1)}, u32[]{:S(2)}, u32[]{:S(2)}) collective-permute-start(bf16[576,128]{1,0:T(8,128)(2,1)S(1)} %pack.7), channel_id=1, source_target_pairs={{0,1},{1,0},{2,3},{3,2},{4,5},{5,4},{6,7},{7,6},{8,9},{9,8},{10,11... | collective-permute-start | bytes 442376 | tf_op jit(solution)/shard_map/ppermute | solution.py:333
  19.2 5.2 %collective-permute-start.3 = (bf16[384,128]{1,0:T(8,128)(2,1)S(1)}, bf16[384,128]{1,0:T(8,128)(2,1)S(1)}, u32[]{:S(2)}, u32[]{:S(2)}) collective-permute-start(bf16[384,128]{1,0:T(8,128)(2,1)S(1)} %collective-permute-done.2.refs_0_.refs_1_), channel_id=1, source_target_pairs={{0,2},{1,3},{2,0},{3,1},{4,6},{5,7},{6,4},{7,5},{8,10},{9,11},{10,... | collective-permute-start | bytes 294920 | tf_op jit(solution)/shard_map/ppermute | solution.py:333
  20.8 3.8 %collective-permute-start.8 = (bf16[768,128]{1,0:T(8,128)(2,1)S(1)}, bf16[768,128]{1,0:T(8,128)(2,1)S(1)}, u32[]{:S(2)}, u32[]{:S(2)}) collective-permute-start(bf16[768,128]{1,0:T(8,128)(2,1)S(1)} %pack.8.refs_0_), channel_id=1, source_target_pairs={{0,1},{1,0},{2,3},{3,2},{4,5},{5,4},{6,7},{7,6},{8,9},{9,8},{10,11... | collective-permute-start | bytes 589832 | tf_op jit(solution)/shard_map/ppermute | solution.py:333
  22.5 2.1 %collective-permute-start.10 = (bf16[768,128]{1,0:T(8,128)(2,1)S(1)}, bf16[768,128]{1,0:T(8,128)(2,1)S(1)}, u32[]{:S(2)}, u32[]{:S(2)}) collective-permute-start(bf16[768,128]{1,0:T(8,128)(2,1)S(1)} %pack.9), channel_id=1, source_target_pairs={{0,1},{1,0},{2,3},{3,2},{4,5},{5,4},{6,7},{7,6},{8,9},{9,8},{10,11... | collective-permute-start | bytes 589832 | tf_op jit(solution)/shard_map/ppermute | solution.py:333
  24.4 1.7 %collective-permute-start.4 = (bf16[768,128]{1,0:T(8,128)(2,1)S(1)}, bf16[768,128]{1,0:T(8,128)(2,1)S(1)}, u32[]{:S(2)}, u32[]{:S(2)}) collective-permute-start(bf16[768,128]{1,0:T(8,128)(2,1)S(1)} %pack.6), channel_id=1, source_target_pairs={{0,1},{1,0},{2,3},{3,2},{4,5},{5,4},{6,7},{7,6},{8,9},{9,8},{10,11... | collective-permute-start | bytes 589832 | tf_op jit(solution)/shard_map/ppermute | solution.py:333

commit v10 on v8

--- a/solution.py
+++ b/solution.py
@@ -20,7 +20,7 @@
 def features_kernel(*refs, packs, parts, pieces):
     args, refs = refs[:9], refs[9:]
     outs, wf_hbm, refs = refs[: len(packs)], refs[len(packs)], refs[len(packs) + 1 :]
-    held, (lo_ref, hi_ref, left_ref, turned_ref, rows_ref, right_ref, wf_ref, sems) = refs[:9], refs[9:]
+    held, (left_ref, turned_ref, rows_ref, right_ref, wf_ref, sems) = refs[:9], refs[9:]
     x_ref, gain_ref, bias_ref, lm_ref, lb_ref, rm_ref, rb_ref, w_ref, shift_ref = held
     seqs, residues, depth = x_ref.shape
     hidden = lm_ref.shape[0]
@@ -44,30 +44,8 @@
         copy.start()
     free = pieces + len(rest)
 
-    def norm(p):
-        gain = gain_ref[...].reshape(1, depth)
-        bias = bias_ref[...].reshape(1, depth)
-        step = min(4, piece)
-        for s in range(p * piece, (p + 1) * piece, step):
-            x = x_ref[s : s + step].reshape(step * residues, depth).astype(jnp.float32)
-            x = x - jnp.mean(x, axis=-1, keepdims=True)
-            spread = jnp.mean(x * x, axis=-1, keepdims=True)
-            x = x * lax.rsqrt(spread + 1e-05) * gain + bias
-            rows = pl.ds(s * residues, step * residues)
-            lo_ref[rows, :] = x[:, :LANES]
-            hi_ref[rows, :] = x[:, LANES:]
-
-    for copy in rest[:2]:
+    for copy in rest[:-2]:
         copy.wait()
-    for p in range(pieces - 1):
-        copies[p].wait()
-        norm(p)
-    for copy in copies[-1:] + rest[2:]:
-        copy.wait()
-    count = w_ref.shape[0]
-    wf_ref[:count] = w_ref[...].astype(jnp.float32)
-    wf_ref[count:] = jnp.broadcast_to(shift_ref[...].reshape(1, -1), (8, shift_ref.shape[0]))
-    norm(pieces - 1)
 
     column, row = iota((hidden, LANES), 1) % hidden, iota((hidden, LANES), 0)
     spread_l = (column == row).astype(jnp.float32)
@@ -87,30 +65,47 @@
 
     weights = jnp.concatenate(
         [widen(lm_ref[...], spread_l), widen(rm_ref[...], spread_r)], axis=1
-    )
+    ).astype(jnp.bfloat16)
     shift = jnp.concatenate(
         [widen_bias(lb_ref[...], spread_l), widen_bias(rb_ref[...], spread_r)], axis=1
     )
-    place = iota((depth, 2 * LANES), 1) % LANES // hidden
+    gain = gain_ref[...].reshape(1, depth)
+    bias = bias_ref[...].reshape(1, depth)
+    average = jnp.full((depth, LANES), 1.0 / depth, jnp.bfloat16)
+
+    cols = LANES // piece
+    out_row, in_row = iota((LANES // per, LANES), 0), iota((LANES // per, LANES), 1)
+    gather = (in_row // cols == out_row % piece) & (in_row % cols // per == out_row // piece)
+    gather = gather.astype(jnp.bfloat16)
+    rows = piece * residues
+    mine = iota((rows, 2 * LANES), 0) % per == iota((rows, 2 * LANES), 1) % LANES // hidden
+
+    grouped = [[] for _ in range(groups)]
+    for p in range(pieces):
+        copies[p].wait()
+        x = x_ref[p * piece : (p + 1) * piece].reshape(rows, depth)
+        center = jnp.dot(x, average, preferred_element_type=jnp.float32)
+        x = x.astype(jnp.float32)
+        x = [x[:, h * LANES : (h + 1) * LANES] - center for h in range(depth // LANES)]
+        spread = sum(h * h for h in x)
+        scale = lax.rsqrt(jnp.sum(spread, axis=-1, keepdims=True) * (1.0 / depth) + 1e-05)
+        x = jnp.concatenate([h * scale for h in x], axis=1) * gain + bias
+        y = jnp.dot(x.astype(jnp.bfloat16), weights, preferred_element_type=jnp.float32) + shift
+        y = jnp.where(mine, y, 0.0).astype(jnp.bfloat16).reshape(piece, residues, 2 * LANES)
+        for b in range(residues // cols):
+            block = y[:, b * cols : (b + 1) * cols].reshape(LANES, 2 * LANES)
+            block = jnp.dot(gather, block, preferred_element_type=jnp.float32)
+            for g in range(cols // per):
+                grouped[b * (cols // per) + g].append(block[g * piece : (g + 1) * piece])
+    total = jnp.concatenate([rows for group in grouped for rows in group], axis=0)
+
+    for copy in rest[-2:]:
+        copy.wait()
+    count = w_ref.shape[0]
+    wf_ref[:count] = w_ref[...].astype(jnp.float32)
+    wf_ref[count:] = jnp.broadcast_to(shift_ref[...].reshape(1, -1), (8, shift_ref.shape[0]))
     sends = [pltpu.make_async_copy(wf_ref, wf_hbm, sems.at[free])]
     sends[0].start()
-
-    total = None
-    for k in range(per):
-        part = jnp.concatenate(
-            [
-                jnp.concatenate(
-                    [half[pl.ds(g * per + k, seqs, stride=residues), :] for half in (lo_ref, hi_ref)],
-                    axis=1,
-                )
-                for g in range(groups)
-            ],
-            axis=0,
-        ).astype(jnp.bfloat16)
-        placed = jnp.where(place == k, weights, 0.0).astype(jnp.bfloat16)
-        term = jnp.dot(part, placed, preferred_element_type=jnp.float32)
-        total = term if total is None else total + term
-    total = total + shift
     left_ref[...] = total[:, :LANES].astype(left_ref.dtype)
 
     slot = iota((minor, LANES), 1) // seqs
@@ -126,8 +121,17 @@
                         moved = pltpu.roll(moved, (q - g) % slots * seqs, axis=1)
                     out = moved if out is None else jnp.where(slot == q, moved, out)
                 j = (block * slots + g) * per + k
-                rows_ref[pl.ds(j, minor, stride=residues), :] = out
-    right_ref[...] = rows_ref[...].astype(right_ref.dtype)
+                rows_ref[pl.ds(j * minor, minor), :] = out
+    cols = LANES // minor
+    out_row, in_row = iota((LANES, LANES), 0), iota((LANES, LANES), 1)
+    turn = (in_row // minor == out_row % cols) & (in_row % minor == out_row // cols)
+    turn = turn.astype(jnp.bfloat16)
+    for b in range(residues // cols):
+        block = rows_ref[b * LANES : (b + 1) * LANES].astype(jnp.bfloat16)
+        block = jnp.dot(turn, block, preferred_element_type=jnp.float32).astype(right_ref.dtype)
+        for e in range(minor):
+            at = e * residues + b * cols
+            right_ref[at : at + cols] = block[e * cols : (e + 1) * cols]
 
     mine = left_ref.shape[0] // parts
     for out, pack in zip(outs, packs):
@@ -292,7 +296,7 @@
     minor = hidden // slots
     own_rows = residues // narrow
     groups = own_rows // per
-    pieces = 4
+    pieces = seqs // 8
     hbm = pl.BlockSpec(memory_space=pltpu.HBM)
     vmem = pl.BlockSpec(memory_space=pltpu.VMEM)
     params = pltpu.CompilerParams(vmem_limit_bytes=VMEM_LIMIT)
@@ -316,8 +320,6 @@
         out_specs=(hbm,) * (len(packs) + 1),
         scratch_shapes=[pltpu.VMEM(a.shape, a.dtype) for a in args]
         + [
-            pltpu.VMEM((seqs * residues, LANES), jnp.float32),
-            pltpu.VMEM((seqs * residues, LANES), jnp.float32),
             pltpu.VMEM((residues // per * seqs, LANES), jnp.bfloat16),
             pltpu.VMEM((LANES, LANES), jnp.float32),
             pltpu.VMEM((minor * residues, LANES), jnp.float32),

time: 27.9 us -> 29.3 us (1.050)
  Pallas kernels: 8.52 us -> 9.86 us
    pallas_call x1, Pallas kernels: 3.8 us -> 5.14 us  [on_device(): pl.pallas_call(functools.partial(features_kernel, packs=packs, parts=narr...]
where the time goes in v10:
time: 29.3 us; the launch traced here: 29.1 us
  starting transfers between devices  11 us (38%)
  Pallas kernels  9.86 us (34%)
  waiting for transfers between devices  8.15 us (28%)
    ppermute x3, starting transfers between devices, along(): return lax.ppermute(a, 'wide', [(i, i ^ d) for i in range(wide)])  6.53 us
    pallas_call x1, Pallas kernels, on_device(): pl.pallas_call(functools.partial(features_kernel, packs=packs, parts=narr...  5.14 us
    ppermute x3, waiting for transfers between devices, along(): return lax.ppermute(a, 'wide', [(i, i ^ d) for i in range(wide)])  4.87 us
    pallas_call x3, Pallas kernels, pairs(): pl.pallas_call(functools.partial(pair_kernel, operands=count, rights=plac...  4.67 us
    ppermute x8, starting transfers between devices, across(): return lax.ppermute(a, 'narrow', [(i, i ^ m) for i in range(narrow)])  4.47 us
    ppermute x8, waiting for transfers between devices, across(): return lax.ppermute(a, 'narrow', [(i, i ^ m) for i in range(narrow)])  3.28 us
  transfers between devices with their start and end apart: 11, of which 6 were waited for; matrix products, arithmetic and copies ran while one was open for 0% of the time, Pallas kernels for 11%

profile of v10, /device:TPU:0, one launch (start us, length us, event | category | flops | bytes accessed | tf_op | source)
XLA Modules:
  0.0 29.1 jit_solution(11910337765892698606)
XLA Ops:
  0.0 5.1 %features.1 = (bf16[96,128]{1,0:T(8,128)(2,1)}, bf16[384,128]{1,0:T(8,128)(2,1)}, bf16[480,128]{1,0:T(8,128)(2,1)}, bf16[576,128]{1,0:T(8,128)(2,1)}, f32[1032,128]{1,0:T(8,128)}) custom-call(bf16[32,48,256]{2,1,0:T(8,128)(2,1)} %refs_0_.1, f32[256]{0:T(256)} %refs_1_.1, f32[256]{0:T(256)} %refs_2_.1, bf16[32,256]{1,0:T(8,128)(2,1)} %bitcast.2, f32[32]{0:T(128)} %refs_4_.1, ...), custom_call_target="tpu_custom_call" | custom-call | tf_op jit(solution)/shard_map/features/pallas_call | solution.py:310
  5.1 4.1 %collective-permute-start = (bf16[384,128]{1,0:T(8,128)(2,1)}, bf16[384,128]{1,0:T(8,128)(2,1)S(1)}, u32[]{:S(2)}, u32[]{:S(2)}) collective-permute-start(bf16[384,128]{1,0:T(8,128)(2,1)} %get-tuple-element.14.refs_0_), channel_id=1, source_target_pairs={{0,8},{4,12},{8,0},{12,4},{1,9},{5,13},{9,1},{13,5},{2,10},{6,14},... | collective-permute-start | bytes 294920 | tf_op jit(solution)/shard_map/ppermute | solution.py:338
  9.3 1.5 %collective-permute-start.5 = (bf16[576,128]{1,0:T(8,128)(2,1)}, bf16[576,128]{1,0:T(8,128)(2,1)S(1)}, u32[]{:S(2)}, u32[]{:S(2)}) collective-permute-start(bf16[576,128]{1,0:T(8,128)(2,1)} %get-tuple-element.16), channel_id=1, source_target_pairs={{0,2},{1,3},{2,0},{3,1},{4,6},{5,7},{6,4},{7,5},{8,10},{9,11},{10,... | collective-permute-start | bytes 442376 | tf_op jit(solution)/shard_map/ppermute | solution.py:335
  10.7 0.0 copy-start
  10.7 0.0 collective-permute-start.4
  10.7 1.6 %collective-permute-start.7 = (bf16[384,128]{1,0:T(8,128)(2,1)}, bf16[384,128]{1,0:T(8,128)(2,1)S(1)}, u32[]{:S(2)}, u32[]{:S(2)}) collective-permute-start(bf16[384,128]{1,0:T(8,128)(2,1)} %get-tuple-element.14.refs_0_), channel_id=1, source_target_pairs={{0,4},{4,0},{8,12},{12,8},{1,5},{5,1},{9,13},{13,9},{2,6},{6,2},{1... | collective-permute-start | bytes 294920 | tf_op jit(solution)/shard_map/ppermute | solution.py:338
  12.3 2.1 %collective-permute-done.refs_1_ = bf16[384,128]{1,0:T(8,128)(2,1)S(1)} collective-permute-done((bf16[384,128]{1,0:T(8,128)(2,1)}, bf16[384,128]{1,0:T(8,128)(2,1)S(1)}, u32[]{:S(2)}, u32[]{:S(2)}) %collective-permute-start) | collective-permute-done | bytes 98336 | tf_op jit(solution)/shard_map/ppermute | solution.py:338
  14.4 0.8 %collective-permute-start.1 = (bf16[384,128]{1,0:T(8,128)(2,1)S(1)}, bf16[384,128]{1,0:T(8,128)(2,1)S(1)}, u32[]{:S(2)}, u32[]{:S(2)}) collective-permute-start(bf16[384,128]{1,0:T(8,128)(2,1)S(1)} %collective-permute-done.refs_1_), channel_id=1, source_target_pairs={{0,4},{4,0},{8,12},{12,8},{1,5},{5,1},{9,13},{13,9},{2,6},{6,2},{1... | collective-permute-start | bytes 294920 | tf_op jit(solution)/shard_map/ppermute | solution.py:338
  15.2 1.4 %collective-permute-done.7.refs_0_ = bf16[384,128]{1,0:T(8,128)(2,1)S(1)} collective-permute-done((bf16[384,128]{1,0:T(8,128)(2,1)}, bf16[384,128]{1,0:T(8,128)(2,1)S(1)}, u32[]{:S(2)}, u32[]{:S(2)}) %collective-permute-start.7) | collective-permute-done | bytes 98336 | tf_op jit(solution)/shard_map/ppermute | solution.py:338
  16.6 0.0 collective-permute-done.4.refs_1_.refs_5_.refs_3_
  16.6 0.0 collective-permute-done.5.refs_0_.refs_2_.refs_6_
  16.7 0.0 copy-start.1
  16.7 0.0 copy-start.2
  16.7 0.9 %collective-permute-start.9 = (bf16[768,128]{1,0:T(8,128)(2,1)S(1)}, bf16[768,128]{1,0:T(8,128)(2,1)S(1)}, u32[]{:S(2)}, u32[]{:S(2)}) collective-permute-start(bf16[768,128]{1,0:T(8,128)(2,1)S(1)} %pack.6.refs_0_), channel_id=1, source_target_pairs={{0,2},{1,3},{2,0},{3,1},{4,6},{5,7},{6,4},{7,5},{8,10},{9,11},{10,... | collective-permute-start | bytes 589832 | tf_op jit(solution)/shard_map/ppermute | solution.py:335
  17.6 1.4 %collective-permute-done.1.refs_0_.refs_1_ = bf16[384,128]{1,0:T(8,128)(2,1)S(1)} collective-permute-done((bf16[384,128]{1,0:T(8,128)(2,1)S(1)}, bf16[384,128]{1,0:T(8,128)(2,1)S(1)}, u32[]{:S(2)}, u32[]{:S(2)}) %collective-permute-start.1) | collective-permute-done | bytes 98336 | tf_op jit(solution)/shard_map/ppermute | solution.py:338
  19.0 0.1 collective-permute-start.6
  19.1 1.7 %collective-permute-start.2 = (bf16[384,128]{1,0:T(8,128)(2,1)S(1)}, bf16[384,128]{1,0:T(8,128)(2,1)S(1)}, u32[]{:S(2)}, u32[]{:S(2)}) collective-permute-start(bf16[384,128]{1,0:T(8,128)(2,1)S(1)} %collective-permute-done.1.refs_0_.refs_1_), channel_id=1, source_target_pairs={{0,2},{1,3},{2,0},{3,1},{4,6},{5,7},{6,4},{7,5},{8,10},{9,11},{10,... | collective-permute-start | bytes 294920 | tf_op jit(solution)/shard_map/ppermute | solution.py:335
  20.8 0.2 collective-permute-start.8
  21.0 0.0 collective-permute-done.6.refs_3_.refs_7_
  21.0 0.0 copy-done
  21.0 0.0 copy-done.1
  21.0 0.0 copy-done.2
  21.0 1.5 %pairs_0.1 = (bf16[12,48,128]{2,1,0:T(8,128)(2,1)S(1)}, bf16[4,2,32,768]{3,2,1,0:T(8,128)(2,1)S(1)}, bf16[2048,256]{1,0:T(8,128)(2,1)S(1)}, f32[8,128]{1,0:T(8,128)S(1)}) custom-call(bf16[384,128]{1,0:T(8,128)(2,1)S(1)} %copy-done.1, bf16[480,128]{1,0:T(8,128)(2,1)S(1)} %collective-permute-done.4.refs_1_.refs_5_.refs_3_, ...), custom_call_target="tpu_custom_call" | custom-call | flops 1000 | bytes 1000 | tf_op jit(solution)/shard_map/pairs_0/pallas_call | solution.py:420
  22.4 1.9 %collective-permute-done.9.refs_0_.refs_2_ = bf16[768,128]{1,0:T(8,128)(2,1)S(1)} collective-permute-done((bf16[768,128]{1,0:T(8,128)(2,1)S(1)}, bf16[768,128]{1,0:T(8,128)(2,1)S(1)}, u32[]{:S(2)}, u32[]{:S(2)}) %collective-permute-start.9) | collective-permute-done | bytes 196640 | tf_op jit(solution)/shard_map/ppermute | solution.py:335
  24.4 0.1 collective-permute-start.10
  24.5 1.0 %collective-permute-done.2.refs_1_.refs_2_ = bf16[384,128]{1,0:T(8,128)(2,1)S(1)} collective-permute-done((bf16[384,128]{1,0:T(8,128)(2,1)S(1)}, bf16[384,128]{1,0:T(8,128)(2,1)S(1)}, u32[]{:S(2)}, u32[]{:S(2)}) %collective-permute-start.2) | collective-permute-done | bytes 98336 | tf_op jit(solution)/shard_map/ppermute | solution.py:335
  25.5 0.1 collective-permute-start.3
  25.5 0.0 collective-permute-done.8.refs_1_
  25.5 0.4 %collective-permute-done.10.refs_3_ = bf16[768,128]{1,0:T(8,128)(2,1)S(1)} collective-permute-done((bf16[768,128]{1,0:T(8,128)(2,1)S(1)}, bf16[768,128]{1,0:T(8,128)(2,1)S(1)}, u32[]{:S(2)}, u32[]{:S(2)}) %collective-permute-start.10) | collective-permute-done | bytes 196640 | tf_op jit(solution)/shard_map/ppermute | solution.py:335
  25.9 1.6 %pairs_1.1.refs_8_ = bf16[12,96,128]{2,1,0:T(8,128)(2,1)S(1)} custom-call(bf16[768,128]{1,0:T(8,128)(2,1)S(1)} %pack.6.refs_0_, bf16[768,128]{1,0:T(8,128)(2,1)S(1)} %collective-permute-done.8.refs_1_, bf16[768,128]{1,0:T(8,128)(2,1)S(1)} %collective-permute-done.9.refs_0_.refs_2_, bf16[768,128]{1,0:T(8,128)(2,1)S(1)} %collective-permute-done.10.refs_3_, ...), custom_call_target="tpu_custom_call" | custom-call | flops 1000 | bytes 1000 | tf_op jit(solution)/shard_map/pairs_1/pallas_call | solution.py:420
  27.5 0.0 collective-permute-done.3.refs_1_.refs_3_
  27.5 1.6 %pairs_3.1 = bf16[12,192,128]{2,1,0:T(8,128)(2,1)} custom-call(bf16[384,128]{1,0:T(8,128)(2,1)S(1)} %collective-permute-done.1.refs_0_.refs_1_, bf16[768,128]{1,0:T(8,128)(2,1)S(1)} %collective-permute-done.3.refs_1_.refs_3_, bf16[384,128]{1,0:T(8,128)(2,1)S(1)} %collective-permute-done.2.refs_1_.refs_2_, ...), custom_call_target="tpu_custom_call" | custom-call | flops 1000 | bytes 1000 | tf_op jit(solution)/shard_map/pairs_3/pallas_call | solution.py:420
  (4 shorter events, 0.1 us)
Async XLA Ops:
  5.1 9.2 %collective-permute-start = (bf16[384,128]{1,0:T(8,128)(2,1)}, bf16[384,128]{1,0:T(8,128)(2,1)S(1)}, u32[]{:S(2)}, u32[]{:S(2)}) collective-permute-start(bf16[384,128]{1,0:T(8,128)(2,1)} %get-tuple-element.14.refs_0_), channel_id=1, source_target_pairs={{0,8},{4,12},{8,0},{12,4},{1,9},{5,13},{9,1},{13,5},{2,10},{6,14},... | collective-permute-start | bytes 294920 | tf_op jit(solution)/shard_map/ppermute | solution.py:338
  9.3 7.4 %collective-permute-start.5 = (bf16[576,128]{1,0:T(8,128)(2,1)}, bf16[576,128]{1,0:T(8,128)(2,1)S(1)}, u32[]{:S(2)}, u32[]{:S(2)}) collective-permute-start(bf16[576,128]{1,0:T(8,128)(2,1)} %get-tuple-element.16), channel_id=1, source_target_pairs={{0,2},{1,3},{2,0},{3,1},{4,6},{5,7},{6,4},{7,5},{8,10},{9,11},{10,... | collective-permute-start | bytes 442376 | tf_op jit(solution)/shard_map/ppermute | solution.py:335
  10.7 10.2 %copy-start = (f32[1032,128]{1,0:T(8,128)S(1)}, f32[1032,128]{1,0:T(8,128)}, u32[]{:S(2)}) copy-start(f32[1032,128]{1,0:T(8,128)} %get-tuple-element.18.refs_8_) | copy-start | bytes 1585156
  10.7 5.9 %collective-permute-start.4 = (bf16[480,128]{1,0:T(8,128)(2,1)}, bf16[480,128]{1,0:T(8,128)(2,1)S(1)}, u32[]{:S(2)}, u32[]{:S(2)}) collective-permute-start(bf16[480,128]{1,0:T(8,128)(2,1)} %get-tuple-element.15), channel_id=1, source_target_pairs={{0,1},{1,0},{2,3},{3,2},{4,5},{5,4},{6,7},{7,6},{8,9},{9,8},{10,11... | collective-permute-start | bytes 368648 | tf_op jit(solution)/shard_map/ppermute | solution.py:335
  10.7 5.9 %collective-permute-start.7 = (bf16[384,128]{1,0:T(8,128)(2,1)}, bf16[384,128]{1,0:T(8,128)(2,1)S(1)}, u32[]{:S(2)}, u32[]{:S(2)}) collective-permute-start(bf16[384,128]{1,0:T(8,128)(2,1)} %get-tuple-element.14.refs_0_), channel_id=1, source_target_pairs={{0,4},{4,0},{8,12},{12,8},{1,5},{5,1},{9,13},{13,9},{2,6},{6,2},{1... | collective-permute-start | bytes 294920 | tf_op jit(solution)/shard_map/ppermute | solution.py:338
  14.4 4.6 %collective-permute-start.1 = (bf16[384,128]{1,0:T(8,128)(2,1)S(1)}, bf16[384,128]{1,0:T(8,128)(2,1)S(1)}, u32[]{:S(2)}, u32[]{:S(2)}) collective-permute-start(bf16[384,128]{1,0:T(8,128)(2,1)S(1)} %collective-permute-done.refs_1_), channel_id=1, source_target_pairs={{0,4},{4,0},{8,12},{12,8},{1,5},{5,1},{9,13},{13,9},{2,6},{6,2},{1... | collective-permute-start | bytes 294920 | tf_op jit(solution)/shard_map/ppermute | solution.py:338
  16.7 4.3 %copy-start.1 = (bf16[384,128]{1,0:T(8,128)(2,1)S(1)}, bf16[384,128]{1,0:T(8,128)(2,1)}, u32[]{:S(2)}) copy-start(bf16[384,128]{1,0:T(8,128)(2,1)} %get-tuple-element.14.refs_0_) | copy-start | bytes 294916
  16.7 4.3 %copy-start.2 = (bf16[96,128]{1,0:T(8,128)(2,1)S(1)}, bf16[96,128]{1,0:T(8,128)(2,1)}, u32[]{:S(2)}) copy-start(bf16[96,128]{1,0:T(8,128)(2,1)} %get-tuple-element.17.refs_4_) | copy-start | bytes 73732
  16.7 7.7 %collective-permute-start.9 = (bf16[768,128]{1,0:T(8,128)(2,1)S(1)}, bf16[768,128]{1,0:T(8,128)(2,1)S(1)}, u32[]{:S(2)}, u32[]{:S(2)}) collective-permute-start(bf16[768,128]{1,0:T(8,128)(2,1)S(1)} %pack.6.refs_0_), channel_id=1, source_target_pairs={{0,2},{1,3},{2,0},{3,1},{4,6},{5,7},{6,4},{7,5},{8,10},{9,11},{10,... | collective-permute-start | bytes 589832 | tf_op jit(solution)/shard_map/ppermute | solution.py:335
  19.0 1.9 %collective-permute-start.6 = (bf16[576,128]{1,0:T(8,128)(2,1)S(1)}, bf16[576,128]{1,0:T(8,128)(2,1)S(1)}, u32[]{:S(2)}, u32[]{:S(2)}) collective-permute-start(bf16[576,128]{1,0:T(8,128)(2,1)S(1)} %pack.5), channel_id=1, source_target_pairs={{0,1},{1,0},{2,3},{3,2},{4,5},{5,4},{6,7},{7,6},{8,9},{9,8},{10,11... | collective-permute-start | bytes 442376 | tf_op jit(solution)/shard_map/ppermute | solution.py:335
  19.1 6.3 %collective-permute-start.2 = (bf16[384,128]{1,0:T(8,128)(2,1)S(1)}, bf16[384,128]{1,0:T(8,128)(2,1)S(1)}, u32[]{:S(2)}, u32[]{:S(2)}) collective-permute-start(bf16[384,128]{1,0:T(8,128)(2,1)S(1)} %collective-permute-done.1.refs_0_.refs_1_), channel_id=1, source_target_pairs={{0,2},{1,3},{2,0},{3,1},{4,6},{5,7},{6,4},{7,5},{8,10},{9,11},{10,... | collective-permute-start | bytes 294920 | tf_op jit(solution)/shard_map/ppermute | solution.py:335
  20.8 4.8 %collective-permute-start.8 = (bf16[768,128]{1,0:T(8,128)(2,1)S(1)}, bf16[768,128]{1,0:T(8,128)(2,1)S(1)}, u32[]{:S(2)}, u32[]{:S(2)}) collective-permute-start(bf16[768,128]{1,0:T(8,128)(2,1)S(1)} %pack.6.refs_0_), channel_id=1, source_target_pairs={{0,1},{1,0},{2,3},{3,2},{4,5},{5,4},{6,7},{7,6},{8,9},{9,8},{10,11... | collective-permute-start | bytes 589832 | tf_op jit(solution)/shard_map/ppermute | solution.py:335
  24.4 1.5 %collective-permute-start.10 = (bf16[768,128]{1,0:T(8,128)(2,1)S(1)}, bf16[768,128]{1,0:T(8,128)(2,1)S(1)}, u32[]{:S(2)}, u32[]{:S(2)}) collective-permute-start(bf16[768,128]{1,0:T(8,128)(2,1)S(1)} %pack.7), channel_id=1, source_target_pairs={{0,1},{1,0},{2,3},{3,2},{4,5},{5,4},{6,7},{7,6},{8,9},{9,8},{10,11... | collective-permute-start | bytes 589832 | tf_op jit(solution)/shard_map/ppermute | solution.py:335
  25.5 2.1 %collective-permute-start.3 = (bf16[768,128]{1,0:T(8,128)(2,1)S(1)}, bf16[768,128]{1,0:T(8,128)(2,1)S(1)}, u32[]{:S(2)}, u32[]{:S(2)}) collective-permute-start(bf16[768,128]{1,0:T(8,128)(2,1)S(1)} %pack.4), channel_id=1, source_target_pairs={{0,1},{1,0},{2,3},{3,2},{4,5},{5,4},{6,7},{7,6},{8,9},{9,8},{10,11... | collective-permute-start | bytes 589832 | tf_op jit(solution)/shard_map/ppermute | solution.py:335

commit v11 on v8

--- a/solution.py
+++ b/solution.py
@@ -18,10 +18,10 @@
 
 
 def features_kernel(*refs, packs, parts, pieces):
-    args, refs = refs[:9], refs[9:]
-    outs, wf_hbm, refs = refs[: len(packs)], refs[len(packs)], refs[len(packs) + 1 :]
-    held, (lo_ref, hi_ref, left_ref, turned_ref, rows_ref, right_ref, wf_ref, sems) = refs[:9], refs[9:]
-    x_ref, gain_ref, bias_ref, lm_ref, lb_ref, rm_ref, rb_ref, w_ref, shift_ref = held
+    args, passed, refs = refs[:7], refs[7:9], refs[9:]
+    outs, refs = refs[: len(packs) + 2], refs[len(packs) + 2 :]
+    held, (lo_ref, hi_ref, left_ref, turned_ref, rows_ref, right_ref, sems) = refs[:7], refs[7:]
+    x_ref, gain_ref, bias_ref, lm_ref, lb_ref, rm_ref, rb_ref = held
     seqs, residues, depth = x_ref.shape
     hidden = lm_ref.shape[0]
     per = LANES // hidden
@@ -40,34 +40,13 @@
     rest = [
         pltpu.make_async_copy(a, b, sems.at[pieces + i]) for i, (a, b) in enumerate(zip(args[1:], held[1:]))
     ]
-    for copy in copies[:1] + rest[:2] + copies[1:] + rest[2:]:
+    free = pieces + len(rest)
+    sends = [pltpu.make_async_copy(a, b, sems.at[free + i]) for i, (a, b) in enumerate(zip(passed, outs[-2:]))]
+    free += len(sends)
+    for copy in copies + rest + sends:
         copy.start()
-    free = pieces + len(rest)
-
-    def norm(p):
-        gain = gain_ref[...].reshape(1, depth)
-        bias = bias_ref[...].reshape(1, depth)
-        step = min(4, piece)
-        for s in range(p * piece, (p + 1) * piece, step):
-            x = x_ref[s : s + step].reshape(step * residues, depth).astype(jnp.float32)
-            x = x - jnp.mean(x, axis=-1, keepdims=True)
-            spread = jnp.mean(x * x, axis=-1, keepdims=True)
-            x = x * lax.rsqrt(spread + 1e-05) * gain + bias
-            rows = pl.ds(s * residues, step * residues)
-            lo_ref[rows, :] = x[:, :LANES]
-            hi_ref[rows, :] = x[:, LANES:]
-
-    for copy in rest[:2]:
+    for copy in copies + rest:
         copy.wait()
-    for p in range(pieces - 1):
-        copies[p].wait()
-        norm(p)
-    for copy in copies[-1:] + rest[2:]:
-        copy.wait()
-    count = w_ref.shape[0]
-    wf_ref[:count] = w_ref[...].astype(jnp.float32)
-    wf_ref[count:] = jnp.broadcast_to(shift_ref[...].reshape(1, -1), (8, shift_ref.shape[0]))
-    norm(pieces - 1)
 
     column, row = iota((hidden, LANES), 1) % hidden, iota((hidden, LANES), 0)
     spread_l = (column == row).astype(jnp.float32)
@@ -92,8 +71,18 @@
         [widen_bias(lb_ref[...], spread_l), widen_bias(rb_ref[...], spread_r)], axis=1
     )
     place = iota((depth, 2 * LANES), 1) % LANES // hidden
-    sends = [pltpu.make_async_copy(wf_ref, wf_hbm, sems.at[free])]
-    sends[0].start()
+
+    gain = gain_ref[...].reshape(1, depth)
+    bias = bias_ref[...].reshape(1, depth)
+    step = 4
+    for s in range(0, seqs, step):
+        x = x_ref[s : s + step].reshape(step * residues, depth).astype(jnp.float32)
+        x = x - jnp.mean(x, axis=-1, keepdims=True)
+        spread = jnp.mean(x * x, axis=-1, keepdims=True)
+        x = x * lax.rsqrt(spread + 1e-05) * gain + bias
+        rows = pl.ds(s * residues, step * residues)
+        lo_ref[rows, :] = x[:, :LANES]
+        hi_ref[rows, :] = x[:, LANES:]
 
     total = None
     for k in range(per):
@@ -137,23 +126,24 @@
                 rows = right_ref
             else:
                 rows = left_ref.at[pl.ds(pl.multiple_of((own ^ item) * mine, 16), mine)]
-            free += 1
             sends.append(
                 pltpu.make_async_copy(rows, out.at[pl.ds(at, rows.shape[0])], sems.at[free])
             )
+            free += 1
             sends[-1].start()
             at += rows.shape[0]
     for copy in sends:
         copy.wait()
 
 
-def block_weights(wf_ref, wide_ref, *, parts, minor):
+def block_weights(w_ref, wide_ref, wf_ref, *, parts, minor):
     cz = wf_ref.shape[1]
     hidden = parts * minor
     half = minor // 2
     rows_each = wide_ref.shape[0] // hidden // hidden
     own = lax.axis_index("narrow")
     wide_ref[...] = jnp.zeros_like(wide_ref)
+    wf_ref[...] = w_ref[...].astype(jnp.float32)
     for e in range(hidden):
         rows = wf_ref[pl.ds(e ^ (own * minor), hidden, stride=hidden), :].astype(jnp.bfloat16)
         q, e2, t = e // minor, e % minor // half, e % half
@@ -220,10 +210,9 @@
     parts, minor = sizes["parts"], sizes["minor"]
     inputs, refs = refs[:operands], refs[operands:]
     if lefts is not None:
-        wf_ref, done_ref, spread_ref, wide_ref, shift_ref, outer_ref = refs
+        w_ref, shift_ref, done_ref, spread_ref, wide_ref, outer_ref, wf_ref = refs
         own_rows = done_ref.shape[0]
-        block_weights(wf_ref, wide_ref, parts=parts, minor=minor)
-        shift_ref[...] = wf_ref[wf_ref.shape[0] - 8 :]
+        block_weights(w_ref, wide_ref, wf_ref, parts=parts, minor=minor)
         count = own_rows * minor
         spread_left(lambda m: inputs[lefts[m][0]][lefts[m][1] : lefts[m][1] + count, :], spread_ref, parts=parts)
     elif not earlier:
@@ -258,7 +247,8 @@
     def store(row, pair):
         done_ref[row] = pair.astype(done_ref.dtype)
 
-    pair_rows(spread_ref, right_of, wide_ref, shift_ref[:1], outer_ref, store, wides=len(blocks), **sizes)
+    shift = shift_ref[...].reshape(1, -1)
+    pair_rows(spread_ref, right_of, wide_ref, shift, outer_ref, store, wides=len(blocks), **sizes)
     if earlier:
         write(done_ref, blocks)
         for copy in copies:
@@ -266,11 +256,12 @@
 
 
 def pair_blocks_kernel(*refs, wides, parts, minor, **sizes):
-    left_refs, (right_ref, wf_ref, out_ref, spread_ref, wide_ref, outer_ref) = refs[:parts], refs[parts:]
+    left_refs, refs = refs[:parts], refs[parts:]
+    right_ref, w_ref, shift_ref, out_ref, spread_ref, wide_ref, outer_ref, wf_ref = refs
 
     @pl.when(pl.program_id(0) == 0)
     def _():
-        block_weights(wf_ref, wide_ref, parts=parts, minor=minor)
+        block_weights(w_ref, wide_ref, wf_ref, parts=parts, minor=minor)
         spread_left(lambda m: left_refs[m][...], spread_ref, parts=parts)
 
     def store(row, pair):
@@ -278,7 +269,7 @@
 
     pair_rows(
         spread_ref, lambda d, m: right_ref[d, m],
-        wide_ref, wf_ref[wf_ref.shape[0] - 8 :][:1], outer_ref, store,
+        wide_ref, shift_ref[...].reshape(1, -1), outer_ref, store,
         wides=wides, parts=parts, minor=minor, **sizes,
     )
 
@@ -303,7 +294,7 @@
         packs = tuple((m,) for m in range(narrow)) + ((RIGHT,),)
     left_count, right_count = groups * seqs, minor * residues
     args = (x, gain, bias, lm.T, lb, rm.T, rb, w, shift)
-    *made, w = pl.pallas_call(
+    *made, w, shift = pl.pallas_call(
         functools.partial(features_kernel, packs=packs, parts=narrow, pieces=pieces),
         out_shape=tuple(
             jax.ShapeDtypeStruct(
@@ -311,10 +302,10 @@
             )
             for pack in packs
         )
-        + (jax.ShapeDtypeStruct((w.shape[0] + 8, cz), jnp.float32),),
+        + (jax.ShapeDtypeStruct(w.shape, w.dtype), jax.ShapeDtypeStruct(shift.shape, shift.dtype)),
         in_specs=[hbm] * len(args),
-        out_specs=(hbm,) * (len(packs) + 1),
-        scratch_shapes=[pltpu.VMEM(a.shape, a.dtype) for a in args]
+        out_specs=(hbm,) * (len(packs) + 2),
+        scratch_shapes=[pltpu.VMEM(a.shape, a.dtype) for a in args[:7]]
         + [
             pltpu.VMEM((seqs * residues, LANES), jnp.float32),
             pltpu.VMEM((seqs * residues, LANES), jnp.float32),
@@ -322,7 +313,6 @@
             pltpu.VMEM((LANES, LANES), jnp.float32),
             pltpu.VMEM((minor * residues, LANES), jnp.float32),
             pltpu.VMEM((minor * residues, LANES), jnp.bfloat16),
-            pltpu.VMEM((w.shape[0] + 8, cz), jnp.float32),
             pltpu.SemaphoreType.DMA((pieces + len(args) + sum(len(pack) for pack in packs),)),
         ],
         compiler_params=pltpu.CompilerParams(vmem_limit_bytes=VMEM_ALL),
@@ -338,7 +328,7 @@
     sizes = dict(parts=narrow, minor=minor, seqs_total=seqs * narrow)
     out_shape = jax.ShapeDtypeStruct((own_rows, wide * residues, cz), jnp.bfloat16)
     if direct:
-        return pairs_by_block(made, across, along, w, out_shape, residues, sizes, params)
+        return pairs_by_block(made, across, along, w, shift, out_shape, residues, sizes, params)
 
     lefts = [made[0]] + [across(made[m], m) for m in range(1, narrow)]
     every = lax.all_gather(made[narrow], ("wide", "narrow"), axis=0, tiled=False)
@@ -355,6 +345,7 @@
         + [
             pl.BlockSpec((block, narrow, right_count, LANES), lambda b: (b, 0, 0, 0)),
             pl.BlockSpec(w.shape, lambda b: (0, 0)),
+            pl.BlockSpec(shift.shape, lambda b: (0,)),
         ],
         out_specs=pl.BlockSpec((own_rows, cols, cz), lambda b: (0, b, 0)),
         out_shape=out_shape,
@@ -362,13 +353,14 @@
             pltpu.VMEM((narrow, 2, seqs, 2 * groups * LANES), jnp.bfloat16),
             pltpu.VMEM((hidden * LANES // 2, 2 * cz), jnp.bfloat16),
             pltpu.VMEM((2 * groups * cols, hidden * LANES // 2), jnp.bfloat16),
+            pltpu.VMEM(w.shape, jnp.float32),
         ],
         compiler_params=params,
         name="pairs",
-    )(*lefts, every, w)
-
-
-def pairs_by_block(made, across, along, w, out_shape, residues, sizes, params):
+    )(*lefts, every, w, shift)
+
+
+def pairs_by_block(made, across, along, w, shift, out_shape, residues, sizes, params):
     left_own, right, to_core, to_chip = made
     left_count, right_count = left_own.shape[0], right.shape[0]
     hbm = pl.BlockSpec(memory_space=pltpu.HBM)
@@ -405,9 +397,9 @@
             shapes += [
                 jax.ShapeDtypeStruct((narrow, 2, LANES // narrow, 2 * groups * LANES), jnp.bfloat16),
                 jax.ShapeDtypeStruct((hidden * LANES // 2, 2 * cz), jnp.bfloat16),
-                jax.ShapeDtypeStruct((8, cz), jnp.float32),
             ]
-            outs += [vmem] * 3
+            outs += [vmem] * 2
+            scratch.append(pltpu.VMEM(w.shape, jnp.float32))
         if earlier:
             operands += [ref for ref, _ in earlier]
             shapes, outs = [out_shape], [hbm]
@@ -439,7 +431,8 @@
     both = across(pack(chip, after=(last,)), 1)
     lefts = ((left_own, 0), (core, 0), (chip, 0), (both, left_count))
     own = ((right, 0), (core, left_count), (chip, 2 * left_count), (both, 2 * left_count))
-    first, *shared = pairs(own, (0,), w, lefts=lefts)
+    first, *shared = pairs(own, (0,), w, shift, lefts=lefts)
+    shared.append(shift)
 
     other = across(middle, 2)
     onward = across(pack(other, after=shared[1:2]), 1)

time: 27.9 us -> 33.4 us (1.20)
  Pallas kernels: 8.52 us -> 14 us
  waiting for transfers between devices: 8.17 us -> 7.5 us
  local copies, waits for them, and re-layouts: 0.01 us -> 0.62 us
    pallas_call x1, Pallas kernels: 3.8 us -> 9.25 us  [on_device(): pl.pallas_call(functools.partial(features_kernel, packs=packs, parts=narr...]
    ppermute x8, waiting for transfers between devices: 3.28 us -> 2.63 us  [across(): return lax.ppermute(a, 'narrow', [(i, i ^ m) for i in range(narrow)])]
    unnamed x6 -> x8, local copies, waits for them, and re-layouts: 0.01 us -> 0.62 us
  transfers between devices with their start and end apart: 11 -> 11, of which waited for: 6 -> 6; matrix products, arithmetic and copies ran while one was open for 0% -> 0% of each run, Pallas kernels for 11% -> 10%
where the time goes in v11:
time: 33.4 us; the launch traced here: 33.2 us
  Pallas kernels  14 us (42%)
  starting transfers between devices  11 us (33%)
  waiting for transfers between devices  7.5 us (22%)
  local copies, waits for them, and re-layouts  0.62 us (2%)
    pallas_call x1, Pallas kernels, on_device(): pl.pallas_call(functools.partial(features_kernel, packs=packs, parts=narr...  9.25 us
    ppermute x3, starting transfers between devices, along(): return lax.ppermute(a, 'wide', [(i, i ^ d) for i in range(wide)])  6.52 us
    ppermute x3, waiting for transfers between devices, along(): return lax.ppermute(a, 'wide', [(i, i ^ d) for i in range(wide)])  4.87 us
    pallas_call x3, Pallas kernels, pairs(): pl.pallas_call(functools.partial(pair_kernel, operands=count, rights=plac...  4.68 us
    ppermute x8, starting transfers between devices, across(): return lax.ppermute(a, 'narrow', [(i, i ^ m) for i in range(narrow)])  4.47 us
    ppermute x8, waiting for transfers between devices, across(): return lax.ppermute(a, 'narrow', [(i, i ^ m) for i in range(narrow)])  2.63 us
  transfers between devices with their start and end apart: 11, of which 6 were waited for; matrix products, arithmetic and copies ran while one was open for 0% of the time, Pallas kernels for 10%

profile of v11, /device:TPU:0, one launch (start us, length us, event | category | flops | bytes accessed | tf_op | source)
XLA Modules:
  0.0 33.2 jit_solution(13392672412053943055)
XLA Ops:
  0.0 9.3 %features.1 = (bf16[96,128]{1,0:T(8,128)(2,1)}, bf16[384,128]{1,0:T(8,128)(2,1)}, bf16[480,128]{1,0:T(8,128)(2,1)}, bf16[576,128]{1,0:T(8,128)(2,1)}, bf16[1024,128]{1,0:T(8,128)(2,1)}, /*index=5*/f32[128]{0:T(128)}) custom-call(bf16[32,48,256]{2,1,0:T(8,128)(2,1)} %refs_0_.1, f32[256]{0:T(256)} %refs_1_.1, f32[256]{0:T(256)} %refs_2_.1, ...), custom_call_target="tpu_custom_call" | custom-call | tf_op jit(solution)/shard_map/features/pallas_call | solution.py:297
  9.3 4.1 %collective-permute-start = (bf16[384,128]{1,0:T(8,128)(2,1)}, bf16[384,128]{1,0:T(8,128)(2,1)S(1)}, u32[]{:S(2)}, u32[]{:S(2)}) collective-permute-start(bf16[384,128]{1,0:T(8,128)(2,1)} %get-tuple-element.14.refs_0_), channel_id=1, source_target_pairs={{0,8},{4,12},{8,0},{12,4},{1,9},{5,13},{9,1},{13,5},{2,10},{6,14},... | collective-permute-start | bytes 294920 | tf_op jit(solution)/shard_map/ppermute | solution.py:326
  13.4 1.5 %collective-permute-start.5 = (bf16[576,128]{1,0:T(8,128)(2,1)}, bf16[576,128]{1,0:T(8,128)(2,1)S(1)}, u32[]{:S(2)}, u32[]{:S(2)}) collective-permute-start(bf16[576,128]{1,0:T(8,128)(2,1)} %get-tuple-element.16), channel_id=1, source_target_pairs={{0,2},{1,3},{2,0},{3,1},{4,6},{5,7},{6,4},{7,5},{8,10},{9,11},{10,... | collective-permute-start | bytes 442376 | tf_op jit(solution)/shard_map/ppermute | solution.py:323
  14.9 0.0 collective-permute-start.4
  14.9 1.6 %collective-permute-start.7 = (bf16[384,128]{1,0:T(8,128)(2,1)}, bf16[384,128]{1,0:T(8,128)(2,1)S(1)}, u32[]{:S(2)}, u32[]{:S(2)}) collective-permute-start(bf16[384,128]{1,0:T(8,128)(2,1)} %get-tuple-element.14.refs_0_), channel_id=1, source_target_pairs={{0,4},{4,0},{8,12},{12,8},{1,5},{5,1},{9,13},{13,9},{2,6},{6,2},{1... | collective-permute-start | bytes 294920 | tf_op jit(solution)/shard_map/ppermute | solution.py:326
  16.4 2.1 %collective-permute-done.refs_1_ = bf16[384,128]{1,0:T(8,128)(2,1)S(1)} collective-permute-done((bf16[384,128]{1,0:T(8,128)(2,1)}, bf16[384,128]{1,0:T(8,128)(2,1)S(1)}, u32[]{:S(2)}, u32[]{:S(2)}) %collective-permute-start) | collective-permute-done | bytes 98336 | tf_op jit(solution)/shard_map/ppermute | solution.py:326
  18.5 0.8 %collective-permute-start.1 = (bf16[384,128]{1,0:T(8,128)(2,1)S(1)}, bf16[384,128]{1,0:T(8,128)(2,1)S(1)}, u32[]{:S(2)}, u32[]{:S(2)}) collective-permute-start(bf16[384,128]{1,0:T(8,128)(2,1)S(1)} %collective-permute-done.refs_1_), channel_id=1, source_target_pairs={{0,4},{4,0},{8,12},{12,8},{1,5},{5,1},{9,13},{13,9},{2,6},{6,2},{1... | collective-permute-start | bytes 294920 | tf_op jit(solution)/shard_map/ppermute | solution.py:326
  19.3 1.4 %collective-permute-done.7.refs_0_ = bf16[384,128]{1,0:T(8,128)(2,1)S(1)} collective-permute-done((bf16[384,128]{1,0:T(8,128)(2,1)}, bf16[384,128]{1,0:T(8,128)(2,1)S(1)}, u32[]{:S(2)}, u32[]{:S(2)}) %collective-permute-start.7) | collective-permute-done | bytes 98336 | tf_op jit(solution)/shard_map/ppermute | solution.py:326
  20.7 0.0 collective-permute-done.4.refs_1_.refs_5_.refs_3_
  20.7 0.0 collective-permute-done.5.refs_0_.refs_2_.refs_6_
  20.8 0.0 copy-start
  20.8 0.0 copy-start.1
  20.8 0.0 copy-start.2
  20.8 0.9 %collective-permute-start.9 = (bf16[768,128]{1,0:T(8,128)(2,1)S(1)}, bf16[768,128]{1,0:T(8,128)(2,1)S(1)}, u32[]{:S(2)}, u32[]{:S(2)}) collective-permute-start(bf16[768,128]{1,0:T(8,128)(2,1)S(1)} %pack.6.refs_0_), channel_id=1, source_target_pairs={{0,2},{1,3},{2,0},{3,1},{4,6},{5,7},{6,4},{7,5},{8,10},{9,11},{10,... | collective-permute-start | bytes 589832 | tf_op jit(solution)/shard_map/ppermute | solution.py:323
  21.7 1.4 %collective-permute-done.1.refs_0_.refs_1_ = bf16[384,128]{1,0:T(8,128)(2,1)S(1)} collective-permute-done((bf16[384,128]{1,0:T(8,128)(2,1)S(1)}, bf16[384,128]{1,0:T(8,128)(2,1)S(1)}, u32[]{:S(2)}, u32[]{:S(2)}) %collective-permute-start.1) | collective-permute-done | bytes 98336 | tf_op jit(solution)/shard_map/ppermute | solution.py:326
  23.1 0.1 collective-permute-start.6
  23.2 1.7 %collective-permute-start.2 = (bf16[384,128]{1,0:T(8,128)(2,1)S(1)}, bf16[384,128]{1,0:T(8,128)(2,1)S(1)}, u32[]{:S(2)}, u32[]{:S(2)}) collective-permute-start(bf16[384,128]{1,0:T(8,128)(2,1)S(1)} %collective-permute-done.1.refs_0_.refs_1_), channel_id=1, source_target_pairs={{0,2},{1,3},{2,0},{3,1},{4,6},{5,7},{6,4},{7,5},{8,10},{9,11},{10,... | collective-permute-start | bytes 294920 | tf_op jit(solution)/shard_map/ppermute | solution.py:323
  24.9 0.2 collective-permute-start.8
  25.1 0.0 collective-permute-done.6.refs_3_.refs_7_
  25.1 0.0 copy-start.3
  25.1 0.0 copy-done
  25.1 0.0 copy-done.1
  25.1 0.0 copy-done.2
  25.1 0.6 %copy-done.3 = f32[128]{0:T(128)S(1)} copy-done((f32[128]{0:T(128)S(1)}, f32[128]{0:T(128)}, u32[]{:S(2)}) %copy-start.3) | copy-done | bytes 536
  25.7 1.5 %pairs_0.1 = (bf16[12,48,128]{2,1,0:T(8,128)(2,1)S(1)}, bf16[4,2,32,768]{3,2,1,0:T(8,128)(2,1)S(1)}, bf16[2048,256]{1,0:T(8,128)(2,1)S(1)}) custom-call(bf16[384,128]{1,0:T(8,128)(2,1)S(1)} %copy-done.1, bf16[480,128]{1,0:T(8,128)(2,1)S(1)} %collective-permute-done.4.refs_1_.refs_5_.refs_3_, ...), custom_call_target="tpu_custom_call" | custom-call | flops 1000 | bytes 1000 | tf_op jit(solution)/shard_map/pairs_0/pallas_call | solution.py:410
  27.2 1.3 %collective-permute-done.9.refs_0_.refs_2_ = bf16[768,128]{1,0:T(8,128)(2,1)S(1)} collective-permute-done((bf16[768,128]{1,0:T(8,128)(2,1)S(1)}, bf16[768,128]{1,0:T(8,128)(2,1)S(1)}, u32[]{:S(2)}, u32[]{:S(2)}) %collective-permute-start.9) | collective-permute-done | bytes 196640 | tf_op jit(solution)/shard_map/ppermute | solution.py:323
  28.5 0.1 collective-permute-start.10
  28.6 1.0 %collective-permute-done.2.refs_1_.refs_2_ = bf16[384,128]{1,0:T(8,128)(2,1)S(1)} collective-permute-done((bf16[384,128]{1,0:T(8,128)(2,1)S(1)}, bf16[384,128]{1,0:T(8,128)(2,1)S(1)}, u32[]{:S(2)}, u32[]{:S(2)}) %collective-permute-start.2) | collective-permute-done | bytes 98336 | tf_op jit(solution)/shard_map/ppermute | solution.py:323
  29.6 0.1 collective-permute-start.3
  29.7 0.0 collective-permute-done.8.refs_1_
  29.7 0.4 %collective-permute-done.10.refs_3_ = bf16[768,128]{1,0:T(8,128)(2,1)S(1)} collective-permute-done((bf16[768,128]{1,0:T(8,128)(2,1)S(1)}, bf16[768,128]{1,0:T(8,128)(2,1)S(1)}, u32[]{:S(2)}, u32[]{:S(2)}) %collective-permute-start.10) | collective-permute-done | bytes 196640 | tf_op jit(solution)/shard_map/ppermute | solution.py:323
  30.0 1.6 %pairs_1.1.refs_8_ = bf16[12,96,128]{2,1,0:T(8,128)(2,1)S(1)} custom-call(bf16[768,128]{1,0:T(8,128)(2,1)S(1)} %pack.6.refs_0_, bf16[768,128]{1,0:T(8,128)(2,1)S(1)} %collective-permute-done.8.refs_1_, bf16[768,128]{1,0:T(8,128)(2,1)S(1)} %collective-permute-done.9.refs_0_.refs_2_, bf16[768,128]{1,0:T(8,128)(2,1)S(1)} %collective-permute-done.10.refs_3_, ...), custom_call_target="tpu_custom_call" | custom-call | flops 1000 | bytes 1000 | tf_op jit(solution)/shard_map/pairs_1/pallas_call | solution.py:410
  31.6 0.0 collective-permute-done.3.refs_1_.refs_3_
  31.6 1.6 %pairs_3.1 = bf16[12,192,128]{2,1,0:T(8,128)(2,1)} custom-call(bf16[384,128]{1,0:T(8,128)(2,1)S(1)} %collective-permute-done.1.refs_0_.refs_1_, bf16[768,128]{1,0:T(8,128)(2,1)S(1)} %collective-permute-done.3.refs_1_.refs_3_, bf16[384,128]{1,0:T(8,128)(2,1)S(1)} %collective-permute-done.2.refs_1_.refs_2_, ...), custom_call_target="tpu_custom_call" | custom-call | flops 1000 | bytes 1000 | tf_op jit(solution)/shard_map/pairs_3/pallas_call | solution.py:410
  (4 shorter events, 0.1 us)
Async XLA Ops:
  9.3 9.2 %collective-permute-start = (bf16[384,128]{1,0:T(8,128)(2,1)}, bf16[384,128]{1,0:T(8,128)(2,1)S(1)}, u32[]{:S(2)}, u32[]{:S(2)}) collective-permute-start(bf16[384,128]{1,0:T(8,128)(2,1)} %get-tuple-element.14.refs_0_), channel_id=1, source_target_pairs={{0,8},{4,12},{8,0},{12,4},{1,9},{5,13},{9,1},{13,5},{2,10},{6,14},... | collective-permute-start | bytes 294920 | tf_op jit(solution)/shard_map/ppermute | solution.py:326
  13.4 7.4 %collective-permute-start.5 = (bf16[576,128]{1,0:T(8,128)(2,1)}, bf16[576,128]{1,0:T(8,128)(2,1)S(1)}, u32[]{:S(2)}, u32[]{:S(2)}) collective-permute-start(bf16[576,128]{1,0:T(8,128)(2,1)} %get-tuple-element.16), channel_id=1, source_target_pairs={{0,2},{1,3},{2,0},{3,1},{4,6},{5,7},{6,4},{7,5},{8,10},{9,11},{10,... | collective-permute-start | bytes 442376 | tf_op jit(solution)/shard_map/ppermute | solution.py:323
  14.9 5.9 %collective-permute-start.4 = (bf16[480,128]{1,0:T(8,128)(2,1)}, bf16[480,128]{1,0:T(8,128)(2,1)S(1)}, u32[]{:S(2)}, u32[]{:S(2)}) collective-permute-start(bf16[480,128]{1,0:T(8,128)(2,1)} %get-tuple-element.15), channel_id=1, source_target_pairs={{0,1},{1,0},{2,3},{3,2},{4,5},{5,4},{6,7},{7,6},{8,9},{9,8},{10,11... | collective-permute-start | bytes 368648 | tf_op jit(solution)/shard_map/ppermute | solution.py:323
  14.9 5.9 %collective-permute-start.7 = (bf16[384,128]{1,0:T(8,128)(2,1)}, bf16[384,128]{1,0:T(8,128)(2,1)S(1)}, u32[]{:S(2)}, u32[]{:S(2)}) collective-permute-start(bf16[384,128]{1,0:T(8,128)(2,1)} %get-tuple-element.14.refs_0_), channel_id=1, source_target_pairs={{0,4},{4,0},{8,12},{12,8},{1,5},{5,1},{9,13},{13,9},{2,6},{6,2},{1... | collective-permute-start | bytes 294920 | tf_op jit(solution)/shard_map/ppermute | solution.py:326
  18.5 4.6 %collective-permute-start.1 = (bf16[384,128]{1,0:T(8,128)(2,1)S(1)}, bf16[384,128]{1,0:T(8,128)(2,1)S(1)}, u32[]{:S(2)}, u32[]{:S(2)}) collective-permute-start(bf16[384,128]{1,0:T(8,128)(2,1)S(1)} %collective-permute-done.refs_1_), channel_id=1, source_target_pairs={{0,4},{4,0},{8,12},{12,8},{1,5},{5,1},{9,13},{13,9},{2,6},{6,2},{1... | collective-permute-start | bytes 294920 | tf_op jit(solution)/shard_map/ppermute | solution.py:326
  20.8 4.3 %copy-start = (bf16[1024,128]{1,0:T(8,128)(2,1)S(1)}, bf16[1024,128]{1,0:T(8,128)(2,1)}, u32[]{:S(2)}) copy-start(bf16[1024,128]{1,0:T(8,128)(2,1)} %get-tuple-element.18.refs_8_) | copy-start | bytes 786436
  20.8 4.3 %copy-start.1 = (bf16[384,128]{1,0:T(8,128)(2,1)S(1)}, bf16[384,128]{1,0:T(8,128)(2,1)}, u32[]{:S(2)}) copy-start(bf16[384,128]{1,0:T(8,128)(2,1)} %get-tuple-element.14.refs_0_) | copy-start | bytes 294916
  20.8 4.3 %copy-start.2 = (bf16[96,128]{1,0:T(8,128)(2,1)S(1)}, bf16[96,128]{1,0:T(8,128)(2,1)}, u32[]{:S(2)}) copy-start(bf16[96,128]{1,0:T(8,128)(2,1)} %get-tuple-element.17.refs_4_) | copy-start | bytes 73732
  20.8 7.7 %collective-permute-start.9 = (bf16[768,128]{1,0:T(8,128)(2,1)S(1)}, bf16[768,128]{1,0:T(8,128)(2,1)S(1)}, u32[]{:S(2)}, u32[]{:S(2)}) collective-permute-start(bf16[768,128]{1,0:T(8,128)(2,1)S(1)} %pack.6.refs_0_), channel_id=1, source_target_pairs={{0,2},{1,3},{2,0},{3,1},{4,6},{5,7},{6,4},{7,5},{8,10},{9,11},{10,... | collective-permute-start | bytes 589832 | tf_op jit(solution)/shard_map/ppermute | solution.py:323
  23.1 1.9 %collective-permute-start.6 = (bf16[576,128]{1,0:T(8,128)(2,1)S(1)}, bf16[576,128]{1,0:T(8,128)(2,1)S(1)}, u32[]{:S(2)}, u32[]{:S(2)}) collective-permute-start(bf16[576,128]{1,0:T(8,128)(2,1)S(1)} %pack.5), channel_id=1, source_target_pairs={{0,1},{1,0},{2,3},{3,2},{4,5},{5,4},{6,7},{7,6},{8,9},{9,8},{10,11... | collective-permute-start | bytes 442376 | tf_op jit(solution)/shard_map/ppermute | solution.py:323
  23.2 6.4 %collective-permute-start.2 = (bf16[384,128]{1,0:T(8,128)(2,1)S(1)}, bf16[384,128]{1,0:T(8,128)(2,1)S(1)}, u32[]{:S(2)}, u32[]{:S(2)}) collective-permute-start(bf16[384,128]{1,0:T(8,128)(2,1)S(1)} %collective-permute-done.1.refs_0_.refs_1_), channel_id=1, source_target_pairs={{0,2},{1,3},{2,0},{3,1},{4,6},{5,7},{6,4},{7,5},{8,10},{9,11},{10,... | collective-permute-start | bytes 294920 | tf_op jit(solution)/shard_map/ppermute | solution.py:323
  24.9 4.8 %collective-permute-start.8 = (bf16[768,128]{1,0:T(8,128)(2,1)S(1)}, bf16[768,128]{1,0:T(8,128)(2,1)S(1)}, u32[]{:S(2)}, u32[]{:S(2)}) collective-permute-start(bf16[768,128]{1,0:T(8,128)(2,1)S(1)} %pack.6.refs_0_), channel_id=1, source_target_pairs={{0,1},{1,0},{2,3},{3,2},{4,5},{5,4},{6,7},{7,6},{8,9},{9,8},{10,11... | collective-permute-start | bytes 589832 | tf_op jit(solution)/shard_map/ppermute | solution.py:323
  25.1 0.6 %copy-start.3 = (f32[128]{0:T(128)S(1)}, f32[128]{0:T(128)}, u32[]{:S(2)}) copy-start(f32[128]{0:T(128)} %get-tuple-element.19.refs_9_.refs_6_) | copy-start | bytes 1540
  28.5 1.5 %collective-permute-start.10 = (bf16[768,128]{1,0:T(8,128)(2,1)S(1)}, bf16[768,128]{1,0:T(8,128)(2,1)S(1)}, u32[]{:S(2)}, u32[]{:S(2)}) collective-permute-start(bf16[768,128]{1,0:T(8,128)(2,1)S(1)} %pack.7), channel_id=1, source_target_pairs={{0,1},{1,0},{2,3},{3,2},{4,5},{5,4},{6,7},{7,6},{8,9},{9,8},{10,11... | collective-permute-start | bytes 589832 | tf_op jit(solution)/shard_map/ppermute | solution.py:323
  29.6 2.1 %collective-permute-start.3 = (bf16[768,128]{1,0:T(8,128)(2,1)S(1)}, bf16[768,128]{1,0:T(8,128)(2,1)S(1)}, u32[]{:S(2)}, u32[]{:S(2)}) collective-permute-start(bf16[768,128]{1,0:T(8,128)(2,1)S(1)} %pack.4), channel_id=1, source_target_pairs={{0,1},{1,0},{2,3},{3,2},{4,5},{5,4},{6,7},{7,6},{8,9},{9,8},{10,11... | collective-permute-start | bytes 589832 | tf_op jit(solution)/shard_map/ppermute | solution.py:323

commit v12 on v8

--- a/solution.py
+++ b/solution.py
@@ -378,13 +378,14 @@
     hidden = narrow * sizes["minor"]
     groups = own_rows * hidden // LANES
 
-    def pack(*chunks, after):
+    def pack(*chunks, after, weight=1):
         return pl.pallas_call(
             functools.partial(pack_kernel, count=len(chunks)),
             out_shape=jax.ShapeDtypeStruct((sum(c.shape[0] for c in chunks), LANES), jnp.bfloat16),
             in_specs=[vmem] * (len(chunks) + len(after)),
             out_specs=vmem,
             compiler_params=params,
+            cost_estimate=pl.CostEstimate(flops=weight, bytes_accessed=1000, transcendentals=0),
             name="pack",
         )(*chunks, *after)
 
@@ -434,15 +435,15 @@
     last = along(far, 1)
     chip = across(to_chip, 2)
     core = across(to_core, 1)
-    middle = pack(near, far, after=(chip, core))
+    middle = pack(near, far, after=(), weight=4_000_000_000)
     beside = across(middle, 1)
-    both = across(pack(chip, after=(last,)), 1)
+    both = across(pack(chip, after=(last, core)), 1)
     lefts = ((left_own, 0), (core, 0), (chip, 0), (both, left_count))
     own = ((right, 0), (core, left_count), (chip, 2 * left_count), (both, 2 * left_count))
     first, *shared = pairs(own, (0,), w, lefts=lefts)
 
     other = across(middle, 2)
-    onward = across(pack(other, after=shared[1:2]), 1)
+    onward = across(pack(other, after=(shared[1],)), 1)
     (second,) = pairs(((middle, 0), (beside, 0), (other, 0), (onward, 0)), (1, 2), *shared)
 
     other = across(last, 2)

time: 27.9 us -> 26.4 us (0.946)
  waiting for transfers between devices: 8.17 us -> 5.31 us
  starting transfers between devices: 11 us -> 12.2 us
    ppermute x8, waiting for transfers between devices: 3.28 us -> 1.3 us  [across(): return lax.ppermute(a, 'narrow', [(i, i ^ m) for i in range(narrow)])]
    ppermute x8, starting transfers between devices: 4.46 us -> 5.58 us  [across(): return lax.ppermute(a, 'narrow', [(i, i ^ m) for i in range(narrow)])]
    ppermute x3, waiting for transfers between devices: 4.89 us -> 4.01 us  [along(): return lax.ppermute(a, 'wide', [(i, i ^ d) for i in range(wide)])]
  transfers between devices with their start and end apart: 11 -> 11, of which waited for: 6 -> 3; matrix products, arithmetic and copies ran while one was open for 0% -> 0% of each run, Pallas kernels for 11% -> 12%
where the time goes in v12:
time: 26.4 us; the launch traced here: 26.2 us
  starting transfers between devices  12.2 us (46%)
  Pallas kernels  8.56 us (32%)
  waiting for transfers between devices  5.31 us (20%)
    ppermute x3, starting transfers between devices, along(): return lax.ppermute(a, 'wide', [(i, i ^ d) for i in range(wide)])  6.61 us
    ppermute x8, starting transfers between devices, across(): return lax.ppermute(a, 'narrow', [(i, i ^ m) for i in range(narrow)])  5.58 us
    pallas_call x3, Pallas kernels, pairs(): pl.pallas_call(functools.partial(pair_kernel, operands=count, rights=plac...  4.71 us
    ppermute x3, waiting for transfers between devices, along(): return lax.ppermute(a, 'wide', [(i, i ^ d) for i in range(wide)])  4.01 us
    pallas_call x1, Pallas kernels, on_device(): pl.pallas_call(functools.partial(features_kernel, packs=packs, parts=narr...  3.8 us
    ppermute x8, waiting for transfers between devices, across(): return lax.ppermute(a, 'narrow', [(i, i ^ m) for i in range(narrow)])  1.3 us
  transfers between devices with their start and end apart: 11, of which 3 were waited for; matrix products, arithmetic and copies ran while one was open for 0% of the time, Pallas kernels for 12%

profile of v12, /device:TPU:0, one launch (start us, length us, event | category | flops | bytes accessed | tf_op | source)
XLA Modules:
  0.0 26.2 jit_solution(15339512727929719010)
XLA Ops:
  0.0 3.8 %features.1 = (bf16[96,128]{1,0:T(8,128)(2,1)}, bf16[384,128]{1,0:T(8,128)(2,1)}, bf16[480,128]{1,0:T(8,128)(2,1)}, bf16[576,128]{1,0:T(8,128)(2,1)}, f32[1032,128]{1,0:T(8,128)}) custom-call(bf16[32,48,256]{2,1,0:T(8,128)(2,1)} %refs_0_.1, f32[256]{0:T(256)} %refs_1_.1, f32[256]{0:T(256)} %refs_2_.1, bf16[32,256]{1,0:T(8,128)(2,1)} %bitcast.2, f32[32]{0:T(128)} %refs_4_.1, ...), custom_call_target="tpu_custom_call" | custom-call | tf_op jit(solution)/shard_map/features/pallas_call | solution.py:306
  3.8 4.1 %collective-permute-start = (bf16[384,128]{1,0:T(8,128)(2,1)}, bf16[384,128]{1,0:T(8,128)(2,1)S(1)}, u32[]{:S(2)}, u32[]{:S(2)}) collective-permute-start(bf16[384,128]{1,0:T(8,128)(2,1)} %get-tuple-element.14.refs_0_), channel_id=1, source_target_pairs={{0,8},{4,12},{8,0},{12,4},{1,9},{5,13},{9,1},{13,5},{2,10},{6,14},... | collective-permute-start | bytes 294920 | tf_op jit(solution)/shard_map/ppermute | solution.py:336
  7.9 1.6 %collective-permute-start.7 = (bf16[384,128]{1,0:T(8,128)(2,1)}, bf16[384,128]{1,0:T(8,128)(2,1)S(1)}, u32[]{:S(2)}, u32[]{:S(2)}) collective-permute-start(bf16[384,128]{1,0:T(8,128)(2,1)} %get-tuple-element.14.refs_0_), channel_id=1, source_target_pairs={{0,4},{4,0},{8,12},{12,8},{1,5},{5,1},{9,13},{13,9},{2,6},{6,2},{1... | collective-permute-start | bytes 294920 | tf_op jit(solution)/shard_map/ppermute | solution.py:336
  9.5 1.5 %collective-permute-start.5 = (bf16[576,128]{1,0:T(8,128)(2,1)}, bf16[576,128]{1,0:T(8,128)(2,1)S(1)}, u32[]{:S(2)}, u32[]{:S(2)}) collective-permute-start(bf16[576,128]{1,0:T(8,128)(2,1)} %get-tuple-element.16), channel_id=1, source_target_pairs={{0,2},{1,3},{2,0},{3,1},{4,6},{5,7},{6,4},{7,5},{8,10},{9,11},{10,... | collective-permute-start | bytes 442376 | tf_op jit(solution)/shard_map/ppermute | solution.py:333
  11.0 0.0 collective-permute-start.4
  11.0 1.9 %collective-permute-done.refs_1_ = bf16[384,128]{1,0:T(8,128)(2,1)S(1)} collective-permute-done((bf16[384,128]{1,0:T(8,128)(2,1)}, bf16[384,128]{1,0:T(8,128)(2,1)S(1)}, u32[]{:S(2)}, u32[]{:S(2)}) %collective-permute-start) | collective-permute-done | bytes 98336 | tf_op jit(solution)/shard_map/ppermute | solution.py:336
  12.9 0.9 %collective-permute-start.1 = (bf16[384,128]{1,0:T(8,128)(2,1)S(1)}, bf16[384,128]{1,0:T(8,128)(2,1)S(1)}, u32[]{:S(2)}, u32[]{:S(2)}) collective-permute-start(bf16[384,128]{1,0:T(8,128)(2,1)S(1)} %collective-permute-done.refs_1_), channel_id=1, source_target_pairs={{0,4},{4,0},{8,12},{12,8},{1,5},{5,1},{9,13},{13,9},{2,6},{6,2},{1... | collective-permute-start | bytes 294920 | tf_op jit(solution)/shard_map/ppermute | solution.py:336
  13.8 0.0 collective-permute-done.7.refs_0_
  13.8 0.0 copy-start
  13.9 0.0 copy-start.1
  13.9 0.0 copy-start.2
  13.9 1.6 %collective-permute-start.9 = (bf16[768,128]{1,0:T(8,128)(2,1)S(1)}, bf16[768,128]{1,0:T(8,128)(2,1)S(1)}, u32[]{:S(2)}, u32[]{:S(2)}) collective-permute-start(bf16[768,128]{1,0:T(8,128)(2,1)S(1)} %pack.6.refs_0_), channel_id=1, source_target_pairs={{0,2},{1,3},{2,0},{3,1},{4,6},{5,7},{6,4},{7,5},{8,10},{9,11},{10,... | collective-permute-start | bytes 589832 | tf_op jit(solution)/shard_map/ppermute | solution.py:333
  15.4 0.0 collective-permute-done.4.refs_2_.refs_1_.refs_5_
  15.4 0.0 collective-permute-done.5.refs_0_.refs_2_.refs_6_
  15.4 2.1 %collective-permute-done.1.refs_0_.refs_1_ = bf16[384,128]{1,0:T(8,128)(2,1)S(1)} collective-permute-done((bf16[384,128]{1,0:T(8,128)(2,1)S(1)}, bf16[384,128]{1,0:T(8,128)(2,1)S(1)}, u32[]{:S(2)}, u32[]{:S(2)}) %collective-permute-start.1) | collective-permute-done | bytes 98336 | tf_op jit(solution)/shard_map/ppermute | solution.py:336
  17.5 0.1 collective-permute-start.6
  17.6 1.8 %collective-permute-start.2 = (bf16[384,128]{1,0:T(8,128)(2,1)S(1)}, bf16[384,128]{1,0:T(8,128)(2,1)S(1)}, u32[]{:S(2)}, u32[]{:S(2)}) collective-permute-start(bf16[384,128]{1,0:T(8,128)(2,1)S(1)} %collective-permute-done.1.refs_0_.refs_1_), channel_id=1, source_target_pairs={{0,2},{1,3},{2,0},{3,1},{4,6},{5,7},{6,4},{7,5},{8,10},{9,11},{10,... | collective-permute-start | bytes 294920 | tf_op jit(solution)/shard_map/ppermute | solution.py:333
  19.4 0.2 collective-permute-start.8
  19.6 0.0 collective-permute-done.6.refs_3_.refs_7_
  19.6 0.0 copy-done
  19.6 0.0 copy-done.1
  19.6 0.0 copy-done.2
  19.6 1.5 %pairs_0.1 = (bf16[12,48,128]{2,1,0:T(8,128)(2,1)S(1)}, bf16[4,2,32,768]{3,2,1,0:T(8,128)(2,1)S(1)}, bf16[2048,256]{1,0:T(8,128)(2,1)S(1)}, f32[8,128]{1,0:T(8,128)S(1)}) custom-call(bf16[384,128]{1,0:T(8,128)(2,1)S(1)} %copy-done.1, bf16[480,128]{1,0:T(8,128)(2,1)S(1)} %collective-permute-done.4.refs_2_.refs_1_.refs_5_, ...), custom_call_target="tpu_custom_call" | custom-call | flops 1000 | bytes 1000 | tf_op jit(solution)/shard_map/pairs_0/pallas_call | solution.py:419
  21.1 0.0 collective-permute-done.9.refs_0_.refs_2_
  21.1 0.4 %collective-permute-start.10 = (bf16[768,128]{1,0:T(8,128)(2,1)S(1)}, bf16[768,128]{1,0:T(8,128)(2,1)S(1)}, u32[]{:S(2)}, u32[]{:S(2)}) collective-permute-start(bf16[768,128]{1,0:T(8,128)(2,1)S(1)} %pack.7), channel_id=1, source_target_pairs={{0,1},{1,0},{2,3},{3,2},{4,5},{5,4},{6,7},{7,6},{8,9},{9,8},{10,11... | collective-permute-start | bytes 589832 | tf_op jit(solution)/shard_map/ppermute | solution.py:333
  21.5 1.3 %collective-permute-done.2.refs_1_.refs_2_ = bf16[384,128]{1,0:T(8,128)(2,1)S(1)} collective-permute-done((bf16[384,128]{1,0:T(8,128)(2,1)S(1)}, bf16[384,128]{1,0:T(8,128)(2,1)S(1)}, u32[]{:S(2)}, u32[]{:S(2)}) %collective-permute-start.2) | collective-permute-done | bytes 98336 | tf_op jit(solution)/shard_map/ppermute | solution.py:333
  22.8 0.1 collective-permute-start.3
  22.9 0.0 collective-permute-done.8.refs_1_
  22.9 0.0 collective-permute-done.10.refs_3_
  22.9 1.6 %pairs_1.1.refs_8_ = bf16[12,96,128]{2,1,0:T(8,128)(2,1)S(1)} custom-call(bf16[768,128]{1,0:T(8,128)(2,1)S(1)} %pack.6.refs_0_, bf16[768,128]{1,0:T(8,128)(2,1)S(1)} %collective-permute-done.8.refs_1_, bf16[768,128]{1,0:T(8,128)(2,1)S(1)} %collective-permute-done.9.refs_0_.refs_2_, bf16[768,128]{1,0:T(8,128)(2,1)S(1)} %collective-permute-done.10.refs_3_, ...), custom_call_target="tpu_custom_call" | custom-call | flops 1000 | bytes 1000 | tf_op jit(solution)/shard_map/pairs_1/pallas_call | solution.py:419
  24.6 0.0 collective-permute-done.3.refs_1_.refs_3_
  24.6 1.6 %pairs_3.1 = bf16[12,192,128]{2,1,0:T(8,128)(2,1)} custom-call(bf16[384,128]{1,0:T(8,128)(2,1)S(1)} %collective-permute-done.1.refs_0_.refs_1_, bf16[768,128]{1,0:T(8,128)(2,1)S(1)} %collective-permute-done.3.refs_1_.refs_3_, bf16[384,128]{1,0:T(8,128)(2,1)S(1)} %collective-permute-done.2.refs_1_.refs_2_, ...), custom_call_target="tpu_custom_call" | custom-call | flops 1000 | bytes 1000 | tf_op jit(solution)/shard_map/pairs_3/pallas_call | solution.py:419
  (4 shorter events, 0.1 us)
Async XLA Ops:
  3.8 9.1 %collective-permute-start = (bf16[384,128]{1,0:T(8,128)(2,1)}, bf16[384,128]{1,0:T(8,128)(2,1)S(1)}, u32[]{:S(2)}, u32[]{:S(2)}) collective-permute-start(bf16[384,128]{1,0:T(8,128)(2,1)} %get-tuple-element.14.refs_0_), channel_id=1, source_target_pairs={{0,8},{4,12},{8,0},{12,4},{1,9},{5,13},{9,1},{13,5},{2,10},{6,14},... | collective-permute-start | bytes 294920 | tf_op jit(solution)/shard_map/ppermute | solution.py:336
  7.9 5.9 %collective-permute-start.7 = (bf16[384,128]{1,0:T(8,128)(2,1)}, bf16[384,128]{1,0:T(8,128)(2,1)S(1)}, u32[]{:S(2)}, u32[]{:S(2)}) collective-permute-start(bf16[384,128]{1,0:T(8,128)(2,1)} %get-tuple-element.14.refs_0_), channel_id=1, source_target_pairs={{0,4},{4,0},{8,12},{12,8},{1,5},{5,1},{9,13},{13,9},{2,6},{6,2},{1... | collective-permute-start | bytes 294920 | tf_op jit(solution)/shard_map/ppermute | solution.py:336
  9.5 6.0 %collective-permute-start.5 = (bf16[576,128]{1,0:T(8,128)(2,1)}, bf16[576,128]{1,0:T(8,128)(2,1)S(1)}, u32[]{:S(2)}, u32[]{:S(2)}) collective-permute-start(bf16[576,128]{1,0:T(8,128)(2,1)} %get-tuple-element.16), channel_id=1, source_target_pairs={{0,2},{1,3},{2,0},{3,1},{4,6},{5,7},{6,4},{7,5},{8,10},{9,11},{10,... | collective-permute-start | bytes 442376 | tf_op jit(solution)/shard_map/ppermute | solution.py:333
  11.0 4.5 %collective-permute-start.4 = (bf16[480,128]{1,0:T(8,128)(2,1)}, bf16[480,128]{1,0:T(8,128)(2,1)S(1)}, u32[]{:S(2)}, u32[]{:S(2)}) collective-permute-start(bf16[480,128]{1,0:T(8,128)(2,1)} %get-tuple-element.15), channel_id=1, source_target_pairs={{0,1},{1,0},{2,3},{3,2},{4,5},{5,4},{6,7},{7,6},{8,9},{9,8},{10,11... | collective-permute-start | bytes 368648 | tf_op jit(solution)/shard_map/ppermute | solution.py:333
  12.9 4.6 %collective-permute-start.1 = (bf16[384,128]{1,0:T(8,128)(2,1)S(1)}, bf16[384,128]{1,0:T(8,128)(2,1)S(1)}, u32[]{:S(2)}, u32[]{:S(2)}) collective-permute-start(bf16[384,128]{1,0:T(8,128)(2,1)S(1)} %collective-permute-done.refs_1_), channel_id=1, source_target_pairs={{0,4},{4,0},{8,12},{12,8},{1,5},{5,1},{9,13},{13,9},{2,6},{6,2},{1... | collective-permute-start | bytes 294920 | tf_op jit(solution)/shard_map/ppermute | solution.py:336
  13.8 5.8 %copy-start = (f32[1032,128]{1,0:T(8,128)S(1)}, f32[1032,128]{1,0:T(8,128)}, u32[]{:S(2)}) copy-start(f32[1032,128]{1,0:T(8,128)} %get-tuple-element.18.refs_8_) | copy-start | bytes 1585156
  13.9 5.7 %copy-start.1 = (bf16[384,128]{1,0:T(8,128)(2,1)S(1)}, bf16[384,128]{1,0:T(8,128)(2,1)}, u32[]{:S(2)}) copy-start(bf16[384,128]{1,0:T(8,128)(2,1)} %get-tuple-element.14.refs_0_) | copy-start | bytes 294916
  13.9 5.7 %copy-start.2 = (bf16[96,128]{1,0:T(8,128)(2,1)S(1)}, bf16[96,128]{1,0:T(8,128)(2,1)}, u32[]{:S(2)}) copy-start(bf16[96,128]{1,0:T(8,128)(2,1)} %get-tuple-element.17.refs_4_) | copy-start | bytes 73732
  13.9 7.2 %collective-permute-start.9 = (bf16[768,128]{1,0:T(8,128)(2,1)S(1)}, bf16[768,128]{1,0:T(8,128)(2,1)S(1)}, u32[]{:S(2)}, u32[]{:S(2)}) collective-permute-start(bf16[768,128]{1,0:T(8,128)(2,1)S(1)} %pack.6.refs_0_), channel_id=1, source_target_pairs={{0,2},{1,3},{2,0},{3,1},{4,6},{5,7},{6,4},{7,5},{8,10},{9,11},{10,... | collective-permute-start | bytes 589832 | tf_op jit(solution)/shard_map/ppermute | solution.py:333
  17.5 2.1 %collective-permute-start.6 = (bf16[576,128]{1,0:T(8,128)(2,1)S(1)}, bf16[576,128]{1,0:T(8,128)(2,1)S(1)}, u32[]{:S(2)}, u32[]{:S(2)}) collective-permute-start(bf16[576,128]{1,0:T(8,128)(2,1)S(1)} %pack.5), channel_id=1, source_target_pairs={{0,1},{1,0},{2,3},{3,2},{4,5},{5,4},{6,7},{7,6},{8,9},{9,8},{10,11... | collective-permute-start | bytes 442376 | tf_op jit(solution)/shard_map/ppermute | solution.py:333
  17.6 5.2 %collective-permute-start.2 = (bf16[384,128]{1,0:T(8,128)(2,1)S(1)}, bf16[384,128]{1,0:T(8,128)(2,1)S(1)}, u32[]{:S(2)}, u32[]{:S(2)}) collective-permute-start(bf16[384,128]{1,0:T(8,128)(2,1)S(1)} %collective-permute-done.1.refs_0_.refs_1_), channel_id=1, source_target_pairs={{0,2},{1,3},{2,0},{3,1},{4,6},{5,7},{6,4},{7,5},{8,10},{9,11},{10,... | collective-permute-start | bytes 294920 | tf_op jit(solution)/shard_map/ppermute | solution.py:333
  19.4 3.5 %collective-permute-start.8 = (bf16[768,128]{1,0:T(8,128)(2,1)S(1)}, bf16[768,128]{1,0:T(8,128)(2,1)S(1)}, u32[]{:S(2)}, u32[]{:S(2)}) collective-permute-start(bf16[768,128]{1,0:T(8,128)(2,1)S(1)} %pack.6.refs_0_), channel_id=1, source_target_pairs={{0,1},{1,0},{2,3},{3,2},{4,5},{5,4},{6,7},{7,6},{8,9},{9,8},{10,11... | collective-permute-start | bytes 589832 | tf_op jit(solution)/shard_map/ppermute | solution.py:333
  21.1 1.8 %collective-permute-start.10 = (bf16[768,128]{1,0:T(8,128)(2,1)S(1)}, bf16[768,128]{1,0:T(8,128)(2,1)S(1)}, u32[]{:S(2)}, u32[]{:S(2)}) collective-permute-start(bf16[768,128]{1,0:T(8,128)(2,1)S(1)} %pack.7), channel_id=1, source_target_pairs={{0,1},{1,0},{2,3},{3,2},{4,5},{5,4},{6,7},{7,6},{8,9},{9,8},{10,11... | collective-permute-start | bytes 589832 | tf_op jit(solution)/shard_map/ppermute | solution.py:333
  22.8 1.7 %collective-permute-start.3 = (bf16[768,128]{1,0:T(8,128)(2,1)S(1)}, bf16[768,128]{1,0:T(8,128)(2,1)S(1)}, u32[]{:S(2)}, u32[]{:S(2)}) collective-permute-start(bf16[768,128]{1,0:T(8,128)(2,1)S(1)} %pack.4), channel_id=1, source_target_pairs={{0,1},{1,0},{2,3},{3,2},{4,5},{5,4},{6,7},{7,6},{8,9},{9,8},{10,11... | collective-permute-start | bytes 589832 | tf_op jit(solution)/shard_map/ppermute | solution.py:333

commit v13 on v12

--- a/solution.py
+++ b/solution.py
@@ -192,7 +192,9 @@
     residues = right_of(0, 0).shape[0] // minor
     cols = wides * residues
     slot = iota((minor * residues, LANES), 1) // seqs
-    for q in range(parts):
+    width = half * LANES
+
+    def outer_of(q):
         left = jnp.concatenate([spread_ref[q ^ k, i] for i in range(2) for k in range(parts)], axis=0)
         for d in range(wides):
             right = None
@@ -205,10 +207,20 @@
                 for g in range(halves):
                     outer_ref[
                         pl.ds(g * cols + d * residues, residues),
-                        (q * half + t) * LANES : (q * half + t + 1) * LANES,
+                        q * width + t * LANES : q * width + (t + 1) * LANES,
                     ] = outer[t * residues : (t + 1) * residues, g * LANES : (g + 1) * LANES]
 
-    pairs = jnp.dot(outer_ref[...], wide_ref[...], preferred_element_type=jnp.float32)
+    def share_of(q):
+        lanes = slice(q * width, (q + 1) * width)
+        return jnp.dot(outer_ref[:, lanes], wide_ref[lanes], preferred_element_type=jnp.float32)
+
+    outer_of(0)
+    pairs = None
+    for q in range(1, parts + 1):
+        if q < parts:
+            outer_of(q)
+        share = share_of(q - 1)
+        pairs = share if pairs is None else pairs + share
     rows_each = wide_ref.shape[1] // cz
     for g in range(halves):
         for k in range(rows_each):

time: 26.4 us -> 26.7 us (1.011)
  Pallas kernels: 8.56 us -> 8.88 us
    pallas_call x3, Pallas kernels: 4.71 us -> 5.03 us  [pairs(): pl.pallas_call(functools.partial(pair_kernel, operands=count, rights=plac...]
where the time goes in v13:
time: 26.7 us; the launch traced here: 26.6 us
  starting transfers between devices  12.2 us (46%)
  Pallas kernels  8.88 us (33%)
  waiting for transfers between devices  5.35 us (20%)
    ppermute x3, starting transfers between devices, along(): return lax.ppermute(a, 'wide', [(i, i ^ d) for i in range(wide)])  6.61 us
    ppermute x8, starting transfers between devices, across(): return lax.ppermute(a, 'narrow', [(i, i ^ m) for i in range(narrow)])  5.58 us
    pallas_call x3, Pallas kernels, pairs(): pl.pallas_call(functools.partial(pair_kernel, operands=count, rights=plac...  5.03 us
    ppermute x3, waiting for transfers between devices, along(): return lax.ppermute(a, 'wide', [(i, i ^ d) for i in range(wide)])  4.01 us
    pallas_call x1, Pallas kernels, on_device(): pl.pallas_call(functools.partial(features_kernel, packs=packs, parts=narr...  3.8 us
    ppermute x8, waiting for transfers between devices, across(): return lax.ppermute(a, 'narrow', [(i, i ^ m) for i in range(narrow)])  1.34 us
  transfers between devices with their start and end apart: 11, of which 3 were waited for; matrix products, arithmetic and copies ran while one was open for 0% of the time, Pallas kernels for 12%

profile of v13, /device:TPU:0, one launch (start us, length us, event | category | flops | bytes accessed | tf_op | source)
XLA Modules:
  0.0 26.6 jit_solution(18087909399106648544)
XLA Ops:
  0.0 3.8 %features.1 = (bf16[96,128]{1,0:T(8,128)(2,1)}, bf16[384,128]{1,0:T(8,128)(2,1)}, bf16[480,128]{1,0:T(8,128)(2,1)}, bf16[576,128]{1,0:T(8,128)(2,1)}, f32[1032,128]{1,0:T(8,128)}) custom-call(bf16[32,48,256]{2,1,0:T(8,128)(2,1)} %refs_0_.1, f32[256]{0:T(256)} %refs_1_.1, f32[256]{0:T(256)} %refs_2_.1, bf16[32,256]{1,0:T(8,128)(2,1)} %bitcast.2, f32[32]{0:T(128)} %refs_4_.1, ...), custom_call_target="tpu_custom_call" | custom-call | tf_op jit(solution)/shard_map/features/pallas_call | solution.py:318
  3.8 4.1 %collective-permute-start = (bf16[384,128]{1,0:T(8,128)(2,1)}, bf16[384,128]{1,0:T(8,128)(2,1)S(1)}, u32[]{:S(2)}, u32[]{:S(2)}) collective-permute-start(bf16[384,128]{1,0:T(8,128)(2,1)} %get-tuple-element.14.refs_0_), channel_id=1, source_target_pairs={{0,8},{4,12},{8,0},{12,4},{1,9},{5,13},{9,1},{13,5},{2,10},{6,14},... | collective-permute-start | bytes 294920 | tf_op jit(solution)/shard_map/ppermute | solution.py:348
  7.9 1.6 %collective-permute-start.7 = (bf16[384,128]{1,0:T(8,128)(2,1)}, bf16[384,128]{1,0:T(8,128)(2,1)S(1)}, u32[]{:S(2)}, u32[]{:S(2)}) collective-permute-start(bf16[384,128]{1,0:T(8,128)(2,1)} %get-tuple-element.14.refs_0_), channel_id=1, source_target_pairs={{0,4},{4,0},{8,12},{12,8},{1,5},{5,1},{9,13},{13,9},{2,6},{6,2},{1... | collective-permute-start | bytes 294920 | tf_op jit(solution)/shard_map/ppermute | solution.py:348
  9.5 1.5 %collective-permute-start.5 = (bf16[576,128]{1,0:T(8,128)(2,1)}, bf16[576,128]{1,0:T(8,128)(2,1)S(1)}, u32[]{:S(2)}, u32[]{:S(2)}) collective-permute-start(bf16[576,128]{1,0:T(8,128)(2,1)} %get-tuple-element.16), channel_id=1, source_target_pairs={{0,2},{1,3},{2,0},{3,1},{4,6},{5,7},{6,4},{7,5},{8,10},{9,11},{10,... | collective-permute-start | bytes 442376 | tf_op jit(solution)/shard_map/ppermute | solution.py:345
  11.0 0.0 collective-permute-start.4
  11.0 1.9 %collective-permute-done.refs_1_ = bf16[384,128]{1,0:T(8,128)(2,1)S(1)} collective-permute-done((bf16[384,128]{1,0:T(8,128)(2,1)}, bf16[384,128]{1,0:T(8,128)(2,1)S(1)}, u32[]{:S(2)}, u32[]{:S(2)}) %collective-permute-start) | collective-permute-done | bytes 98336 | tf_op jit(solution)/shard_map/ppermute | solution.py:348
  12.9 0.9 %collective-permute-start.1 = (bf16[384,128]{1,0:T(8,128)(2,1)S(1)}, bf16[384,128]{1,0:T(8,128)(2,1)S(1)}, u32[]{:S(2)}, u32[]{:S(2)}) collective-permute-start(bf16[384,128]{1,0:T(8,128)(2,1)S(1)} %collective-permute-done.refs_1_), channel_id=1, source_target_pairs={{0,4},{4,0},{8,12},{12,8},{1,5},{5,1},{9,13},{13,9},{2,6},{6,2},{1... | collective-permute-start | bytes 294920 | tf_op jit(solution)/shard_map/ppermute | solution.py:348
  13.8 0.0 collective-permute-done.7.refs_0_
  13.8 0.0 copy-start
  13.9 0.0 copy-start.1
  13.9 0.0 copy-start.2
  13.9 1.6 %collective-permute-start.9 = (bf16[768,128]{1,0:T(8,128)(2,1)S(1)}, bf16[768,128]{1,0:T(8,128)(2,1)S(1)}, u32[]{:S(2)}, u32[]{:S(2)}) collective-permute-start(bf16[768,128]{1,0:T(8,128)(2,1)S(1)} %pack.6.refs_0_), channel_id=1, source_target_pairs={{0,2},{1,3},{2,0},{3,1},{4,6},{5,7},{6,4},{7,5},{8,10},{9,11},{10,... | collective-permute-start | bytes 589832 | tf_op jit(solution)/shard_map/ppermute | solution.py:345
  15.4 0.0 collective-permute-done.4.refs_2_.refs_1_.refs_5_
  15.4 0.0 collective-permute-done.5.refs_0_.refs_2_.refs_6_
  15.4 2.1 %collective-permute-done.1.refs_0_.refs_1_ = bf16[384,128]{1,0:T(8,128)(2,1)S(1)} collective-permute-done((bf16[384,128]{1,0:T(8,128)(2,1)S(1)}, bf16[384,128]{1,0:T(8,128)(2,1)S(1)}, u32[]{:S(2)}, u32[]{:S(2)}) %collective-permute-start.1) | collective-permute-done | bytes 98336 | tf_op jit(solution)/shard_map/ppermute | solution.py:348
  17.5 0.1 collective-permute-start.6
  17.6 1.8 %collective-permute-start.2 = (bf16[384,128]{1,0:T(8,128)(2,1)S(1)}, bf16[384,128]{1,0:T(8,128)(2,1)S(1)}, u32[]{:S(2)}, u32[]{:S(2)}) collective-permute-start(bf16[384,128]{1,0:T(8,128)(2,1)S(1)} %collective-permute-done.1.refs_0_.refs_1_), channel_id=1, source_target_pairs={{0,2},{1,3},{2,0},{3,1},{4,6},{5,7},{6,4},{7,5},{8,10},{9,11},{10,... | collective-permute-start | bytes 294920 | tf_op jit(solution)/shard_map/ppermute | solution.py:345
  19.4 0.2 collective-permute-start.8
  19.6 0.0 collective-permute-done.6.refs_3_.refs_7_
  19.6 0.0 copy-done
  19.6 0.0 copy-done.1
  19.6 0.0 copy-done.2
  19.6 1.4 %pairs_0.1 = (bf16[12,48,128]{2,1,0:T(8,128)(2,1)S(1)}, bf16[4,2,32,768]{3,2,1,0:T(8,128)(2,1)S(1)}, bf16[2048,256]{1,0:T(8,128)(2,1)S(1)}, f32[8,128]{1,0:T(8,128)S(1)}) custom-call(bf16[384,128]{1,0:T(8,128)(2,1)S(1)} %copy-done.1, bf16[480,128]{1,0:T(8,128)(2,1)S(1)} %collective-permute-done.4.refs_2_.refs_1_.refs_5_, ...), custom_call_target="tpu_custom_call" | custom-call | flops 1000 | bytes 1000 | tf_op jit(solution)/shard_map/pairs_0/pallas_call | solution.py:431
  21.1 0.0 collective-permute-done.9.refs_0_.refs_2_
  21.1 0.4 %collective-permute-start.10 = (bf16[768,128]{1,0:T(8,128)(2,1)S(1)}, bf16[768,128]{1,0:T(8,128)(2,1)S(1)}, u32[]{:S(2)}, u32[]{:S(2)}) collective-permute-start(bf16[768,128]{1,0:T(8,128)(2,1)S(1)} %pack.7), channel_id=1, source_target_pairs={{0,1},{1,0},{2,3},{3,2},{4,5},{5,4},{6,7},{7,6},{8,9},{9,8},{10,11... | collective-permute-start | bytes 589832 | tf_op jit(solution)/shard_map/ppermute | solution.py:345
  21.5 1.3 %collective-permute-done.2.refs_1_.refs_2_ = bf16[384,128]{1,0:T(8,128)(2,1)S(1)} collective-permute-done((bf16[384,128]{1,0:T(8,128)(2,1)S(1)}, bf16[384,128]{1,0:T(8,128)(2,1)S(1)}, u32[]{:S(2)}, u32[]{:S(2)}) %collective-permute-start.2) | collective-permute-done | bytes 98336 | tf_op jit(solution)/shard_map/ppermute | solution.py:345
  22.8 0.1 collective-permute-start.3
  22.9 0.0 collective-permute-done.8.refs_1_
  22.9 0.0 collective-permute-done.10.refs_3_
  22.9 1.8 %pairs_1.1.refs_8_ = bf16[12,96,128]{2,1,0:T(8,128)(2,1)S(1)} custom-call(bf16[768,128]{1,0:T(8,128)(2,1)S(1)} %pack.6.refs_0_, bf16[768,128]{1,0:T(8,128)(2,1)S(1)} %collective-permute-done.8.refs_1_, bf16[768,128]{1,0:T(8,128)(2,1)S(1)} %collective-permute-done.9.refs_0_.refs_2_, bf16[768,128]{1,0:T(8,128)(2,1)S(1)} %collective-permute-done.10.refs_3_, ...), custom_call_target="tpu_custom_call" | custom-call | flops 1000 | bytes 1000 | tf_op jit(solution)/shard_map/pairs_1/pallas_call | solution.py:431
  24.8 0.0 collective-permute-done.3.refs_1_.refs_3_
  24.8 1.8 %pairs_3.1 = bf16[12,192,128]{2,1,0:T(8,128)(2,1)} custom-call(bf16[384,128]{1,0:T(8,128)(2,1)S(1)} %collective-permute-done.1.refs_0_.refs_1_, bf16[768,128]{1,0:T(8,128)(2,1)S(1)} %collective-permute-done.3.refs_1_.refs_3_, bf16[384,128]{1,0:T(8,128)(2,1)S(1)} %collective-permute-done.2.refs_1_.refs_2_, ...), custom_call_target="tpu_custom_call" | custom-call | flops 1000 | bytes 1000 | tf_op jit(solution)/shard_map/pairs_3/pallas_call | solution.py:431
  (4 shorter events, 0.1 us)
Async XLA Ops:
  3.8 9.1 %collective-permute-start = (bf16[384,128]{1,0:T(8,128)(2,1)}, bf16[384,128]{1,0:T(8,128)(2,1)S(1)}, u32[]{:S(2)}, u32[]{:S(2)}) collective-permute-start(bf16[384,128]{1,0:T(8,128)(2,1)} %get-tuple-element.14.refs_0_), channel_id=1, source_target_pairs={{0,8},{4,12},{8,0},{12,4},{1,9},{5,13},{9,1},{13,5},{2,10},{6,14},... | collective-permute-start | bytes 294920 | tf_op jit(solution)/shard_map/ppermute | solution.py:348
  7.9 5.9 %collective-permute-start.7 = (bf16[384,128]{1,0:T(8,128)(2,1)}, bf16[384,128]{1,0:T(8,128)(2,1)S(1)}, u32[]{:S(2)}, u32[]{:S(2)}) collective-permute-start(bf16[384,128]{1,0:T(8,128)(2,1)} %get-tuple-element.14.refs_0_), channel_id=1, source_target_pairs={{0,4},{4,0},{8,12},{12,8},{1,5},{5,1},{9,13},{13,9},{2,6},{6,2},{1... | collective-permute-start | bytes 294920 | tf_op jit(solution)/shard_map/ppermute | solution.py:348
  9.5 6.0 %collective-permute-start.5 = (bf16[576,128]{1,0:T(8,128)(2,1)}, bf16[576,128]{1,0:T(8,128)(2,1)S(1)}, u32[]{:S(2)}, u32[]{:S(2)}) collective-permute-start(bf16[576,128]{1,0:T(8,128)(2,1)} %get-tuple-element.16), channel_id=1, source_target_pairs={{0,2},{1,3},{2,0},{3,1},{4,6},{5,7},{6,4},{7,5},{8,10},{9,11},{10,... | collective-permute-start | bytes 442376 | tf_op jit(solution)/shard_map/ppermute | solution.py:345
  11.0 4.5 %collective-permute-start.4 = (bf16[480,128]{1,0:T(8,128)(2,1)}, bf16[480,128]{1,0:T(8,128)(2,1)S(1)}, u32[]{:S(2)}, u32[]{:S(2)}) collective-permute-start(bf16[480,128]{1,0:T(8,128)(2,1)} %get-tuple-element.15), channel_id=1, source_target_pairs={{0,1},{1,0},{2,3},{3,2},{4,5},{5,4},{6,7},{7,6},{8,9},{9,8},{10,11... | collective-permute-start | bytes 368648 | tf_op jit(solution)/shard_map/ppermute | solution.py:345
  12.9 4.6 %collective-permute-start.1 = (bf16[384,128]{1,0:T(8,128)(2,1)S(1)}, bf16[384,128]{1,0:T(8,128)(2,1)S(1)}, u32[]{:S(2)}, u32[]{:S(2)}) collective-permute-start(bf16[384,128]{1,0:T(8,128)(2,1)S(1)} %collective-permute-done.refs_1_), channel_id=1, source_target_pairs={{0,4},{4,0},{8,12},{12,8},{1,5},{5,1},{9,13},{13,9},{2,6},{6,2},{1... | collective-permute-start | bytes 294920 | tf_op jit(solution)/shard_map/ppermute | solution.py:348
  13.8 5.8 %copy-start = (f32[1032,128]{1,0:T(8,128)S(1)}, f32[1032,128]{1,0:T(8,128)}, u32[]{:S(2)}) copy-start(f32[1032,128]{1,0:T(8,128)} %get-tuple-element.18.refs_8_) | copy-start | bytes 1585156
  13.9 5.7 %copy-start.1 = (bf16[384,128]{1,0:T(8,128)(2,1)S(1)}, bf16[384,128]{1,0:T(8,128)(2,1)}, u32[]{:S(2)}) copy-start(bf16[384,128]{1,0:T(8,128)(2,1)} %get-tuple-element.14.refs_0_) | copy-start | bytes 294916
  13.9 5.7 %copy-start.2 = (bf16[96,128]{1,0:T(8,128)(2,1)S(1)}, bf16[96,128]{1,0:T(8,128)(2,1)}, u32[]{:S(2)}) copy-start(bf16[96,128]{1,0:T(8,128)(2,1)} %get-tuple-element.17.refs_4_) | copy-start | bytes 73732
  13.9 7.2 %collective-permute-start.9 = (bf16[768,128]{1,0:T(8,128)(2,1)S(1)}, bf16[768,128]{1,0:T(8,128)(2,1)S(1)}, u32[]{:S(2)}, u32[]{:S(2)}) collective-permute-start(bf16[768,128]{1,0:T(8,128)(2,1)S(1)} %pack.6.refs_0_), channel_id=1, source_target_pairs={{0,2},{1,3},{2,0},{3,1},{4,6},{5,7},{6,4},{7,5},{8,10},{9,11},{10,... | collective-permute-start | bytes 589832 | tf_op jit(solution)/shard_map/ppermute | solution.py:345
  17.5 2.1 %collective-permute-start.6 = (bf16[576,128]{1,0:T(8,128)(2,1)S(1)}, bf16[576,128]{1,0:T(8,128)(2,1)S(1)}, u32[]{:S(2)}, u32[]{:S(2)}) collective-permute-start(bf16[576,128]{1,0:T(8,128)(2,1)S(1)} %pack.5), channel_id=1, source_target_pairs={{0,1},{1,0},{2,3},{3,2},{4,5},{5,4},{6,7},{7,6},{8,9},{9,8},{10,11... | collective-permute-start | bytes 442376 | tf_op jit(solution)/shard_map/ppermute | solution.py:345
  17.6 5.2 %collective-permute-start.2 = (bf16[384,128]{1,0:T(8,128)(2,1)S(1)}, bf16[384,128]{1,0:T(8,128)(2,1)S(1)}, u32[]{:S(2)}, u32[]{:S(2)}) collective-permute-start(bf16[384,128]{1,0:T(8,128)(2,1)S(1)} %collective-permute-done.1.refs_0_.refs_1_), channel_id=1, source_target_pairs={{0,2},{1,3},{2,0},{3,1},{4,6},{5,7},{6,4},{7,5},{8,10},{9,11},{10,... | collective-permute-start | bytes 294920 | tf_op jit(solution)/shard_map/ppermute | solution.py:345
  19.4 3.5 %collective-permute-start.8 = (bf16[768,128]{1,0:T(8,128)(2,1)S(1)}, bf16[768,128]{1,0:T(8,128)(2,1)S(1)}, u32[]{:S(2)}, u32[]{:S(2)}) collective-permute-start(bf16[768,128]{1,0:T(8,128)(2,1)S(1)} %pack.6.refs_0_), channel_id=1, source_target_pairs={{0,1},{1,0},{2,3},{3,2},{4,5},{5,4},{6,7},{7,6},{8,9},{9,8},{10,11... | collective-permute-start | bytes 589832 | tf_op jit(solution)/shard_map/ppermute | solution.py:345
  21.1 1.8 %collective-permute-start.10 = (bf16[768,128]{1,0:T(8,128)(2,1)S(1)}, bf16[768,128]{1,0:T(8,128)(2,1)S(1)}, u32[]{:S(2)}, u32[]{:S(2)}) collective-permute-start(bf16[768,128]{1,0:T(8,128)(2,1)S(1)} %pack.7), channel_id=1, source_target_pairs={{0,1},{1,0},{2,3},{3,2},{4,5},{5,4},{6,7},{7,6},{8,9},{9,8},{10,11... | collective-permute-start | bytes 589832 | tf_op jit(solution)/shard_map/ppermute | solution.py:345
  22.8 1.9 %collective-permute-start.3 = (bf16[768,128]{1,0:T(8,128)(2,1)S(1)}, bf16[768,128]{1,0:T(8,128)(2,1)S(1)}, u32[]{:S(2)}, u32[]{:S(2)}) collective-permute-start(bf16[768,128]{1,0:T(8,128)(2,1)S(1)} %pack.4), channel_id=1, source_target_pairs={{0,1},{1,0},{2,3},{3,2},{4,5},{5,4},{6,7},{7,6},{8,9},{9,8},{10,11... | collective-permute-start | bytes 589832 | tf_op jit(solution)/shard_map/ppermute | solution.py:345

commit v14 on v12

--- a/solution.py
+++ b/solution.py
@@ -44,30 +44,46 @@
         copy.start()
     free = pieces + len(rest)
 
-    def norm(p):
-        gain = gain_ref[...].reshape(1, depth)
-        bias = bias_ref[...].reshape(1, depth)
-        step = min(4, piece)
-        for s in range(p * piece, (p + 1) * piece, step):
-            x = x_ref[s : s + step].reshape(step * residues, depth).astype(jnp.float32)
-            x = x - jnp.mean(x, axis=-1, keepdims=True)
-            spread = jnp.mean(x * x, axis=-1, keepdims=True)
-            x = x * lax.rsqrt(spread + 1e-05) * gain + bias
-            rows = pl.ds(s * residues, step * residues)
-            lo_ref[rows, :] = x[:, :LANES]
-            hi_ref[rows, :] = x[:, LANES:]
-
-    for copy in rest[:2]:
+    for copy in copies + rest:
         copy.wait()
-    for p in range(pieces - 1):
-        copies[p].wait()
-        norm(p)
-    for copy in copies[-1:] + rest[2:]:
-        copy.wait()
+
+    gain = gain_ref[...].reshape(1, depth)
+    bias = bias_ref[...].reshape(1, depth)
+    average = jnp.full((depth, LANES), 1.0 / depth, jnp.bfloat16)
+    span = piece * residues
+
+    def centered(p, center):
+        x = x_ref[p * piece : (p + 1) * piece].reshape(span, depth).astype(jnp.float32)
+        return [x[:, h * LANES : (h + 1) * LANES] - center for h in range(depth // LANES)]
+
+    centers = [
+        jnp.dot(
+            x_ref[p * piece : (p + 1) * piece].reshape(span, depth), average,
+            preferred_element_type=jnp.float32,
+        )
+        for p in range(pieces)
+    ]
+    spreads = []
+    for p in range(pieces):
+        square = sum(h * h for h in centered(p, centers[p]))
+        coarse = square.astype(jnp.bfloat16)
+        fine = (square - coarse.astype(jnp.float32)).astype(jnp.bfloat16)
+        spreads.append(
+            jnp.dot(
+                jnp.concatenate([coarse, fine], axis=1), average, preferred_element_type=jnp.float32
+            )
+        )
+    for p in range(pieces):
+        scale = lax.rsqrt(spreads[p] + 1e-05)
+        for h, ref in zip(range(depth // LANES), (lo_ref, hi_ref)):
+            lanes = slice(h * LANES, (h + 1) * LANES)
+            ref[p * span : (p + 1) * span, :] = (
+                centered(p, centers[p])[h] * scale * gain[:, lanes] + bias[:, lanes]
+            )
+
     count = w_ref.shape[0]
     wf_ref[:count] = w_ref[...].astype(jnp.float32)
     wf_ref[count:] = jnp.broadcast_to(shift_ref[...].reshape(1, -1), (8, shift_ref.shape[0]))
-    norm(pieces - 1)
 
     column, row = iota((hidden, LANES), 1) % hidden, iota((hidden, LANES), 0)
     spread_l = (column == row).astype(jnp.float32)
@@ -194,19 +210,23 @@
     slot = iota((minor * residues, LANES), 1) // seqs
     for q in range(parts):
         left = jnp.concatenate([spread_ref[q ^ k, i] for i in range(2) for k in range(parts)], axis=0)
+        rights = []
         for d in range(wides):
             right = None
             for k in range(parts):
                 chunk = right_of(d, q ^ k)
                 right = chunk if right is None else jnp.where(slot == k, chunk, right)
-            right = jnp.concatenate([right[: half * residues], right[half * residues :]], axis=1)
-            outer = jnp.dot(right, left, preferred_element_type=jnp.float32).astype(jnp.bfloat16)
+            rights.append(jnp.concatenate([right[: half * residues], right[half * residues :]], axis=1))
+        right = jnp.concatenate(rights, axis=0)
+        outer = jnp.dot(right, left, preferred_element_type=jnp.float32).astype(jnp.bfloat16)
+        for d in range(wides):
             for t in range(half):
+                at = (d * half + t) * residues
                 for g in range(halves):
                     outer_ref[
                         pl.ds(g * cols + d * residues, residues),
                         (q * half + t) * LANES : (q * half + t + 1) * LANES,
-                    ] = outer[t * residues : (t + 1) * residues, g * LANES : (g + 1) * LANES]
+                    ] = outer[at : at + residues, g * LANES : (g + 1) * LANES]
 
     pairs = jnp.dot(outer_ref[...], wide_ref[...], preferred_element_type=jnp.float32)
     rows_each = wide_ref.shape[1] // cz
@@ -251,8 +271,7 @@
             write(ref, places)
 
     def right_of(d, m):
-        ref, at = rights[m]
-        at += d * minor * residues
+        ref, at = rights[d][m]
         return inputs[ref][at : at + minor * residues, :]
 
     def store(row, pair):
@@ -390,12 +409,14 @@
         )(*chunks, *after)
 
     def pairs(rights, blocks, *shared, lefts=None, earlier=()):
-        operands, places = [], []
-        for chunks in (rights, lefts or ()):
-            places.append([])
-            for chunk, at in chunks:
-                places[-1].append((len(operands), at))
-                operands.append(chunk)
+        operands = []
+
+        def place(chunk, at):
+            operands.append(chunk)
+            return len(operands) - 1, at
+
+        rights = [[place(*chunk) for chunk in block] for block in rights]
+        lefts = lefts and [place(*chunk) for chunk in lefts]
         count = len(operands)
         operands += shared
         cols = len(blocks) * residues
@@ -418,8 +439,8 @@
             ]
         return pl.pallas_call(
             functools.partial(
-                pair_kernel, operands=count, rights=places[0], blocks=blocks,
-                earlier=[b for _, b in earlier], lefts=lefts and places[1], **sizes,
+                pair_kernel, operands=count, rights=rights, blocks=blocks,
+                earlier=[b for _, b in earlier], lefts=lefts, **sizes,
             ),
             out_shape=shapes,
             in_specs=[vmem] * len(operands),
@@ -440,16 +461,20 @@
     both = across(pack(chip, after=(last, core)), 1)
     lefts = ((left_own, 0), (core, 0), (chip, 0), (both, left_count))
     own = ((right, 0), (core, left_count), (chip, 2 * left_count), (both, 2 * left_count))
-    first, *shared = pairs(own, (0,), w, lefts=lefts)
+    first, *shared = pairs((own,), (0,), w, lefts=lefts)
 
     other = across(middle, 2)
     onward = across(pack(other, after=(shared[1],)), 1)
-    (second,) = pairs(((middle, 0), (beside, 0), (other, 0), (onward, 0)), (1, 2), *shared)
+    onward = ((onward, 0), (onward, right_count))
+    blocks = [
+        ((middle, at), (beside, at), (other, at), onward[i]) for i, at in enumerate((0, right_count))
+    ]
+    (second,) = pairs(blocks, (1, 2), *shared)
 
     other = across(last, 2)
     both = across(pack(last, other, after=()), 1)
     (out,) = pairs(
-        ((last, 0), (both, 0), (other, 0), (both, right_count)), (3,), *shared,
+        (((last, 0), (both, 0), (other, 0), (both, right_count)),), (3,), *shared,
         earlier=((first, (0,)), (second, (1, 2))),
     )
     return out

time: 26.4 us -> 26.7 us (1.011)
  Pallas kernels: 8.56 us -> 8.85 us
    pallas_call x1, Pallas kernels: 3.8 us -> 4.17 us  [on_device(): pl.pallas_call(functools.partial(features_kernel, packs=packs, parts=narr...]
where the time goes in v14:
time: 26.7 us; the launch traced here: 26.5 us
  starting transfers between devices  12.2 us (46%)
  Pallas kernels  8.85 us (33%)
  waiting for transfers between devices  5.31 us (20%)
    ppermute x3, starting transfers between devices, along(): return lax.ppermute(a, 'wide', [(i, i ^ d) for i in range(wide)])  6.61 us
    ppermute x8, starting transfers between devices, across(): return lax.ppermute(a, 'narrow', [(i, i ^ m) for i in range(narrow)])  5.6 us
    pallas_call x3, Pallas kernels, pairs(): pl.pallas_call(functools.partial(pair_kernel, operands=count, rights=righ...  4.63 us
    pallas_call x1, Pallas kernels, on_device(): pl.pallas_call(functools.partial(features_kernel, packs=packs, parts=narr...  4.17 us
    ppermute x3, waiting for transfers between devices, along(): return lax.ppermute(a, 'wide', [(i, i ^ d) for i in range(wide)])  4.01 us
    ppermute x8, waiting for transfers between devices, across(): return lax.ppermute(a, 'narrow', [(i, i ^ m) for i in range(narrow)])  1.3 us
  transfers between devices with their start and end apart: 11, of which 3 were waited for; matrix products, arithmetic and copies ran while one was open for 0% of the time, Pallas kernels for 12%

profile of v14, /device:TPU:0, one launch (start us, length us, event | category | flops | bytes accessed | tf_op | source)
XLA Modules:
  0.0 26.5 jit_solution(3091389973864959566)
XLA Ops:
  0.0 4.2 %features.1 = (bf16[96,128]{1,0:T(8,128)(2,1)}, bf16[384,128]{1,0:T(8,128)(2,1)}, bf16[480,128]{1,0:T(8,128)(2,1)}, bf16[576,128]{1,0:T(8,128)(2,1)}, f32[1032,128]{1,0:T(8,128)}) custom-call(bf16[32,48,256]{2,1,0:T(8,128)(2,1)} %refs_0_.1, f32[256]{0:T(256)} %refs_1_.1, f32[256]{0:T(256)} %refs_2_.1, bf16[32,256]{1,0:T(8,128)(2,1)} %bitcast.2, f32[32]{0:T(128)} %refs_4_.1, ...), custom_call_target="tpu_custom_call" | custom-call | tf_op jit(solution)/shard_map/features/pallas_call | solution.py:325
  4.2 4.1 %collective-permute-start = (bf16[384,128]{1,0:T(8,128)(2,1)}, bf16[384,128]{1,0:T(8,128)(2,1)S(1)}, u32[]{:S(2)}, u32[]{:S(2)}) collective-permute-start(bf16[384,128]{1,0:T(8,128)(2,1)} %get-tuple-element.14.refs_0_), channel_id=1, source_target_pairs={{0,8},{4,12},{8,0},{12,4},{1,9},{5,13},{9,1},{13,5},{2,10},{6,14},... | collective-permute-start | bytes 294920 | tf_op jit(solution)/shard_map/ppermute | solution.py:355
  8.3 1.6 %collective-permute-start.7 = (bf16[384,128]{1,0:T(8,128)(2,1)}, bf16[384,128]{1,0:T(8,128)(2,1)S(1)}, u32[]{:S(2)}, u32[]{:S(2)}) collective-permute-start(bf16[384,128]{1,0:T(8,128)(2,1)} %get-tuple-element.14.refs_0_), channel_id=1, source_target_pairs={{0,4},{4,0},{8,12},{12,8},{1,5},{5,1},{9,13},{13,9},{2,6},{6,2},{1... | collective-permute-start | bytes 294920 | tf_op jit(solution)/shard_map/ppermute | solution.py:355
  9.9 1.5 %collective-permute-start.5 = (bf16[576,128]{1,0:T(8,128)(2,1)}, bf16[576,128]{1,0:T(8,128)(2,1)S(1)}, u32[]{:S(2)}, u32[]{:S(2)}) collective-permute-start(bf16[576,128]{1,0:T(8,128)(2,1)} %get-tuple-element.16), channel_id=1, source_target_pairs={{0,2},{1,3},{2,0},{3,1},{4,6},{5,7},{6,4},{7,5},{8,10},{9,11},{10,... | collective-permute-start | bytes 442376 | tf_op jit(solution)/shard_map/ppermute | solution.py:352
  11.4 0.0 collective-permute-start.4
  11.4 1.9 %collective-permute-done.refs_1_ = bf16[384,128]{1,0:T(8,128)(2,1)S(1)} collective-permute-done((bf16[384,128]{1,0:T(8,128)(2,1)}, bf16[384,128]{1,0:T(8,128)(2,1)S(1)}, u32[]{:S(2)}, u32[]{:S(2)}) %collective-permute-start) | collective-permute-done | bytes 98336 | tf_op jit(solution)/shard_map/ppermute | solution.py:355
  13.3 0.9 %collective-permute-start.1 = (bf16[384,128]{1,0:T(8,128)(2,1)S(1)}, bf16[384,128]{1,0:T(8,128)(2,1)S(1)}, u32[]{:S(2)}, u32[]{:S(2)}) collective-permute-start(bf16[384,128]{1,0:T(8,128)(2,1)S(1)} %collective-permute-done.refs_1_), channel_id=1, source_target_pairs={{0,4},{4,0},{8,12},{12,8},{1,5},{5,1},{9,13},{13,9},{2,6},{6,2},{1... | collective-permute-start | bytes 294920 | tf_op jit(solution)/shard_map/ppermute | solution.py:355
  14.2 0.0 collective-permute-done.7.refs_0_
  14.2 0.0 copy-start
  14.2 0.0 copy-start.1
  14.3 0.0 copy-start.2
  14.3 1.6 %collective-permute-start.9 = (bf16[768,128]{1,0:T(8,128)(2,1)S(1)}, bf16[768,128]{1,0:T(8,128)(2,1)S(1)}, u32[]{:S(2)}, u32[]{:S(2)}) collective-permute-start(bf16[768,128]{1,0:T(8,128)(2,1)S(1)} %pack.6.refs_0_.refs_4_), channel_id=1, source_target_pairs={{0,2},{1,3},{2,0},{3,1},{4,6},{5,7},{6,4},{7,5},{8,10},{9,11},{10,... | collective-permute-start | bytes 589832 | tf_op jit(solution)/shard_map/ppermute | solution.py:352
  15.8 0.0 collective-permute-done.4.refs_2_.refs_1_.refs_5_
  15.8 0.0 collective-permute-done.5.refs_0_.refs_2_.refs_6_
  15.8 2.1 %collective-permute-done.1.refs_0_.refs_1_ = bf16[384,128]{1,0:T(8,128)(2,1)S(1)} collective-permute-done((bf16[384,128]{1,0:T(8,128)(2,1)S(1)}, bf16[384,128]{1,0:T(8,128)(2,1)S(1)}, u32[]{:S(2)}, u32[]{:S(2)}) %collective-permute-start.1) | collective-permute-done | bytes 98336 | tf_op jit(solution)/shard_map/ppermute | solution.py:355
  17.9 0.1 collective-permute-start.6
  18.0 1.8 %collective-permute-start.2 = (bf16[384,128]{1,0:T(8,128)(2,1)S(1)}, bf16[384,128]{1,0:T(8,128)(2,1)S(1)}, u32[]{:S(2)}, u32[]{:S(2)}) collective-permute-start(bf16[384,128]{1,0:T(8,128)(2,1)S(1)} %collective-permute-done.1.refs_0_.refs_1_), channel_id=1, source_target_pairs={{0,2},{1,3},{2,0},{3,1},{4,6},{5,7},{6,4},{7,5},{8,10},{9,11},{10,... | collective-permute-start | bytes 294920 | tf_op jit(solution)/shard_map/ppermute | solution.py:352
  19.8 0.2 collective-permute-start.8
  20.0 0.0 collective-permute-done.6.refs_3_.refs_7_
  20.0 0.0 copy-done
  20.0 0.0 copy-done.1
  20.0 0.0 copy-done.2
  20.0 1.5 %pairs_0.1 = (bf16[12,48,128]{2,1,0:T(8,128)(2,1)S(1)}, bf16[4,2,32,768]{3,2,1,0:T(8,128)(2,1)S(1)}, bf16[2048,256]{1,0:T(8,128)(2,1)S(1)}, f32[8,128]{1,0:T(8,128)S(1)}) custom-call(bf16[384,128]{1,0:T(8,128)(2,1)S(1)} %copy-done.1, bf16[480,128]{1,0:T(8,128)(2,1)S(1)} %collective-permute-done.4.refs_2_.refs_1_.refs_5_, ...), custom_call_target="tpu_custom_call" | custom-call | flops 1000 | bytes 1000 | tf_op jit(solution)/shard_map/pairs_0/pallas_call | solution.py:440
  21.5 0.0 collective-permute-done.9.refs_0_.refs_2_.refs_6_
  21.5 0.4 %collective-permute-start.10 = (bf16[768,128]{1,0:T(8,128)(2,1)S(1)}, bf16[768,128]{1,0:T(8,128)(2,1)S(1)}, u32[]{:S(2)}, u32[]{:S(2)}) collective-permute-start(bf16[768,128]{1,0:T(8,128)(2,1)S(1)} %pack.7), channel_id=1, source_target_pairs={{0,1},{1,0},{2,3},{3,2},{4,5},{5,4},{6,7},{7,6},{8,9},{9,8},{10,11... | collective-permute-start | bytes 589832 | tf_op jit(solution)/shard_map/ppermute | solution.py:352
  21.9 1.3 %collective-permute-done.2.refs_1_.refs_2_ = bf16[384,128]{1,0:T(8,128)(2,1)S(1)} collective-permute-done((bf16[384,128]{1,0:T(8,128)(2,1)S(1)}, bf16[384,128]{1,0:T(8,128)(2,1)S(1)}, u32[]{:S(2)}, u32[]{:S(2)}) %collective-permute-start.2) | collective-permute-done | bytes 98336 | tf_op jit(solution)/shard_map/ppermute | solution.py:352
  23.2 0.1 collective-permute-start.3
  23.3 0.0 collective-permute-done.8.refs_1_.refs_5_
  23.3 0.0 collective-permute-done.10.refs_3_.refs_7_
  23.3 1.6 %pairs_1.1.refs_8_ = bf16[12,96,128]{2,1,0:T(8,128)(2,1)S(1)} custom-call(bf16[768,128]{1,0:T(8,128)(2,1)S(1)} %pack.6.refs_0_.refs_4_, bf16[768,128]{1,0:T(8,128)(2,1)S(1)} %collective-permute-done.8.refs_1_.refs_5_, bf16[768,128]{1,0:T(8,128)(2,1)S(1)} %collective-permute-done.9.refs_0_.refs_2_.refs_6_, ...), custom_call_target="tpu_custom_call" | custom-call | flops 1000 | bytes 1000 | tf_op jit(solution)/shard_map/pairs_1/pallas_call | solution.py:440
  24.9 0.0 collective-permute-done.3.refs_1_.refs_3_
  24.9 1.6 %pairs_3.1 = bf16[12,192,128]{2,1,0:T(8,128)(2,1)} custom-call(bf16[384,128]{1,0:T(8,128)(2,1)S(1)} %collective-permute-done.1.refs_0_.refs_1_, bf16[768,128]{1,0:T(8,128)(2,1)S(1)} %collective-permute-done.3.refs_1_.refs_3_, bf16[384,128]{1,0:T(8,128)(2,1)S(1)} %collective-permute-done.2.refs_1_.refs_2_, ...), custom_call_target="tpu_custom_call" | custom-call | flops 1000 | bytes 1000 | tf_op jit(solution)/shard_map/pairs_3/pallas_call | solution.py:440
  (4 shorter events, 0.1 us)
Async XLA Ops:
  4.2 9.1 %collective-permute-start = (bf16[384,128]{1,0:T(8,128)(2,1)}, bf16[384,128]{1,0:T(8,128)(2,1)S(1)}, u32[]{:S(2)}, u32[]{:S(2)}) collective-permute-start(bf16[384,128]{1,0:T(8,128)(2,1)} %get-tuple-element.14.refs_0_), channel_id=1, source_target_pairs={{0,8},{4,12},{8,0},{12,4},{1,9},{5,13},{9,1},{13,5},{2,10},{6,14},... | collective-permute-start | bytes 294920 | tf_op jit(solution)/shard_map/ppermute | solution.py:355
  8.3 5.9 %collective-permute-start.7 = (bf16[384,128]{1,0:T(8,128)(2,1)}, bf16[384,128]{1,0:T(8,128)(2,1)S(1)}, u32[]{:S(2)}, u32[]{:S(2)}) collective-permute-start(bf16[384,128]{1,0:T(8,128)(2,1)} %get-tuple-element.14.refs_0_), channel_id=1, source_target_pairs={{0,4},{4,0},{8,12},{12,8},{1,5},{5,1},{9,13},{13,9},{2,6},{6,2},{1... | collective-permute-start | bytes 294920 | tf_op jit(solution)/shard_map/ppermute | solution.py:355
  9.9 6.0 %collective-permute-start.5 = (bf16[576,128]{1,0:T(8,128)(2,1)}, bf16[576,128]{1,0:T(8,128)(2,1)S(1)}, u32[]{:S(2)}, u32[]{:S(2)}) collective-permute-start(bf16[576,128]{1,0:T(8,128)(2,1)} %get-tuple-element.16), channel_id=1, source_target_pairs={{0,2},{1,3},{2,0},{3,1},{4,6},{5,7},{6,4},{7,5},{8,10},{9,11},{10,... | collective-permute-start | bytes 442376 | tf_op jit(solution)/shard_map/ppermute | solution.py:352
  11.4 4.5 %collective-permute-start.4 = (bf16[480,128]{1,0:T(8,128)(2,1)}, bf16[480,128]{1,0:T(8,128)(2,1)S(1)}, u32[]{:S(2)}, u32[]{:S(2)}) collective-permute-start(bf16[480,128]{1,0:T(8,128)(2,1)} %get-tuple-element.15), channel_id=1, source_target_pairs={{0,1},{1,0},{2,3},{3,2},{4,5},{5,4},{6,7},{7,6},{8,9},{9,8},{10,11... | collective-permute-start | bytes 368648 | tf_op jit(solution)/shard_map/ppermute | solution.py:352
  13.3 4.6 %collective-permute-start.1 = (bf16[384,128]{1,0:T(8,128)(2,1)S(1)}, bf16[384,128]{1,0:T(8,128)(2,1)S(1)}, u32[]{:S(2)}, u32[]{:S(2)}) collective-permute-start(bf16[384,128]{1,0:T(8,128)(2,1)S(1)} %collective-permute-done.refs_1_), channel_id=1, source_target_pairs={{0,4},{4,0},{8,12},{12,8},{1,5},{5,1},{9,13},{13,9},{2,6},{6,2},{1... | collective-permute-start | bytes 294920 | tf_op jit(solution)/shard_map/ppermute | solution.py:355
  14.2 5.8 %copy-start = (f32[1032,128]{1,0:T(8,128)S(1)}, f32[1032,128]{1,0:T(8,128)}, u32[]{:S(2)}) copy-start(f32[1032,128]{1,0:T(8,128)} %get-tuple-element.18.refs_8_) | copy-start | bytes 1585156
  14.2 5.7 %copy-start.1 = (bf16[384,128]{1,0:T(8,128)(2,1)S(1)}, bf16[384,128]{1,0:T(8,128)(2,1)}, u32[]{:S(2)}) copy-start(bf16[384,128]{1,0:T(8,128)(2,1)} %get-tuple-element.14.refs_0_) | copy-start | bytes 294916
  14.3 5.7 %copy-start.2 = (bf16[96,128]{1,0:T(8,128)(2,1)S(1)}, bf16[96,128]{1,0:T(8,128)(2,1)}, u32[]{:S(2)}) copy-start(bf16[96,128]{1,0:T(8,128)(2,1)} %get-tuple-element.17.refs_4_) | copy-start | bytes 73732
  14.3 7.2 %collective-permute-start.9 = (bf16[768,128]{1,0:T(8,128)(2,1)S(1)}, bf16[768,128]{1,0:T(8,128)(2,1)S(1)}, u32[]{:S(2)}, u32[]{:S(2)}) collective-permute-start(bf16[768,128]{1,0:T(8,128)(2,1)S(1)} %pack.6.refs_0_.refs_4_), channel_id=1, source_target_pairs={{0,2},{1,3},{2,0},{3,1},{4,6},{5,7},{6,4},{7,5},{8,10},{9,11},{10,... | collective-permute-start | bytes 589832 | tf_op jit(solution)/shard_map/ppermute | solution.py:352
  17.9 2.1 %collective-permute-start.6 = (bf16[576,128]{1,0:T(8,128)(2,1)S(1)}, bf16[576,128]{1,0:T(8,128)(2,1)S(1)}, u32[]{:S(2)}, u32[]{:S(2)}) collective-permute-start(bf16[576,128]{1,0:T(8,128)(2,1)S(1)} %pack.5), channel_id=1, source_target_pairs={{0,1},{1,0},{2,3},{3,2},{4,5},{5,4},{6,7},{7,6},{8,9},{9,8},{10,11... | collective-permute-start | bytes 442376 | tf_op jit(solution)/shard_map/ppermute | solution.py:352
  18.0 5.2 %collective-permute-start.2 = (bf16[384,128]{1,0:T(8,128)(2,1)S(1)}, bf16[384,128]{1,0:T(8,128)(2,1)S(1)}, u32[]{:S(2)}, u32[]{:S(2)}) collective-permute-start(bf16[384,128]{1,0:T(8,128)(2,1)S(1)} %collective-permute-done.1.refs_0_.refs_1_), channel_id=1, source_target_pairs={{0,2},{1,3},{2,0},{3,1},{4,6},{5,7},{6,4},{7,5},{8,10},{9,11},{10,... | collective-permute-start | bytes 294920 | tf_op jit(solution)/shard_map/ppermute | solution.py:352
  19.8 3.5 %collective-permute-start.8 = (bf16[768,128]{1,0:T(8,128)(2,1)S(1)}, bf16[768,128]{1,0:T(8,128)(2,1)S(1)}, u32[]{:S(2)}, u32[]{:S(2)}) collective-permute-start(bf16[768,128]{1,0:T(8,128)(2,1)S(1)} %pack.6.refs_0_.refs_4_), channel_id=1, source_target_pairs={{0,1},{1,0},{2,3},{3,2},{4,5},{5,4},{6,7},{7,6},{8,9},{9,8},{10,11... | collective-permute-start | bytes 589832 | tf_op jit(solution)/shard_map/ppermute | solution.py:352
  21.5 1.8 %collective-permute-start.10 = (bf16[768,128]{1,0:T(8,128)(2,1)S(1)}, bf16[768,128]{1,0:T(8,128)(2,1)S(1)}, u32[]{:S(2)}, u32[]{:S(2)}) collective-permute-start(bf16[768,128]{1,0:T(8,128)(2,1)S(1)} %pack.7), channel_id=1, source_target_pairs={{0,1},{1,0},{2,3},{3,2},{4,5},{5,4},{6,7},{7,6},{8,9},{9,8},{10,11... | collective-permute-start | bytes 589832 | tf_op jit(solution)/shard_map/ppermute | solution.py:352
  23.2 1.7 %collective-permute-start.3 = (bf16[768,128]{1,0:T(8,128)(2,1)S(1)}, bf16[768,128]{1,0:T(8,128)(2,1)S(1)}, u32[]{:S(2)}, u32[]{:S(2)}) collective-permute-start(bf16[768,128]{1,0:T(8,128)(2,1)S(1)} %pack.4), channel_id=1, source_target_pairs={{0,1},{1,0},{2,3},{3,2},{4,5},{5,4},{6,7},{7,6},{8,9},{9,8},{10,11... | collective-permute-start | bytes 589832 | tf_op jit(solution)/shard_map/ppermute | solution.py:352

commit v15 on v12

--- a/solution.py
+++ b/solution.py
@@ -79,18 +79,28 @@
             preferred_element_type=jnp.float32,
         )
 
-    def widen_bias(b, pick):
-        b = jnp.broadcast_to(b.reshape(1, hidden), (8, hidden))
-        return jnp.dot(
-            b, pick, precision=lax.Precision.HIGHEST, preferred_element_type=jnp.float32
-        )[:1]
+    lane = iota((8, LANES), 1)
+
+    def widen_bias(b):
+        b = jnp.concatenate([b.reshape(1, hidden)] * per, axis=1)
+        return jnp.broadcast_to(b, (8, LANES))
+
+    def swapped(b):
+        bit = 1
+        while bit < slots:
+            step = bit * minor
+            up, down = pltpu.roll(b, step, axis=1), pltpu.roll(b, LANES - step, axis=1)
+            other = jnp.where(lane & step != 0, up, down)
+            b = jnp.where(own & bit != 0, other, b)
+            bit *= 2
+        return b
 
     weights = jnp.concatenate(
         [widen(lm_ref[...], spread_l), widen(rm_ref[...], spread_r)], axis=1
     )
     shift = jnp.concatenate(
-        [widen_bias(lb_ref[...], spread_l), widen_bias(rb_ref[...], spread_r)], axis=1
-    )
+        [widen_bias(lb_ref[...]), swapped(widen_bias(rb_ref[...]))], axis=1
+    )[:1]
     place = iota((depth, 2 * LANES), 1) % LANES // hidden
     sends = [pltpu.make_async_copy(wf_ref, wf_hbm, sems.at[free])]
     sends[0].start()
@@ -194,19 +204,23 @@
     slot = iota((minor * residues, LANES), 1) // seqs
     for q in range(parts):
         left = jnp.concatenate([spread_ref[q ^ k, i] for i in range(2) for k in range(parts)], axis=0)
+        rights = []
         for d in range(wides):
             right = None
             for k in range(parts):
                 chunk = right_of(d, q ^ k)
                 right = chunk if right is None else jnp.where(slot == k, chunk, right)
-            right = jnp.concatenate([right[: half * residues], right[half * residues :]], axis=1)
-            outer = jnp.dot(right, left, preferred_element_type=jnp.float32).astype(jnp.bfloat16)
+            rights.append(jnp.concatenate([right[: half * residues], right[half * residues :]], axis=1))
+        right = jnp.concatenate(rights, axis=0)
+        outer = jnp.dot(right, left, preferred_element_type=jnp.float32).astype(jnp.bfloat16)
+        for d in range(wides):
             for t in range(half):
+                at = (d * half + t) * residues
                 for g in range(halves):
                     outer_ref[
                         pl.ds(g * cols + d * residues, residues),
                         (q * half + t) * LANES : (q * half + t + 1) * LANES,
-                    ] = outer[t * residues : (t + 1) * residues, g * LANES : (g + 1) * LANES]
+                    ] = outer[at : at + residues, g * LANES : (g + 1) * LANES]
 
     pairs = jnp.dot(outer_ref[...], wide_ref[...], preferred_element_type=jnp.float32)
     rows_each = wide_ref.shape[1] // cz
@@ -251,8 +265,7 @@
             write(ref, places)
 
     def right_of(d, m):
-        ref, at = rights[m]
-        at += d * minor * residues
+        ref, at = rights[d][m]
         return inputs[ref][at : at + minor * residues, :]
 
     def store(row, pair):
@@ -390,12 +403,14 @@
         )(*chunks, *after)
 
     def pairs(rights, blocks, *shared, lefts=None, earlier=()):
-        operands, places = [], []
-        for chunks in (rights, lefts or ()):
-            places.append([])
-            for chunk, at in chunks:
-                places[-1].append((len(operands), at))
-                operands.append(chunk)
+        operands = []
+
+        def place(chunk, at):
+            operands.append(chunk)
+            return len(operands) - 1, at
+
+        rights = [[place(*chunk) for chunk in block] for block in rights]
+        lefts = lefts and [place(*chunk) for chunk in lefts]
         count = len(operands)
         operands += shared
         cols = len(blocks) * residues
@@ -418,8 +433,8 @@
             ]
         return pl.pallas_call(
             functools.partial(
-                pair_kernel, operands=count, rights=places[0], blocks=blocks,
-                earlier=[b for _, b in earlier], lefts=lefts and places[1], **sizes,
+                pair_kernel, operands=count, rights=rights, blocks=blocks,
+                earlier=[b for _, b in earlier], lefts=lefts, **sizes,
             ),
             out_shape=shapes,
             in_specs=[vmem] * len(operands),
@@ -440,16 +455,20 @@
     both = across(pack(chip, after=(last, core)), 1)
     lefts = ((left_own, 0), (core, 0), (chip, 0), (both, left_count))
     own = ((right, 0), (core, left_count), (chip, 2 * left_count), (both, 2 * left_count))
-    first, *shared = pairs(own, (0,), w, lefts=lefts)
+    first, *shared = pairs((own,), (0,), w, lefts=lefts)
 
     other = across(middle, 2)
     onward = across(pack(other, after=(shared[1],)), 1)
-    (second,) = pairs(((middle, 0), (beside, 0), (other, 0), (onward, 0)), (1, 2), *shared)
+    onward = ((onward, 0), (onward, right_count))
+    blocks = [
+        ((middle, at), (beside, at), (other, at), onward[i]) for i, at in enumerate((0, right_count))
+    ]
+    (second,) = pairs(blocks, (1, 2), *shared)
 
     other = across(last, 2)
     both = across(pack(last, other, after=()), 1)
     (out,) = pairs(
-        ((last, 0), (both, 0), (other, 0), (both, right_count)), (3,), *shared,
+        (((last, 0), (both, 0), (other, 0), (both, right_count)),), (3,), *shared,
         earlier=((first, (0,)), (second, (1, 2))),
     )
     return out

time: 26.4 us -> 26.3 us (level)
  no operation moved by 1% of the time
where the time goes in v15:
time: 26.3 us; the launch traced here: 26.1 us
  starting transfers between devices  12.2 us (46%)
  Pallas kernels  8.44 us (32%)
  waiting for transfers between devices  5.29 us (20%)
    ppermute x3, starting transfers between devices, along(): return lax.ppermute(a, 'wide', [(i, i ^ d) for i in range(wide)])  6.62 us
    ppermute x8, starting transfers between devices, across(): return lax.ppermute(a, 'narrow', [(i, i ^ m) for i in range(narrow)])  5.6 us
    pallas_call x3, Pallas kernels, pairs(): pl.pallas_call(functools.partial(pair_kernel, operands=count, rights=righ...  4.63 us
    ppermute x3, waiting for transfers between devices, along(): return lax.ppermute(a, 'wide', [(i, i ^ d) for i in range(wide)])  3.99 us
    pallas_call x1, Pallas kernels, on_device(): pl.pallas_call(functools.partial(features_kernel, packs=packs, parts=narr...  3.76 us
    ppermute x8, waiting for transfers between devices, across(): return lax.ppermute(a, 'narrow', [(i, i ^ m) for i in range(narrow)])  1.3 us
  transfers between devices with their start and end apart: 11, of which 3 were waited for; matrix products, arithmetic and copies ran while one was open for 0% of the time, Pallas kernels for 12%

profile of v15, /device:TPU:0, one launch (start us, length us, event | category | flops | bytes accessed | tf_op | source)
XLA Modules:
  0.0 26.1 jit_solution(18073070191715875359)
XLA Ops:
  0.0 3.8 %features.1 = (bf16[96,128]{1,0:T(8,128)(2,1)}, bf16[384,128]{1,0:T(8,128)(2,1)}, bf16[480,128]{1,0:T(8,128)(2,1)}, bf16[576,128]{1,0:T(8,128)(2,1)}, f32[1032,128]{1,0:T(8,128)}) custom-call(bf16[32,48,256]{2,1,0:T(8,128)(2,1)} %refs_0_.1, f32[256]{0:T(256)} %refs_1_.1, f32[256]{0:T(256)} %refs_2_.1, bf16[32,256]{1,0:T(8,128)(2,1)} %bitcast.2, f32[32]{0:T(128)} %refs_4_.1, ...), custom_call_target="tpu_custom_call" | custom-call | tf_op jit(solution)/shard_map/features/pallas_call | solution.py:319
  3.8 4.1 %collective-permute-start = (bf16[384,128]{1,0:T(8,128)(2,1)}, bf16[384,128]{1,0:T(8,128)(2,1)S(1)}, u32[]{:S(2)}, u32[]{:S(2)}) collective-permute-start(bf16[384,128]{1,0:T(8,128)(2,1)} %get-tuple-element.14.refs_0_), channel_id=1, source_target_pairs={{0,8},{4,12},{8,0},{12,4},{1,9},{5,13},{9,1},{13,5},{2,10},{6,14},... | collective-permute-start | bytes 294920 | tf_op jit(solution)/shard_map/ppermute | solution.py:349
  7.9 1.6 %collective-permute-start.7 = (bf16[384,128]{1,0:T(8,128)(2,1)}, bf16[384,128]{1,0:T(8,128)(2,1)S(1)}, u32[]{:S(2)}, u32[]{:S(2)}) collective-permute-start(bf16[384,128]{1,0:T(8,128)(2,1)} %get-tuple-element.14.refs_0_), channel_id=1, source_target_pairs={{0,4},{4,0},{8,12},{12,8},{1,5},{5,1},{9,13},{13,9},{2,6},{6,2},{1... | collective-permute-start | bytes 294920 | tf_op jit(solution)/shard_map/ppermute | solution.py:349
  9.4 1.5 %collective-permute-start.5 = (bf16[576,128]{1,0:T(8,128)(2,1)}, bf16[576,128]{1,0:T(8,128)(2,1)S(1)}, u32[]{:S(2)}, u32[]{:S(2)}) collective-permute-start(bf16[576,128]{1,0:T(8,128)(2,1)} %get-tuple-element.16), channel_id=1, source_target_pairs={{0,2},{1,3},{2,0},{3,1},{4,6},{5,7},{6,4},{7,5},{8,10},{9,11},{10,... | collective-permute-start | bytes 442376 | tf_op jit(solution)/shard_map/ppermute | solution.py:346
  10.9 0.0 collective-permute-start.4
  10.9 1.9 %collective-permute-done.refs_1_ = bf16[384,128]{1,0:T(8,128)(2,1)S(1)} collective-permute-done((bf16[384,128]{1,0:T(8,128)(2,1)}, bf16[384,128]{1,0:T(8,128)(2,1)S(1)}, u32[]{:S(2)}, u32[]{:S(2)}) %collective-permute-start) | collective-permute-done | bytes 98336 | tf_op jit(solution)/shard_map/ppermute | solution.py:349
  12.9 0.9 %collective-permute-start.1 = (bf16[384,128]{1,0:T(8,128)(2,1)S(1)}, bf16[384,128]{1,0:T(8,128)(2,1)S(1)}, u32[]{:S(2)}, u32[]{:S(2)}) collective-permute-start(bf16[384,128]{1,0:T(8,128)(2,1)S(1)} %collective-permute-done.refs_1_), channel_id=1, source_target_pairs={{0,4},{4,0},{8,12},{12,8},{1,5},{5,1},{9,13},{13,9},{2,6},{6,2},{1... | collective-permute-start | bytes 294920 | tf_op jit(solution)/shard_map/ppermute | solution.py:349
  13.8 0.0 collective-permute-done.7.refs_0_
  13.8 0.0 copy-start
  13.8 0.0 copy-start.1
  13.8 0.0 copy-start.2
  13.8 1.6 %collective-permute-start.9 = (bf16[768,128]{1,0:T(8,128)(2,1)S(1)}, bf16[768,128]{1,0:T(8,128)(2,1)S(1)}, u32[]{:S(2)}, u32[]{:S(2)}) collective-permute-start(bf16[768,128]{1,0:T(8,128)(2,1)S(1)} %pack.6.refs_0_.refs_4_), channel_id=1, source_target_pairs={{0,2},{1,3},{2,0},{3,1},{4,6},{5,7},{6,4},{7,5},{8,10},{9,11},{10,... | collective-permute-start | bytes 589832 | tf_op jit(solution)/shard_map/ppermute | solution.py:346
  15.4 0.0 collective-permute-done.4.refs_2_.refs_1_.refs_5_
  15.4 0.0 collective-permute-done.5.refs_0_.refs_2_.refs_6_
  15.4 2.1 %collective-permute-done.1.refs_0_.refs_1_ = bf16[384,128]{1,0:T(8,128)(2,1)S(1)} collective-permute-done((bf16[384,128]{1,0:T(8,128)(2,1)S(1)}, bf16[384,128]{1,0:T(8,128)(2,1)S(1)}, u32[]{:S(2)}, u32[]{:S(2)}) %collective-permute-start.1) | collective-permute-done | bytes 98336 | tf_op jit(solution)/shard_map/ppermute | solution.py:349
  17.5 0.1 collective-permute-start.6
  17.6 1.8 %collective-permute-start.2 = (bf16[384,128]{1,0:T(8,128)(2,1)S(1)}, bf16[384,128]{1,0:T(8,128)(2,1)S(1)}, u32[]{:S(2)}, u32[]{:S(2)}) collective-permute-start(bf16[384,128]{1,0:T(8,128)(2,1)S(1)} %collective-permute-done.1.refs_0_.refs_1_), channel_id=1, source_target_pairs={{0,2},{1,3},{2,0},{3,1},{4,6},{5,7},{6,4},{7,5},{8,10},{9,11},{10,... | collective-permute-start | bytes 294920 | tf_op jit(solution)/shard_map/ppermute | solution.py:346
  19.4 0.2 collective-permute-start.8
  19.6 0.0 collective-permute-done.6.refs_3_.refs_7_
  19.6 0.0 copy-done
  19.6 0.0 copy-done.1
  19.6 0.0 copy-done.2
  19.6 1.5 %pairs_0.1 = (bf16[12,48,128]{2,1,0:T(8,128)(2,1)S(1)}, bf16[4,2,32,768]{3,2,1,0:T(8,128)(2,1)S(1)}, bf16[2048,256]{1,0:T(8,128)(2,1)S(1)}, f32[8,128]{1,0:T(8,128)S(1)}) custom-call(bf16[384,128]{1,0:T(8,128)(2,1)S(1)} %copy-done.1, bf16[480,128]{1,0:T(8,128)(2,1)S(1)} %collective-permute-done.4.refs_2_.refs_1_.refs_5_, ...), custom_call_target="tpu_custom_call" | custom-call | flops 1000 | bytes 1000 | tf_op jit(solution)/shard_map/pairs_0/pallas_call | solution.py:434
  21.1 0.0 collective-permute-done.9.refs_0_.refs_2_.refs_6_
  21.1 0.4 %collective-permute-start.10 = (bf16[768,128]{1,0:T(8,128)(2,1)S(1)}, bf16[768,128]{1,0:T(8,128)(2,1)S(1)}, u32[]{:S(2)}, u32[]{:S(2)}) collective-permute-start(bf16[768,128]{1,0:T(8,128)(2,1)S(1)} %pack.7), channel_id=1, source_target_pairs={{0,1},{1,0},{2,3},{3,2},{4,5},{5,4},{6,7},{7,6},{8,9},{9,8},{10,11... | collective-permute-start | bytes 589832 | tf_op jit(solution)/shard_map/ppermute | solution.py:346
  21.5 1.3 %collective-permute-done.2.refs_1_.refs_2_ = bf16[384,128]{1,0:T(8,128)(2,1)S(1)} collective-permute-done((bf16[384,128]{1,0:T(8,128)(2,1)S(1)}, bf16[384,128]{1,0:T(8,128)(2,1)S(1)}, u32[]{:S(2)}, u32[]{:S(2)}) %collective-permute-start.2) | collective-permute-done | bytes 98336 | tf_op jit(solution)/shard_map/ppermute | solution.py:346
  22.8 0.1 collective-permute-start.3
  22.9 0.0 collective-permute-done.8.refs_1_.refs_5_
  22.9 0.0 collective-permute-done.10.refs_3_.refs_7_
  22.9 1.6 %pairs_1.1.refs_8_ = bf16[12,96,128]{2,1,0:T(8,128)(2,1)S(1)} custom-call(bf16[768,128]{1,0:T(8,128)(2,1)S(1)} %pack.6.refs_0_.refs_4_, bf16[768,128]{1,0:T(8,128)(2,1)S(1)} %collective-permute-done.8.refs_1_.refs_5_, bf16[768,128]{1,0:T(8,128)(2,1)S(1)} %collective-permute-done.9.refs_0_.refs_2_.refs_6_, ...), custom_call_target="tpu_custom_call" | custom-call | flops 1000 | bytes 1000 | tf_op jit(solution)/shard_map/pairs_1/pallas_call | solution.py:434
  24.5 0.0 collective-permute-done.3.refs_1_.refs_3_
  24.5 1.6 %pairs_3.1 = bf16[12,192,128]{2,1,0:T(8,128)(2,1)} custom-call(bf16[384,128]{1,0:T(8,128)(2,1)S(1)} %collective-permute-done.1.refs_0_.refs_1_, bf16[768,128]{1,0:T(8,128)(2,1)S(1)} %collective-permute-done.3.refs_1_.refs_3_, bf16[384,128]{1,0:T(8,128)(2,1)S(1)} %collective-permute-done.2.refs_1_.refs_2_, ...), custom_call_target="tpu_custom_call" | custom-call | flops 1000 | bytes 1000 | tf_op jit(solution)/shard_map/pairs_3/pallas_call | solution.py:434
  (4 shorter events, 0.1 us)
Async XLA Ops:
  3.8 9.1 %collective-permute-start = (bf16[384,128]{1,0:T(8,128)(2,1)}, bf16[384,128]{1,0:T(8,128)(2,1)S(1)}, u32[]{:S(2)}, u32[]{:S(2)}) collective-permute-start(bf16[384,128]{1,0:T(8,128)(2,1)} %get-tuple-element.14.refs_0_), channel_id=1, source_target_pairs={{0,8},{4,12},{8,0},{12,4},{1,9},{5,13},{9,1},{13,5},{2,10},{6,14},... | collective-permute-start | bytes 294920 | tf_op jit(solution)/shard_map/ppermute | solution.py:349
  7.9 5.9 %collective-permute-start.7 = (bf16[384,128]{1,0:T(8,128)(2,1)}, bf16[384,128]{1,0:T(8,128)(2,1)S(1)}, u32[]{:S(2)}, u32[]{:S(2)}) collective-permute-start(bf16[384,128]{1,0:T(8,128)(2,1)} %get-tuple-element.14.refs_0_), channel_id=1, source_target_pairs={{0,4},{4,0},{8,12},{12,8},{1,5},{5,1},{9,13},{13,9},{2,6},{6,2},{1... | collective-permute-start | bytes 294920 | tf_op jit(solution)/shard_map/ppermute | solution.py:349
  9.4 6.0 %collective-permute-start.5 = (bf16[576,128]{1,0:T(8,128)(2,1)}, bf16[576,128]{1,0:T(8,128)(2,1)S(1)}, u32[]{:S(2)}, u32[]{:S(2)}) collective-permute-start(bf16[576,128]{1,0:T(8,128)(2,1)} %get-tuple-element.16), channel_id=1, source_target_pairs={{0,2},{1,3},{2,0},{3,1},{4,6},{5,7},{6,4},{7,5},{8,10},{9,11},{10,... | collective-permute-start | bytes 442376 | tf_op jit(solution)/shard_map/ppermute | solution.py:346
  10.9 4.5 %collective-permute-start.4 = (bf16[480,128]{1,0:T(8,128)(2,1)}, bf16[480,128]{1,0:T(8,128)(2,1)S(1)}, u32[]{:S(2)}, u32[]{:S(2)}) collective-permute-start(bf16[480,128]{1,0:T(8,128)(2,1)} %get-tuple-element.15), channel_id=1, source_target_pairs={{0,1},{1,0},{2,3},{3,2},{4,5},{5,4},{6,7},{7,6},{8,9},{9,8},{10,11... | collective-permute-start | bytes 368648 | tf_op jit(solution)/shard_map/ppermute | solution.py:346
  12.9 4.6 %collective-permute-start.1 = (bf16[384,128]{1,0:T(8,128)(2,1)S(1)}, bf16[384,128]{1,0:T(8,128)(2,1)S(1)}, u32[]{:S(2)}, u32[]{:S(2)}) collective-permute-start(bf16[384,128]{1,0:T(8,128)(2,1)S(1)} %collective-permute-done.refs_1_), channel_id=1, source_target_pairs={{0,4},{4,0},{8,12},{12,8},{1,5},{5,1},{9,13},{13,9},{2,6},{6,2},{1... | collective-permute-start | bytes 294920 | tf_op jit(solution)/shard_map/ppermute | solution.py:349
  13.8 5.8 %copy-start = (f32[1032,128]{1,0:T(8,128)S(1)}, f32[1032,128]{1,0:T(8,128)}, u32[]{:S(2)}) copy-start(f32[1032,128]{1,0:T(8,128)} %get-tuple-element.18.refs_8_) | copy-start | bytes 1585156
  13.8 5.7 %copy-start.1 = (bf16[384,128]{1,0:T(8,128)(2,1)S(1)}, bf16[384,128]{1,0:T(8,128)(2,1)}, u32[]{:S(2)}) copy-start(bf16[384,128]{1,0:T(8,128)(2,1)} %get-tuple-element.14.refs_0_) | copy-start | bytes 294916
  13.8 5.7 %copy-start.2 = (bf16[96,128]{1,0:T(8,128)(2,1)S(1)}, bf16[96,128]{1,0:T(8,128)(2,1)}, u32[]{:S(2)}) copy-start(bf16[96,128]{1,0:T(8,128)(2,1)} %get-tuple-element.17.refs_4_) | copy-start | bytes 73732
  13.8 7.2 %collective-permute-start.9 = (bf16[768,128]{1,0:T(8,128)(2,1)S(1)}, bf16[768,128]{1,0:T(8,128)(2,1)S(1)}, u32[]{:S(2)}, u32[]{:S(2)}) collective-permute-start(bf16[768,128]{1,0:T(8,128)(2,1)S(1)} %pack.6.refs_0_.refs_4_), channel_id=1, source_target_pairs={{0,2},{1,3},{2,0},{3,1},{4,6},{5,7},{6,4},{7,5},{8,10},{9,11},{10,... | collective-permute-start | bytes 589832 | tf_op jit(solution)/shard_map/ppermute | solution.py:346
  17.5 2.1 %collective-permute-start.6 = (bf16[576,128]{1,0:T(8,128)(2,1)S(1)}, bf16[576,128]{1,0:T(8,128)(2,1)S(1)}, u32[]{:S(2)}, u32[]{:S(2)}) collective-permute-start(bf16[576,128]{1,0:T(8,128)(2,1)S(1)} %pack.5), channel_id=1, source_target_pairs={{0,1},{1,0},{2,3},{3,2},{4,5},{5,4},{6,7},{7,6},{8,9},{9,8},{10,11... | collective-permute-start | bytes 442376 | tf_op jit(solution)/shard_map/ppermute | solution.py:346
  17.6 5.2 %collective-permute-start.2 = (bf16[384,128]{1,0:T(8,128)(2,1)S(1)}, bf16[384,128]{1,0:T(8,128)(2,1)S(1)}, u32[]{:S(2)}, u32[]{:S(2)}) collective-permute-start(bf16[384,128]{1,0:T(8,128)(2,1)S(1)} %collective-permute-done.1.refs_0_.refs_1_), channel_id=1, source_target_pairs={{0,2},{1,3},{2,0},{3,1},{4,6},{5,7},{6,4},{7,5},{8,10},{9,11},{10,... | collective-permute-start | bytes 294920 | tf_op jit(solution)/shard_map/ppermute | solution.py:346
  19.4 3.5 %collective-permute-start.8 = (bf16[768,128]{1,0:T(8,128)(2,1)S(1)}, bf16[768,128]{1,0:T(8,128)(2,1)S(1)}, u32[]{:S(2)}, u32[]{:S(2)}) collective-permute-start(bf16[768,128]{1,0:T(8,128)(2,1)S(1)} %pack.6.refs_0_.refs_4_), channel_id=1, source_target_pairs={{0,1},{1,0},{2,3},{3,2},{4,5},{5,4},{6,7},{7,6},{8,9},{9,8},{10,11... | collective-permute-start | bytes 589832 | tf_op jit(solution)/shard_map/ppermute | solution.py:346
  21.1 1.8 %collective-permute-start.10 = (bf16[768,128]{1,0:T(8,128)(2,1)S(1)}, bf16[768,128]{1,0:T(8,128)(2,1)S(1)}, u32[]{:S(2)}, u32[]{:S(2)}) collective-permute-start(bf16[768,128]{1,0:T(8,128)(2,1)S(1)} %pack.7), channel_id=1, source_target_pairs={{0,1},{1,0},{2,3},{3,2},{4,5},{5,4},{6,7},{7,6},{8,9},{9,8},{10,11... | collective-permute-start | bytes 589832 | tf_op jit(solution)/shard_map/ppermute | solution.py:346
  22.8 1.7 %collective-permute-start.3 = (bf16[768,128]{1,0:T(8,128)(2,1)S(1)}, bf16[768,128]{1,0:T(8,128)(2,1)S(1)}, u32[]{:S(2)}, u32[]{:S(2)}) collective-permute-start(bf16[768,128]{1,0:T(8,128)(2,1)S(1)} %pack.4), channel_id=1, source_target_pairs={{0,1},{1,0},{2,3},{3,2},{4,5},{5,4},{6,7},{7,6},{8,9},{9,8},{10,11... | collective-permute-start | bytes 589832 | tf_op jit(solution)/shard_map/ppermute | solution.py:346

commit v16 on v15

--- a/solution.py
+++ b/solution.py
@@ -123,6 +123,27 @@
     total = total + shift
     left_ref[...] = total[:, :LANES].astype(left_ref.dtype)
 
+    mine = left_ref.shape[0] // parts
+
+    def send(is_right):
+        number = free
+        for out, pack in zip(outs, packs):
+            at = 0
+            for item in pack:
+                if item == RIGHT:
+                    rows = right_ref
+                else:
+                    rows = left_ref.at[pl.ds(pl.multiple_of((own ^ item) * mine, 16), mine)]
+                number += 1
+                if (item == RIGHT) == is_right:
+                    sends.append(
+                        pltpu.make_async_copy(rows, out.at[pl.ds(at, rows.shape[0])], sems.at[number])
+                    )
+                    sends[-1].start()
+                at += rows.shape[0]
+
+    send(False)
+
     slot = iota((minor, LANES), 1) // seqs
     for block in range(groups // slots):
         turned_ref[...] = total[block * LANES : (block + 1) * LANES, LANES:].T
@@ -139,20 +160,7 @@
                 rows_ref[pl.ds(j, minor, stride=residues), :] = out
     right_ref[...] = rows_ref[...].astype(right_ref.dtype)
 
-    mine = left_ref.shape[0] // parts
-    for out, pack in zip(outs, packs):
-        at = 0
-        for item in pack:
-            if item == RIGHT:
-                rows = right_ref
-            else:
-                rows = left_ref.at[pl.ds(pl.multiple_of((own ^ item) * mine, 16), mine)]
-            free += 1
-            sends.append(
-                pltpu.make_async_copy(rows, out.at[pl.ds(at, rows.shape[0])], sems.at[free])
-            )
-            sends[-1].start()
-            at += rows.shape[0]
+    send(True)
     for copy in sends:
         copy.wait()
 

time: 26.3 us -> 26.3 us (level)
  no operation moved by 1% of the time
where the time goes in v16:
time: 26.3 us; the launch traced here: 26.1 us
  starting transfers between devices  12.2 us (46%)
  Pallas kernels  8.44 us (32%)
  waiting for transfers between devices  5.29 us (20%)
    ppermute x3, starting transfers between devices, along(): return lax.ppermute(a, 'wide', [(i, i ^ d) for i in range(wide)])  6.62 us
    ppermute x8, starting transfers between devices, across(): return lax.ppermute(a, 'narrow', [(i, i ^ m) for i in range(narrow)])  5.6 us
    pallas_call x3, Pallas kernels, pairs(): pl.pallas_call(functools.partial(pair_kernel, operands=count, rights=righ...  4.63 us
    ppermute x3, waiting for transfers between devices, along(): return lax.ppermute(a, 'wide', [(i, i ^ d) for i in range(wide)])  3.99 us
    pallas_call x1, Pallas kernels, on_device(): pl.pallas_call(functools.partial(features_kernel, packs=packs, parts=narr...  3.76 us
    ppermute x8, waiting for transfers between devices, across(): return lax.ppermute(a, 'narrow', [(i, i ^ m) for i in range(narrow)])  1.3 us
  transfers between devices with their start and end apart: 11, of which 3 were waited for; matrix products, arithmetic and copies ran while one was open for 0% of the time, Pallas kernels for 12%

profile of v16, /device:TPU:0, one launch (start us, length us, event | category | flops | bytes accessed | tf_op | source)
XLA Modules:
  0.0 26.1 jit_solution(8333960880083778891)
XLA Ops:
  0.0 3.8 %features.1 = (bf16[96,128]{1,0:T(8,128)(2,1)}, bf16[384,128]{1,0:T(8,128)(2,1)}, bf16[480,128]{1,0:T(8,128)(2,1)}, bf16[576,128]{1,0:T(8,128)(2,1)}, f32[1032,128]{1,0:T(8,128)}) custom-call(bf16[32,48,256]{2,1,0:T(8,128)(2,1)} %refs_0_.1, f32[256]{0:T(256)} %refs_1_.1, f32[256]{0:T(256)} %refs_2_.1, bf16[32,256]{1,0:T(8,128)(2,1)} %bitcast.2, f32[32]{0:T(128)} %refs_4_.1, ...), custom_call_target="tpu_custom_call" | custom-call | tf_op jit(solution)/shard_map/features/pallas_call | solution.py:327
  3.8 4.1 %collective-permute-start = (bf16[384,128]{1,0:T(8,128)(2,1)}, bf16[384,128]{1,0:T(8,128)(2,1)S(1)}, u32[]{:S(2)}, u32[]{:S(2)}) collective-permute-start(bf16[384,128]{1,0:T(8,128)(2,1)} %get-tuple-element.14.refs_0_), channel_id=1, source_target_pairs={{0,8},{4,12},{8,0},{12,4},{1,9},{5,13},{9,1},{13,5},{2,10},{6,14},... | collective-permute-start | bytes 294920 | tf_op jit(solution)/shard_map/ppermute | solution.py:357
  7.9 1.6 %collective-permute-start.7 = (bf16[384,128]{1,0:T(8,128)(2,1)}, bf16[384,128]{1,0:T(8,128)(2,1)S(1)}, u32[]{:S(2)}, u32[]{:S(2)}) collective-permute-start(bf16[384,128]{1,0:T(8,128)(2,1)} %get-tuple-element.14.refs_0_), channel_id=1, source_target_pairs={{0,4},{4,0},{8,12},{12,8},{1,5},{5,1},{9,13},{13,9},{2,6},{6,2},{1... | collective-permute-start | bytes 294920 | tf_op jit(solution)/shard_map/ppermute | solution.py:357
  9.4 1.5 %collective-permute-start.5 = (bf16[576,128]{1,0:T(8,128)(2,1)}, bf16[576,128]{1,0:T(8,128)(2,1)S(1)}, u32[]{:S(2)}, u32[]{:S(2)}) collective-permute-start(bf16[576,128]{1,0:T(8,128)(2,1)} %get-tuple-element.16), channel_id=1, source_target_pairs={{0,2},{1,3},{2,0},{3,1},{4,6},{5,7},{6,4},{7,5},{8,10},{9,11},{10,... | collective-permute-start | bytes 442376 | tf_op jit(solution)/shard_map/ppermute | solution.py:354
  10.9 0.0 collective-permute-start.4
  10.9 1.9 %collective-permute-done.refs_1_ = bf16[384,128]{1,0:T(8,128)(2,1)S(1)} collective-permute-done((bf16[384,128]{1,0:T(8,128)(2,1)}, bf16[384,128]{1,0:T(8,128)(2,1)S(1)}, u32[]{:S(2)}, u32[]{:S(2)}) %collective-permute-start) | collective-permute-done | bytes 98336 | tf_op jit(solution)/shard_map/ppermute | solution.py:357
  12.9 0.9 %collective-permute-start.1 = (bf16[384,128]{1,0:T(8,128)(2,1)S(1)}, bf16[384,128]{1,0:T(8,128)(2,1)S(1)}, u32[]{:S(2)}, u32[]{:S(2)}) collective-permute-start(bf16[384,128]{1,0:T(8,128)(2,1)S(1)} %collective-permute-done.refs_1_), channel_id=1, source_target_pairs={{0,4},{4,0},{8,12},{12,8},{1,5},{5,1},{9,13},{13,9},{2,6},{6,2},{1... | collective-permute-start | bytes 294920 | tf_op jit(solution)/shard_map/ppermute | solution.py:357
  13.8 0.0 collective-permute-done.7.refs_0_
  13.8 0.0 copy-start
  13.8 0.0 copy-start.1
  13.8 0.0 copy-start.2
  13.8 1.6 %collective-permute-start.9 = (bf16[768,128]{1,0:T(8,128)(2,1)S(1)}, bf16[768,128]{1,0:T(8,128)(2,1)S(1)}, u32[]{:S(2)}, u32[]{:S(2)}) collective-permute-start(bf16[768,128]{1,0:T(8,128)(2,1)S(1)} %pack.6.refs_0_.refs_4_), channel_id=1, source_target_pairs={{0,2},{1,3},{2,0},{3,1},{4,6},{5,7},{6,4},{7,5},{8,10},{9,11},{10,... | collective-permute-start | bytes 589832 | tf_op jit(solution)/shard_map/ppermute | solution.py:354
  15.4 0.0 collective-permute-done.4.refs_2_.refs_1_.refs_5_
  15.4 0.0 collective-permute-done.5.refs_0_.refs_2_.refs_6_
  15.4 2.1 %collective-permute-done.1.refs_0_.refs_1_ = bf16[384,128]{1,0:T(8,128)(2,1)S(1)} collective-permute-done((bf16[384,128]{1,0:T(8,128)(2,1)S(1)}, bf16[384,128]{1,0:T(8,128)(2,1)S(1)}, u32[]{:S(2)}, u32[]{:S(2)}) %collective-permute-start.1) | collective-permute-done | bytes 98336 | tf_op jit(solution)/shard_map/ppermute | solution.py:357
  17.5 0.1 collective-permute-start.6
  17.6 1.8 %collective-permute-start.2 = (bf16[384,128]{1,0:T(8,128)(2,1)S(1)}, bf16[384,128]{1,0:T(8,128)(2,1)S(1)}, u32[]{:S(2)}, u32[]{:S(2)}) collective-permute-start(bf16[384,128]{1,0:T(8,128)(2,1)S(1)} %collective-permute-done.1.refs_0_.refs_1_), channel_id=1, source_target_pairs={{0,2},{1,3},{2,0},{3,1},{4,6},{5,7},{6,4},{7,5},{8,10},{9,11},{10,... | collective-permute-start | bytes 294920 | tf_op jit(solution)/shard_map/ppermute | solution.py:354
  19.4 0.2 collective-permute-start.8
  19.6 0.0 collective-permute-done.6.refs_3_.refs_7_
  19.6 0.0 copy-done
  19.6 0.0 copy-done.1
  19.6 0.0 copy-done.2
  19.6 1.5 %pairs_0.1 = (bf16[12,48,128]{2,1,0:T(8,128)(2,1)S(1)}, bf16[4,2,32,768]{3,2,1,0:T(8,128)(2,1)S(1)}, bf16[2048,256]{1,0:T(8,128)(2,1)S(1)}, f32[8,128]{1,0:T(8,128)S(1)}) custom-call(bf16[384,128]{1,0:T(8,128)(2,1)S(1)} %copy-done.1, bf16[480,128]{1,0:T(8,128)(2,1)S(1)} %collective-permute-done.4.refs_2_.refs_1_.refs_5_, ...), custom_call_target="tpu_custom_call" | custom-call | flops 1000 | bytes 1000 | tf_op jit(solution)/shard_map/pairs_0/pallas_call | solution.py:442
  21.1 0.0 collective-permute-done.9.refs_0_.refs_2_.refs_6_
  21.1 0.4 %collective-permute-start.10 = (bf16[768,128]{1,0:T(8,128)(2,1)S(1)}, bf16[768,128]{1,0:T(8,128)(2,1)S(1)}, u32[]{:S(2)}, u32[]{:S(2)}) collective-permute-start(bf16[768,128]{1,0:T(8,128)(2,1)S(1)} %pack.7), channel_id=1, source_target_pairs={{0,1},{1,0},{2,3},{3,2},{4,5},{5,4},{6,7},{7,6},{8,9},{9,8},{10,11... | collective-permute-start | bytes 589832 | tf_op jit(solution)/shard_map/ppermute | solution.py:354
  21.5 1.3 %collective-permute-done.2.refs_1_.refs_2_ = bf16[384,128]{1,0:T(8,128)(2,1)S(1)} collective-permute-done((bf16[384,128]{1,0:T(8,128)(2,1)S(1)}, bf16[384,128]{1,0:T(8,128)(2,1)S(1)}, u32[]{:S(2)}, u32[]{:S(2)}) %collective-permute-start.2) | collective-permute-done | bytes 98336 | tf_op jit(solution)/shard_map/ppermute | solution.py:354
  22.8 0.1 collective-permute-start.3
  22.9 0.0 collective-permute-done.8.refs_1_.refs_5_
  22.9 0.0 collective-permute-done.10.refs_3_.refs_7_
  22.9 1.6 %pairs_1.1.refs_8_ = bf16[12,96,128]{2,1,0:T(8,128)(2,1)S(1)} custom-call(bf16[768,128]{1,0:T(8,128)(2,1)S(1)} %pack.6.refs_0_.refs_4_, bf16[768,128]{1,0:T(8,128)(2,1)S(1)} %collective-permute-done.8.refs_1_.refs_5_, bf16[768,128]{1,0:T(8,128)(2,1)S(1)} %collective-permute-done.9.refs_0_.refs_2_.refs_6_, ...), custom_call_target="tpu_custom_call" | custom-call | flops 1000 | bytes 1000 | tf_op jit(solution)/shard_map/pairs_1/pallas_call | solution.py:442
  24.5 0.0 collective-permute-done.3.refs_1_.refs_3_
  24.5 1.6 %pairs_3.1 = bf16[12,192,128]{2,1,0:T(8,128)(2,1)} custom-call(bf16[384,128]{1,0:T(8,128)(2,1)S(1)} %collective-permute-done.1.refs_0_.refs_1_, bf16[768,128]{1,0:T(8,128)(2,1)S(1)} %collective-permute-done.3.refs_1_.refs_3_, bf16[384,128]{1,0:T(8,128)(2,1)S(1)} %collective-permute-done.2.refs_1_.refs_2_, ...), custom_call_target="tpu_custom_call" | custom-call | flops 1000 | bytes 1000 | tf_op jit(solution)/shard_map/pairs_3/pallas_call | solution.py:442
  (4 shorter events, 0.1 us)
Async XLA Ops:
  3.8 9.1 %collective-permute-start = (bf16[384,128]{1,0:T(8,128)(2,1)}, bf16[384,128]{1,0:T(8,128)(2,1)S(1)}, u32[]{:S(2)}, u32[]{:S(2)}) collective-permute-start(bf16[384,128]{1,0:T(8,128)(2,1)} %get-tuple-element.14.refs_0_), channel_id=1, source_target_pairs={{0,8},{4,12},{8,0},{12,4},{1,9},{5,13},{9,1},{13,5},{2,10},{6,14},... | collective-permute-start | bytes 294920 | tf_op jit(solution)/shard_map/ppermute | solution.py:357
  7.9 5.9 %collective-permute-start.7 = (bf16[384,128]{1,0:T(8,128)(2,1)}, bf16[384,128]{1,0:T(8,128)(2,1)S(1)}, u32[]{:S(2)}, u32[]{:S(2)}) collective-permute-start(bf16[384,128]{1,0:T(8,128)(2,1)} %get-tuple-element.14.refs_0_), channel_id=1, source_target_pairs={{0,4},{4,0},{8,12},{12,8},{1,5},{5,1},{9,13},{13,9},{2,6},{6,2},{1... | collective-permute-start | bytes 294920 | tf_op jit(solution)/shard_map/ppermute | solution.py:357
  9.4 6.0 %collective-permute-start.5 = (bf16[576,128]{1,0:T(8,128)(2,1)}, bf16[576,128]{1,0:T(8,128)(2,1)S(1)}, u32[]{:S(2)}, u32[]{:S(2)}) collective-permute-start(bf16[576,128]{1,0:T(8,128)(2,1)} %get-tuple-element.16), channel_id=1, source_target_pairs={{0,2},{1,3},{2,0},{3,1},{4,6},{5,7},{6,4},{7,5},{8,10},{9,11},{10,... | collective-permute-start | bytes 442376 | tf_op jit(solution)/shard_map/ppermute | solution.py:354
  10.9 4.5 %collective-permute-start.4 = (bf16[480,128]{1,0:T(8,128)(2,1)}, bf16[480,128]{1,0:T(8,128)(2,1)S(1)}, u32[]{:S(2)}, u32[]{:S(2)}) collective-permute-start(bf16[480,128]{1,0:T(8,128)(2,1)} %get-tuple-element.15), channel_id=1, source_target_pairs={{0,1},{1,0},{2,3},{3,2},{4,5},{5,4},{6,7},{7,6},{8,9},{9,8},{10,11... | collective-permute-start | bytes 368648 | tf_op jit(solution)/shard_map/ppermute | solution.py:354
  12.9 4.6 %collective-permute-start.1 = (bf16[384,128]{1,0:T(8,128)(2,1)S(1)}, bf16[384,128]{1,0:T(8,128)(2,1)S(1)}, u32[]{:S(2)}, u32[]{:S(2)}) collective-permute-start(bf16[384,128]{1,0:T(8,128)(2,1)S(1)} %collective-permute-done.refs_1_), channel_id=1, source_target_pairs={{0,4},{4,0},{8,12},{12,8},{1,5},{5,1},{9,13},{13,9},{2,6},{6,2},{1... | collective-permute-start | bytes 294920 | tf_op jit(solution)/shard_map/ppermute | solution.py:357
  13.8 5.8 %copy-start = (f32[1032,128]{1,0:T(8,128)S(1)}, f32[1032,128]{1,0:T(8,128)}, u32[]{:S(2)}) copy-start(f32[1032,128]{1,0:T(8,128)} %get-tuple-element.18.refs_8_) | copy-start | bytes 1585156
  13.8 5.7 %copy-start.1 = (bf16[384,128]{1,0:T(8,128)(2,1)S(1)}, bf16[384,128]{1,0:T(8,128)(2,1)}, u32[]{:S(2)}) copy-start(bf16[384,128]{1,0:T(8,128)(2,1)} %get-tuple-element.14.refs_0_) | copy-start | bytes 294916
  13.8 5.7 %copy-start.2 = (bf16[96,128]{1,0:T(8,128)(2,1)S(1)}, bf16[96,128]{1,0:T(8,128)(2,1)}, u32[]{:S(2)}) copy-start(bf16[96,128]{1,0:T(8,128)(2,1)} %get-tuple-element.17.refs_4_) | copy-start | bytes 73732
  13.8 7.2 %collective-permute-start.9 = (bf16[768,128]{1,0:T(8,128)(2,1)S(1)}, bf16[768,128]{1,0:T(8,128)(2,1)S(1)}, u32[]{:S(2)}, u32[]{:S(2)}) collective-permute-start(bf16[768,128]{1,0:T(8,128)(2,1)S(1)} %pack.6.refs_0_.refs_4_), channel_id=1, source_target_pairs={{0,2},{1,3},{2,0},{3,1},{4,6},{5,7},{6,4},{7,5},{8,10},{9,11},{10,... | collective-permute-start | bytes 589832 | tf_op jit(solution)/shard_map/ppermute | solution.py:354
  17.5 2.1 %collective-permute-start.6 = (bf16[576,128]{1,0:T(8,128)(2,1)S(1)}, bf16[576,128]{1,0:T(8,128)(2,1)S(1)}, u32[]{:S(2)}, u32[]{:S(2)}) collective-permute-start(bf16[576,128]{1,0:T(8,128)(2,1)S(1)} %pack.5), channel_id=1, source_target_pairs={{0,1},{1,0},{2,3},{3,2},{4,5},{5,4},{6,7},{7,6},{8,9},{9,8},{10,11... | collective-permute-start | bytes 442376 | tf_op jit(solution)/shard_map/ppermute | solution.py:354
  17.6 5.2 %collective-permute-start.2 = (bf16[384,128]{1,0:T(8,128)(2,1)S(1)}, bf16[384,128]{1,0:T(8,128)(2,1)S(1)}, u32[]{:S(2)}, u32[]{:S(2)}) collective-permute-start(bf16[384,128]{1,0:T(8,128)(2,1)S(1)} %collective-permute-done.1.refs_0_.refs_1_), channel_id=1, source_target_pairs={{0,2},{1,3},{2,0},{3,1},{4,6},{5,7},{6,4},{7,5},{8,10},{9,11},{10,... | collective-permute-start | bytes 294920 | tf_op jit(solution)/shard_map/ppermute | solution.py:354
  19.4 3.5 %collective-permute-start.8 = (bf16[768,128]{1,0:T(8,128)(2,1)S(1)}, bf16[768,128]{1,0:T(8,128)(2,1)S(1)}, u32[]{:S(2)}, u32[]{:S(2)}) collective-permute-start(bf16[768,128]{1,0:T(8,128)(2,1)S(1)} %pack.6.refs_0_.refs_4_), channel_id=1, source_target_pairs={{0,1},{1,0},{2,3},{3,2},{4,5},{5,4},{6,7},{7,6},{8,9},{9,8},{10,11... | collective-permute-start | bytes 589832 | tf_op jit(solution)/shard_map/ppermute | solution.py:354
  21.1 1.8 %collective-permute-start.10 = (bf16[768,128]{1,0:T(8,128)(2,1)S(1)}, bf16[768,128]{1,0:T(8,128)(2,1)S(1)}, u32[]{:S(2)}, u32[]{:S(2)}) collective-permute-start(bf16[768,128]{1,0:T(8,128)(2,1)S(1)} %pack.7), channel_id=1, source_target_pairs={{0,1},{1,0},{2,3},{3,2},{4,5},{5,4},{6,7},{7,6},{8,9},{9,8},{10,11... | collective-permute-start | bytes 589832 | tf_op jit(solution)/shard_map/ppermute | solution.py:354
  22.8 1.7 %collective-permute-start.3 = (bf16[768,128]{1,0:T(8,128)(2,1)S(1)}, bf16[768,128]{1,0:T(8,128)(2,1)S(1)}, u32[]{:S(2)}, u32[]{:S(2)}) collective-permute-start(bf16[768,128]{1,0:T(8,128)(2,1)S(1)} %pack.4), channel_id=1, source_target_pairs={{0,1},{1,0},{2,3},{3,2},{4,5},{5,4},{6,7},{7,6},{8,9},{9,8},{10,11... | collective-permute-start | bytes 589832 | tf_op jit(solution)/shard_map/ppermute | solution.py:354

commit v17 on v15

--- a/solution.py
+++ b/solution.py
@@ -66,7 +66,9 @@
         copy.wait()
     count = w_ref.shape[0]
     wf_ref[:count] = w_ref[...].astype(jnp.float32)
-    wf_ref[count:] = jnp.broadcast_to(shift_ref[...].reshape(1, -1), (8, shift_ref.shape[0]))
+    wf_ref[count:] = jnp.broadcast_to(
+        shift_ref[...].reshape(1, -1), (wf_ref.shape[0] - count, shift_ref.shape[0])
+    )
     norm(pieces - 1)
 
     column, row = iota((hidden, LANES), 1) % hidden, iota((hidden, LANES), 0)
@@ -137,7 +139,7 @@
                     out = moved if out is None else jnp.where(slot == q, moved, out)
                 j = (block * slots + g) * per + k
                 rows_ref[pl.ds(j, minor, stride=residues), :] = out
-    right_ref[...] = rows_ref[...].astype(right_ref.dtype)
+    right_ref[...] = rows_ref[: minor * residues].astype(right_ref.dtype)
 
     mine = left_ref.shape[0] // parts
     for out, pack in zip(outs, packs):
@@ -324,18 +326,18 @@
             )
             for pack in packs
         )
-        + (jax.ShapeDtypeStruct((w.shape[0] + 8, cz), jnp.float32),),
+        + (jax.ShapeDtypeStruct((w.shape[0] + hidden + 8, cz), jnp.float32),),
         in_specs=[hbm] * len(args),
         out_specs=(hbm,) * (len(packs) + 1),
         scratch_shapes=[pltpu.VMEM(a.shape, a.dtype) for a in args]
         + [
-            pltpu.VMEM((seqs * residues, LANES), jnp.float32),
-            pltpu.VMEM((seqs * residues, LANES), jnp.float32),
+            pltpu.VMEM(((seqs + 1) * residues, LANES), jnp.float32),
+            pltpu.VMEM(((seqs + 1) * residues, LANES), jnp.float32),
             pltpu.VMEM((residues // per * seqs, LANES), jnp.bfloat16),
             pltpu.VMEM((LANES, LANES), jnp.float32),
-            pltpu.VMEM((minor * residues, LANES), jnp.float32),
+            pltpu.VMEM(((minor + 1) * residues, LANES), jnp.float32),
             pltpu.VMEM((minor * residues, LANES), jnp.bfloat16),
-            pltpu.VMEM((w.shape[0] + 8, cz), jnp.float32),
+            pltpu.VMEM((w.shape[0] + hidden + 8, cz), jnp.float32),
             pltpu.SemaphoreType.DMA((pieces + len(args) + sum(len(pack) for pack in packs),)),
         ],
         compiler_params=pltpu.CompilerParams(vmem_limit_bytes=VMEM_ALL),

time: 26.3 us -> 26.3 us (level)
  no operation moved by 1% of the time
where the time goes in v17:
time: 26.3 us; the launch traced here: 26.1 us
  starting transfers between devices  12.2 us (46%)
  Pallas kernels  8.44 us (32%)
  waiting for transfers between devices  5.3 us (20%)
    ppermute x3, starting transfers between devices, along(): return lax.ppermute(a, 'wide', [(i, i ^ d) for i in range(wide)])  6.62 us
    ppermute x8, starting transfers between devices, across(): return lax.ppermute(a, 'narrow', [(i, i ^ m) for i in range(narrow)])  5.59 us
    pallas_call x3, Pallas kernels, pairs(): pl.pallas_call(functools.partial(pair_kernel, operands=count, rights=righ...  4.63 us
    ppermute x3, waiting for transfers between devices, along(): return lax.ppermute(a, 'wide', [(i, i ^ d) for i in range(wide)])  3.99 us
    pallas_call x1, Pallas kernels, on_device(): pl.pallas_call(functools.partial(features_kernel, packs=packs, parts=narr...  3.76 us
    ppermute x8, waiting for transfers between devices, across(): return lax.ppermute(a, 'narrow', [(i, i ^ m) for i in range(narrow)])  1.3 us
  transfers between devices with their start and end apart: 11, of which 3 were waited for; matrix products, arithmetic and copies ran while one was open for 0% of the time, Pallas kernels for 12%

profile of v17, /device:TPU:0, one launch (start us, length us, event | category | flops | bytes accessed | tf_op | source)
XLA Modules:
  0.0 26.1 jit_solution(9109214750337003749)
XLA Ops:
  0.0 3.8 %features.1 = (bf16[96,128]{1,0:T(8,128)(2,1)}, bf16[384,128]{1,0:T(8,128)(2,1)}, bf16[480,128]{1,0:T(8,128)(2,1)}, bf16[576,128]{1,0:T(8,128)(2,1)}, f32[1064,128]{1,0:T(8,128)}) custom-call(bf16[32,48,256]{2,1,0:T(8,128)(2,1)} %refs_0_.1, f32[256]{0:T(256)} %refs_1_.1, f32[256]{0:T(256)} %refs_2_.1, bf16[32,256]{1,0:T(8,128)(2,1)} %bitcast.2, f32[32]{0:T(128)} %refs_4_.1, ...), custom_call_target="tpu_custom_call" | custom-call | tf_op jit(solution)/shard_map/features/pallas_call | solution.py:321
  3.8 4.1 %collective-permute-start = (bf16[384,128]{1,0:T(8,128)(2,1)}, bf16[384,128]{1,0:T(8,128)(2,1)S(1)}, u32[]{:S(2)}, u32[]{:S(2)}) collective-permute-start(bf16[384,128]{1,0:T(8,128)(2,1)} %get-tuple-element.14.refs_0_), channel_id=1, source_target_pairs={{0,8},{4,12},{8,0},{12,4},{1,9},{5,13},{9,1},{13,5},{2,10},{6,14},... | collective-permute-start | bytes 294920 | tf_op jit(solution)/shard_map/ppermute | solution.py:351
  7.9 1.6 %collective-permute-start.7 = (bf16[384,128]{1,0:T(8,128)(2,1)}, bf16[384,128]{1,0:T(8,128)(2,1)S(1)}, u32[]{:S(2)}, u32[]{:S(2)}) collective-permute-start(bf16[384,128]{1,0:T(8,128)(2,1)} %get-tuple-element.14.refs_0_), channel_id=1, source_target_pairs={{0,4},{4,0},{8,12},{12,8},{1,5},{5,1},{9,13},{13,9},{2,6},{6,2},{1... | collective-permute-start | bytes 294920 | tf_op jit(solution)/shard_map/ppermute | solution.py:351
  9.4 1.5 %collective-permute-start.5 = (bf16[576,128]{1,0:T(8,128)(2,1)}, bf16[576,128]{1,0:T(8,128)(2,1)S(1)}, u32[]{:S(2)}, u32[]{:S(2)}) collective-permute-start(bf16[576,128]{1,0:T(8,128)(2,1)} %get-tuple-element.16), channel_id=1, source_target_pairs={{0,2},{1,3},{2,0},{3,1},{4,6},{5,7},{6,4},{7,5},{8,10},{9,11},{10,... | collective-permute-start | bytes 442376 | tf_op jit(solution)/shard_map/ppermute | solution.py:348
  10.9 0.0 collective-permute-start.4
  10.9 1.9 %collective-permute-done.refs_1_ = bf16[384,128]{1,0:T(8,128)(2,1)S(1)} collective-permute-done((bf16[384,128]{1,0:T(8,128)(2,1)}, bf16[384,128]{1,0:T(8,128)(2,1)S(1)}, u32[]{:S(2)}, u32[]{:S(2)}) %collective-permute-start) | collective-permute-done | bytes 98336 | tf_op jit(solution)/shard_map/ppermute | solution.py:351
  12.9 0.9 %collective-permute-start.1 = (bf16[384,128]{1,0:T(8,128)(2,1)S(1)}, bf16[384,128]{1,0:T(8,128)(2,1)S(1)}, u32[]{:S(2)}, u32[]{:S(2)}) collective-permute-start(bf16[384,128]{1,0:T(8,128)(2,1)S(1)} %collective-permute-done.refs_1_), channel_id=1, source_target_pairs={{0,4},{4,0},{8,12},{12,8},{1,5},{5,1},{9,13},{13,9},{2,6},{6,2},{1... | collective-permute-start | bytes 294920 | tf_op jit(solution)/shard_map/ppermute | solution.py:351
  13.8 0.0 collective-permute-done.7.refs_0_
  13.8 0.0 copy-start
  13.8 0.0 copy-start.1
  13.8 0.0 copy-start.2
  13.9 1.6 %collective-permute-start.9 = (bf16[768,128]{1,0:T(8,128)(2,1)S(1)}, bf16[768,128]{1,0:T(8,128)(2,1)S(1)}, u32[]{:S(2)}, u32[]{:S(2)}) collective-permute-start(bf16[768,128]{1,0:T(8,128)(2,1)S(1)} %pack.6.refs_0_.refs_4_), channel_id=1, source_target_pairs={{0,2},{1,3},{2,0},{3,1},{4,6},{5,7},{6,4},{7,5},{8,10},{9,11},{10,... | collective-permute-start | bytes 589832 | tf_op jit(solution)/shard_map/ppermute | solution.py:348
  15.4 0.0 collective-permute-done.4.refs_2_.refs_1_.refs_5_
  15.4 0.0 collective-permute-done.5.refs_0_.refs_2_.refs_6_
  15.4 2.1 %collective-permute-done.1.refs_0_.refs_1_ = bf16[384,128]{1,0:T(8,128)(2,1)S(1)} collective-permute-done((bf16[384,128]{1,0:T(8,128)(2,1)S(1)}, bf16[384,128]{1,0:T(8,128)(2,1)S(1)}, u32[]{:S(2)}, u32[]{:S(2)}) %collective-permute-start.1) | collective-permute-done | bytes 98336 | tf_op jit(solution)/shard_map/ppermute | solution.py:351
  17.5 0.1 collective-permute-start.6
  17.6 1.8 %collective-permute-start.2 = (bf16[384,128]{1,0:T(8,128)(2,1)S(1)}, bf16[384,128]{1,0:T(8,128)(2,1)S(1)}, u32[]{:S(2)}, u32[]{:S(2)}) collective-permute-start(bf16[384,128]{1,0:T(8,128)(2,1)S(1)} %collective-permute-done.1.refs_0_.refs_1_), channel_id=1, source_target_pairs={{0,2},{1,3},{2,0},{3,1},{4,6},{5,7},{6,4},{7,5},{8,10},{9,11},{10,... | collective-permute-start | bytes 294920 | tf_op jit(solution)/shard_map/ppermute | solution.py:348
  19.4 0.2 collective-permute-start.8
  19.6 0.0 collective-permute-done.6.refs_3_.refs_7_
  19.6 0.0 copy-done
  19.6 0.0 copy-done.1
  19.6 0.0 copy-done.2
  19.6 1.5 %pairs_0.1 = (bf16[12,48,128]{2,1,0:T(8,128)(2,1)S(1)}, bf16[4,2,32,768]{3,2,1,0:T(8,128)(2,1)S(1)}, bf16[2048,256]{1,0:T(8,128)(2,1)S(1)}, f32[8,128]{1,0:T(8,128)S(1)}) custom-call(bf16[384,128]{1,0:T(8,128)(2,1)S(1)} %copy-done.1, bf16[480,128]{1,0:T(8,128)(2,1)S(1)} %collective-permute-done.4.refs_2_.refs_1_.refs_5_, ...), custom_call_target="tpu_custom_call" | custom-call | flops 1000 | bytes 1000 | tf_op jit(solution)/shard_map/pairs_0/pallas_call | solution.py:436
  21.1 0.0 collective-permute-done.9.refs_0_.refs_2_.refs_6_
  21.1 0.4 %collective-permute-start.10 = (bf16[768,128]{1,0:T(8,128)(2,1)S(1)}, bf16[768,128]{1,0:T(8,128)(2,1)S(1)}, u32[]{:S(2)}, u32[]{:S(2)}) collective-permute-start(bf16[768,128]{1,0:T(8,128)(2,1)S(1)} %pack.7), channel_id=1, source_target_pairs={{0,1},{1,0},{2,3},{3,2},{4,5},{5,4},{6,7},{7,6},{8,9},{9,8},{10,11... | collective-permute-start | bytes 589832 | tf_op jit(solution)/shard_map/ppermute | solution.py:348
  21.5 1.3 %collective-permute-done.2.refs_1_.refs_2_ = bf16[384,128]{1,0:T(8,128)(2,1)S(1)} collective-permute-done((bf16[384,128]{1,0:T(8,128)(2,1)S(1)}, bf16[384,128]{1,0:T(8,128)(2,1)S(1)}, u32[]{:S(2)}, u32[]{:S(2)}) %collective-permute-start.2) | collective-permute-done | bytes 98336 | tf_op jit(solution)/shard_map/ppermute | solution.py:348
  22.8 0.1 collective-permute-start.3
  22.9 0.0 collective-permute-done.8.refs_1_.refs_5_
  22.9 0.0 collective-permute-done.10.refs_3_.refs_7_
  22.9 1.6 %pairs_1.1.refs_8_ = bf16[12,96,128]{2,1,0:T(8,128)(2,1)S(1)} custom-call(bf16[768,128]{1,0:T(8,128)(2,1)S(1)} %pack.6.refs_0_.refs_4_, bf16[768,128]{1,0:T(8,128)(2,1)S(1)} %collective-permute-done.8.refs_1_.refs_5_, bf16[768,128]{1,0:T(8,128)(2,1)S(1)} %collective-permute-done.9.refs_0_.refs_2_.refs_6_, ...), custom_call_target="tpu_custom_call" | custom-call | flops 1000 | bytes 1000 | tf_op jit(solution)/shard_map/pairs_1/pallas_call | solution.py:436
  24.5 0.0 collective-permute-done.3.refs_1_.refs_3_
  24.5 1.6 %pairs_3.1 = bf16[12,192,128]{2,1,0:T(8,128)(2,1)} custom-call(bf16[384,128]{1,0:T(8,128)(2,1)S(1)} %collective-permute-done.1.refs_0_.refs_1_, bf16[768,128]{1,0:T(8,128)(2,1)S(1)} %collective-permute-done.3.refs_1_.refs_3_, bf16[384,128]{1,0:T(8,128)(2,1)S(1)} %collective-permute-done.2.refs_1_.refs_2_, ...), custom_call_target="tpu_custom_call" | custom-call | flops 1000 | bytes 1000 | tf_op jit(solution)/shard_map/pairs_3/pallas_call | solution.py:436
  (4 shorter events, 0.1 us)
Async XLA Ops:
  3.8 9.1 %collective-permute-start = (bf16[384,128]{1,0:T(8,128)(2,1)}, bf16[384,128]{1,0:T(8,128)(2,1)S(1)}, u32[]{:S(2)}, u32[]{:S(2)}) collective-permute-start(bf16[384,128]{1,0:T(8,128)(2,1)} %get-tuple-element.14.refs_0_), channel_id=1, source_target_pairs={{0,8},{4,12},{8,0},{12,4},{1,9},{5,13},{9,1},{13,5},{2,10},{6,14},... | collective-permute-start | bytes 294920 | tf_op jit(solution)/shard_map/ppermute | solution.py:351
  7.9 5.9 %collective-permute-start.7 = (bf16[384,128]{1,0:T(8,128)(2,1)}, bf16[384,128]{1,0:T(8,128)(2,1)S(1)}, u32[]{:S(2)}, u32[]{:S(2)}) collective-permute-start(bf16[384,128]{1,0:T(8,128)(2,1)} %get-tuple-element.14.refs_0_), channel_id=1, source_target_pairs={{0,4},{4,0},{8,12},{12,8},{1,5},{5,1},{9,13},{13,9},{2,6},{6,2},{1... | collective-permute-start | bytes 294920 | tf_op jit(solution)/shard_map/ppermute | solution.py:351
  9.4 6.0 %collective-permute-start.5 = (bf16[576,128]{1,0:T(8,128)(2,1)}, bf16[576,128]{1,0:T(8,128)(2,1)S(1)}, u32[]{:S(2)}, u32[]{:S(2)}) collective-permute-start(bf16[576,128]{1,0:T(8,128)(2,1)} %get-tuple-element.16), channel_id=1, source_target_pairs={{0,2},{1,3},{2,0},{3,1},{4,6},{5,7},{6,4},{7,5},{8,10},{9,11},{10,... | collective-permute-start | bytes 442376 | tf_op jit(solution)/shard_map/ppermute | solution.py:348
  10.9 4.5 %collective-permute-start.4 = (bf16[480,128]{1,0:T(8,128)(2,1)}, bf16[480,128]{1,0:T(8,128)(2,1)S(1)}, u32[]{:S(2)}, u32[]{:S(2)}) collective-permute-start(bf16[480,128]{1,0:T(8,128)(2,1)} %get-tuple-element.15), channel_id=1, source_target_pairs={{0,1},{1,0},{2,3},{3,2},{4,5},{5,4},{6,7},{7,6},{8,9},{9,8},{10,11... | collective-permute-start | bytes 368648 | tf_op jit(solution)/shard_map/ppermute | solution.py:348
  12.9 4.6 %collective-permute-start.1 = (bf16[384,128]{1,0:T(8,128)(2,1)S(1)}, bf16[384,128]{1,0:T(8,128)(2,1)S(1)}, u32[]{:S(2)}, u32[]{:S(2)}) collective-permute-start(bf16[384,128]{1,0:T(8,128)(2,1)S(1)} %collective-permute-done.refs_1_), channel_id=1, source_target_pairs={{0,4},{4,0},{8,12},{12,8},{1,5},{5,1},{9,13},{13,9},{2,6},{6,2},{1... | collective-permute-start | bytes 294920 | tf_op jit(solution)/shard_map/ppermute | solution.py:351
  13.8 5.8 %copy-start = (f32[1064,128]{1,0:T(8,128)S(1)}, f32[1064,128]{1,0:T(8,128)}, u32[]{:S(2)}) copy-start(f32[1064,128]{1,0:T(8,128)} %get-tuple-element.18.refs_8_) | copy-start | bytes 1634308
  13.8 5.7 %copy-start.1 = (bf16[384,128]{1,0:T(8,128)(2,1)S(1)}, bf16[384,128]{1,0:T(8,128)(2,1)}, u32[]{:S(2)}) copy-start(bf16[384,128]{1,0:T(8,128)(2,1)} %get-tuple-element.14.refs_0_) | copy-start | bytes 294916
  13.8 5.7 %copy-start.2 = (bf16[96,128]{1,0:T(8,128)(2,1)S(1)}, bf16[96,128]{1,0:T(8,128)(2,1)}, u32[]{:S(2)}) copy-start(bf16[96,128]{1,0:T(8,128)(2,1)} %get-tuple-element.17.refs_4_) | copy-start | bytes 73732
  13.9 7.2 %collective-permute-start.9 = (bf16[768,128]{1,0:T(8,128)(2,1)S(1)}, bf16[768,128]{1,0:T(8,128)(2,1)S(1)}, u32[]{:S(2)}, u32[]{:S(2)}) collective-permute-start(bf16[768,128]{1,0:T(8,128)(2,1)S(1)} %pack.6.refs_0_.refs_4_), channel_id=1, source_target_pairs={{0,2},{1,3},{2,0},{3,1},{4,6},{5,7},{6,4},{7,5},{8,10},{9,11},{10,... | collective-permute-start | bytes 589832 | tf_op jit(solution)/shard_map/ppermute | solution.py:348
  17.5 2.1 %collective-permute-start.6 = (bf16[576,128]{1,0:T(8,128)(2,1)S(1)}, bf16[576,128]{1,0:T(8,128)(2,1)S(1)}, u32[]{:S(2)}, u32[]{:S(2)}) collective-permute-start(bf16[576,128]{1,0:T(8,128)(2,1)S(1)} %pack.5), channel_id=1, source_target_pairs={{0,1},{1,0},{2,3},{3,2},{4,5},{5,4},{6,7},{7,6},{8,9},{9,8},{10,11... | collective-permute-start | bytes 442376 | tf_op jit(solution)/shard_map/ppermute | solution.py:348
  17.6 5.2 %collective-permute-start.2 = (bf16[384,128]{1,0:T(8,128)(2,1)S(1)}, bf16[384,128]{1,0:T(8,128)(2,1)S(1)}, u32[]{:S(2)}, u32[]{:S(2)}) collective-permute-start(bf16[384,128]{1,0:T(8,128)(2,1)S(1)} %collective-permute-done.1.refs_0_.refs_1_), channel_id=1, source_target_pairs={{0,2},{1,3},{2,0},{3,1},{4,6},{5,7},{6,4},{7,5},{8,10},{9,11},{10,... | collective-permute-start | bytes 294920 | tf_op jit(solution)/shard_map/ppermute | solution.py:348
  19.4 3.5 %collective-permute-start.8 = (bf16[768,128]{1,0:T(8,128)(2,1)S(1)}, bf16[768,128]{1,0:T(8,128)(2,1)S(1)}, u32[]{:S(2)}, u32[]{:S(2)}) collective-permute-start(bf16[768,128]{1,0:T(8,128)(2,1)S(1)} %pack.6.refs_0_.refs_4_), channel_id=1, source_target_pairs={{0,1},{1,0},{2,3},{3,2},{4,5},{5,4},{6,7},{7,6},{8,9},{9,8},{10,11... | collective-permute-start | bytes 589832 | tf_op jit(solution)/shard_map/ppermute | solution.py:348
  21.1 1.8 %collective-permute-start.10 = (bf16[768,128]{1,0:T(8,128)(2,1)S(1)}, bf16[768,128]{1,0:T(8,128)(2,1)S(1)}, u32[]{:S(2)}, u32[]{:S(2)}) collective-permute-start(bf16[768,128]{1,0:T(8,128)(2,1)S(1)} %pack.7), channel_id=1, source_target_pairs={{0,1},{1,0},{2,3},{3,2},{4,5},{5,4},{6,7},{7,6},{8,9},{9,8},{10,11... | collective-permute-start | bytes 589832 | tf_op jit(solution)/shard_map/ppermute | solution.py:348
  22.8 1.7 %collective-permute-start.3 = (bf16[768,128]{1,0:T(8,128)(2,1)S(1)}, bf16[768,128]{1,0:T(8,128)(2,1)S(1)}, u32[]{:S(2)}, u32[]{:S(2)}) collective-permute-start(bf16[768,128]{1,0:T(8,128)(2,1)S(1)} %pack.4), channel_id=1, source_target_pairs={{0,1},{1,0},{2,3},{3,2},{4,5},{5,4},{6,7},{7,6},{8,9},{9,8},{10,11... | collective-permute-start | bytes 589832 | tf_op jit(solution)/shard_map/ppermute | solution.py:348

commit v18 on v17

--- a/solution.py
+++ b/solution.py
@@ -18,10 +18,10 @@
 
 
 def features_kernel(*refs, packs, parts, pieces):
-    args, refs = refs[:9], refs[9:]
-    outs, wf_hbm, refs = refs[: len(packs)], refs[len(packs)], refs[len(packs) + 1 :]
-    held, (lo_ref, hi_ref, left_ref, turned_ref, rows_ref, right_ref, wf_ref, sems) = refs[:9], refs[9:]
-    x_ref, gain_ref, bias_ref, lm_ref, lb_ref, rm_ref, rb_ref, w_ref, shift_ref = held
+    args, refs = refs[:7], refs[7:]
+    outs, refs = refs[: len(packs)], refs[len(packs) :]
+    held, (lo_ref, hi_ref, left_ref, turned_ref, rows_ref, right_ref, sems) = refs[:7], refs[7:]
+    x_ref, gain_ref, bias_ref, lm_ref, lb_ref, rm_ref, rb_ref = held
     seqs, residues, depth = x_ref.shape
     hidden = lm_ref.shape[0]
     per = LANES // hidden
@@ -64,11 +64,6 @@
         norm(p)
     for copy in copies[-1:] + rest[2:]:
         copy.wait()
-    count = w_ref.shape[0]
-    wf_ref[:count] = w_ref[...].astype(jnp.float32)
-    wf_ref[count:] = jnp.broadcast_to(
-        shift_ref[...].reshape(1, -1), (wf_ref.shape[0] - count, shift_ref.shape[0])
-    )
     norm(pieces - 1)
 
     column, row = iota((hidden, LANES), 1) % hidden, iota((hidden, LANES), 0)
@@ -104,8 +99,7 @@
         [widen_bias(lb_ref[...]), swapped(widen_bias(rb_ref[...]))], axis=1
     )[:1]
     place = iota((depth, 2 * LANES), 1) % LANES // hidden
-    sends = [pltpu.make_async_copy(wf_ref, wf_hbm, sems.at[free])]
-    sends[0].start()
+    sends = []
 
     total = None
     for k in range(per):
@@ -157,6 +151,15 @@
             at += rows.shape[0]
     for copy in sends:
         copy.wait()
+
+
+def load_kernel(w_ref, shift_ref, after_ref, wf_ref):
+    del after_ref
+    count = w_ref.shape[0]
+    wf_ref[:count] = w_ref[...].astype(jnp.float32)
+    wf_ref[count:] = jnp.broadcast_to(
+        shift_ref[...].reshape(1, -1), (wf_ref.shape[0] - count, shift_ref.shape[0])
+    )
 
 
 def block_weights(wf_ref, wide_ref, *, parts, minor):
@@ -317,18 +320,17 @@
     else:
         packs = tuple((m,) for m in range(narrow)) + ((RIGHT,),)
     left_count, right_count = groups * seqs, minor * residues
-    args = (x, gain, bias, lm.T, lb, rm.T, rb, w, shift)
-    *made, w = pl.pallas_call(
+    args = (x, gain, bias, lm.T, lb, rm.T, rb)
+    made = pl.pallas_call(
         functools.partial(features_kernel, packs=packs, parts=narrow, pieces=pieces),
         out_shape=tuple(
             jax.ShapeDtypeStruct(
                 (sum(right_count if i == RIGHT else left_count for i in pack), LANES), jnp.bfloat16
             )
             for pack in packs
-        )
-        + (jax.ShapeDtypeStruct((w.shape[0] + hidden + 8, cz), jnp.float32),),
+        ),
         in_specs=[hbm] * len(args),
-        out_specs=(hbm,) * (len(packs) + 1),
+        out_specs=(hbm,) * len(packs),
         scratch_shapes=[pltpu.VMEM(a.shape, a.dtype) for a in args]
         + [
             pltpu.VMEM(((seqs + 1) * residues, LANES), jnp.float32),
@@ -337,13 +339,23 @@
             pltpu.VMEM((LANES, LANES), jnp.float32),
             pltpu.VMEM(((minor + 1) * residues, LANES), jnp.float32),
             pltpu.VMEM((minor * residues, LANES), jnp.bfloat16),
-            pltpu.VMEM((w.shape[0] + hidden + 8, cz), jnp.float32),
             pltpu.SemaphoreType.DMA((pieces + len(args) + sum(len(pack) for pack in packs),)),
         ],
         compiler_params=pltpu.CompilerParams(vmem_limit_bytes=VMEM_ALL),
         name="features",
     )(*args)
 
+    def load(after):
+        return pl.pallas_call(
+            load_kernel,
+            out_shape=jax.ShapeDtypeStruct((w.shape[0] + hidden + 8, cz), jnp.float32),
+            in_specs=[vmem] * 3,
+            out_specs=vmem,
+            compiler_params=params,
+            cost_estimate=pl.CostEstimate(flops=1, bytes_accessed=1000, transcendentals=0),
+            name="load",
+        )(w, shift, after)
+
     def across(a, m):
         return lax.ppermute(a, "narrow", [(i, i ^ m) for i in range(narrow)])
 
@@ -353,7 +365,7 @@
     sizes = dict(parts=narrow, minor=minor, seqs_total=seqs * narrow)
     out_shape = jax.ShapeDtypeStruct((own_rows, wide * residues, cz), jnp.bfloat16)
     if direct:
-        return pairs_by_block(made, across, along, w, out_shape, residues, sizes, params)
+        return pairs_by_block(made, across, along, load, out_shape, residues, sizes, params)
 
     lefts = [made[0]] + [across(made[m], m) for m in range(1, narrow)]
     every = lax.all_gather(made[narrow], ("wide", "narrow"), axis=0, tiled=False)
@@ -369,7 +381,7 @@
         in_specs=[pl.BlockSpec((left_count, LANES), lambda b: (0, 0))] * narrow
         + [
             pl.BlockSpec((block, narrow, right_count, LANES), lambda b: (b, 0, 0, 0)),
-            pl.BlockSpec(w.shape, lambda b: (0, 0)),
+            pl.BlockSpec((w.shape[0] + hidden + 8, cz), lambda b: (0, 0)),
         ],
         out_specs=pl.BlockSpec((own_rows, cols, cz), lambda b: (0, b, 0)),
         out_shape=out_shape,
@@ -380,10 +392,10 @@
         ],
         compiler_params=params,
         name="pairs",
-    )(*lefts, every, w)
-
-
-def pairs_by_block(made, across, along, w, out_shape, residues, sizes, params):
+    )(*lefts, every, load(lefts[0]))
+
+
+def pairs_by_block(made, across, along, load, out_shape, residues, sizes, params):
     left_own, right, to_core, to_chip = made
     left_count, right_count = left_own.shape[0], right.shape[0]
     hbm = pl.BlockSpec(memory_space=pltpu.HBM)
@@ -454,7 +466,8 @@
     core = across(to_core, 1)
     middle = pack(near, far, after=(), weight=4_000_000_000)
     beside = across(middle, 1)
-    both = across(pack(chip, after=(last, core)), 1)
+    w = load(chip)
+    both = across(pack(chip, after=(last, core, w)), 1)
     lefts = ((left_own, 0), (core, 0), (chip, 0), (both, left_count))
     own = ((right, 0), (core, left_count), (chip, 2 * left_count), (both, 2 * left_count))
     first, *shared = pairs((own,), (0,), w, lefts=lefts)

time: 26.3 us -> 26.1 us (level)
  no operation moved by 1% of the time
where the time goes in v18:
time: 26.1 us; the launch traced here: 25.9 us
  starting transfers between devices  12.2 us (47%)
  Pallas kernels  8.31 us (32%)
  waiting for transfers between devices  5.26 us (20%)
    ppermute x3, starting transfers between devices, along(): return lax.ppermute(a, 'wide', [(i, i ^ d) for i in range(wide)])  6.61 us
    ppermute x8, starting transfers between devices, across(): return lax.ppermute(a, 'narrow', [(i, i ^ m) for i in range(narrow)])  5.59 us
    pallas_call x3, Pallas kernels, pairs(): pl.pallas_call(functools.partial(pair_kernel, operands=count, rights=righ...  4.63 us
    ppermute x3, waiting for transfers between devices, along(): return lax.ppermute(a, 'wide', [(i, i ^ d) for i in range(wide)])  3.94 us
    pallas_call x1, Pallas kernels, on_device(): pl.pallas_call(functools.partial(features_kernel, packs=packs, parts=narr...  3.59 us
    ppermute x8, waiting for transfers between devices, across(): return lax.ppermute(a, 'narrow', [(i, i ^ m) for i in range(narrow)])  1.31 us
  transfers between devices with their start and end apart: 11, of which 3 were waited for; matrix products, arithmetic and copies ran while one was open for 0% of the time, Pallas kernels for 12%

profile of v18, /device:TPU:0, one launch (start us, length us, event | category | flops | bytes accessed | tf_op | source)
XLA Modules:
  0.0 25.9 jit_solution(278491538642319242)
XLA Ops:
  0.0 3.6 %features.1 = (bf16[96,128]{1,0:T(8,128)(2,1)}, bf16[384,128]{1,0:T(8,128)(2,1)}, bf16[480,128]{1,0:T(8,128)(2,1)}, bf16[576,128]{1,0:T(8,128)(2,1)}) custom-call(bf16[32,48,256]{2,1,0:T(8,128)(2,1)} %refs_0_.1, f32[256]{0:T(256)} %refs_1_.1, f32[256]{0:T(256)} %refs_2_.1, bf16[32,256]{1,0:T(8,128)(2,1)} %bitcast.2, f32[32]{0:T(128)} %refs_4_.1, ...), custom_call_target="tpu_custom_call" | custom-call | tf_op jit(solution)/shard_map/features/pallas_call | solution.py:324
  3.6 4.1 %collective-permute-start = (bf16[384,128]{1,0:T(8,128)(2,1)}, bf16[384,128]{1,0:T(8,128)(2,1)S(1)}, u32[]{:S(2)}, u32[]{:S(2)}) collective-permute-start(bf16[384,128]{1,0:T(8,128)(2,1)} %get-tuple-element.13.refs_0_), channel_id=1, source_target_pairs={{0,8},{4,12},{8,0},{12,4},{1,9},{5,13},{9,1},{13,5},{2,10},{6,14},... | collective-permute-start | bytes 294920 | tf_op jit(solution)/shard_map/ppermute | solution.py:363
  7.7 1.6 %collective-permute-start.7 = (bf16[384,128]{1,0:T(8,128)(2,1)}, bf16[384,128]{1,0:T(8,128)(2,1)S(1)}, u32[]{:S(2)}, u32[]{:S(2)}) collective-permute-start(bf16[384,128]{1,0:T(8,128)(2,1)} %get-tuple-element.13.refs_0_), channel_id=1, source_target_pairs={{0,4},{4,0},{8,12},{12,8},{1,5},{5,1},{9,13},{13,9},{2,6},{6,2},{1... | collective-permute-start | bytes 294920 | tf_op jit(solution)/shard_map/ppermute | solution.py:363
  9.3 1.5 %collective-permute-start.5 = (bf16[576,128]{1,0:T(8,128)(2,1)}, bf16[576,128]{1,0:T(8,128)(2,1)S(1)}, u32[]{:S(2)}, u32[]{:S(2)}) collective-permute-start(bf16[576,128]{1,0:T(8,128)(2,1)} %get-tuple-element.15), channel_id=1, source_target_pairs={{0,2},{1,3},{2,0},{3,1},{4,6},{5,7},{6,4},{7,5},{8,10},{9,11},{10,... | collective-permute-start | bytes 442376 | tf_op jit(solution)/shard_map/ppermute | solution.py:360
  10.8 0.0 copy-start
  10.8 0.0 copy-start.3
  10.8 0.0 collective-permute-start.4
  10.8 1.9 %collective-permute-done.refs_1_ = bf16[384,128]{1,0:T(8,128)(2,1)S(1)} collective-permute-done((bf16[384,128]{1,0:T(8,128)(2,1)}, bf16[384,128]{1,0:T(8,128)(2,1)S(1)}, u32[]{:S(2)}, u32[]{:S(2)}) %collective-permute-start) | collective-permute-done | bytes 98336 | tf_op jit(solution)/shard_map/ppermute | solution.py:363
  12.7 0.9 %collective-permute-start.1 = (bf16[384,128]{1,0:T(8,128)(2,1)S(1)}, bf16[384,128]{1,0:T(8,128)(2,1)S(1)}, u32[]{:S(2)}, u32[]{:S(2)}) collective-permute-start(bf16[384,128]{1,0:T(8,128)(2,1)S(1)} %collective-permute-done.refs_1_), channel_id=1, source_target_pairs={{0,4},{4,0},{8,12},{12,8},{1,5},{5,1},{9,13},{13,9},{2,6},{6,2},{1... | collective-permute-start | bytes 294920 | tf_op jit(solution)/shard_map/ppermute | solution.py:363
  13.6 0.0 collective-permute-done.7.refs_0_
  13.7 1.6 %collective-permute-start.9 = (bf16[768,128]{1,0:T(8,128)(2,1)S(1)}, bf16[768,128]{1,0:T(8,128)(2,1)S(1)}, u32[]{:S(2)}, u32[]{:S(2)}) collective-permute-start(bf16[768,128]{1,0:T(8,128)(2,1)S(1)} %pack.6.refs_0_.refs_4_), channel_id=1, source_target_pairs={{0,2},{1,3},{2,0},{3,1},{4,6},{5,7},{6,4},{7,5},{8,10},{9,11},{10,... | collective-permute-start | bytes 589832 | tf_op jit(solution)/shard_map/ppermute | solution.py:360
  15.2 0.0 collective-permute-done.5.after_ref.refs_0_.refs_2_.refs_6_
  15.2 0.0 copy-done
  15.2 0.0 copy-done.3
  15.3 0.0 copy-start.1
  15.3 0.0 copy-start.2
  15.3 0.0 collective-permute-done.4.refs_2_.refs_1_.refs_5_
  15.3 2.0 %collective-permute-done.1.refs_0_.refs_1_ = bf16[384,128]{1,0:T(8,128)(2,1)S(1)} collective-permute-done((bf16[384,128]{1,0:T(8,128)(2,1)S(1)}, bf16[384,128]{1,0:T(8,128)(2,1)S(1)}, u32[]{:S(2)}, u32[]{:S(2)}) %collective-permute-start.1) | collective-permute-done | bytes 98336 | tf_op jit(solution)/shard_map/ppermute | solution.py:363
  17.3 0.1 collective-permute-start.6
  17.4 1.8 %collective-permute-start.2 = (bf16[384,128]{1,0:T(8,128)(2,1)S(1)}, bf16[384,128]{1,0:T(8,128)(2,1)S(1)}, u32[]{:S(2)}, u32[]{:S(2)}) collective-permute-start(bf16[384,128]{1,0:T(8,128)(2,1)S(1)} %collective-permute-done.1.refs_0_.refs_1_), channel_id=1, source_target_pairs={{0,2},{1,3},{2,0},{3,1},{4,6},{5,7},{6,4},{7,5},{8,10},{9,11},{10,... | collective-permute-start | bytes 294920 | tf_op jit(solution)/shard_map/ppermute | solution.py:360
  19.2 0.2 collective-permute-start.8
  19.4 0.0 collective-permute-done.6.refs_3_.refs_7_
  19.4 0.0 copy-done.1
  19.4 0.0 copy-done.2
  19.4 1.5 %pairs_0.1 = (bf16[12,48,128]{2,1,0:T(8,128)(2,1)S(1)}, bf16[4,2,32,768]{3,2,1,0:T(8,128)(2,1)S(1)}, bf16[2048,256]{1,0:T(8,128)(2,1)S(1)}, f32[8,128]{1,0:T(8,128)S(1)}) custom-call(bf16[384,128]{1,0:T(8,128)(2,1)S(1)} %copy-done.1, bf16[480,128]{1,0:T(8,128)(2,1)S(1)} %collective-permute-done.4.refs_2_.refs_1_.refs_5_, ...), custom_call_target="tpu_custom_call" | custom-call | flops 1000 | bytes 1000 | tf_op jit(solution)/shard_map/pairs_0/pallas_call | solution.py:448
  20.9 0.0 collective-permute-done.9.refs_0_.refs_2_.refs_6_
  20.9 0.4 %collective-permute-start.10 = (bf16[768,128]{1,0:T(8,128)(2,1)S(1)}, bf16[768,128]{1,0:T(8,128)(2,1)S(1)}, u32[]{:S(2)}, u32[]{:S(2)}) collective-permute-start(bf16[768,128]{1,0:T(8,128)(2,1)S(1)} %pack.7), channel_id=1, source_target_pairs={{0,1},{1,0},{2,3},{3,2},{4,5},{5,4},{6,7},{7,6},{8,9},{9,8},{10,11... | collective-permute-start | bytes 589832 | tf_op jit(solution)/shard_map/ppermute | solution.py:360
  21.3 1.3 %collective-permute-done.2.refs_1_.refs_2_ = bf16[384,128]{1,0:T(8,128)(2,1)S(1)} collective-permute-done((bf16[384,128]{1,0:T(8,128)(2,1)S(1)}, bf16[384,128]{1,0:T(8,128)(2,1)S(1)}, u32[]{:S(2)}, u32[]{:S(2)}) %collective-permute-start.2) | collective-permute-done | bytes 98336 | tf_op jit(solution)/shard_map/ppermute | solution.py:360
  22.6 0.1 collective-permute-start.3
  22.7 0.0 collective-permute-done.8.refs_1_.refs_5_
  22.7 0.0 collective-permute-done.10.refs_3_.refs_7_
  22.7 1.6 %pairs_1.1.refs_8_ = bf16[12,96,128]{2,1,0:T(8,128)(2,1)S(1)} custom-call(bf16[768,128]{1,0:T(8,128)(2,1)S(1)} %pack.6.refs_0_.refs_4_, bf16[768,128]{1,0:T(8,128)(2,1)S(1)} %collective-permute-done.8.refs_1_.refs_5_, bf16[768,128]{1,0:T(8,128)(2,1)S(1)} %collective-permute-done.9.refs_0_.refs_2_.refs_6_, ...), custom_call_target="tpu_custom_call" | custom-call | flops 1000 | bytes 1000 | tf_op jit(solution)/shard_map/pairs_1/pallas_call | solution.py:448
  24.3 0.0 collective-permute-done.3.refs_1_.refs_3_
  24.3 1.6 %pairs_3.1 = bf16[12,192,128]{2,1,0:T(8,128)(2,1)} custom-call(bf16[384,128]{1,0:T(8,128)(2,1)S(1)} %collective-permute-done.1.refs_0_.refs_1_, bf16[768,128]{1,0:T(8,128)(2,1)S(1)} %collective-permute-done.3.refs_1_.refs_3_, bf16[384,128]{1,0:T(8,128)(2,1)S(1)} %collective-permute-done.2.refs_1_.refs_2_, ...), custom_call_target="tpu_custom_call" | custom-call | flops 1000 | bytes 1000 | tf_op jit(solution)/shard_map/pairs_3/pallas_call | solution.py:448
  (5 shorter events, 0.1 us)
Async XLA Ops:
  3.6 9.1 %collective-permute-start = (bf16[384,128]{1,0:T(8,128)(2,1)}, bf16[384,128]{1,0:T(8,128)(2,1)S(1)}, u32[]{:S(2)}, u32[]{:S(2)}) collective-permute-start(bf16[384,128]{1,0:T(8,128)(2,1)} %get-tuple-element.13.refs_0_), channel_id=1, source_target_pairs={{0,8},{4,12},{8,0},{12,4},{1,9},{5,13},{9,1},{13,5},{2,10},{6,14},... | collective-permute-start | bytes 294920 | tf_op jit(solution)/shard_map/ppermute | solution.py:363
  7.7 5.9 %collective-permute-start.7 = (bf16[384,128]{1,0:T(8,128)(2,1)}, bf16[384,128]{1,0:T(8,128)(2,1)S(1)}, u32[]{:S(2)}, u32[]{:S(2)}) collective-permute-start(bf16[384,128]{1,0:T(8,128)(2,1)} %get-tuple-element.13.refs_0_), channel_id=1, source_target_pairs={{0,4},{4,0},{8,12},{12,8},{1,5},{5,1},{9,13},{13,9},{2,6},{6,2},{1... | collective-permute-start | bytes 294920 | tf_op jit(solution)/shard_map/ppermute | solution.py:363
  9.3 5.9 %collective-permute-start.5 = (bf16[576,128]{1,0:T(8,128)(2,1)}, bf16[576,128]{1,0:T(8,128)(2,1)S(1)}, u32[]{:S(2)}, u32[]{:S(2)}) collective-permute-start(bf16[576,128]{1,0:T(8,128)(2,1)} %get-tuple-element.15), channel_id=1, source_target_pairs={{0,2},{1,3},{2,0},{3,1},{4,6},{5,7},{6,4},{7,5},{8,10},{9,11},{10,... | collective-permute-start | bytes 442376 | tf_op jit(solution)/shard_map/ppermute | solution.py:360
  10.8 4.5 %copy-start = (bf16[1024,128]{1,0:T(8,128)(2,1)S(1)}, bf16[1024,128]{1,0:T(8,128)(2,1)}, u32[]{:S(2)}) copy-start(bf16[1024,128]{1,0:T(8,128)(2,1)} %w_ref.1) | copy-start | bytes 786436
  10.8 4.5 %copy-start.3 = (f32[128]{0:T(128)S(1)}, f32[128]{0:T(128)}, u32[]{:S(2)}) copy-start(f32[128]{0:T(128)} %shift_ref.1) | copy-start | bytes 1540
  10.8 4.5 %collective-permute-start.4 = (bf16[480,128]{1,0:T(8,128)(2,1)}, bf16[480,128]{1,0:T(8,128)(2,1)S(1)}, u32[]{:S(2)}, u32[]{:S(2)}) collective-permute-start(bf16[480,128]{1,0:T(8,128)(2,1)} %get-tuple-element.14), channel_id=1, source_target_pairs={{0,1},{1,0},{2,3},{3,2},{4,5},{5,4},{6,7},{7,6},{8,9},{9,8},{10,11... | collective-permute-start | bytes 368648 | tf_op jit(solution)/shard_map/ppermute | solution.py:360
  12.7 4.6 %collective-permute-start.1 = (bf16[384,128]{1,0:T(8,128)(2,1)S(1)}, bf16[384,128]{1,0:T(8,128)(2,1)S(1)}, u32[]{:S(2)}, u32[]{:S(2)}) collective-permute-start(bf16[384,128]{1,0:T(8,128)(2,1)S(1)} %collective-permute-done.refs_1_), channel_id=1, source_target_pairs={{0,4},{4,0},{8,12},{12,8},{1,5},{5,1},{9,13},{13,9},{2,6},{6,2},{1... | collective-permute-start | bytes 294920 | tf_op jit(solution)/shard_map/ppermute | solution.py:363
  13.7 7.2 %collective-permute-start.9 = (bf16[768,128]{1,0:T(8,128)(2,1)S(1)}, bf16[768,128]{1,0:T(8,128)(2,1)S(1)}, u32[]{:S(2)}, u32[]{:S(2)}) collective-permute-start(bf16[768,128]{1,0:T(8,128)(2,1)S(1)} %pack.6.refs_0_.refs_4_), channel_id=1, source_target_pairs={{0,2},{1,3},{2,0},{3,1},{4,6},{5,7},{6,4},{7,5},{8,10},{9,11},{10,... | collective-permute-start | bytes 589832 | tf_op jit(solution)/shard_map/ppermute | solution.py:360
  15.3 4.1 %copy-start.1 = (bf16[384,128]{1,0:T(8,128)(2,1)S(1)}, bf16[384,128]{1,0:T(8,128)(2,1)}, u32[]{:S(2)}) copy-start(bf16[384,128]{1,0:T(8,128)(2,1)} %get-tuple-element.13.refs_0_) | copy-start | bytes 294916
  15.3 4.1 %copy-start.2 = (bf16[96,128]{1,0:T(8,128)(2,1)S(1)}, bf16[96,128]{1,0:T(8,128)(2,1)}, u32[]{:S(2)}) copy-start(bf16[96,128]{1,0:T(8,128)(2,1)} %get-tuple-element.16.refs_4_) | copy-start | bytes 73732
  17.3 2.1 %collective-permute-start.6 = (bf16[576,128]{1,0:T(8,128)(2,1)S(1)}, bf16[576,128]{1,0:T(8,128)(2,1)S(1)}, u32[]{:S(2)}, u32[]{:S(2)}) collective-permute-start(bf16[576,128]{1,0:T(8,128)(2,1)S(1)} %pack.5), channel_id=1, source_target_pairs={{0,1},{1,0},{2,3},{3,2},{4,5},{5,4},{6,7},{7,6},{8,9},{9,8},{10,11... | collective-permute-start | bytes 442376 | tf_op jit(solution)/shard_map/ppermute | solution.py:360
  17.4 5.2 %collective-permute-start.2 = (bf16[384,128]{1,0:T(8,128)(2,1)S(1)}, bf16[384,128]{1,0:T(8,128)(2,1)S(1)}, u32[]{:S(2)}, u32[]{:S(2)}) collective-permute-start(bf16[384,128]{1,0:T(8,128)(2,1)S(1)} %collective-permute-done.1.refs_0_.refs_1_), channel_id=1, source_target_pairs={{0,2},{1,3},{2,0},{3,1},{4,6},{5,7},{6,4},{7,5},{8,10},{9,11},{10,... | collective-permute-start | bytes 294920 | tf_op jit(solution)/shard_map/ppermute | solution.py:360
  19.2 3.5 %collective-permute-start.8 = (bf16[768,128]{1,0:T(8,128)(2,1)S(1)}, bf16[768,128]{1,0:T(8,128)(2,1)S(1)}, u32[]{:S(2)}, u32[]{:S(2)}) collective-permute-start(bf16[768,128]{1,0:T(8,128)(2,1)S(1)} %pack.6.refs_0_.refs_4_), channel_id=1, source_target_pairs={{0,1},{1,0},{2,3},{3,2},{4,5},{5,4},{6,7},{7,6},{8,9},{9,8},{10,11... | collective-permute-start | bytes 589832 | tf_op jit(solution)/shard_map/ppermute | solution.py:360
  20.9 1.8 %collective-permute-start.10 = (bf16[768,128]{1,0:T(8,128)(2,1)S(1)}, bf16[768,128]{1,0:T(8,128)(2,1)S(1)}, u32[]{:S(2)}, u32[]{:S(2)}) collective-permute-start(bf16[768,128]{1,0:T(8,128)(2,1)S(1)} %pack.7), channel_id=1, source_target_pairs={{0,1},{1,0},{2,3},{3,2},{4,5},{5,4},{6,7},{7,6},{8,9},{9,8},{10,11... | collective-permute-start | bytes 589832 | tf_op jit(solution)/shard_map/ppermute | solution.py:360
  22.6 1.7 %collective-permute-start.3 = (bf16[768,128]{1,0:T(8,128)(2,1)S(1)}, bf16[768,128]{1,0:T(8,128)(2,1)S(1)}, u32[]{:S(2)}, u32[]{:S(2)}) collective-permute-start(bf16[768,128]{1,0:T(8,128)(2,1)S(1)} %pack.4), channel_id=1, source_target_pairs={{0,1},{1,0},{2,3},{3,2},{4,5},{5,4},{6,7},{7,6},{8,9},{9,8},{10,11... | collective-permute-start | bytes 589832 | tf_op jit(solution)/shard_map/ppermute | solution.py:360

commit v19 on v18

--- a/solution.py
+++ b/solution.py
@@ -40,7 +40,7 @@
     rest = [
         pltpu.make_async_copy(a, b, sems.at[pieces + i]) for i, (a, b) in enumerate(zip(args[1:], held[1:]))
     ]
-    for copy in copies[:1] + rest[:2] + copies[1:] + rest[2:]:
+    for copy in rest + copies:
         copy.start()
     free = pieces + len(rest)
 
@@ -57,14 +57,8 @@
             lo_ref[rows, :] = x[:, :LANES]
             hi_ref[rows, :] = x[:, LANES:]
 
-    for copy in rest[:2]:
+    for copy in rest:
         copy.wait()
-    for p in range(pieces - 1):
-        copies[p].wait()
-        norm(p)
-    for copy in copies[-1:] + rest[2:]:
-        copy.wait()
-    norm(pieces - 1)
 
     column, row = iota((hidden, LANES), 1) % hidden, iota((hidden, LANES), 0)
     spread_l = (column == row).astype(jnp.float32)
@@ -99,6 +93,10 @@
         [widen_bias(lb_ref[...]), swapped(widen_bias(rb_ref[...]))], axis=1
     )[:1]
     place = iota((depth, 2 * LANES), 1) % LANES // hidden
+
+    for p in range(pieces):
+        copies[p].wait()
+        norm(p)
     sends = []
 
     total = None

time: 26.1 us -> 26.2 us (level)
  no operation moved by 1% of the time
where the time goes in v19:
time: 26.2 us; the launch traced here: 26 us
  starting transfers between devices  12.2 us (47%)
  Pallas kernels  8.38 us (32%)
  waiting for transfers between devices  5.26 us (20%)
    ppermute x3, starting transfers between devices, along(): return lax.ppermute(a, 'wide', [(i, i ^ d) for i in range(wide)])  6.62 us
    ppermute x8, starting transfers between devices, across(): return lax.ppermute(a, 'narrow', [(i, i ^ m) for i in range(narrow)])  5.58 us
    pallas_call x3, Pallas kernels, pairs(): pl.pallas_call(functools.partial(pair_kernel, operands=count, rights=righ...  4.63 us
    ppermute x3, waiting for transfers between devices, along(): return lax.ppermute(a, 'wide', [(i, i ^ d) for i in range(wide)])  3.95 us
    pallas_call x1, Pallas kernels, on_device(): pl.pallas_call(functools.partial(features_kernel, packs=packs, parts=narr...  3.66 us
    ppermute x8, waiting for transfers between devices, across(): return lax.ppermute(a, 'narrow', [(i, i ^ m) for i in range(narrow)])  1.32 us
  transfers between devices with their start and end apart: 11, of which 3 were waited for; matrix products, arithmetic and copies ran while one was open for 0% of the time, Pallas kernels for 12%

profile of v19, /device:TPU:0, one launch (start us, length us, event | category | flops | bytes accessed | tf_op | source)
XLA Modules:
  0.0 26.0 jit_solution(5842092234715683306)
XLA Ops:
  0.0 3.7 %features.1 = (bf16[96,128]{1,0:T(8,128)(2,1)}, bf16[384,128]{1,0:T(8,128)(2,1)}, bf16[480,128]{1,0:T(8,128)(2,1)}, bf16[576,128]{1,0:T(8,128)(2,1)}) custom-call(bf16[32,48,256]{2,1,0:T(8,128)(2,1)} %refs_0_.1, f32[256]{0:T(256)} %refs_1_.1, f32[256]{0:T(256)} %refs_2_.1, bf16[32,256]{1,0:T(8,128)(2,1)} %bitcast.2, f32[32]{0:T(128)} %refs_4_.1, ...), custom_call_target="tpu_custom_call" | custom-call | tf_op jit(solution)/shard_map/features/pallas_call | solution.py:322
  3.7 4.1 %collective-permute-start = (bf16[384,128]{1,0:T(8,128)(2,1)}, bf16[384,128]{1,0:T(8,128)(2,1)S(1)}, u32[]{:S(2)}, u32[]{:S(2)}) collective-permute-start(bf16[384,128]{1,0:T(8,128)(2,1)} %get-tuple-element.13.refs_0_), channel_id=1, source_target_pairs={{0,8},{4,12},{8,0},{12,4},{1,9},{5,13},{9,1},{13,5},{2,10},{6,14},... | collective-permute-start | bytes 294920 | tf_op jit(solution)/shard_map/ppermute | solution.py:361
  7.8 1.6 %collective-permute-start.7 = (bf16[384,128]{1,0:T(8,128)(2,1)}, bf16[384,128]{1,0:T(8,128)(2,1)S(1)}, u32[]{:S(2)}, u32[]{:S(2)}) collective-permute-start(bf16[384,128]{1,0:T(8,128)(2,1)} %get-tuple-element.13.refs_0_), channel_id=1, source_target_pairs={{0,4},{4,0},{8,12},{12,8},{1,5},{5,1},{9,13},{13,9},{2,6},{6,2},{1... | collective-permute-start | bytes 294920 | tf_op jit(solution)/shard_map/ppermute | solution.py:361
  9.4 1.5 %collective-permute-start.5 = (bf16[576,128]{1,0:T(8,128)(2,1)}, bf16[576,128]{1,0:T(8,128)(2,1)S(1)}, u32[]{:S(2)}, u32[]{:S(2)}) collective-permute-start(bf16[576,128]{1,0:T(8,128)(2,1)} %get-tuple-element.15), channel_id=1, source_target_pairs={{0,2},{1,3},{2,0},{3,1},{4,6},{5,7},{6,4},{7,5},{8,10},{9,11},{10,... | collective-permute-start | bytes 442376 | tf_op jit(solution)/shard_map/ppermute | solution.py:358
  10.8 0.0 copy-start
  10.8 0.0 copy-start.3
  10.8 0.0 collective-permute-start.4
  10.9 1.9 %collective-permute-done.refs_1_ = bf16[384,128]{1,0:T(8,128)(2,1)S(1)} collective-permute-done((bf16[384,128]{1,0:T(8,128)(2,1)}, bf16[384,128]{1,0:T(8,128)(2,1)S(1)}, u32[]{:S(2)}, u32[]{:S(2)}) %collective-permute-start) | collective-permute-done | bytes 98336 | tf_op jit(solution)/shard_map/ppermute | solution.py:361
  12.8 0.9 %collective-permute-start.1 = (bf16[384,128]{1,0:T(8,128)(2,1)S(1)}, bf16[384,128]{1,0:T(8,128)(2,1)S(1)}, u32[]{:S(2)}, u32[]{:S(2)}) collective-permute-start(bf16[384,128]{1,0:T(8,128)(2,1)S(1)} %collective-permute-done.refs_1_), channel_id=1, source_target_pairs={{0,4},{4,0},{8,12},{12,8},{1,5},{5,1},{9,13},{13,9},{2,6},{6,2},{1... | collective-permute-start | bytes 294920 | tf_op jit(solution)/shard_map/ppermute | solution.py:361
  13.7 0.0 collective-permute-done.7.refs_0_
  13.7 1.6 %collective-permute-start.9 = (bf16[768,128]{1,0:T(8,128)(2,1)S(1)}, bf16[768,128]{1,0:T(8,128)(2,1)S(1)}, u32[]{:S(2)}, u32[]{:S(2)}) collective-permute-start(bf16[768,128]{1,0:T(8,128)(2,1)S(1)} %pack.6.refs_0_.refs_4_), channel_id=1, source_target_pairs={{0,2},{1,3},{2,0},{3,1},{4,6},{5,7},{6,4},{7,5},{8,10},{9,11},{10,... | collective-permute-start | bytes 589832 | tf_op jit(solution)/shard_map/ppermute | solution.py:358
  15.3 0.0 collective-permute-done.5.after_ref.refs_0_.refs_2_.refs_6_
  15.3 0.0 copy-done
  15.3 0.0 copy-done.3
  15.4 0.0 copy-start.1
  15.4 0.0 copy-start.2
  15.4 0.0 collective-permute-done.4.refs_2_.refs_1_.refs_5_
  15.4 2.0 %collective-permute-done.1.refs_0_.refs_1_ = bf16[384,128]{1,0:T(8,128)(2,1)S(1)} collective-permute-done((bf16[384,128]{1,0:T(8,128)(2,1)S(1)}, bf16[384,128]{1,0:T(8,128)(2,1)S(1)}, u32[]{:S(2)}, u32[]{:S(2)}) %collective-permute-start.1) | collective-permute-done | bytes 98336 | tf_op jit(solution)/shard_map/ppermute | solution.py:361
  17.4 0.1 collective-permute-start.6
  17.5 1.8 %collective-permute-start.2 = (bf16[384,128]{1,0:T(8,128)(2,1)S(1)}, bf16[384,128]{1,0:T(8,128)(2,1)S(1)}, u32[]{:S(2)}, u32[]{:S(2)}) collective-permute-start(bf16[384,128]{1,0:T(8,128)(2,1)S(1)} %collective-permute-done.1.refs_0_.refs_1_), channel_id=1, source_target_pairs={{0,2},{1,3},{2,0},{3,1},{4,6},{5,7},{6,4},{7,5},{8,10},{9,11},{10,... | collective-permute-start | bytes 294920 | tf_op jit(solution)/shard_map/ppermute | solution.py:358
  19.3 0.2 collective-permute-start.8
  19.5 0.0 collective-permute-done.6.refs_3_.refs_7_
  19.5 0.0 copy-done.1
  19.5 0.0 copy-done.2
  19.5 1.5 %pairs_0.1 = (bf16[12,48,128]{2,1,0:T(8,128)(2,1)S(1)}, bf16[4,2,32,768]{3,2,1,0:T(8,128)(2,1)S(1)}, bf16[2048,256]{1,0:T(8,128)(2,1)S(1)}, f32[8,128]{1,0:T(8,128)S(1)}) custom-call(bf16[384,128]{1,0:T(8,128)(2,1)S(1)} %copy-done.1, bf16[480,128]{1,0:T(8,128)(2,1)S(1)} %collective-permute-done.4.refs_2_.refs_1_.refs_5_, ...), custom_call_target="tpu_custom_call" | custom-call | flops 1000 | bytes 1000 | tf_op jit(solution)/shard_map/pairs_0/pallas_call | solution.py:446
  21.0 0.0 collective-permute-done.9.refs_0_.refs_2_.refs_6_
  21.0 0.4 %collective-permute-start.10 = (bf16[768,128]{1,0:T(8,128)(2,1)S(1)}, bf16[768,128]{1,0:T(8,128)(2,1)S(1)}, u32[]{:S(2)}, u32[]{:S(2)}) collective-permute-start(bf16[768,128]{1,0:T(8,128)(2,1)S(1)} %pack.7), channel_id=1, source_target_pairs={{0,1},{1,0},{2,3},{3,2},{4,5},{5,4},{6,7},{7,6},{8,9},{9,8},{10,11... | collective-permute-start | bytes 589832 | tf_op jit(solution)/shard_map/ppermute | solution.py:358
  21.4 1.3 %collective-permute-done.2.refs_1_.refs_2_ = bf16[384,128]{1,0:T(8,128)(2,1)S(1)} collective-permute-done((bf16[384,128]{1,0:T(8,128)(2,1)S(1)}, bf16[384,128]{1,0:T(8,128)(2,1)S(1)}, u32[]{:S(2)}, u32[]{:S(2)}) %collective-permute-start.2) | collective-permute-done | bytes 98336 | tf_op jit(solution)/shard_map/ppermute | solution.py:358
  22.7 0.1 collective-permute-start.3
  22.8 0.0 collective-permute-done.8.refs_1_.refs_5_
  22.8 0.0 collective-permute-done.10.refs_3_.refs_7_
  22.8 1.5 %pairs_1.1.refs_8_ = bf16[12,96,128]{2,1,0:T(8,128)(2,1)S(1)} custom-call(bf16[768,128]{1,0:T(8,128)(2,1)S(1)} %pack.6.refs_0_.refs_4_, bf16[768,128]{1,0:T(8,128)(2,1)S(1)} %collective-permute-done.8.refs_1_.refs_5_, bf16[768,128]{1,0:T(8,128)(2,1)S(1)} %collective-permute-done.9.refs_0_.refs_2_.refs_6_, ...), custom_call_target="tpu_custom_call" | custom-call | flops 1000 | bytes 1000 | tf_op jit(solution)/shard_map/pairs_1/pallas_call | solution.py:446
  24.4 0.0 collective-permute-done.3.refs_1_.refs_3_
  24.4 1.6 %pairs_3.1 = bf16[12,192,128]{2,1,0:T(8,128)(2,1)} custom-call(bf16[384,128]{1,0:T(8,128)(2,1)S(1)} %collective-permute-done.1.refs_0_.refs_1_, bf16[768,128]{1,0:T(8,128)(2,1)S(1)} %collective-permute-done.3.refs_1_.refs_3_, bf16[384,128]{1,0:T(8,128)(2,1)S(1)} %collective-permute-done.2.refs_1_.refs_2_, ...), custom_call_target="tpu_custom_call" | custom-call | flops 1000 | bytes 1000 | tf_op jit(solution)/shard_map/pairs_3/pallas_call | solution.py:446
  (5 shorter events, 0.1 us)
Async XLA Ops:
  3.7 9.1 %collective-permute-start = (bf16[384,128]{1,0:T(8,128)(2,1)}, bf16[384,128]{1,0:T(8,128)(2,1)S(1)}, u32[]{:S(2)}, u32[]{:S(2)}) collective-permute-start(bf16[384,128]{1,0:T(8,128)(2,1)} %get-tuple-element.13.refs_0_), channel_id=1, source_target_pairs={{0,8},{4,12},{8,0},{12,4},{1,9},{5,13},{9,1},{13,5},{2,10},{6,14},... | collective-permute-start | bytes 294920 | tf_op jit(solution)/shard_map/ppermute | solution.py:361
  7.8 5.9 %collective-permute-start.7 = (bf16[384,128]{1,0:T(8,128)(2,1)}, bf16[384,128]{1,0:T(8,128)(2,1)S(1)}, u32[]{:S(2)}, u32[]{:S(2)}) collective-permute-start(bf16[384,128]{1,0:T(8,128)(2,1)} %get-tuple-element.13.refs_0_), channel_id=1, source_target_pairs={{0,4},{4,0},{8,12},{12,8},{1,5},{5,1},{9,13},{13,9},{2,6},{6,2},{1... | collective-permute-start | bytes 294920 | tf_op jit(solution)/shard_map/ppermute | solution.py:361
  9.4 5.9 %collective-permute-start.5 = (bf16[576,128]{1,0:T(8,128)(2,1)}, bf16[576,128]{1,0:T(8,128)(2,1)S(1)}, u32[]{:S(2)}, u32[]{:S(2)}) collective-permute-start(bf16[576,128]{1,0:T(8,128)(2,1)} %get-tuple-element.15), channel_id=1, source_target_pairs={{0,2},{1,3},{2,0},{3,1},{4,6},{5,7},{6,4},{7,5},{8,10},{9,11},{10,... | collective-permute-start | bytes 442376 | tf_op jit(solution)/shard_map/ppermute | solution.py:358
  10.8 4.5 %copy-start = (bf16[1024,128]{1,0:T(8,128)(2,1)S(1)}, bf16[1024,128]{1,0:T(8,128)(2,1)}, u32[]{:S(2)}) copy-start(bf16[1024,128]{1,0:T(8,128)(2,1)} %w_ref.1) | copy-start | bytes 786436
  10.8 4.5 %copy-start.3 = (f32[128]{0:T(128)S(1)}, f32[128]{0:T(128)}, u32[]{:S(2)}) copy-start(f32[128]{0:T(128)} %shift_ref.1) | copy-start | bytes 1540
  10.8 4.5 %collective-permute-start.4 = (bf16[480,128]{1,0:T(8,128)(2,1)}, bf16[480,128]{1,0:T(8,128)(2,1)S(1)}, u32[]{:S(2)}, u32[]{:S(2)}) collective-permute-start(bf16[480,128]{1,0:T(8,128)(2,1)} %get-tuple-element.14), channel_id=1, source_target_pairs={{0,1},{1,0},{2,3},{3,2},{4,5},{5,4},{6,7},{7,6},{8,9},{9,8},{10,11... | collective-permute-start | bytes 368648 | tf_op jit(solution)/shard_map/ppermute | solution.py:358
  12.8 4.6 %collective-permute-start.1 = (bf16[384,128]{1,0:T(8,128)(2,1)S(1)}, bf16[384,128]{1,0:T(8,128)(2,1)S(1)}, u32[]{:S(2)}, u32[]{:S(2)}) collective-permute-start(bf16[384,128]{1,0:T(8,128)(2,1)S(1)} %collective-permute-done.refs_1_), channel_id=1, source_target_pairs={{0,4},{4,0},{8,12},{12,8},{1,5},{5,1},{9,13},{13,9},{2,6},{6,2},{1... | collective-permute-start | bytes 294920 | tf_op jit(solution)/shard_map/ppermute | solution.py:361
  13.7 7.2 %collective-permute-start.9 = (bf16[768,128]{1,0:T(8,128)(2,1)S(1)}, bf16[768,128]{1,0:T(8,128)(2,1)S(1)}, u32[]{:S(2)}, u32[]{:S(2)}) collective-permute-start(bf16[768,128]{1,0:T(8,128)(2,1)S(1)} %pack.6.refs_0_.refs_4_), channel_id=1, source_target_pairs={{0,2},{1,3},{2,0},{3,1},{4,6},{5,7},{6,4},{7,5},{8,10},{9,11},{10,... | collective-permute-start | bytes 589832 | tf_op jit(solution)/shard_map/ppermute | solution.py:358
  15.4 4.1 %copy-start.1 = (bf16[384,128]{1,0:T(8,128)(2,1)S(1)}, bf16[384,128]{1,0:T(8,128)(2,1)}, u32[]{:S(2)}) copy-start(bf16[384,128]{1,0:T(8,128)(2,1)} %get-tuple-element.13.refs_0_) | copy-start | bytes 294916
  15.4 4.1 %copy-start.2 = (bf16[96,128]{1,0:T(8,128)(2,1)S(1)}, bf16[96,128]{1,0:T(8,128)(2,1)}, u32[]{:S(2)}) copy-start(bf16[96,128]{1,0:T(8,128)(2,1)} %get-tuple-element.16.refs_4_) | copy-start | bytes 73732
  17.4 2.1 %collective-permute-start.6 = (bf16[576,128]{1,0:T(8,128)(2,1)S(1)}, bf16[576,128]{1,0:T(8,128)(2,1)S(1)}, u32[]{:S(2)}, u32[]{:S(2)}) collective-permute-start(bf16[576,128]{1,0:T(8,128)(2,1)S(1)} %pack.5), channel_id=1, source_target_pairs={{0,1},{1,0},{2,3},{3,2},{4,5},{5,4},{6,7},{7,6},{8,9},{9,8},{10,11... | collective-permute-start | bytes 442376 | tf_op jit(solution)/shard_map/ppermute | solution.py:358
  17.5 5.2 %collective-permute-start.2 = (bf16[384,128]{1,0:T(8,128)(2,1)S(1)}, bf16[384,128]{1,0:T(8,128)(2,1)S(1)}, u32[]{:S(2)}, u32[]{:S(2)}) collective-permute-start(bf16[384,128]{1,0:T(8,128)(2,1)S(1)} %collective-permute-done.1.refs_0_.refs_1_), channel_id=1, source_target_pairs={{0,2},{1,3},{2,0},{3,1},{4,6},{5,7},{6,4},{7,5},{8,10},{9,11},{10,... | collective-permute-start | bytes 294920 | tf_op jit(solution)/shard_map/ppermute | solution.py:358
  19.3 3.5 %collective-permute-start.8 = (bf16[768,128]{1,0:T(8,128)(2,1)S(1)}, bf16[768,128]{1,0:T(8,128)(2,1)S(1)}, u32[]{:S(2)}, u32[]{:S(2)}) collective-permute-start(bf16[768,128]{1,0:T(8,128)(2,1)S(1)} %pack.6.refs_0_.refs_4_), channel_id=1, source_target_pairs={{0,1},{1,0},{2,3},{3,2},{4,5},{5,4},{6,7},{7,6},{8,9},{9,8},{10,11... | collective-permute-start | bytes 589832 | tf_op jit(solution)/shard_map/ppermute | solution.py:358
  21.0 1.8 %collective-permute-start.10 = (bf16[768,128]{1,0:T(8,128)(2,1)S(1)}, bf16[768,128]{1,0:T(8,128)(2,1)S(1)}, u32[]{:S(2)}, u32[]{:S(2)}) collective-permute-start(bf16[768,128]{1,0:T(8,128)(2,1)S(1)} %pack.7), channel_id=1, source_target_pairs={{0,1},{1,0},{2,3},{3,2},{4,5},{5,4},{6,7},{7,6},{8,9},{9,8},{10,11... | collective-permute-start | bytes 589832 | tf_op jit(solution)/shard_map/ppermute | solution.py:358
  22.7 1.7 %collective-permute-start.3 = (bf16[768,128]{1,0:T(8,128)(2,1)S(1)}, bf16[768,128]{1,0:T(8,128)(2,1)S(1)}, u32[]{:S(2)}, u32[]{:S(2)}) collective-permute-start(bf16[768,128]{1,0:T(8,128)(2,1)S(1)} %pack.4), channel_id=1, source_target_pairs={{0,1},{1,0},{2,3},{3,2},{4,5},{5,4},{6,7},{7,6},{8,9},{9,8},{10,11... | collective-permute-start | bytes 589832 | tf_op jit(solution)/shard_map/ppermute | solution.py:358

commit v20 on v19

--- a/solution.py
+++ b/solution.py
@@ -308,7 +308,7 @@
     minor = hidden // slots
     own_rows = residues // narrow
     groups = own_rows // per
-    pieces = 4
+    pieces = 2
     hbm = pl.BlockSpec(memory_space=pltpu.HBM)
     vmem = pl.BlockSpec(memory_space=pltpu.VMEM)
     params = pltpu.CompilerParams(vmem_limit_bytes=VMEM_LIMIT)

time: 26.2 us -> 26 us (level)
  no operation moved by 1% of the time
where the time goes in v20:
time: 26 us; the launch traced here: 25.8 us
  starting transfers between devices  12.2 us (47%)
  Pallas kernels  8.17 us (31%)
  waiting for transfers between devices  5.26 us (20%)
    ppermute x3, starting transfers between devices, along(): return lax.ppermute(a, 'wide', [(i, i ^ d) for i in range(wide)])  6.61 us
    ppermute x8, starting transfers between devices, across(): return lax.ppermute(a, 'narrow', [(i, i ^ m) for i in range(narrow)])  5.59 us
    pallas_call x3, Pallas kernels, pairs(): pl.pallas_call(functools.partial(pair_kernel, operands=count, rights=righ...  4.63 us
    ppermute x3, waiting for transfers between devices, along(): return lax.ppermute(a, 'wide', [(i, i ^ d) for i in range(wide)])  3.94 us
    pallas_call x1, Pallas kernels, on_device(): pl.pallas_call(functools.partial(features_kernel, packs=packs, parts=narr...  3.45 us
    ppermute x8, waiting for transfers between devices, across(): return lax.ppermute(a, 'narrow', [(i, i ^ m) for i in range(narrow)])  1.32 us
  transfers between devices with their start and end apart: 11, of which 3 were waited for; matrix products, arithmetic and copies ran while one was open for 0% of the time, Pallas kernels for 12%

profile of v20, /device:TPU:0, one launch (start us, length us, event | category | flops | bytes accessed | tf_op | source)
XLA Modules:
  0.0 25.8 jit_solution(2501148335643224819)
XLA Ops:
  0.0 3.5 %features.1 = (bf16[96,128]{1,0:T(8,128)(2,1)}, bf16[384,128]{1,0:T(8,128)(2,1)}, bf16[480,128]{1,0:T(8,128)(2,1)}, bf16[576,128]{1,0:T(8,128)(2,1)}) custom-call(bf16[32,48,256]{2,1,0:T(8,128)(2,1)} %refs_0_.1, f32[256]{0:T(256)} %refs_1_.1, f32[256]{0:T(256)} %refs_2_.1, bf16[32,256]{1,0:T(8,128)(2,1)} %bitcast.2, f32[32]{0:T(128)} %refs_4_.1, ...), custom_call_target="tpu_custom_call" | custom-call | tf_op jit(solution)/shard_map/features/pallas_call | solution.py:322
  3.5 4.1 %collective-permute-start = (bf16[384,128]{1,0:T(8,128)(2,1)}, bf16[384,128]{1,0:T(8,128)(2,1)S(1)}, u32[]{:S(2)}, u32[]{:S(2)}) collective-permute-start(bf16[384,128]{1,0:T(8,128)(2,1)} %get-tuple-element.13.refs_0_), channel_id=1, source_target_pairs={{0,8},{4,12},{8,0},{12,4},{1,9},{5,13},{9,1},{13,5},{2,10},{6,14},... | collective-permute-start | bytes 294920 | tf_op jit(solution)/shard_map/ppermute | solution.py:361
  7.6 1.6 %collective-permute-start.7 = (bf16[384,128]{1,0:T(8,128)(2,1)}, bf16[384,128]{1,0:T(8,128)(2,1)S(1)}, u32[]{:S(2)}, u32[]{:S(2)}) collective-permute-start(bf16[384,128]{1,0:T(8,128)(2,1)} %get-tuple-element.13.refs_0_), channel_id=1, source_target_pairs={{0,4},{4,0},{8,12},{12,8},{1,5},{5,1},{9,13},{13,9},{2,6},{6,2},{1... | collective-permute-start | bytes 294920 | tf_op jit(solution)/shard_map/ppermute | solution.py:361
  9.1 1.5 %collective-permute-start.5 = (bf16[576,128]{1,0:T(8,128)(2,1)}, bf16[576,128]{1,0:T(8,128)(2,1)S(1)}, u32[]{:S(2)}, u32[]{:S(2)}) collective-permute-start(bf16[576,128]{1,0:T(8,128)(2,1)} %get-tuple-element.15), channel_id=1, source_target_pairs={{0,2},{1,3},{2,0},{3,1},{4,6},{5,7},{6,4},{7,5},{8,10},{9,11},{10,... | collective-permute-start | bytes 442376 | tf_op jit(solution)/shard_map/ppermute | solution.py:358
  10.6 0.0 copy-start
  10.6 0.0 copy-start.3
  10.6 0.0 collective-permute-start.4
  10.6 1.9 %collective-permute-done.refs_1_ = bf16[384,128]{1,0:T(8,128)(2,1)S(1)} collective-permute-done((bf16[384,128]{1,0:T(8,128)(2,1)}, bf16[384,128]{1,0:T(8,128)(2,1)S(1)}, u32[]{:S(2)}, u32[]{:S(2)}) %collective-permute-start) | collective-permute-done | bytes 98336 | tf_op jit(solution)/shard_map/ppermute | solution.py:361
  12.6 0.9 %collective-permute-start.1 = (bf16[384,128]{1,0:T(8,128)(2,1)S(1)}, bf16[384,128]{1,0:T(8,128)(2,1)S(1)}, u32[]{:S(2)}, u32[]{:S(2)}) collective-permute-start(bf16[384,128]{1,0:T(8,128)(2,1)S(1)} %collective-permute-done.refs_1_), channel_id=1, source_target_pairs={{0,4},{4,0},{8,12},{12,8},{1,5},{5,1},{9,13},{13,9},{2,6},{6,2},{1... | collective-permute-start | bytes 294920 | tf_op jit(solution)/shard_map/ppermute | solution.py:361
  13.5 0.0 collective-permute-done.7.refs_0_
  13.5 1.6 %collective-permute-start.9 = (bf16[768,128]{1,0:T(8,128)(2,1)S(1)}, bf16[768,128]{1,0:T(8,128)(2,1)S(1)}, u32[]{:S(2)}, u32[]{:S(2)}) collective-permute-start(bf16[768,128]{1,0:T(8,128)(2,1)S(1)} %pack.6.refs_0_.refs_4_), channel_id=1, source_target_pairs={{0,2},{1,3},{2,0},{3,1},{4,6},{5,7},{6,4},{7,5},{8,10},{9,11},{10,... | collective-permute-start | bytes 589832 | tf_op jit(solution)/shard_map/ppermute | solution.py:358
  15.1 0.0 collective-permute-done.5.after_ref.refs_0_.refs_2_.refs_6_
  15.1 0.0 copy-done
  15.1 0.0 copy-done.3
  15.1 0.0 copy-start.1
  15.1 0.0 copy-start.2
  15.2 0.0 collective-permute-done.4.refs_2_.refs_1_.refs_5_
  15.2 2.0 %collective-permute-done.1.refs_0_.refs_1_ = bf16[384,128]{1,0:T(8,128)(2,1)S(1)} collective-permute-done((bf16[384,128]{1,0:T(8,128)(2,1)S(1)}, bf16[384,128]{1,0:T(8,128)(2,1)S(1)}, u32[]{:S(2)}, u32[]{:S(2)}) %collective-permute-start.1) | collective-permute-done | bytes 98336 | tf_op jit(solution)/shard_map/ppermute | solution.py:361
  17.2 0.1 collective-permute-start.6
  17.3 1.8 %collective-permute-start.2 = (bf16[384,128]{1,0:T(8,128)(2,1)S(1)}, bf16[384,128]{1,0:T(8,128)(2,1)S(1)}, u32[]{:S(2)}, u32[]{:S(2)}) collective-permute-start(bf16[384,128]{1,0:T(8,128)(2,1)S(1)} %collective-permute-done.1.refs_0_.refs_1_), channel_id=1, source_target_pairs={{0,2},{1,3},{2,0},{3,1},{4,6},{5,7},{6,4},{7,5},{8,10},{9,11},{10,... | collective-permute-start | bytes 294920 | tf_op jit(solution)/shard_map/ppermute | solution.py:358
  19.1 0.2 collective-permute-start.8
  19.3 0.0 collective-permute-done.6.refs_3_.refs_7_
  19.3 0.0 copy-done.1
  19.3 0.0 copy-done.2
  19.3 1.5 %pairs_0.1 = (bf16[12,48,128]{2,1,0:T(8,128)(2,1)S(1)}, bf16[4,2,32,768]{3,2,1,0:T(8,128)(2,1)S(1)}, bf16[2048,256]{1,0:T(8,128)(2,1)S(1)}, f32[8,128]{1,0:T(8,128)S(1)}) custom-call(bf16[384,128]{1,0:T(8,128)(2,1)S(1)} %copy-done.1, bf16[480,128]{1,0:T(8,128)(2,1)S(1)} %collective-permute-done.4.refs_2_.refs_1_.refs_5_, ...), custom_call_target="tpu_custom_call" | custom-call | flops 1000 | bytes 1000 | tf_op jit(solution)/shard_map/pairs_0/pallas_call | solution.py:446
  20.7 0.0 collective-permute-done.9.refs_0_.refs_2_.refs_6_
  20.8 0.4 %collective-permute-start.10 = (bf16[768,128]{1,0:T(8,128)(2,1)S(1)}, bf16[768,128]{1,0:T(8,128)(2,1)S(1)}, u32[]{:S(2)}, u32[]{:S(2)}) collective-permute-start(bf16[768,128]{1,0:T(8,128)(2,1)S(1)} %pack.7), channel_id=1, source_target_pairs={{0,1},{1,0},{2,3},{3,2},{4,5},{5,4},{6,7},{7,6},{8,9},{9,8},{10,11... | collective-permute-start | bytes 589832 | tf_op jit(solution)/shard_map/ppermute | solution.py:358
  21.2 1.3 %collective-permute-done.2.refs_1_.refs_2_ = bf16[384,128]{1,0:T(8,128)(2,1)S(1)} collective-permute-done((bf16[384,128]{1,0:T(8,128)(2,1)S(1)}, bf16[384,128]{1,0:T(8,128)(2,1)S(1)}, u32[]{:S(2)}, u32[]{:S(2)}) %collective-permute-start.2) | collective-permute-done | bytes 98336 | tf_op jit(solution)/shard_map/ppermute | solution.py:358
  22.5 0.1 collective-permute-start.3
  22.6 0.0 collective-permute-done.8.refs_1_.refs_5_
  22.6 0.0 collective-permute-done.10.refs_3_.refs_7_
  22.6 1.6 %pairs_1.1.refs_8_ = bf16[12,96,128]{2,1,0:T(8,128)(2,1)S(1)} custom-call(bf16[768,128]{1,0:T(8,128)(2,1)S(1)} %pack.6.refs_0_.refs_4_, bf16[768,128]{1,0:T(8,128)(2,1)S(1)} %collective-permute-done.8.refs_1_.refs_5_, bf16[768,128]{1,0:T(8,128)(2,1)S(1)} %collective-permute-done.9.refs_0_.refs_2_.refs_6_, ...), custom_call_target="tpu_custom_call" | custom-call | flops 1000 | bytes 1000 | tf_op jit(solution)/shard_map/pairs_1/pallas_call | solution.py:446
  24.2 0.0 collective-permute-done.3.refs_1_.refs_3_
  24.2 1.6 %pairs_3.1 = bf16[12,192,128]{2,1,0:T(8,128)(2,1)} custom-call(bf16[384,128]{1,0:T(8,128)(2,1)S(1)} %collective-permute-done.1.refs_0_.refs_1_, bf16[768,128]{1,0:T(8,128)(2,1)S(1)} %collective-permute-done.3.refs_1_.refs_3_, bf16[384,128]{1,0:T(8,128)(2,1)S(1)} %collective-permute-done.2.refs_1_.refs_2_, ...), custom_call_target="tpu_custom_call" | custom-call | flops 1000 | bytes 1000 | tf_op jit(solution)/shard_map/pairs_3/pallas_call | solution.py:446
  (5 shorter events, 0.1 us)
Async XLA Ops:
  3.5 9.1 %collective-permute-start = (bf16[384,128]{1,0:T(8,128)(2,1)}, bf16[384,128]{1,0:T(8,128)(2,1)S(1)}, u32[]{:S(2)}, u32[]{:S(2)}) collective-permute-start(bf16[384,128]{1,0:T(8,128)(2,1)} %get-tuple-element.13.refs_0_), channel_id=1, source_target_pairs={{0,8},{4,12},{8,0},{12,4},{1,9},{5,13},{9,1},{13,5},{2,10},{6,14},... | collective-permute-start | bytes 294920 | tf_op jit(solution)/shard_map/ppermute | solution.py:361
  7.6 5.9 %collective-permute-start.7 = (bf16[384,128]{1,0:T(8,128)(2,1)}, bf16[384,128]{1,0:T(8,128)(2,1)S(1)}, u32[]{:S(2)}, u32[]{:S(2)}) collective-permute-start(bf16[384,128]{1,0:T(8,128)(2,1)} %get-tuple-element.13.refs_0_), channel_id=1, source_target_pairs={{0,4},{4,0},{8,12},{12,8},{1,5},{5,1},{9,13},{13,9},{2,6},{6,2},{1... | collective-permute-start | bytes 294920 | tf_op jit(solution)/shard_map/ppermute | solution.py:361
  9.1 5.9 %collective-permute-start.5 = (bf16[576,128]{1,0:T(8,128)(2,1)}, bf16[576,128]{1,0:T(8,128)(2,1)S(1)}, u32[]{:S(2)}, u32[]{:S(2)}) collective-permute-start(bf16[576,128]{1,0:T(8,128)(2,1)} %get-tuple-element.15), channel_id=1, source_target_pairs={{0,2},{1,3},{2,0},{3,1},{4,6},{5,7},{6,4},{7,5},{8,10},{9,11},{10,... | collective-permute-start | bytes 442376 | tf_op jit(solution)/shard_map/ppermute | solution.py:358
  10.6 4.5 %copy-start = (bf16[1024,128]{1,0:T(8,128)(2,1)S(1)}, bf16[1024,128]{1,0:T(8,128)(2,1)}, u32[]{:S(2)}) copy-start(bf16[1024,128]{1,0:T(8,128)(2,1)} %w_ref.1) | copy-start | bytes 786436
  10.6 4.5 %copy-start.3 = (f32[128]{0:T(128)S(1)}, f32[128]{0:T(128)}, u32[]{:S(2)}) copy-start(f32[128]{0:T(128)} %shift_ref.1) | copy-start | bytes 1540
  10.6 4.5 %collective-permute-start.4 = (bf16[480,128]{1,0:T(8,128)(2,1)}, bf16[480,128]{1,0:T(8,128)(2,1)S(1)}, u32[]{:S(2)}, u32[]{:S(2)}) collective-permute-start(bf16[480,128]{1,0:T(8,128)(2,1)} %get-tuple-element.14), channel_id=1, source_target_pairs={{0,1},{1,0},{2,3},{3,2},{4,5},{5,4},{6,7},{7,6},{8,9},{9,8},{10,11... | collective-permute-start | bytes 368648 | tf_op jit(solution)/shard_map/ppermute | solution.py:358
  12.6 4.6 %collective-permute-start.1 = (bf16[384,128]{1,0:T(8,128)(2,1)S(1)}, bf16[384,128]{1,0:T(8,128)(2,1)S(1)}, u32[]{:S(2)}, u32[]{:S(2)}) collective-permute-start(bf16[384,128]{1,0:T(8,128)(2,1)S(1)} %collective-permute-done.refs_1_), channel_id=1, source_target_pairs={{0,4},{4,0},{8,12},{12,8},{1,5},{5,1},{9,13},{13,9},{2,6},{6,2},{1... | collective-permute-start | bytes 294920 | tf_op jit(solution)/shard_map/ppermute | solution.py:361
  13.5 7.2 %collective-permute-start.9 = (bf16[768,128]{1,0:T(8,128)(2,1)S(1)}, bf16[768,128]{1,0:T(8,128)(2,1)S(1)}, u32[]{:S(2)}, u32[]{:S(2)}) collective-permute-start(bf16[768,128]{1,0:T(8,128)(2,1)S(1)} %pack.6.refs_0_.refs_4_), channel_id=1, source_target_pairs={{0,2},{1,3},{2,0},{3,1},{4,6},{5,7},{6,4},{7,5},{8,10},{9,11},{10,... | collective-permute-start | bytes 589832 | tf_op jit(solution)/shard_map/ppermute | solution.py:358
  15.1 4.1 %copy-start.1 = (bf16[384,128]{1,0:T(8,128)(2,1)S(1)}, bf16[384,128]{1,0:T(8,128)(2,1)}, u32[]{:S(2)}) copy-start(bf16[384,128]{1,0:T(8,128)(2,1)} %get-tuple-element.13.refs_0_) | copy-start | bytes 294916
  15.1 4.1 %copy-start.2 = (bf16[96,128]{1,0:T(8,128)(2,1)S(1)}, bf16[96,128]{1,0:T(8,128)(2,1)}, u32[]{:S(2)}) copy-start(bf16[96,128]{1,0:T(8,128)(2,1)} %get-tuple-element.16.refs_4_) | copy-start | bytes 73732
  17.2 2.1 %collective-permute-start.6 = (bf16[576,128]{1,0:T(8,128)(2,1)S(1)}, bf16[576,128]{1,0:T(8,128)(2,1)S(1)}, u32[]{:S(2)}, u32[]{:S(2)}) collective-permute-start(bf16[576,128]{1,0:T(8,128)(2,1)S(1)} %pack.5), channel_id=1, source_target_pairs={{0,1},{1,0},{2,3},{3,2},{4,5},{5,4},{6,7},{7,6},{8,9},{9,8},{10,11... | collective-permute-start | bytes 442376 | tf_op jit(solution)/shard_map/ppermute | solution.py:358
  17.3 5.2 %collective-permute-start.2 = (bf16[384,128]{1,0:T(8,128)(2,1)S(1)}, bf16[384,128]{1,0:T(8,128)(2,1)S(1)}, u32[]{:S(2)}, u32[]{:S(2)}) collective-permute-start(bf16[384,128]{1,0:T(8,128)(2,1)S(1)} %collective-permute-done.1.refs_0_.refs_1_), channel_id=1, source_target_pairs={{0,2},{1,3},{2,0},{3,1},{4,6},{5,7},{6,4},{7,5},{8,10},{9,11},{10,... | collective-permute-start | bytes 294920 | tf_op jit(solution)/shard_map/ppermute | solution.py:358
  19.1 3.5 %collective-permute-start.8 = (bf16[768,128]{1,0:T(8,128)(2,1)S(1)}, bf16[768,128]{1,0:T(8,128)(2,1)S(1)}, u32[]{:S(2)}, u32[]{:S(2)}) collective-permute-start(bf16[768,128]{1,0:T(8,128)(2,1)S(1)} %pack.6.refs_0_.refs_4_), channel_id=1, source_target_pairs={{0,1},{1,0},{2,3},{3,2},{4,5},{5,4},{6,7},{7,6},{8,9},{9,8},{10,11... | collective-permute-start | bytes 589832 | tf_op jit(solution)/shard_map/ppermute | solution.py:358
  20.8 1.8 %collective-permute-start.10 = (bf16[768,128]{1,0:T(8,128)(2,1)S(1)}, bf16[768,128]{1,0:T(8,128)(2,1)S(1)}, u32[]{:S(2)}, u32[]{:S(2)}) collective-permute-start(bf16[768,128]{1,0:T(8,128)(2,1)S(1)} %pack.7), channel_id=1, source_target_pairs={{0,1},{1,0},{2,3},{3,2},{4,5},{5,4},{6,7},{7,6},{8,9},{9,8},{10,11... | collective-permute-start | bytes 589832 | tf_op jit(solution)/shard_map/ppermute | solution.py:358
  22.5 1.7 %collective-permute-start.3 = (bf16[768,128]{1,0:T(8,128)(2,1)S(1)}, bf16[768,128]{1,0:T(8,128)(2,1)S(1)}, u32[]{:S(2)}, u32[]{:S(2)}) collective-permute-start(bf16[768,128]{1,0:T(8,128)(2,1)S(1)} %pack.4), channel_id=1, source_target_pairs={{0,1},{1,0},{2,3},{3,2},{4,5},{5,4},{6,7},{7,6},{8,9},{9,8},{10,11... | collective-permute-start | bytes 589832 | tf_op jit(solution)/shard_map/ppermute | solution.py:358
